TPU v7x, 32 devices: a whole 2x2x4 slice. The times are simulated.
32 devices in a mesh: dp: 2 (over y), ctx: 4 (over z), tp: 4 (over x, core).
Axes of the slice: x: 2, y: 2, z: 4, core: 2. Of those that a mesh axis runs over, the one named last changes fastest.
Arguments:
- tokens: bfloat16 [24576, 768], P(('dp', 'ctx', 'tp')), may hold values from -6 to 6
- cotangent: bfloat16 [24576, 768], P(('dp', 'ctx', 'tp')), may hold values from -6 to 6
- gains: float32 [2, 768], replicated, may hold values from 0.1 to 1.9
- qkv_weight: bfloat16 [3, 768, 768], P(None, ('dp', 'ctx'), 'tp'), may hold values from -0.21875 to 0.21875
- proj_weight: bfloat16 [768, 768], P('tp', ('dp', 'ctx')), may hold values from -3 to 3
- router_weight: bfloat16 [768, 8], P(('dp', 'ctx')), may hold values from -0.15625 to 0.15625
- expert_up: bfloat16 [8, 768, 3072], P(('dp', 'tp'), None, 'ctx'), may hold values from -0.21875 to 0.21875
- expert_down: bfloat16 [8, 3072, 768], P(('dp', 'tp'), 'ctx'), may hold values from -1.1953125 to 1.1953125
- expert_ids: int32 [24576, 1], P(('dp', 'ctx', 'tp')), may hold values from 0 to 7
- slot_order: int32 [32, 768], P(('dp', 'ctx', 'tp')), may hold values from 0 to 767, each once within a row
- segment_ids: int32 [96], P(('dp', 'ctx')), may hold values from 0 to 5
Outputs:
- output: bfloat16 [24576, 768], P(('dp', 'ctx', 'tp'))
- grad_tokens: float32 [24576, 768], P(('dp', 'ctx', 'tp'))
- grad_gains: float32 [2, 768], P(None, ('dp', 'ctx'))
- grad_qkv: float32 [3, 768, 768], P(None, ('dp', 'ctx'), 'tp')
- grad_proj: float32 [768, 768], P('tp', ('dp', 'ctx'))
- grad_router: float32 [768, 8], P(('dp', 'ctx'))
- grad_up: float32 [8, 768, 3072], P(('dp', 'tp'), None, 'ctx')
- grad_down: float32 [8, 3072, 768], P(('dp', 'tp'), 'ctx')
Inputs may be any that keep to these rules, and one draw needn't show every extreme that they name: `slot_order`: each row lists the 768 tokens of one device, from the first to take a slot to the last. `segment_ids`: continuations are numbered within their index of dp, ctx index first.
All inputs are finite; a program needn't handle non-finite values.
Results may differ from a plain program's by a relative error of at most 0.017.
Values may be sent and summed in bfloat16 or wider, within the bound.
No kernel may reach another device: no remote copies, remote signals or barrier semaphores. Data moves between devices by JAX's collectives and lax.ppermute only.
A program may use at most 256 MiB of HBM per device.

v0:
```python
import jax
import jax.numpy as jnp
from jax import lax
from jax.sharding import PartitionSpec as P

D = 768
HD = 64
EXP_DEV = 1
PLEN = 1024
CLEN = 128
CONTS = 8


EPSILON = 1e-06
NEGATIVE = -1e30
PRECISE = lax.Precision.HIGHEST


def rms_unit(values):
    factor = lax.rsqrt(jnp.mean(values * values, axis=-1, keepdims=True) + EPSILON)
    return (values * factor, factor)


def rms_backward(grad_normed, unit_part, factor, gain):
    scaled = grad_normed * gain
    inner = jnp.mean(scaled * unit_part, axis=-1, keepdims=True)
    return (factor * (scaled - unit_part * inner), jnp.sum(grad_normed * unit_part, axis=0))


def masked_scores(queries, key_rows, visible):
    scores = (
        jnp.einsum("brhe,bkhe->bhrk", queries, key_rows, preferred_element_type=jnp.float32) * 0.125
    )
    return jnp.where(visible, scores, NEGATIVE)


def attend_forward(queries, key_rows, value_rows, visible):
    scores = masked_scores(queries, key_rows, visible)
    peak = jnp.max(scores, axis=-1, keepdims=True)
    shifted = jnp.exp(scores - peak)
    total = jnp.sum(shifted, axis=-1, keepdims=True)
    weights = (shifted / total).astype(jnp.bfloat16)
    mixed = jnp.einsum("bhrk,bkhe->brhe", weights, value_rows, preferred_element_type=jnp.float32)
    return (mixed.astype(jnp.bfloat16), peak + jnp.log(total))


def attend_backward(queries, key_rows, value_rows, visible, log_total, grad_mixed):
    weights = jnp.exp(masked_scores(queries, key_rows, visible) - log_total)
    grad_weights = jnp.einsum(
        "brhe,bkhe->bhrk", grad_mixed, value_rows, preferred_element_type=jnp.float32
    )
    centre = jnp.sum(weights * grad_weights, axis=-1, keepdims=True)
    grad_scores = (weights * (grad_weights - centre)).astype(jnp.bfloat16)
    grad_queries = (
        jnp.einsum("bhrk,bkhe->brhe", grad_scores, key_rows, preferred_element_type=jnp.float32)
        * 0.125
    )
    grad_keys = (
        jnp.einsum("bhrk,brhe->bkhe", grad_scores, queries, preferred_element_type=jnp.float32)
        * 0.125
    )
    grad_values = jnp.einsum(
        "bhrk,brhe->bkhe",
        weights.astype(jnp.bfloat16),
        grad_mixed,
        preferred_element_type=jnp.float32,
    )
    return (grad_queries, grad_keys, grad_values)


def expert_forward(arrived_rows, weight_up, weight_down):
    hidden_pre = jnp.einsum(
        "sxcd,xdf->sxcf", arrived_rows, weight_up, preferred_element_type=jnp.float32
    )
    hidden = jax.nn.gelu(hidden_pre).astype(jnp.bfloat16)
    produced = jnp.einsum("sxcf,xfd->sxcd", hidden, weight_down, preferred_element_type=jnp.float32)
    return (hidden_pre, hidden, produced)


def expert_backward(arrived_rows, hidden_pre, hidden, grad_rows, weight_up, weight_down):
    grad_hidden = jnp.einsum(
        "sxcd,xfd->sxcf", grad_rows, weight_down, preferred_element_type=jnp.float32
    )
    slope = jax.vjp(jax.nn.gelu, hidden_pre)[1]
    grad_pre = slope(grad_hidden)[0].astype(jnp.bfloat16)
    grad_down = jnp.einsum("sxcf,sxcd->xfd", hidden, grad_rows, preferred_element_type=jnp.float32)
    grad_up = jnp.einsum(
        "sxcd,sxcf->xdf", arrived_rows, grad_pre, preferred_element_type=jnp.float32
    )
    grad_arrived = jnp.einsum(
        "sxcf,xdf->sxcd", grad_pre, weight_up, preferred_element_type=jnp.float32
    )
    return (grad_arrived, grad_up, grad_down)


def routed(slots):
    moved = lax.all_to_all(slots, ("dp", "tp"), split_axis=0, concat_axis=0, tiled=True)
    return moved


def side_terms(gain_one, gain_two, router_part, tp_count):
    gain_terms = jnp.broadcast_to(
        jnp.stack([gain_one, gain_two])[None], (tp_count, 2, gain_one.shape[0])
    )
    router_terms = jnp.broadcast_to(router_part[None], (tp_count,) + router_part.shape)
    return (gain_terms, router_terms)


def shards(
    tokens,
    cotangent,
    gains,
    qkv_weight,
    proj_weight,
    router_weight,
    expert_up,
    expert_down,
    expert_ids,
    slot_order,
    segment_ids,
):
    ctx_count = lax.axis_size("ctx")
    ctx_index = lax.axis_index("ctx")
    tp_count = lax.axis_size("tp")
    tok_dev = tokens.shape[0]
    expert_count = router_weight.shape[1]
    capacity = 5 * tok_dev // (4 * expert_count)
    prompt_rows = PLEN // ctx_count
    conts_here = segment_ids.shape[0]
    prompts_here = conts_here * ctx_count // CONTS
    head_rows = prompts_here * prompt_rows
    local_width = qkv_weight.shape[2]
    local_heads = local_width // HD
    full_qkv, full_proj, full_router = (
        lax.all_gather(qkv_weight, ("dp", "ctx"), axis=1, tiled=True),
        lax.all_gather(proj_weight, ("dp", "ctx"), axis=1, tiled=True),
        lax.all_gather(router_weight, ("dp", "ctx"), axis=0, tiled=True),
    )
    block_rows = lax.all_gather(tokens, "tp", axis=0, tiled=True)
    unit_one, factor_one = rms_unit(block_rows.astype(jnp.float32))
    normed_one = (gains[0] * unit_one).astype(jnp.bfloat16)
    projected = jnp.einsum(
        "rd,jdc->jrc", normed_one, full_qkv, preferred_element_type=jnp.float32
    ).astype(jnp.bfloat16)
    prompt_shape = (prompts_here, prompt_rows, local_heads, HD)
    cont_shape = (conts_here, CLEN, local_heads, HD)
    query_prompt = projected[0, :head_rows].reshape(prompt_shape)
    key_prompt = projected[1, :head_rows].reshape(prompt_shape)
    value_prompt = projected[2, :head_rows].reshape(prompt_shape)
    query_cont = projected[0, head_rows:].reshape(cont_shape)
    key_cont = projected[1, head_rows:].reshape(cont_shape)
    value_cont = projected[2, head_rows:].reshape(cont_shape)
    keys_all, values_all = (
        lax.all_gather(key_prompt, "ctx", axis=1, tiled=True),
        lax.all_gather(value_prompt, "ctx", axis=1, tiled=True),
    )
    query_pos = ctx_index * prompt_rows + jnp.arange(prompt_rows)
    prompt_visible = query_pos[:, None] >= jnp.arange(PLEN)[None, :]
    columns = jnp.arange(PLEN + CLEN)
    cont_visible = (columns[None, :] < PLEN) | (
        columns[None, :] - PLEN <= jnp.arange(CLEN)[:, None]
    )
    cont_keys = jnp.concatenate([jnp.take(keys_all, segment_ids, axis=0), key_cont], axis=1)
    cont_values = jnp.concatenate([jnp.take(values_all, segment_ids, axis=0), value_cont], axis=1)
    mixed_prompt, total_prompt = attend_forward(query_prompt, keys_all, values_all, prompt_visible)
    mixed_cont, total_cont = attend_forward(query_cont, cont_keys, cont_values, cont_visible)
    attended = jnp.concatenate(
        [mixed_prompt.reshape(head_rows, local_width), mixed_cont.reshape(-1, local_width)], axis=0
    )
    branch = lax.psum_scatter(
        jnp.dot(attended, full_proj, preferred_element_type=jnp.float32),
        "tp",
        scatter_dimension=0,
        tiled=True,
    )
    middle = tokens.astype(jnp.float32) + branch
    unit_two, factor_two = rms_unit(middle)
    normed_two = (gains[1] * unit_two).astype(jnp.bfloat16)
    logits = jnp.dot(normed_two, full_router, preferred_element_type=jnp.float32)
    router_probs = jax.nn.softmax(logits, axis=-1)
    chosen = expert_ids[:, 0]
    expert_range = jnp.arange(expert_count)
    chosen_hot = chosen[:, None] == expert_range[None, :]
    gate_value = jnp.sum(jnp.where(chosen_hot, router_probs, 0.0), axis=-1)
    priority = slot_order[0]
    sorted_hot = (jnp.take(chosen, priority)[:, None] == expert_range[None, :]).astype(jnp.int32)
    earlier = jnp.cumsum(sorted_hot, axis=0) - sorted_hot
    sorted_rank = jnp.sum(earlier * sorted_hot, axis=1)
    slot_rank = jnp.zeros_like(chosen).at[priority].set(sorted_rank)
    slot_hot = slot_rank[:, None] == jnp.arange(capacity)[None, :]
    dispatch = (chosen_hot[:, :, None] & slot_hot[:, None, :]).astype(jnp.bfloat16)
    slots = jnp.einsum(
        "tec,td->ecd", dispatch, normed_two, preferred_element_type=jnp.float32
    ).astype(jnp.bfloat16)
    arrived = routed(slots)
    full_up, full_down = (
        lax.all_gather(expert_up, "ctx", axis=2, tiled=True),
        lax.all_gather(expert_down, "ctx", axis=1, tiled=True),
    )
    arrived_rows = arrived.reshape(-1, EXP_DEV, capacity, D)
    hidden_pre, hidden, produced = expert_forward(arrived_rows, full_up, full_down)
    returned = produced.astype(jnp.bfloat16).reshape(arrived.shape)
    back_rows = routed(returned)
    routed_rows = jnp.einsum("tec,ecd->td", dispatch, back_rows, preferred_element_type=jnp.float32)
    output = (middle + gate_value[:, None] * routed_rows).astype(jnp.bfloat16)
    upstream = cotangent.astype(jnp.float32)
    grad_gate = jnp.sum(upstream * routed_rows, axis=-1)
    weighted = (gate_value[:, None] * upstream).astype(jnp.bfloat16)
    grad_slots = jnp.einsum(
        "tec,td->ecd", dispatch, weighted, preferred_element_type=jnp.float32
    ).astype(jnp.bfloat16)
    grad_arrived = routed(grad_slots)
    rows_grad, up_part, down_part = expert_backward(
        arrived_rows,
        hidden_pre,
        hidden,
        grad_arrived.reshape(arrived_rows.shape),
        full_up,
        full_down,
    )
    grad_up, grad_down = (
        lax.psum_scatter(
            up_part.astype(jnp.bfloat16), "ctx", scatter_dimension=2, tiled=True
        ).astype(jnp.float32),
        lax.psum_scatter(
            down_part.astype(jnp.bfloat16), "ctx", scatter_dimension=1, tiled=True
        ).astype(jnp.float32),
    )
    grad_back = rows_grad.astype(jnp.bfloat16).reshape(arrived.shape)
    grad_returned = routed(grad_back)
    grad_second = jnp.einsum(
        "tec,ecd->td", dispatch, grad_returned, preferred_element_type=jnp.float32
    )
    grad_logits = (
        (grad_gate * gate_value)[:, None] * (chosen_hot.astype(jnp.float32) - router_probs)
    ).astype(jnp.bfloat16)
    router_part = jnp.einsum(
        "td,te->de", normed_two, grad_logits, preferred_element_type=jnp.float32
    )
    grad_second = grad_second + jnp.einsum(
        "te,de->td", grad_logits, full_router, preferred_element_type=jnp.float32
    )
    middle_part, gain_two = rms_backward(grad_second, unit_two, factor_two, gains[1])
    grad_middle = upstream + middle_part
    grad_low = grad_middle.astype(jnp.bfloat16)
    grad_branch = lax.all_gather(grad_low, "tp", axis=0, tiled=True)
    proj_part = jnp.einsum("rc,rd->cd", attended, grad_branch, preferred_element_type=jnp.float32)
    grad_attended = jnp.einsum(
        "rd,cd->rc", grad_branch, full_proj, preferred_element_type=jnp.float32
    ).astype(jnp.bfloat16)
    prompt_grads = attend_backward(
        query_prompt,
        keys_all,
        values_all,
        prompt_visible,
        total_prompt,
        grad_attended[:head_rows].reshape(prompt_shape),
    )
    cont_grads = attend_backward(
        query_cont,
        cont_keys,
        cont_values,
        cont_visible,
        total_cont,
        grad_attended[head_rows:].reshape(cont_shape),
    )
    segment_hot = (segment_ids[:, None] == jnp.arange(prompts_here)[None, :]).astype(jnp.float32)
    key_total = prompt_grads[1] + jnp.einsum(
        "cp,ckhe->pkhe", segment_hot, cont_grads[1][:, :PLEN], precision=PRECISE
    )
    value_total = prompt_grads[2] + jnp.einsum(
        "cp,ckhe->pkhe", segment_hot, cont_grads[2][:, :PLEN], precision=PRECISE
    )
    key_local, value_local = (
        lax.psum_scatter(key_total, "ctx", scatter_dimension=1, tiled=True),
        lax.psum_scatter(value_total, "ctx", scatter_dimension=1, tiled=True),
    )
    grad_query = jnp.concatenate(
        [prompt_grads[0].reshape(head_rows, local_width), cont_grads[0].reshape(-1, local_width)],
        axis=0,
    )
    grad_key = jnp.concatenate(
        [
            key_local.reshape(head_rows, local_width),
            cont_grads[1][:, PLEN:].reshape(-1, local_width),
        ],
        axis=0,
    )
    grad_value = jnp.concatenate(
        [
            value_local.reshape(head_rows, local_width),
            cont_grads[2][:, PLEN:].reshape(-1, local_width),
        ],
        axis=0,
    )
    grad_projected = jnp.stack([grad_query, grad_key, grad_value]).astype(jnp.bfloat16)
    qkv_part = jnp.einsum(
        "rd,jrc->jdc", normed_one, grad_projected, preferred_element_type=jnp.float32
    )
    grad_first = jnp.einsum(
        "jrc,jdc->rd", grad_projected, full_qkv, preferred_element_type=jnp.float32
    )
    rows_part, gain_one = rms_backward(grad_first, unit_one, factor_one, gains[0])
    gain_terms, router_terms = side_terms(gain_one, gain_two, router_part, tp_count)
    row_sums, gain_sums, router_sums = (
        lax.psum_scatter(
            rows_part.astype(jnp.bfloat16), "tp", scatter_dimension=0, tiled=True
        ).astype(jnp.float32),
        lax.psum_scatter(
            gain_terms.astype(jnp.bfloat16), "tp", scatter_dimension=0, tiled=True
        ).astype(jnp.float32),
        lax.psum_scatter(
            router_terms.astype(jnp.bfloat16), "tp", scatter_dimension=0, tiled=True
        ).astype(jnp.float32),
    )
    grad_tokens = row_sums + grad_middle
    grad_qkv, grad_proj, grad_router, grad_gains = (
        lax.psum_scatter(qkv_part, ("dp", "ctx"), scatter_dimension=1, tiled=True),
        lax.psum_scatter(proj_part, ("dp", "ctx"), scatter_dimension=1, tiled=True),
        lax.psum_scatter(router_sums[0], ("dp", "ctx"), scatter_dimension=0, tiled=True),
        lax.psum_scatter(gain_sums[0], ("dp", "ctx"), scatter_dimension=1, tiled=True),
    )
    return (output, grad_tokens, grad_gains, grad_qkv, grad_proj, grad_router, grad_up, grad_down)


def solution(mesh):
    in_specs = (
        P(("dp", "ctx", "tp"), None),
        P(("dp", "ctx", "tp"), None),
        P(),
        P(None, ("dp", "ctx"), "tp"),
        P("tp", ("dp", "ctx")),
        P(("dp", "ctx"), None),
        P(("dp", "tp"), None, "ctx"),
        P(("dp", "tp"), "ctx", None),
        P(("dp", "ctx", "tp"), None),
        P(("dp", "ctx", "tp"), None),
        P(("dp", "ctx")),
    )
    out_specs = (
        P(("dp", "ctx", "tp"), None),
        P(("dp", "ctx", "tp"), None),
        P(None, ("dp", "ctx")),
        P(None, ("dp", "ctx"), "tp"),
        P("tp", ("dp", "ctx")),
        P(("dp", "ctx"), None),
        P(("dp", "tp"), None, "ctx"),
        P(("dp", "tp"), "ctx", None),
    )
    return jax.shard_map(shards, mesh=mesh, in_specs=in_specs, out_specs=out_specs, check_vma=False)
```

profile of v0, /device:TPU:25, one launch (start us, length us, event | category | flops | bytes accessed | tf_op | source)
XLA Modules:
  0.0 1330.7 jit_solution(14185363123010951915)
XLA Ops:
  9.0 33.0 %all_gather.28 = bf16[3,768,192]{2,0,1:T(4,128)(2,1)S(1)} all-gather(bf16[3,96,192]{2,0,1:T(4,128)(2,1)S(1)} %copy.74), channel_id=1, replica_groups=mesh['dp'=2,'ctx'=4,'tp'=4] {'dp','ctx'}, dimensions={1}, use_global_device_ids=true | all-gather | bytes 995328 | tf_op jit(solution)/shard_map/all_gather | solution.py:135
  42.9 5.5 all-gather.8.cloned.1.call-done
  48.5 3.5 fusion.33
  61.8 31.9 %all_gather.31 = bf16[192,768]{0,1:T(8,128)(2,1)S(1)} all-gather(bf16[192,96]{0,1:T(8,128)(2,1)S(1)} %copy.84), channel_id=1, replica_groups=mesh['dp'=2,'ctx'=4,'tp'=4] {'dp','ctx'}, dimensions={1}, use_global_device_ids=true | all-gather | bytes 331776 | tf_op jit(solution)/shard_map/all_gather | solution.py:136
  100.6 14.1 %all-gather.12.cloned.1.call-done = bf16[6,1024,3,64]{1,3,2,0:T(8,128)(2,1)} async-done(((bf16[6,256,3,64]{1,3,2,0:T(8,128)(2,1)}), bf16[6,1024,3,64]{1,3,2,0:T(8,128)(2,1)}) %all-gather.12.cloned.1.call-update) | async-done | bytes 2359312 | tf_op jit(solution)/shard_map/all_gather | solution.py:154
  114.7 9.9 fusion.174
  124.6 9.9 fusion.1
  134.5 31.3 %all-gather.10.cloned.1.call-done = bf16[6,1024,3,64]{1,3,2,0:T(8,128)(2,1)} async-done(((bf16[6,256,3,64]{1,3,2,0:T(8,128)(2,1)}), bf16[6,1024,3,64]{1,3,2,0:T(8,128)(2,1)}) %all-gather.10.cloned.1.call-update) | async-done | bytes 2359312 | tf_op jit(solution)/shard_map/all_gather | solution.py:155
  165.9 9.3 fusion.128
  176.5 4.9 gather_fusion.1
  184.6 4.7 broadcast_select_fusion.1
  189.3 13.7 %fusion.173 = (f32[12,3,128]{2,1,0:T(4,128)S(1)}, f32[12,3,128,1152]{3,2,1,0:T(8,128)}) fusion(bf16[12,128,3,64]{1,3,2,0:T(8,128)(2,1)} %copy.81, bf16[12,1024,3,64]{1,3,2,0:T(8,128)(2,1)S(1)} %get-tuple-element.52, bf16[12,128,3,64]{1,0,3,2:T(8,128)(2,1)} %reshape_squeeze.22, pred[128,1152]{1,0:T(8,128)(4,1)} %fusion.133), kind=kOutput, calls=%fused_computation.228 | convolution fusion | flops 706014720 | bytes 27297792 | tf_op jit(solution)/shard_map/brhe,bkhe->bhrk/dot_general | solution.py:32
  203.0 9.6 fusion
  213.2 9.4 fusion.125
  224.2 5.1 fusion.176
  240.4 68.5 %reduce-scatter.20.cloned.1.call-done = f32[768,768]{1,0:T(8,128)} async-done(((f32[3072,768]{1,0:T(8,128)}), f32[768,768]{1,0:T(8,128)}) %reduce-scatter.20.cloned.1.call-update) | async-done | bytes 2359312 | tf_op jit(solution)/shard_map/reduce_scatter | solution.py:170
  314.2 4.9 all-to-all-start
  319.1 22.8 %all-gather = bf16[8,96,8]{1,2,0:T(8,128)(2,1)S(1)} all-gather(bf16[1,96,8]{1,2,0:T(8,128)(2,1)S(1)} %bitcast.314), channel_id=1, replica_groups=mesh['dp'=2,'ctx'=4,'tp'=4] {'dp','ctx'}, dimensions={0}, use_global_device_ids=true | all-gather | bytes 13824 | tf_op jit(solution)/shard_map/all_gather | solution.py:137
  345.5 3.9 fusion.90
  349.4 9.7 all-to-all-start.2
  359.1 38.5 %all-gather.14.cloned.1.call-done = bf16[1,768,3072]{2,1,0:T(8,128)(2,1)} async-done(((bf16[1,768,768]{2,1,0:T(8,128)(2,1)}), bf16[1,768,3072]{2,1,0:T(8,128)(2,1)}) %all-gather.14.cloned.1.call-update) | async-done | bytes 4718608 | tf_op jit(solution)/shard_map/all_gather | solution.py:197
  397.6 12.4 fusion.67
  409.9 76.8 %all-gather.16.cloned.1.call-done = bf16[1,3072,768]{2,1,0:T(8,128)(2,1)} async-done(((bf16[1,768,768]{2,1,0:T(8,128)(2,1)}), bf16[1,3072,768]{2,1,0:T(8,128)(2,1)}) %all-gather.16.cloned.1.call-update) | async-done | bytes 4718608 | tf_op jit(solution)/shard_map/all_gather | solution.py:198
  486.7 13.8 %fusion.93 = bf16[8,120,768]{2,1,0:T(8,128)(2,1)} fusion(bf16[1,3072,768]{2,1,0:T(8,128)(2,1)} %all-gather.16.cloned.1.call-done, f32[8,120,3072]{2,1,0:T(8,128)} %fusion.67), kind=kOutput, calls=%fused_computation.118 | convolution fusion | flops 4557127680 | bytes 17989632 | tf_op jit(solution)/shard_map/sxcf,xfd->sxcd/dot_general | solution.py:76
  500.6 5.1 all-to-all-start.1
  505.6 14.5 %fusion.14 = bf16[8,1,120,3072]{3,2,0,1:T(8,128)(2,1)S(1)} fusion(f32[8,120,3072]{2,1,0:T(8,128)} %fusion.67, bf16[8,120,768]{2,1,0:T(8,128)(2,1)} %all-to-all-done.2, bf16[1,3072,768]{2,1,0:T(8,128)(2,1)} %all-gather.16.cloned.1.call-done), kind=kOutput, calls=%fused_computation.32 | convolution fusion | flops 4588830720 | bytes 23887872 | tf_op jit(solution)/shard_map/sxcd,xfd->sxcf/dot_general | solution.py:81
  522.7 8.3 fusion.98
  531.1 4.2 all-to-all-start.3
  535.6 4.8 fusion.80
  543.0 8.8 all-to-all-done.3
  551.8 5.0 multiply_reduce_fusion.2
  562.5 37.9 %all-gather.18.cloned.1.call-done = bf16[3072,768]{1,0:T(8,128)(2,1)} async-done(((bf16[768,768]{1,0:T(8,128)(2,1)}), bf16[3072,768]{1,0:T(8,128)(2,1)}) %all-gather.18.cloned.1.call-update) | async-done | bytes 4718608 | tf_op jit(solution)/shard_map/all_gather | solution.py:246
  600.4 4.1 convolution_convert_fusion
  605.6 12.1 fusion.38
  617.7 3.7 slice-done
  621.4 10.0 fusion.4
  631.4 10.6 bitcast_add_fusion
  642.0 15.5 %multiply_reduce_fusion = (f32[12,3,128]{2,1,0:T(4,128)S(1)}, f32[12,3,128,1152]{3,2,1,0:T(8,128)}) fusion(f32[12,3,128,1152]{3,2,1,0:T(8,128)} %get-tuple-element.54, f32[12,3,128]{2,1,0:T(4,128)S(1)} %log_add_fusion, bf16[12,128,3,64]{1,3,2,0:T(8,128)(2,1)S(1)} %copy-done.23, bf16[12,1024,3,64]{1,3,2,0:T(8,128)(2,1)} %copy-done.8, ...), kind=kOutput, calls=%fused_computation.5 | convolution fusion | flops 706014720 | bytes 48402432 | tf_op jit(solution)/shard_map/brhe,bkhe->bhrk/dot_general | solution.py:49
  657.6 15.1 %multiply_convert_fusion = bf16[12,3,128,1152]{3,2,1,0:T(8,128)(2,1)S(1)} fusion(f32[12,3,128,1152]{3,2,1,0:T(8,128)} %get-tuple-element.63, f32[12,3,128,1152]{3,2,1,0:T(8,128)} %get-tuple-element.54, f32[12,3,128]{2,1,0:T(4,128)S(1)} %get-tuple-element.62, f32[12,3,128]{2,1,0:T(4,128)S(1)} %log_add_fusion), kind=kLoop, calls=%fused_computation.4 | loop fusion | flops 21233664 | bytes 53121024 | tf_op jit(solution)/shard_map/convert_element_type | solution.py:53
  672.7 4.0 copy-done.4
  678.4 3.9 copy-done.5
  682.3 5.0 slice.83
  687.3 18.3 %fusion.6 = f32[6,1024,3,64]{1,0,3,2:T(8,128)S(1)} fusion(f32[12,1024,3,64]{1,3,2,0:T(8,128)} %slice.83, s32[12]{0:T(128)S(1)} %copy-done.63), kind=kOutput, calls=%fused_computation.24 | convolution fusion | flops 169869376 | bytes 14155824 | tf_op jit(solution)/shard_map/cp,ckhe->pkhe/dot_general | solution.py:268
  705.6 15.8 %multiply_reduce_fusion.1 = (f32[6,3,256]{2,1,0:T(4,128)S(1)}, f32[6,3,256,1024]{3,2,1,0:T(8,128)}) fusion(f32[6,3,256,1024]{3,2,1,0:T(8,128)} %get-tuple-element.56, f32[6,3,256]{2,1,0:T(4,128)S(1)} %log_add_fusion.1, bf16[6,1024,3,64]{1,3,2,0:T(8,128)(2,1)S(1)} %copy-done.3, bf16[6,256,3,64]{1,0,3,2:T(8,128)(2,1)S(1)} %reshape.279), kind=kOutput, calls=%fused_computation.11 | convolution fusion | flops 618130944 | bytes 40734720 | tf_op jit(solution)/shard_map/brhe,bkhe->bhrk/dot_general | solution.py:49
  721.4 13.5 %multiply_convert_fusion.1 = bf16[6,3,256,1024]{3,2,1,0:T(8,128)(2,1)S(1)} fusion(f32[6,3,256,1024]{3,2,1,0:T(8,128)} %get-tuple-element.65, f32[6,3,256,1024]{3,2,1,0:T(8,128)} %get-tuple-element.56, f32[6,3,256]{2,1,0:T(4,128)S(1)} %get-tuple-element.64, f32[6,3,256]{2,1,0:T(4,128)S(1)} %log_add_fusion.1), kind=kLoop, calls=%fused_computation.10 | loop fusion | flops 18874368 | bytes 47222784 | tf_op jit(solution)/shard_map/convert_element_type | solution.py:53
  734.9 3.6 copy-done.2
  738.5 6.3 bitcast_add_fusion.1
  746.7 11.8 fusion.72
  758.6 9.2 fusion.69
  772.3 9.5 fusion.127
  783.5 7.0 fusion.126
  796.0 34.2 %reduce-scatter.22.cloned.1.call-done = f32[6,256,3,64]{1,3,2,0:T(8,128)} async-done(((f32[6,1024,3,64]{1,3,2,0:T(8,128)}), f32[6,256,3,64]{1,3,2,0:T(8,128)}) %reduce-scatter.22.cloned.1.call-update) | async-done | bytes 1179664 | tf_op jit(solution)/shard_map/reduce_scatter | solution.py:275
  835.0 7.2 fusion.32
  842.2 10.4 all-reduce
  854.4 7.4 fusion.105
  867.6 8.6 fusion.31
  876.3 16.8 %reduce-scatter.40.cloned.1.call-done = f32[96,8]{1,0:T(8,128)} async-done(((f32[768,8]{1,0:T(8,128)}), f32[96,8]{1,0:T(8,128)}) %reduce-scatter.40.cloned.1.call-update) | async-done | bytes 3088
  894.5 87.7 %reduce-scatter.32.cloned.1.call-done = bf16[1,768,768]{2,1,0:T(8,128)(2,1)} async-done(((bf16[1,3072,768]{2,1,0:T(8,128)(2,1)}), bf16[1,768,768]{2,1,0:T(8,128)(2,1)}) %reduce-scatter.32.cloned.1.call-update) | async-done | bytes 1179664 | tf_op jit(solution)/shard_map/reduce_scatter | solution.py:225
  985.1 85.4 %reduce-scatter.30.cloned.1.call-done = bf16[1,768,768]{2,1,0:T(8,128)(2,1)} async-done(((bf16[1,768,3072]{2,1,0:T(8,128)(2,1)}), bf16[1,768,768]{2,1,0:T(8,128)(2,1)}) %reduce-scatter.30.cloned.1.call-update) | async-done | bytes 1179664 | tf_op jit(solution)/shard_map/reduce_scatter | solution.py:222
  1073.3 61.4 %reduce-scatter.38.cloned.1.call-done = f32[96,192]{1,0:T(8,128)} async-done(((f32[768,192]{1,0:T(8,128)}), f32[96,192]{1,0:T(8,128)}) %reduce-scatter.38.cloned.1.call-update) | async-done | bytes 73744
  1136.3 61.6 %reduce-scatter.34.cloned.1.call-done = f32[96,2]{1,0:T(8,128)} async-done(((f32[768,2]{1,0:T(8,128)}), f32[96,2]{1,0:T(8,128)}) %reduce-scatter.34.cloned.1.call-update) | async-done | bytes 784
  1199.4 68.0 %reduce-scatter.36.cloned.1.call-done = f32[96,576]{1,0:T(8,128)} async-done(((f32[768,576]{1,0:T(8,128)}), f32[96,576]{1,0:T(8,128)}) %reduce-scatter.36.cloned.1.call-update) | async-done | bytes 221200
  1271.0 48.5 %reduce-scatter.26.cloned.1.call-done = bf16[768,768]{1,0:T(8,128)(2,1)} async-done(((bf16[3072,768]{1,0:T(8,128)(2,1)}), bf16[768,768]{1,0:T(8,128)(2,1)}) %reduce-scatter.26.cloned.1.call-update) | async-done | bytes 1179664 | tf_op jit(solution)/shard_map/reduce_scatter | solution.py:306
  1319.5 4.5 convert_add_fusion.1
  (292 shorter events, 99.0 us)
Async XLA Ops:
  7.2 35.7 %copy-start.59 = (f32[2,768]{1,0:T(2,128)S(1)}, f32[2,768]{1,0:T(2,128)}, u32[]{:S(2)}) copy-start(f32[2,768]{1,0:T(2,128)} %param.15) | copy-start | bytes 18436
  7.2 41.3 %all-gather.8.cloned.1.call-start = ((), (), s32[]{:S(2)}) async-start(), calls=%async_computation.15 | async-start | bytes 5898240 | tf_op jit(solution)/shard_map/all_gather | solution.py:139
  7.9 106.8 %all-gather.12.cloned.1.call-start = ((), (), s32[]{:S(2)}) async-start(), calls=%async_computation.17 | async-start | bytes 2949120 | tf_op jit(solution)/shard_map/all_gather | solution.py:154
  42.9 12.4 copy-start.26
  42.9 12.4 copy-start.56
  42.9 268.2 %copy-start.38 = (f32[768]{0:T(1024)}, f32[768]{0:T(1024)S(1)}, u32[]{:S(2)}) copy-start(f32[768]{0:T(1024)S(1)} %get-tuple-element.37) | copy-start | bytes 9220
  59.9 106.0 %all-gather.10.cloned.1.call-start = ((), (), s32[]{:S(2)}) async-start(), calls=%async_computation.16 | async-start | bytes 2949120 | tf_op jit(solution)/shard_map/all_gather | solution.py:155
  61.5 247.4 %reduce-scatter.20.cloned.1.call-start = ((), (), s32[]{:S(2)}) async-start(), calls=%async_computation.18 | async-start | bytes 11796480 | tf_op jit(solution)/shard_map/reduce_scatter | solution.py:170
  93.7 129.4 %copy-start.20 = (bf16[192,768]{0,1:T(8,128)(2,1)}, bf16[192,768]{0,1:T(8,128)(2,1)S(1)}, u32[]{:S(2)}) copy-start(bf16[192,768]{0,1:T(8,128)(2,1)S(1)} %all_gather.31) | copy-start | bytes 884740
  99.1 25.5 %copy-start.11 = (bf16[6,256,3,64]{1,0,3,2:T(8,128)(2,1)}, bf16[6,256,3,64]{1,0,3,2:T(8,128)(2,1)S(1)}, u32[]{:S(2)}) copy-start(bf16[6,256,3,64]{1,0,3,2:T(8,128)(2,1)S(1)} %reshape_squeeze.19) | copy-start | bytes 1769476
  124.6 41.3 %copy-start.31 = (f32[6,3,256]{2,1,0:T(4,128)}, f32[6,3,256]{2,1,0:T(4,128)S(1)}, u32[]{:S(2)}) copy-start(f32[6,3,256]{2,1,0:T(4,128)S(1)} %get-tuple-element.55) | copy-start | bytes 55300
  134.5 40.6 %copy-start.36 = (f32[6,3,256]{2,1,0:T(4,128)}, f32[6,3,256]{2,1,0:T(4,128)S(1)}, u32[]{:S(2)}) copy-start(f32[6,3,256]{2,1,0:T(4,128)S(1)} %fusion.1) | copy-start | bytes 55300
  176.5 4.9 copy-start
  189.3 13.7 %copy-start.16 = (bf16[12,1024,3,64]{1,3,2,0:T(8,128)(2,1)}, bf16[12,1024,3,64]{1,3,2,0:T(8,128)(2,1)S(1)}, u32[]{:S(2)}) copy-start(bf16[12,1024,3,64]{1,3,2,0:T(8,128)(2,1)S(1)} %get-tuple-element.52) | copy-start | bytes 14155780
  189.3 23.3 %copy-start.8 = (bf16[12,1024,3,64]{1,3,2,0:T(8,128)(2,1)}, bf16[12,1024,3,64]{1,3,2,0:T(8,128)(2,1)S(1)}, u32[]{:S(2)}) copy-start(bf16[12,1024,3,64]{1,3,2,0:T(8,128)(2,1)S(1)} %get-tuple-element.51) | copy-start | bytes 14155780
  203.0 9.6 copy-start.34
  203.0 10.2 copy-start.22
  213.2 9.8 copy-start.17
  229.3 79.6 %copy-start.13 = (bf16[768,768]{1,0:T(8,128)(2,1)S(1)}, bf16[768,768]{1,0:T(8,128)(2,1)}, u32[]{:S(2)}) copy-start(bf16[768,768]{1,0:T(8,128)(2,1)} %param.13) | copy-start | bytes 3538948
  229.3 168.2 %all-gather.14.cloned.1.call-start = ((), (), s32[]{:S(2)}) async-start(), calls=%async_computation.19 | async-start | bytes 5898240 | tf_op jit(solution)/shard_map/all_gather | solution.py:197
  229.9 256.8 %all-gather.16.cloned.1.call-start = ((), (), s32[]{:S(2)}) async-start(), calls=%async_computation.20 | async-start | bytes 5898240 | tf_op jit(solution)/shard_map/all_gather | solution.py:198
  239.7 71.6 %copy-start.60 = (pred[768,8]{0,1:T(8,128)(4,1)}, pred[768,8]{0,1:T(8,128)(4,1)S(1)}, u32[]{:S(2)}) copy-start(pred[768,8]{0,1:T(8,128)(4,1)S(1)} %iota_compare_fusion.5) | copy-start | bytes 18436
  311.0 245.8 %copy-start.6 = (f32[768,768]{1,0:T(8,128)}, f32[768,768]{1,0:T(8,128)S(1)}, u32[]{:S(2)}) copy-start(f32[768,768]{1,0:T(8,128)S(1)} %get-tuple-element.40) | copy-start | bytes 7077892
  311.8 7.3 copy-start.64
  314.2 35.2 %all-to-all-start = ((bf16[8,120,768]{2,1,0:T(8,128)(2,1)}), bf16[8,120,768]{2,1,0:T(8,128)(2,1)}, u32[]{:S(2)}, u32[]{:S(2)}) async-start(bf16[8,120,768]{2,1,0:T(8,128)(2,1)} %fusion.87), calls=%async_computation.1 | async-start | bytes 2949120 | tf_op jit(solution)/shard_map/all_to_all | solution.py:97
  349.4 151.1 %all-to-all-start.2 = ((bf16[8,120,768]{2,1,0:T(8,128)(2,1)}), bf16[8,120,768]{2,1,0:T(8,128)(2,1)}, u32[]{:S(2)}, u32[]{:S(2)}) async-start(bf16[8,120,768]{2,1,0:T(8,128)(2,1)} %fusion.90), calls=%async_computation.3 | async-start | bytes 2949120 | tf_op jit(solution)/shard_map/all_to_all | solution.py:97
  500.6 30.5 %all-to-all-start.1 = ((bf16[8,120,768]{2,1,0:T(8,128)(2,1)}), bf16[8,120,768]{2,1,0:T(8,128)(2,1)}, u32[]{:S(2)}, u32[]{:S(2)}) async-start(bf16[8,120,768]{2,1,0:T(8,128)(2,1)} %fusion.93), calls=%async_computation.2 | async-start | bytes 2949120 | tf_op jit(solution)/shard_map/all_to_all | solution.py:97
  531.1 20.7 %all-to-all-start.3 = ((bf16[8,120,768]{2,1,0:T(8,128)(2,1)}), bf16[8,120,768]{2,1,0:T(8,128)(2,1)}, u32[]{:S(2)}, u32[]{:S(2)}) async-start(bf16[8,120,768]{2,1,0:T(8,128)(2,1)} %fusion.98), calls=%async_computation.4 | async-start | bytes 2949120 | tf_op jit(solution)/shard_map/all_to_all | solution.py:97
  535.3 65.0 %all-gather.18.cloned.1.call-start = ((), (), s32[]{:S(2)}) async-start(), calls=%async_computation.21 | async-start | bytes 5898240 | tf_op jit(solution)/shard_map/all_gather | solution.py:246
  535.6 4.9 copy-start.52
  535.6 4.9 copy-start.30
  535.6 4.9 copy-start.45
  535.6 4.9 copy-start.55
  543.0 15.2 %copy-start.39 = (f32[768]{0:T(1024)S(1)}, f32[768]{0:T(1024)}, u32[]{:S(2)}) copy-start(f32[768]{0:T(1024)} %copy-done.38) | copy-start | bytes 9220
  551.8 6.4 copy-start.14
  551.8 6.4 copy-start.42
  556.8 4.7 copy-start.33
  559.9 185.1 %reduce-scatter.28.cloned.1.call-start = ((), (), s32[]{:S(2)}) async-start(), calls=%async_computation.25 | async-start | bytes 61440 | tf_op jit(solution)/shard_map/reduce_scatter | solution.py:312
  562.4 231.6 %reduce-scatter.24.cloned.1.call-start = ((), (), s32[]{:S(2)}) async-start(), calls=%async_computation.23 | async-start | bytes 5898240 | tf_op jit(solution)/shard_map/reduce_scatter | solution.py:276
  631.4 10.6 copy-start.23
  657.6 172.6 %reduce-scatter.22.cloned.1.call-start = ((), (), s32[]{:S(2)}) async-start(), calls=%async_computation.22 | async-start | bytes 5898240 | tf_op jit(solution)/shard_map/reduce_scatter | solution.py:275
  657.6 19.1 %copy-start.21 = (bf16[12,128,3,64]{1,0,3,2:T(8,128)(2,1)S(1)}, bf16[12,128,3,64]{1,0,3,2:T(8,128)(2,1)}, u32[]{:S(2)}) copy-start(bf16[12,128,3,64]{1,0,3,2:T(8,128)(2,1)} %reshape_squeeze.22) | copy-start | bytes 1769476
  687.3 18.3 %copy-start.3 = (bf16[6,1024,3,64]{1,3,2,0:T(8,128)(2,1)S(1)}, bf16[6,1024,3,64]{1,3,2,0:T(8,128)(2,1)}, u32[]{:S(2)}) copy-start(bf16[6,1024,3,64]{1,3,2,0:T(8,128)(2,1)} %all-gather.10.cloned.1.call-done) | copy-start | bytes 7077892
  721.4 17.1 %copy-start.12 = (bf16[6,256,3,64]{1,0,3,2:T(8,128)(2,1)S(1)}, bf16[6,256,3,64]{1,0,3,2:T(8,128)(2,1)}, u32[]{:S(2)}) copy-start(bf16[6,256,3,64]{1,0,3,2:T(8,128)(2,1)} %copy-done.11) | copy-start | bytes 1769476
  744.9 148.1 %reduce-scatter.40.cloned.1.call-start = ((), (), s32[]{:S(2)}) async-start(), calls=%async_computation.31 | async-start | bytes 442368
  746.6 235.6 %reduce-scatter.32.cloned.1.call-start = ((), (), s32[]{:S(2)}) async-start(), calls=%async_computation.27 | async-start | bytes 5898240 | tf_op jit(solution)/shard_map/reduce_scatter | solution.py:225
  758.5 311.9 %reduce-scatter.30.cloned.1.call-start = ((), (), s32[]{:S(2)}) async-start(), calls=%async_computation.26 | async-start | bytes 5898240 | tf_op jit(solution)/shard_map/reduce_scatter | solution.py:222
  767.8 4.6 copy-start.28
  767.8 366.9 %reduce-scatter.38.cloned.1.call-start = ((), (), s32[]{:S(2)}) async-start(), calls=%async_computation.30 | async-start | bytes 884736
  781.9 9.2 slice-start.3
  783.5 7.5 slice-start.4
  783.5 7.5 copy-start.19
  794.0 403.9 %reduce-scatter.34.cloned.1.call-start = ((), (), s32[]{:S(2)}) async-start(), calls=%async_computation.28 | async-start | bytes 442368
  795.5 36.9 %slice-start.1 = ((s8[4718592]{0:T(1024)(128)(4,1)}), s8[524288]{0:T(1024)(128)(4,1)S(1)}, s32[]{:S(2)}) async-start(s8[4718592]{0:T(1024)(128)(4,1)} %bitcast.286), calls=%async_computation.33 | async-start | bytes 1048576
  832.1 10.0 copy-start.24
  832.3 9.8 copy-start.25
  854.3 413.0 %reduce-scatter.36.cloned.1.call-start = ((), (), s32[]{:S(2)}) async-start(), calls=%async_computation.29 | async-start | bytes 2211840
  867.5 452.0 %reduce-scatter.26.cloned.1.call-start = ((), (), s32[]{:S(2)}) async-start(), calls=%async_computation.24 | async-start | bytes 5898240 | tf_op jit(solution)/shard_map/reduce_scatter | solution.py:306
  876.2 443.2 %copy-start.7 = (f32[768,768]{1,0:T(8,128)S(1)}, f32[768,768]{1,0:T(8,128)}, u32[]{:S(2)}) copy-start(f32[768,768]{1,0:T(8,128)} %copy-done.6) | copy-start | bytes 7077892
  876.2 443.2 %copy-start.15 = (bf16[768,768]{1,0:T(8,128)(2,1)S(1)}, bf16[768,768]{1,0:T(8,128)(2,1)}, u32[]{:S(2)}) copy-start(bf16[768,768]{1,0:T(8,128)(2,1)} %param.14) | copy-start | bytes 3538948
  876.2 443.2 %copy-start.40 = (f32[768]{0:T(1024)S(1)}, f32[768]{0:T(1024)}, u32[]{:S(2)}) copy-start(f32[768]{0:T(1024)} %copy-done.38) | copy-start | bytes 9220
  876.3 443.2 %copy-start.43 = (f32[768]{0:T(1024)S(1)}, f32[768]{0:T(1024)}, u32[]{:S(2)}) copy-start(f32[768]{0:T(1024)} %copy-done.41) | copy-start | bytes 9220
  876.3 443.2 %copy-start.50 = (f32[768]{0:T(1024)S(1)}, f32[768]{0:T(1024)}, u32[]{:S(2)}) copy-start(f32[768]{0:T(1024)} %copy-done.49) | copy-start | bytes 9220
  876.3 443.2 %copy-start.53 = (f32[768]{0:T(1024)S(1)}, f32[768]{0:T(1024)}, u32[]{:S(2)}) copy-start(f32[768]{0:T(1024)} %copy-done.51) | copy-start | bytes 9220
  (30 other events, 61.2 us)
Sparse Core Ops, SparseCore 0:
  9.6 38.8 all-gather.7
  60.0 54.6 all-gather.11
  116.8 49.0 all-gather.9
  229.4 79.4 reduce-scatter.19
  310.3 87.2 all-gather.13
  399.0 87.6 all-gather.15
  560.0 40.3 all-gather.17
  603.4 18.4 reduce-scatter.27
  657.7 84.3 reduce-scatter.23
  745.0 85.0 reduce-scatter.21
  833.7 59.2 reduce-scatter.39
  895.3 86.8 reduce-scatter.31
  984.6 85.7 reduce-scatter.29
  1074.0 60.6 reduce-scatter.37
  1137.8 60.1 reduce-scatter.33
  1201.3 66.0 reduce-scatter.35
  1269.9 49.5 reduce-scatter.25
where the time goes:
time: 1340 us; the launch traced here: 1330 us
  waiting for transfers between devices  747 us (56%)
  matrix products  268 us (20%)
  blocking collectives  98.1 us (7%)
  other arithmetic  89.3 us (7%)
  local copies, waits for them, and re-layouts  88.3 us (7%)
  starting transfers between devices  24.9 us (2%)
  between operations  15.4 us (1%)
    unnamed x21, waiting for transfers between devices  210 us
    reduce_scatter x1, waiting for transfers between devices, shards(): lax.psum_scatter(down_part.astype(jnp.bfloat16), 'ctx', scatter_dimension...  87.7 us
    reduce_scatter x1, waiting for transfers between devices, shards(): lax.psum_scatter(up_part.astype(jnp.bfloat16), 'ctx', scatter_dimension=2...  85.4 us
    all_gather x1, waiting for transfers between devices, shards(): lax.all_gather(expert_down, 'ctx', axis=1, tiled=True)  76.8 us
    reduce_scatter x1, waiting for transfers between devices, shards(): lax.psum_scatter(jnp.dot(attended, full_proj, preferred_element_type=jnp....  68.5 us
    reduce_scatter x1, waiting for transfers between devices, shards(): lax.psum_scatter(rows_part.astype(jnp.bfloat16), 'tp', scatter_dimension=...  48.5 us
    unnamed x165, local copies, waits for them, and re-layouts  43.9 us
    all_gather x1, waiting for transfers between devices, shards(): lax.all_gather(expert_up, 'ctx', axis=2, tiled=True)  38.5 us
  transfers between devices with their start and end apart: 21, of which 16 were waited for; matrix products, arithmetic and copies ran while one was open for 25% of the time, Pallas kernels for 0%

commit v1 on v0

v1 whole, which is shorter than its diff:
```python
import jax
import jax.numpy as jnp
from jax import lax
from jax.sharding import PartitionSpec as P

HD = 64
PLEN = 1024
CLEN = 128
CONTS = 8

EPSILON = 1e-06
NEGATIVE = -1e30
PRECISE = lax.Precision.HIGHEST
F32 = jnp.float32
BF16 = jnp.bfloat16


def xor_swap(value, axis, size, mask):
    return lax.ppermute(value, axis, [(place, place ^ mask) for place in range(size)])


def ring_step(value, axis, size, shift):
    return lax.ppermute(value, axis, [(place, (place + shift) % size) for place in range(size)])


def pick(stacked, index):
    return lax.dynamic_index_in_dim(stacked, index, 0, keepdims=False)


def xor_gather(value, axis, size, order=None):
    if order is None:
        order = [1 << bit for bit in range(size.bit_length() - 1)]
    have = {0: value}
    for mask in order:
        keys = sorted(have)
        moved = xor_swap(jnp.stack([have[key] for key in keys]), axis, size, mask)
        for place, key in enumerate(keys):
            have[key ^ mask] = moved[place]
    return [have[key] for key in range(size)]


def in_order(pieces, me):
    stacked = jnp.stack(pieces)
    return jnp.stack([pick(stacked, me ^ place) for place in range(len(pieces))])


def xor_exchange(pieces, axis, size):
    return [pieces[0]] + [xor_swap(pieces[mask], axis, size, mask) for mask in range(1, size)]


def rms_unit(values):
    factor = lax.rsqrt(jnp.mean(values * values, axis=-1, keepdims=True) + EPSILON)
    return (values * factor, factor)


def rms_backward(grad_normed, unit_part, factor, gain):
    scaled = grad_normed * gain
    inner = jnp.mean(scaled * unit_part, axis=-1, keepdims=True)
    return (factor * (scaled - unit_part * inner), jnp.sum(grad_normed * unit_part, axis=0))


def masked_scores(queries, key_rows, visible):
    scores = (
        jnp.einsum("brhe,bkhe->bhrk", queries, key_rows, preferred_element_type=F32) * 0.125
    )
    return jnp.where(visible, scores, NEGATIVE)


def attend_forward(queries, key_rows, value_rows, visible):
    scores = masked_scores(queries, key_rows, visible)
    peak = jnp.max(scores, axis=-1, keepdims=True)
    shifted = jnp.exp(scores - peak)
    total = jnp.sum(shifted, axis=-1, keepdims=True)
    weights = (shifted / total).astype(BF16)
    mixed = jnp.einsum("bhrk,bkhe->brhe", weights, value_rows, preferred_element_type=F32)
    return (mixed.astype(BF16), peak + jnp.log(total))


def attend_backward(queries, key_rows, value_rows, visible, log_total, grad_mixed):
    weights = jnp.exp(masked_scores(queries, key_rows, visible) - log_total)
    grad_weights = jnp.einsum("brhe,bkhe->bhrk", grad_mixed, value_rows, preferred_element_type=F32)
    centre = jnp.sum(weights * grad_weights, axis=-1, keepdims=True)
    grad_scores = (weights * (grad_weights - centre)).astype(BF16)
    grad_queries = (
        jnp.einsum("bhrk,bkhe->brhe", grad_scores, key_rows, preferred_element_type=F32) * 0.125
    )
    grad_keys = (
        jnp.einsum("bhrk,brhe->bkhe", grad_scores, queries, preferred_element_type=F32) * 0.125
    )
    grad_values = jnp.einsum(
        "bhrk,brhe->bkhe", weights.astype(BF16), grad_mixed, preferred_element_type=F32
    )
    return (grad_queries, grad_keys, grad_values)


def slot_dispatch(chosen, priority, first, expert_count, capacity):
    tokens = chosen.shape[0]
    expert_range = jnp.arange(expert_count)
    chosen_hot = chosen[:, None] == expert_range[None, :]
    order_hot = (priority[:, None] == jnp.arange(tokens)[None, :]).astype(BF16)
    sorted_hot = jnp.dot(order_hot, chosen_hot.astype(BF16), preferred_element_type=F32)
    places = jnp.arange(tokens)
    before = (places[:, None] > places[None, :]).astype(BF16)
    earlier = jnp.dot(before, sorted_hot.astype(BF16), preferred_element_type=F32)
    sorted_rank = jnp.minimum(jnp.sum(earlier * sorted_hot, axis=1), capacity)
    rank = jnp.einsum(
        "it,i->t", order_hot, sorted_rank.astype(BF16), preferred_element_type=F32
    ).astype(jnp.int32)
    place = jnp.where(rank < capacity, (chosen ^ first) * capacity + rank, -1)
    dispatch = place[:, None] == jnp.arange(expert_count * capacity)[None, :]
    return (chosen_hot, dispatch.astype(BF16))


def shards(
    tokens,
    cotangent,
    gains,
    qkv_weight,
    proj_weight,
    router_weight,
    expert_up,
    expert_down,
    expert_ids,
    slot_order,
    segment_ids,
):
    dp_count, ctx_count, tp_count = (lax.axis_size(name) for name in ("dp", "ctx", "tp"))
    dp_index, ctx_index, tp_index = (lax.axis_index(name) for name in ("dp", "ctx", "tp"))
    group = dp_count * tp_count
    group_index = dp_index * tp_count + tp_index
    tok_dev, width = tokens.shape
    expert_count = router_weight.shape[1]
    capacity = 5 * tok_dev // (4 * expert_count)
    prompt_rows = PLEN // ctx_count
    conts_here = segment_ids.shape[0]
    prompts_here = conts_here * ctx_count // CONTS
    head_rows = prompts_here * prompt_rows
    local_width = qkv_weight.shape[2]
    local_heads = local_width // HD
    shard_rows = qkv_weight.shape[1]
    tp_order = [2, 1]

    full_up = lax.all_gather(expert_up, "ctx", axis=2, tiled=True)[0]
    full_down = lax.all_gather(expert_down, "ctx", axis=1, tiled=True)[0]

    def gather_weights(part):
        by_ctx = in_order(xor_gather(part, "ctx", ctx_count), ctx_index)
        by_dp = in_order(xor_gather(by_ctx, "dp", dp_count), dp_index)
        return by_dp.reshape(dp_count * ctx_count * part.shape[0], part.shape[1])

    full_qkv = gather_weights(qkv_weight.transpose(1, 0, 2).reshape(shard_rows, 3 * local_width))
    proj_router = gather_weights(jnp.concatenate([proj_weight.T, router_weight], axis=1))
    full_router = proj_router[:, local_width:]
    proj_near = jnp.concatenate(
        xor_gather(proj_router[:, :local_width], "tp", tp_count, tp_order), axis=1
    )

    block_rows = in_order(xor_gather(tokens, "tp", tp_count, tp_order), tp_index).reshape(-1, width)
    unit_block, _ = rms_unit(block_rows.astype(F32))
    normed_one = (gains[0] * unit_block).astype(BF16)
    projected = jnp.dot(normed_one, full_qkv, preferred_element_type=F32).astype(BF16)
    query, key, value = (
        projected[:, part * local_width : (part + 1) * local_width] for part in range(3)
    )
    prompt_shape = (prompts_here, prompt_rows, local_heads, HD)
    cont_shape = (conts_here, CLEN, local_heads, HD)
    query_prompt = query[:head_rows].reshape(prompt_shape)
    query_cont = query[head_rows:].reshape(cont_shape)
    key_cont = key[head_rows:].reshape(cont_shape)
    value_cont = value[head_rows:].reshape(cont_shape)
    pair = jnp.stack([key[:head_rows], value[:head_rows]]).reshape((2,) + prompt_shape)
    ring = [pair]
    for _ in range(ctx_count - 1):
        ring.append(ring_step(ring[-1], "ctx", ctx_count, 1))
    pairs_all = jnp.concatenate(ring, axis=2)
    keys_all, values_all = pairs_all[0], pairs_all[1]
    columns = jnp.arange(PLEN + CLEN)
    ring_place = jnp.arange(PLEN) // prompt_rows
    row_range = jnp.arange(prompt_rows)
    prompt_visible = jnp.where(
        ring_place[None, :] == 0,
        row_range[:, None] >= jnp.arange(PLEN)[None, :],
        ring_place[None, :] <= ctx_index,
    )
    cont_visible = (columns[None, :] < PLEN) | (
        columns[None, :] - PLEN <= jnp.arange(CLEN)[:, None]
    )
    cont_keys = jnp.concatenate([jnp.take(keys_all, segment_ids, axis=0), key_cont], axis=1)
    cont_values = jnp.concatenate([jnp.take(values_all, segment_ids, axis=0), value_cont], axis=1)
    mixed_prompt, total_prompt = attend_forward(query_prompt, keys_all, values_all, prompt_visible)
    mixed_cont, total_cont = attend_forward(query_cont, cont_keys, cont_values, cont_visible)
    attended = jnp.concatenate(
        [mixed_prompt.reshape(head_rows, local_width), mixed_cont.reshape(-1, local_width)], axis=0
    ).reshape(tp_count, tok_dev, local_width)
    attended_near = jnp.concatenate(
        xor_exchange([pick(attended, tp_index ^ k) for k in range(tp_count)], "tp", tp_count),
        axis=1,
    )
    branch = jnp.einsum("rc,dc->rd", attended_near, proj_near, preferred_element_type=F32)
    tokens_wide = tokens.astype(F32)
    middle = tokens_wide + branch
    unit_two, factor_two = rms_unit(middle)
    normed_two = (gains[1] * unit_two).astype(BF16)
    logits = jnp.dot(normed_two, full_router, preferred_element_type=F32)
    router_probs = jax.nn.softmax(logits, axis=-1)
    chosen_hot, dispatch = slot_dispatch(
        expert_ids[:, 0], slot_order[0], group_index, expert_count, capacity
    )
    gate_value = jnp.sum(jnp.where(chosen_hot, router_probs, 0.0), axis=-1)

    def to_slots(rows):
        return jnp.einsum("tj,td->jd", dispatch, rows, preferred_element_type=F32).astype(BF16)

    def from_slots(rows):
        return jnp.dot(dispatch, rows, preferred_element_type=F32)

    def exchange_slots(rows):
        pieces = rows.reshape(group, -1, width)
        moved = xor_exchange([pieces[k] for k in range(group)], ("dp", "tp"), group)
        return jnp.concatenate(moved, axis=0)

    upstream = cotangent.astype(F32)
    weighted = (gate_value[:, None] * upstream).astype(BF16)
    arrived = exchange_slots(to_slots(normed_two))
    grad_arrived = exchange_slots(to_slots(weighted))
    hidden_pre = jnp.dot(arrived, full_up, preferred_element_type=F32)
    hidden = jax.nn.gelu(hidden_pre).astype(BF16)
    produced = jnp.dot(hidden, full_down, preferred_element_type=F32).astype(BF16)
    grad_hidden = jnp.einsum("cd,fd->cf", grad_arrived, full_down, preferred_element_type=F32)
    grad_pre = jax.vjp(jax.nn.gelu, hidden_pre)[1](grad_hidden)[0].astype(BF16)
    rows_grad = jnp.einsum("cf,df->cd", grad_pre, full_up, preferred_element_type=F32).astype(BF16)
    down_part = jnp.einsum("cf,cd->fd", hidden, grad_arrived, preferred_element_type=F32)
    up_part = jnp.einsum("cd,cf->df", arrived, grad_pre, preferred_element_type=F32)
    routed_rows = from_slots(exchange_slots(produced))
    grad_returned = from_slots(exchange_slots(rows_grad))
    grad_up = lax.psum_scatter(
        up_part.astype(BF16)[None], "ctx", scatter_dimension=2, tiled=True
    ).astype(F32)
    grad_down = lax.psum_scatter(
        down_part.astype(BF16)[None], "ctx", scatter_dimension=1, tiled=True
    ).astype(F32)

    output = (middle + gate_value[:, None] * routed_rows).astype(BF16)
    grad_gate = jnp.sum(upstream * routed_rows, axis=-1)
    grad_logits = (
        (grad_gate * gate_value)[:, None] * (chosen_hot.astype(F32) - router_probs)
    ).astype(BF16)
    router_part = jnp.einsum("td,te->de", normed_two, grad_logits, preferred_element_type=F32)
    grad_second = grad_returned + jnp.einsum(
        "te,de->td", grad_logits, full_router, preferred_element_type=F32
    )
    middle_part, gain_two = rms_backward(grad_second, unit_two, factor_two, gains[1])
    grad_middle = upstream + middle_part
    grad_low = grad_middle.astype(BF16)
    grad_near = jnp.dot(grad_low, proj_near, preferred_element_type=F32).astype(BF16)
    grad_attended = in_order(
        xor_exchange(
            [grad_near[:, k * local_width : (k + 1) * local_width] for k in range(tp_count)],
            "tp",
            tp_count,
        ),
        tp_index,
    ).reshape(-1, local_width)
    prompt_grads = attend_backward(
        query_prompt,
        keys_all,
        values_all,
        prompt_visible,
        total_prompt,
        grad_attended[:head_rows].reshape(prompt_shape),
    )
    cont_grads = attend_backward(
        query_cont,
        cont_keys,
        cont_values,
        cont_visible,
        total_cont,
        grad_attended[head_rows:].reshape(cont_shape),
    )
    segment_hot = (segment_ids[:, None] == jnp.arange(prompts_here)[None, :]).astype(F32)
    pair_total = [
        prompt_grads[part]
        + jnp.einsum("cp,ckhe->pkhe", segment_hot, cont_grads[part][:, :PLEN], precision=PRECISE)
        for part in (1, 2)
    ]
    pair_total = jnp.stack(pair_total).reshape(
        2, prompts_here, ctx_count, prompt_rows, local_width
    )
    running = pair_total[:, :, ctx_count - 1].astype(BF16)
    for place in range(ctx_count - 2, -1, -1):
        arriving = ring_step(running, "ctx", ctx_count, -1)
        running = (pair_total[:, :, place] + arriving.astype(F32)).astype(BF16)
    grad_projected = jnp.concatenate(
        [
            jnp.concatenate(
                [
                    prompt_grads[0].reshape(head_rows, local_width),
                    cont_grads[0].reshape(-1, local_width),
                ],
                axis=0,
            ).astype(BF16),
            jnp.concatenate(
                [
                    running[0].reshape(head_rows, local_width),
                    cont_grads[1][:, PLEN:].reshape(-1, local_width).astype(BF16),
                ],
                axis=0,
            ),
            jnp.concatenate(
                [
                    running[1].reshape(head_rows, local_width),
                    cont_grads[2][:, PLEN:].reshape(-1, local_width).astype(BF16),
                ],
                axis=0,
            ),
        ],
        axis=1,
    )
    qkv_part = jnp.einsum("rd,rc->dc", normed_one, grad_projected, preferred_element_type=F32)
    grad_blocks = grad_projected.reshape(tp_count, tok_dev, 3 * local_width)
    first_near = [
        jnp.einsum("rc,dc->rd", pick(grad_blocks, tp_index ^ k), full_qkv, preferred_element_type=F32)
        for k in range(tp_count)
    ]

    def scatter_near(pieces, order):
        pieces = dict(enumerate(pieces))
        for mask in order:
            sent = [key for key in sorted(pieces) if key & mask]
            moved = xor_swap(
                jnp.stack([pieces[key].astype(BF16) for key in sent]), "tp", tp_count, mask
            )
            for place, key in enumerate(sent):
                pieces[key ^ mask] = pieces[key ^ mask] + moved[place].astype(F32)
                del pieces[key]
        return pieces[0]

    scatter_order = tp_order[::-1]
    grad_first = scatter_near(first_near, scatter_order)
    unit_one, factor_one = rms_unit(tokens_wide)
    rows_part, gain_one = rms_backward(grad_first, unit_one, factor_one, gains[0])
    grad_tokens = rows_part + grad_middle

    proj_blocks = jnp.einsum("rc,rd->dc", attended_near, grad_low, preferred_element_type=F32)
    proj_part = scatter_near(
        [proj_blocks[:, k * local_width : (k + 1) * local_width] for k in range(tp_count)],
        scatter_order,
    )
    small_part = jnp.concatenate(
        [router_part, jnp.stack([gain_one, gain_two], axis=1)], axis=1
    )
    packed = jnp.concatenate([qkv_part, proj_part, small_part], axis=1)
    packed = packed.reshape(dp_count, ctx_count, shard_rows, -1).astype(BF16)

    def scatter_ordered(values, axis, size, me):
        moved = xor_exchange([pick(values, me ^ k) for k in range(size)], axis, size)
        return sum(piece.astype(F32) for piece in moved)

    summed = scatter_ordered(packed, "dp", dp_count, dp_index).astype(BF16)
    summed = scatter_ordered(summed, "ctx", ctx_count, ctx_index)
    small_sum = summed[:, 4 * local_width :]
    small_all = xor_exchange([small_sum.astype(BF16)] * tp_count, "tp", tp_count)
    small_sum = small_sum + sum(piece.astype(F32) for piece in small_all[1:])
    grad_qkv = summed[:, : 3 * local_width].reshape(shard_rows, 3, local_width).transpose(1, 0, 2)
    grad_proj = summed[:, 3 * local_width : 4 * local_width].T
    grad_router = small_sum[:, :expert_count]
    grad_gains = small_sum[:, expert_count:].T
    return (output, grad_tokens, grad_gains, grad_qkv, grad_proj, grad_router, grad_up, grad_down)


def solution(mesh):
    in_specs = (
        P(("dp", "ctx", "tp"), None),
        P(("dp", "ctx", "tp"), None),
        P(),
        P(None, ("dp", "ctx"), "tp"),
        P("tp", ("dp", "ctx")),
        P(("dp", "ctx"), None),
        P(("dp", "tp"), None, "ctx"),
        P(("dp", "tp"), "ctx", None),
        P(("dp", "ctx", "tp"), None),
        P(("dp", "ctx", "tp"), None),
        P(("dp", "ctx")),
    )
    out_specs = (
        P(("dp", "ctx", "tp"), None),
        P(("dp", "ctx", "tp"), None),
        P(None, ("dp", "ctx")),
        P(None, ("dp", "ctx"), "tp"),
        P("tp", ("dp", "ctx")),
        P(("dp", "ctx"), None),
        P(("dp", "tp"), None, "ctx"),
        P(("dp", "tp"), "ctx", None),
    )
    return jax.shard_map(shards, mesh=mesh, in_specs=in_specs, out_specs=out_specs, check_vma=False)
```

time: 1340 us -> 1010 us (0.75)
  waiting for transfers between devices: 747 us -> 414 us
  blocking collectives: 98.1 us -> 0 us
  starting transfers between devices: 24.9 us -> 89.1 us
  local copies, waits for them, and re-layouts: 88.3 us -> 122 us
  matrix products: 268 us -> 252 us
    ppermute x0 -> x61, waiting for transfers between devices: none -> 414 us  [the longest x55 262 us: xor_swap(): lax.ppermute(value, axis, [(place, place ^ mask) for place in range(size)])]
    reduce_scatter x7 -> x2, waiting for transfers between devices: 324 us -> 0.01 us  [the longest x1 0.01 us: shards(): lax.psum_scatter(down_part.astype(BF16)[None], 'ctx', scatter_dimension=1...]
    unnamed x21 -> x4, waiting for transfers between devices: 210 us -> 0.07 us
    all_gather x6 -> x2, waiting for transfers between devices: 204 us -> 0.01 us  [the longest x1 0.01 us: shards(): full_up = lax.all_gather(expert_up, 'ctx', axis=2, tiled=True)[0]]
    ppermute x0 -> x61, starting transfers between devices: none -> 88.9 us  [the longest x55 87.9 us: xor_swap(): lax.ppermute(value, axis, [(place, place ^ mask) for place in range(size)])]
    all_gather x3 -> x0, blocking collectives: 87.7 us -> none  [the longest x1 33 us: shards(): lax.all_gather(qkv_weight, ('dp', 'ctx'), axis=1, tiled=True)]
    all_to_all x4 -> x0, starting transfers between devices: 23.8 us -> none  [routed(): lax.all_to_all(slots, ('dp', 'tp'), split_axis=0, concat_axis=0, tiled=True)]
    dot_general x22 -> x30, matrix products: 185 us -> 171 us  [the longest x2 23.3 us: attend_backward(): jnp.einsum('bhrk,brhe->bkhe', weights.astype(BF16), grad_mixed, preferred...]
  transfers between devices with their start and end apart: 21 -> 65, of which waited for: 16 -> 31; matrix products, arithmetic and copies ran while one was open for 25% -> 44% of each run, Pallas kernels for 0% -> 0%
where the time goes in v1:
time: 1010 us; the launch traced here: 995 us
  waiting for transfers between devices  414 us (41%)
  matrix products  252 us (25%)
  local copies, waits for them, and re-layouts  122 us (12%)
  other arithmetic  102 us (10%)
  starting transfers between devices  89.1 us (9%)
  between operations  16.5 us (2%)
    ppermute x55, waiting for transfers between devices, xor_swap(): lax.ppermute(value, axis, [(place, place ^ mask) for place in range(size)])  262 us
    ppermute x6, waiting for transfers between devices, ring_step(): lax.ppermute(value, axis, [(place, (place + shift) % size) for place in r...  152 us
    ppermute x55, starting transfers between devices, xor_swap(): lax.ppermute(value, axis, [(place, place ^ mask) for place in range(size)])  87.9 us
    unnamed x270, local copies, waits for them, and re-layouts  44.3 us
    dot_general x2, matrix products, attend_backward(): jnp.einsum('brhe,bkhe->bhrk', grad_mixed, value_rows, preferred_element_t...  31.6 us
    convert_element_type x2, other arithmetic, attend_backward(): grad_scores = (weights * (grad_weights - centre)).astype(BF16)  29.1 us
    dot_general x2, matrix products, attend_backward(): jnp.einsum('bhrk,brhe->bkhe', weights.astype(BF16), grad_mixed, preferred...  23.3 us
    dot_general x2, matrix products, masked_scores(): jnp.einsum('brhe,bkhe->bhrk', queries, key_rows, preferred_element_type=F32)  22.5 us
  transfers between devices with their start and end apart: 65, of which 31 were waited for; matrix products, arithmetic and copies ran while one was open for 44% of the time, Pallas kernels for 0%

profile of v1, /device:TPU:25, one launch (start us, length us, event | category | flops | bytes accessed | tf_op | source)
XLA Modules:
  0.0 995.4 jit_solution(4485168625609288790)
XLA Ops:
  8.6 25.9 %collective-permute-done = bf16[1,768,768]{2,1,0:T(8,128)(2,1)S(1)} collective-permute-done((bf16[1,768,768]{2,1,0:T(8,128)(2,1)}, bf16[1,768,768]{2,1,0:T(8,128)(2,1)S(1)}, u32[]{:S(2)}, u32[]{:S(2)}) %collective-permute-start) | collective-permute-done | bytes 1179680 | tf_op jit(solution)/shard_map/ppermute | solution.py:19
  39.2 18.3 %collective-permute-done.2 = bf16[1,96,576]{1,2,0:T(8,128)(2,1)S(1)} collective-permute-done((bf16[1,96,576]{1,2,0:T(8,128)(2,1)S(1)}, bf16[1,96,576]{1,2,0:T(8,128)(2,1)S(1)}, u32[]{:S(2)}, u32[]{:S(2)}) %collective-permute-start.2) | collective-permute-done | bytes 110624 | tf_op jit(solution)/shard_map/ppermute | solution.py:19
  57.7 34.8 %collective-permute-done.3 = bf16[2,96,576]{1,2,0:T(8,128)(2,1)S(1)} collective-permute-done((bf16[2,96,576]{1,2,0:T(8,128)(2,1)S(1)}, bf16[2,96,576]{1,2,0:T(8,128)(2,1)S(1)}, u32[]{:S(2)}, u32[]{:S(2)}) %collective-permute-start.3) | collective-permute-done | bytes 221216 | tf_op jit(solution)/shard_map/ppermute | solution.py:19
  94.9 10.3 %collective-permute-done.4 = bf16[1,4,96,576]{3,2,1,0:T(8,128)(2,1)S(1)} collective-permute-done((bf16[1,4,96,576]{3,2,1,0:T(8,128)(2,1)S(1)}, bf16[1,4,96,576]{3,2,1,0:T(8,128)(2,1)S(1)}, u32[]{:S(2)}, u32[]{:S(2)}) %collective-permute-start.4) | collective-permute-done | bytes 442400 | tf_op jit(solution)/shard_map/ppermute | solution.py:19
  125.9 50.6 %collective-permute-done.11 = bf16[1,96,200]{1,2,0:T(8,128)(2,1)S(1)} collective-permute-done((bf16[1,96,200]{1,2,0:T(8,128)(2,1)S(1)}, bf16[1,96,200]{1,2,0:T(8,128)(2,1)S(1)}, u32[]{:S(2)}, u32[]{:S(2)}) %collective-permute-start.11) | collective-permute-done | bytes 38432 | tf_op jit(solution)/shard_map/ppermute | solution.py:19
  178.0 7.7 collective-permute-done.12
  193.9 58.6 %collective-permute-done.6 = bf16[2,6,256,3,64]{2,4,3,1,0:T(8,128)(2,1)} collective-permute-done((bf16[2,6,256,3,64]{2,4,3,1,0:T(8,128)(2,1)S(1)}, bf16[2,6,256,3,64]{2,4,3,1,0:T(8,128)(2,1)}, u32[]{:S(2)}, u32[]{:S(2)}) %collective-permute-start.6) | collective-permute-done | bytes 1179680 | tf_op jit(solution)/shard_map/ppermute | solution.py:23
  268.1 9.8 collective-permute-done.7
  284.0 4.8 gather_fusion
  291.9 11.7 %fusion.189 = (f32[6,3,256]{2,1,0:T(4,128)S(1)}, f32[6,3,256,1024]{3,2,1,0:T(8,128)}) fusion(bf16[2,6,1024,3,64]{2,4,3,1,0:T(8,128)(2,1)} %copy-done.1, bf16[6,256,3,64]{1,0,3,2:T(8,128)(2,1)} %reshape.343, pred[256,1024]{1,0:T(8,128)(4,1)} %fusion.114), kind=kOutput, calls=%fused_computation.377 | convolution fusion | flops 618130944 | bytes 22300672 | tf_op jit(solution)/shard_map/brhe,bkhe->bhrk/dot_general | solution.py:64
  303.6 9.5 fusion.1
  313.1 9.7 fusion.104
  323.4 6.9 broadcast_select_fusion.1
  330.4 10.8 %fusion.188 = (f32[12,3,128]{2,1,0:T(4,128)S(1)}, f32[12,3,128,1152]{3,2,1,0:T(8,128)}) fusion(bf16[12,128,3,64]{1,3,2,0:T(8,128)(2,1)S(1)} %copy-done.40, bf16[12,1024,3,64]{1,3,2,0:T(8,128)(2,1)} %get-tuple-element.131, bf16[12,128,3,64]{1,0,3,2:T(8,128)(2,1)S(1)} %copy-done.24, pred[128,1152]{1,0:T(8,128)(4,1)S(1)} %copy-done.62), kind=kOutput, calls=%fused_computation.376 | convolution fusion | flops 706014720 | bytes 27297792 | tf_op jit(solution)/shard_map/brhe,bkhe->bhrk/dot_general | solution.py:64
  341.2 10.3 %fusion = f32[12,3,128]{2,1,0:T(4,128)S(1)} fusion(f32[12,3,128,1152]{3,2,1,0:T(8,128)} %get-tuple-element.133, f32[12,3,128]{2,1,0:T(4,128)S(1)} %get-tuple-element.132), kind=kLoop, calls=%fused_computation.14 | loop fusion | flops 10612224 | bytes 21270528 | tf_op jit(solution)/shard_map/reduce_sum | solution.py:73
  351.5 9.2 fusion.103
  365.3 4.5 collective-permute-start.10
  371.5 6.0 collective-permute-done.10
  377.5 6.3 collective-permute-done.9
  400.3 8.4 collective-permute-done.18
  415.6 5.3 collective-permute-done.20
  424.5 4.2 collective-permute-done.22
  429.5 12.0 %fusion.34 = f32[960,3072]{1,0:T(8,128)} fusion(bf16[960,768]{1,0:T(8,128)(2,1)} %constant_dynamic-update-slice_fusion, bf16[1,768,3072]{2,1,0:T(8,128)(2,1)} %all-gather.3.cloned.1.call-done), kind=kOutput, calls=%fused_computation.60 | convolution fusion | flops 4529848320 | bytes 17989632 | tf_op jit(solution)/shard_map/dot_general | solution.py:226
  441.6 12.6 %fusion.86 = bf16[960,768]{1,0:T(8,128)(2,1)S(1)} fusion(bf16[1,3072,768]{2,1,0:T(8,128)(2,1)} %all-gather.5.cloned.1.call-done, f32[960,3072]{1,0:T(8,128)} %fusion.34), kind=kOutput, calls=%fused_computation.132 | convolution fusion | flops 4557127680 | bytes 17989632 | tf_op jit(solution)/shard_map/dot_general | solution.py:228
  467.9 14.8 %fusion.14 = bf16[960,3072]{1,0:T(8,128)(2,1)} fusion(f32[960,3072]{1,0:T(8,128)} %fusion.34, bf16[960,768]{1,0:T(8,128)(2,1)S(1)} %constant_dynamic-update-slice_fusion.14, bf16[1,3072,768]{2,1,0:T(8,128)(2,1)S(1)} %copy-done.91), kind=kOutput, calls=%fused_computation.30 | convolution fusion | flops 4588830720 | bytes 23887872 | tf_op jit(solution)/shard_map/cd,fd->cf/dot_general | solution.py:229
  482.7 7.4 fusion.83
  494.9 10.7 %collective-permute-done.25 = bf16[120,768]{1,0:T(8,128)(2,1)S(1)} collective-permute-done((bf16[120,768]{1,0:T(8,128)(2,1)S(1)}, bf16[120,768]{1,0:T(8,128)(2,1)S(1)}, u32[]{:S(2)}, u32[]{:S(2)}) %collective-permute-start.25) | collective-permute-done | bytes 184352 | tf_op jit(solution)/shard_map/ppermute | solution.py:19
  506.0 3.8 collective-permute-done.26
  510.4 7.2 collective-permute-done.27
  520.1 5.4 collective-permute-done.29
  530.2 5.6 collective-permute-done.39
  544.5 8.8 fusion.37
  553.4 4.4 collective-permute-done.45
  559.2 12.4 %fusion.25 = f32[12,1152,3,64]{1,3,2,0:T(8,128)} fusion(f32[12,3,128,1152]{3,2,1,0:T(8,128)} %get-tuple-element.133, f32[12,3,128]{2,1,0:T(4,128)S(1)} %copy-done.42, bf16[12,128,3,64]{1,0,3,2:T(8,128)(2,1)S(1)} %reshape.353), kind=kOutput, calls=%fused_computation.44 | convolution fusion | flops 690094080 | bytes 32458752 | tf_op jit(solution)/shard_map/bhrk,brhe->bkhe/dot_general | solution.py:90
  571.5 15.8 %multiply_reduce_fusion = (f32[12,3,128]{2,1,0:T(4,128)S(1)}, f32[12,3,128,1152]{3,2,1,0:T(8,128)}) fusion(f32[12,3,128,1152]{3,2,1,0:T(8,128)} %get-tuple-element.133, f32[12,3,128]{2,1,0:T(4,128)S(1)} %copy-done.42, bf16[12,128,3,64]{1,3,2,0:T(8,128)(2,1)S(1)} %copy-done.34, bf16[12,1024,3,64]{1,3,2,0:T(8,128)(2,1)} %get-tuple-element.130, ...), kind=kOutput, calls=%fused_computation.3 | convolution fusion | flops 706014720 | bytes 48402432 | tf_op jit(solution)/shard_map/brhe,bkhe->bhrk/dot_general | solution.py:81
  592.1 10.0 %fusion.4 = f32[6,1024,3,64]{1,0,3,2:T(8,128)S(1)} fusion(f32[12,1024,3,64]{1,3,2,0:T(8,128)S(1)} %slice-done.6, s32[12]{0:T(128)S(1)} %copy-done.89), kind=kOutput, calls=%fused_computation.20 | convolution fusion | flops 169869376 | bytes 14155824 | tf_op jit(solution)/shard_map/cp,ckhe->pkhe/dot_general | solution.py:283
  602.1 10.9 %bitcast_add_fusion = f32[6,1024,3,64]{1,3,2,0:T(8,128)} fusion(f32[6,1024,3,64]{1,0,3,2:T(8,128)S(1)} %fusion.4, f32[6,3,256,1024]{3,2,1,0:T(8,128)} %get-tuple-element.135, f32[6,3,256]{2,1,0:T(4,128)S(1)} %copy-done.41, bf16[6,256,3,64]{1,0,3,2:T(8,128)(2,1)S(1)} %reshape.351), kind=kOutput, calls=%fused_computation.52 | convolution fusion | flops 614596608 | bytes 28919808 | tf_op jit(solution)/shard_map/bhrk,brhe->bkhe/dot_general | solution.py:90
  613.1 6.6 stack.180
  619.7 14.4 %multiply_convert_fusion = bf16[12,3,128,1152]{3,2,1,0:T(8,128)(2,1)S(1)} fusion(f32[12,3,128,1152]{3,2,1,0:T(8,128)} %get-tuple-element.144, f32[12,3,128,1152]{3,2,1,0:T(8,128)} %get-tuple-element.133, f32[12,3,128]{2,1,0:T(4,128)S(1)} %get-tuple-element.143, f32[12,3,128]{2,1,0:T(4,128)S(1)} %copy-done.42), kind=kLoop, calls=%fused_computation.2 | loop fusion | flops 21233664 | bytes 53121024 | tf_op jit(solution)/shard_map/convert_element_type | solution.py:83
  634.2 4.0 copy-done.2
  638.2 4.8 multiply_bitcast_fusion
  643.0 3.7 slice-done.7
  646.7 12.2 %fusion.6 = f32[6,1024,3,64]{1,0,3,2:T(8,128)} fusion(f32[12,1024,3,64]{1,3,2,0:T(8,128)S(1)} %slice-done.7, s32[12]{0:T(128)S(1)} %copy-done.89), kind=kOutput, calls=%fused_computation.22 | convolution fusion | flops 169869376 | bytes 14155824 | tf_op jit(solution)/shard_map/cp,ckhe->pkhe/dot_general | solution.py:283
  658.9 15.7 %multiply_reduce_fusion.1 = (f32[6,3,256]{2,1,0:T(4,128)S(1)}, f32[6,3,256,1024]{3,2,1,0:T(8,128)}) fusion(f32[6,3,256,1024]{3,2,1,0:T(8,128)} %get-tuple-element.135, f32[6,3,256]{2,1,0:T(4,128)S(1)} %copy-done.41, bf16[2,6,1024,3,64]{2,4,3,1,0:T(8,128)(2,1)S(1)} %bitcast.326, bf16[6,256,3,64]{1,0,3,2:T(8,128)(2,1)S(1)} %reshape.351), kind=kOutput, calls=%fused_computation.9 | convolution fusion | flops 618130944 | bytes 40937472 | tf_op jit(solution)/shard_map/brhe,bkhe->bhrk/dot_general | solution.py:81
  674.6 14.7 %multiply_convert_fusion.1 = bf16[6,3,256,1024]{3,2,1,0:T(8,128)(2,1)S(1)} fusion(f32[6,3,256,1024]{3,2,1,0:T(8,128)} %get-tuple-element.146, f32[6,3,256,1024]{3,2,1,0:T(8,128)} %get-tuple-element.135, f32[6,3,256]{2,1,0:T(4,128)S(1)} %get-tuple-element.145, f32[6,3,256]{2,1,0:T(4,128)S(1)} %copy-done.41), kind=kLoop, calls=%fused_computation.8 | loop fusion | flops 18874368 | bytes 47222784 | tf_op jit(solution)/shard_map/convert_element_type | solution.py:83
  693.0 6.2 bitcast_add_fusion.1
  699.2 6.7 stack.179
  715.9 27.5 %collective-permute-done.47 = bf16[2,6,256,192]{2,3,1,0:T(8,128)(2,1)} collective-permute-done((bf16[2,6,256,192]{2,3,1,0:T(8,128)(2,1)S(1)}, bf16[2,6,256,192]{2,3,1,0:T(8,128)(2,1)}, u32[]{:S(2)}, u32[]{:S(2)}) %collective-permute-start.47) | collective-permute-done | bytes 1179680 | tf_op jit(solution)/shard_map/ppermute | solution.py:23
  746.7 9.2 fusion.36
  760.0 11.4 %fusion.100 = bf16[12,128,3,64]{1,3,2,0:T(8,128)(2,1)} fusion(bf16[12,3,128,1152]{3,2,1,0:T(8,128)(2,1)} %copy-done.2, bf16[12,128,3,64]{1,3,2,0:T(8,128)(2,1)} %copy.174, bf16[12,1024,3,64]{1,3,2,0:T(8,128)(2,1)} %get-tuple-element.131), kind=kOutput, calls=%fused_computation.149 | convolution fusion | flops 690683904 | bytes 16515072 | tf_op jit(solution)/shard_map/bhrk,bkhe->brhe/dot_general | solution.py:85
  773.6 11.1 %collective-permute-done.48 = bf16[2,6,256,192]{2,3,1,0:T(8,128)(2,1)} collective-permute-done((bf16[2,6,256,192]{2,3,1,0:T(8,128)(2,1)}, bf16[2,6,256,192]{2,3,1,0:T(8,128)(2,1)}, u32[]{:S(2)}, u32[]{:S(2)}) %collective-permute-start.48) | collective-permute-done | bytes 1179680 | tf_op jit(solution)/shard_map/ppermute | solution.py:23
  787.0 6.7 fusion.97
  794.4 45.4 %collective-permute-done.49 = bf16[2,6,256,192]{2,3,1,0:T(8,128)(2,1)S(1)} collective-permute-done((bf16[2,6,256,192]{2,3,1,0:T(8,128)(2,1)S(1)}, bf16[2,6,256,192]{2,3,1,0:T(8,128)(2,1)S(1)}, u32[]{:S(2)}, u32[]{:S(2)}) %collective-permute-start.49) | collective-permute-done | bytes 1179680 | tf_op jit(solution)/shard_map/ppermute | solution.py:23
  848.9 7.1 collective-permute-start.50
  864.3 6.6 copy.212
  873.8 3.9 fusion.105
  881.9 7.9 fusion.94
  889.8 16.3 %collective-permute-done.51 = bf16[1,768,768]{1,2,0:T(8,128)(2,1)} collective-permute-done((bf16[1,768,768]{1,2,0:T(8,128)(2,1)}, bf16[1,768,768]{1,2,0:T(8,128)(2,1)}, u32[]{:S(2)}, u32[]{:S(2)}) %collective-permute-start.51) | collective-permute-done | bytes 1179680 | tf_op jit(solution)/shard_map/ppermute | solution.py:19
  906.1 4.9 fusion.57
  917.5 13.1 %collective-permute-done.54 = bf16[4,96,778]{2,1,0:T(8,128)(2,1)} collective-permute-done((bf16[4,96,778]{2,1,0:T(8,128)(2,1)S(1)}, bf16[4,96,778]{2,1,0:T(8,128)(2,1)}, u32[]{:S(2)}, u32[]{:S(2)}) %collective-permute-start.54) | collective-permute-done | bytes 597536 | tf_op jit(solution)/shard_map/ppermute | solution.py:19
  931.9 22.2 %collective-permute-start.55 = (bf16[96,778]{1,0:T(8,128)(2,1)S(1)}, bf16[96,778]{1,0:T(8,128)(2,1)S(1)}, u32[]{:S(2)}, u32[]{:S(2)}) collective-permute-start(bf16[96,778]{1,0:T(8,128)(2,1)S(1)} %get-tuple-element.113), channel_id=1, source_target_pairs={{0,4},{4,0},{8,12},{12,8},{1,5},{5,1},{9,13},{13,9},{2,6},{6,2},{1... | collective-permute-start | bytes 448136 | tf_op jit(solution)/shard_map/ppermute | solution.py:19
  954.1 6.8 collective-permute-start.57
  961.2 4.7 fusion.56
  968.9 6.1 collective-permute-done.56
  (531 shorter events, 213.1 us)
Async XLA Ops:
  7.2 422.4 %all-gather.3.cloned.1.call-start = ((), (), s32[]{:S(2)}) async-start(), calls=%async_computation.2 | async-start | bytes 5898240 | tf_op jit(solution)/shard_map/all_gather | solution.py:143
  7.2 27.2 %collective-permute-start = (bf16[1,768,768]{2,1,0:T(8,128)(2,1)}, bf16[1,768,768]{2,1,0:T(8,128)(2,1)S(1)}, u32[]{:S(2)}, u32[]{:S(2)}) collective-permute-start(bf16[1,768,768]{2,1,0:T(8,128)(2,1)} %bitcast.334), channel_id=1, source_target_pairs={{0,2},{1,3},{2,0},{3,1},{4,6},{5,7},{6,4},{7,5},{8,10},{9,11},{10,... | collective-permute-start | bytes 3538952 | tf_op jit(solution)/shard_map/ppermute | solution.py:19
  8.5 433.1 %all-gather.5.cloned.1.call-start = ((), (), s32[]{:S(2)}) async-start(), calls=%async_computation.3 | async-start | bytes 5898240 | tf_op jit(solution)/shard_map/all_gather | solution.py:144
  37.3 69.8 %collective-permute-start.1 = (bf16[2,768,768]{2,1,0:T(8,128)(2,1)}, bf16[2,768,768]{2,1,0:T(8,128)(2,1)}, u32[]{:S(2)}, u32[]{:S(2)}) collective-permute-start(bf16[2,768,768]{2,1,0:T(8,128)(2,1)} %pad_maximum_fusion.8), channel_id=1, source_target_pairs={{0,1},{1,0},{2,3},{3,2},{4,5},{5,4},{6,7},{7,6},{8,9},{9,8},{10,11... | collective-permute-start | bytes 7077896 | tf_op jit(solution)/shard_map/ppermute | solution.py:19
  38.9 18.6 %collective-permute-start.2 = (bf16[1,96,576]{1,2,0:T(8,128)(2,1)S(1)}, bf16[1,96,576]{1,2,0:T(8,128)(2,1)S(1)}, u32[]{:S(2)}, u32[]{:S(2)}) collective-permute-start(bf16[1,96,576]{1,2,0:T(8,128)(2,1)S(1)} %bitcast.357), channel_id=1, source_target_pairs={{0,4},{4,0},{8,12},{12,8},{1,5},{5,1},{9,13},{13,9},{2,6},{6,2},{1... | collective-permute-start | bytes 331784 | tf_op jit(solution)/shard_map/ppermute | solution.py:19
  57.6 34.9 %collective-permute-start.3 = (bf16[2,96,576]{1,2,0:T(8,128)(2,1)S(1)}, bf16[2,96,576]{1,2,0:T(8,128)(2,1)S(1)}, u32[]{:S(2)}, u32[]{:S(2)}) collective-permute-start(bf16[2,96,576]{1,2,0:T(8,128)(2,1)S(1)} %pad_maximum_fusion.29), channel_id=1, source_target_pairs={{0,8},{4,12},{8,0},{12,4},{1,9},{5,13},{9,1},{13,5},{2,10},{6,14},... | collective-permute-start | bytes 663560 | tf_op jit(solution)/shard_map/ppermute | solution.py:19
  93.2 12.1 %collective-permute-start.4 = (bf16[1,4,96,576]{3,2,1,0:T(8,128)(2,1)S(1)}, bf16[1,4,96,576]{3,2,1,0:T(8,128)(2,1)S(1)}, u32[]{:S(2)}, u32[]{:S(2)}) collective-permute-start(bf16[1,4,96,576]{3,2,1,0:T(8,128)(2,1)S(1)} %copy.166), channel_id=1, source_target_pairs={{0,16},{16,0},{1,17},{17,1},{2,18},{18,2},{3,19},{19,3},{4,20},{20... | collective-permute-start | bytes 1327112 | tf_op jit(solution)/shard_map/ppermute | solution.py:19
  121.9 54.8 %collective-permute-start.5 = (bf16[2,6,256,3,64]{2,4,3,1,0:T(8,128)(2,1)}, bf16[2,6,256,3,64]{2,4,3,1,0:T(8,128)(2,1)S(1)}, u32[]{:S(2)}, u32[]{:S(2)}) collective-permute-start(bf16[2,6,256,3,64]{2,4,3,1,0:T(8,128)(2,1)} %copy_dynamic-update-slice_fusion.2), channel_id=1, source_target_pairs={{0,4},{4,8},{8,12},{12,0},{1,5},{5,9},{9,13},{13,1},{2,6},{6,10},{... | collective-permute-start | bytes 3538952 | tf_op jit(solution)/shard_map/ppermute | solution.py:23
  121.9 54.6 %collective-permute-start.11 = (bf16[1,96,200]{1,2,0:T(8,128)(2,1)S(1)}, bf16[1,96,200]{1,2,0:T(8,128)(2,1)S(1)}, u32[]{:S(2)}, u32[]{:S(2)}) collective-permute-start(bf16[1,96,200]{1,2,0:T(8,128)(2,1)S(1)} %maximum_bitcast_fusion.6), channel_id=1, source_target_pairs={{0,4},{4,0},{8,12},{12,8},{1,5},{5,1},{9,13},{13,9},{2,6},{6,2},{1... | collective-permute-start | bytes 115208 | tf_op jit(solution)/shard_map/ppermute | solution.py:19
  123.5 859.3 %reduce-scatter.5.cloned.1.call-start = ((), (), s32[]{:S(2)}) async-start(), calls=%async_computation.5 | async-start | bytes 5898240 | tf_op jit(solution)/shard_map/reduce_scatter | solution.py:239
  176.6 9.1 collective-permute-start.12
  176.7 75.8 %collective-permute-start.6 = (bf16[2,6,256,3,64]{2,4,3,1,0:T(8,128)(2,1)S(1)}, bf16[2,6,256,3,64]{2,4,3,1,0:T(8,128)(2,1)}, u32[]{:S(2)}, u32[]{:S(2)}) collective-permute-start(bf16[2,6,256,3,64]{2,4,3,1,0:T(8,128)(2,1)S(1)} %collective-permute-done.5), channel_id=1, source_target_pairs={{0,4},{4,8},{8,12},{12,0},{1,5},{5,9},{9,13},{13,1},{2,6},{6,10},{... | collective-permute-start | bytes 3538952 | tf_op jit(solution)/shard_map/ppermute | solution.py:23
  185.9 6.4 collective-permute-start.13
  193.9 58.8 %collective-permute-start.14 = (bf16[1,768,192]{1,2,0:T(8,128)(2,1)S(1)}, bf16[1,768,192]{1,2,0:T(8,128)(2,1)S(1)}, u32[]{:S(2)}, u32[]{:S(2)}) collective-permute-start(bf16[1,768,192]{1,2,0:T(8,128)(2,1)S(1)} %get-tuple-element.125), channel_id=1, source_target_pairs={{0,2},{1,3},{2,0},{3,1},{4,6},{5,7},{6,4},{7,5},{8,10},{9,11},{10,... | collective-permute-start | bytes 884744 | tf_op jit(solution)/shard_map/ppermute | solution.py:19
  252.5 25.4 %collective-permute-start.7 = (bf16[2,6,256,3,64]{2,4,3,1,0:T(8,128)(2,1)}, bf16[2,6,256,3,64]{2,4,3,1,0:T(8,128)(2,1)}, u32[]{:S(2)}, u32[]{:S(2)}) collective-permute-start(bf16[2,6,256,3,64]{2,4,3,1,0:T(8,128)(2,1)} %collective-permute-done.6), channel_id=1, source_target_pairs={{0,4},{4,8},{8,12},{12,0},{1,5},{5,9},{9,13},{13,1},{2,6},{6,10},{... | collective-permute-start | bytes 3538952 | tf_op jit(solution)/shard_map/ppermute | solution.py:23
  253.7 6.8 collective-permute-start.15
  365.3 12.2 %collective-permute-start.10 = (bf16[768,192]{0,1:T(8,128)(2,1)S(1)}, bf16[768,192]{0,1:T(8,128)(2,1)S(1)}, u32[]{:S(2)}, u32[]{:S(2)}) collective-permute-start(bf16[768,192]{0,1:T(8,128)(2,1)S(1)} %bitcast.375), channel_id=1, source_target_pairs={{0,3},{1,2},{2,1},{3,0},{4,7},{5,6},{6,5},{7,4},{8,11},{9,10},{10,... | collective-permute-start | bytes 884744 | tf_op jit(solution)/shard_map/ppermute | solution.py:19
  369.8 7.7 collective-permute-start.8
  369.8 14.1 %collective-permute-start.9 = (bf16[768,192]{0,1:T(8,128)(2,1)S(1)}, bf16[768,192]{0,1:T(8,128)(2,1)S(1)}, u32[]{:S(2)}, u32[]{:S(2)}) collective-permute-start(bf16[768,192]{0,1:T(8,128)(2,1)S(1)} %bitcast.373), channel_id=1, source_target_pairs={{0,2},{1,3},{2,0},{3,1},{4,6},{5,7},{6,4},{7,5},{8,10},{9,11},{10,... | collective-permute-start | bytes 884744 | tf_op jit(solution)/shard_map/ppermute | solution.py:19
  388.3 10.7 %collective-permute-start.17 = (bf16[120,768]{1,0:T(8,128)(2,1)S(1)}, bf16[120,768]{1,0:T(8,128)(2,1)S(1)}, u32[]{:S(2)}, u32[]{:S(2)}) collective-permute-start(bf16[120,768]{1,0:T(8,128)(2,1)S(1)} %get-tuple-element.92), channel_id=1, source_target_pairs={{0,2},{1,3},{2,0},{3,1},{16,18},{17,19},{18,16},{19,17},{4,6},{5,7... | collective-permute-start | bytes 552968 | tf_op jit(solution)/shard_map/ppermute | solution.py:19
  388.5 8.4 collective-permute-start.16
  393.3 73.6 %collective-permute-start.36 = (bf16[120,768]{1,0:T(8,128)(2,1)}, bf16[120,768]{1,0:T(8,128)(2,1)}, u32[]{:S(2)}, u32[]{:S(2)}) collective-permute-start(bf16[120,768]{1,0:T(8,128)(2,1)} %get-tuple-element.71), channel_id=1, source_target_pairs={{0,19},{1,18},{2,17},{3,16},{16,3},{17,2},{18,1},{19,0},{4,23},{5,... | collective-permute-start | bytes 552968 | tf_op jit(solution)/shard_map/ppermute | solution.py:19
  395.3 70.6 %collective-permute-start.35 = (bf16[120,768]{1,0:T(8,128)(2,1)}, bf16[120,768]{1,0:T(8,128)(2,1)}, u32[]{:S(2)}, u32[]{:S(2)}) collective-permute-start(bf16[120,768]{1,0:T(8,128)(2,1)} %get-tuple-element.72), channel_id=1, source_target_pairs={{0,18},{1,19},{2,16},{3,17},{16,2},{17,3},{18,0},{19,1},{4,22},{5,... | collective-permute-start | bytes 552968 | tf_op jit(solution)/shard_map/ppermute | solution.py:19
  395.8 69.2 %collective-permute-start.34 = (bf16[120,768]{1,0:T(8,128)(2,1)}, bf16[120,768]{1,0:T(8,128)(2,1)}, u32[]{:S(2)}, u32[]{:S(2)}) collective-permute-start(bf16[120,768]{1,0:T(8,128)(2,1)} %get-tuple-element.73), channel_id=1, source_target_pairs={{0,17},{1,16},{2,19},{3,18},{16,1},{17,0},{18,3},{19,2},{4,21},{5,... | collective-permute-start | bytes 552968 | tf_op jit(solution)/shard_map/ppermute | solution.py:19
  396.9 11.7 %collective-permute-start.18 = (bf16[120,768]{1,0:T(8,128)(2,1)S(1)}, bf16[120,768]{1,0:T(8,128)(2,1)S(1)}, u32[]{:S(2)}, u32[]{:S(2)}) collective-permute-start(bf16[120,768]{1,0:T(8,128)(2,1)S(1)} %get-tuple-element.91), channel_id=1, source_target_pairs={{0,3},{1,2},{2,1},{3,0},{16,19},{17,18},{18,17},{19,16},{4,7},{5,6... | collective-permute-start | bytes 552968 | tf_op jit(solution)/shard_map/ppermute | solution.py:19
  399.0 14.1 %collective-permute-start.19 = (bf16[120,768]{1,0:T(8,128)(2,1)S(1)}, bf16[120,768]{1,0:T(8,128)(2,1)S(1)}, u32[]{:S(2)}, u32[]{:S(2)}) collective-permute-start(bf16[120,768]{1,0:T(8,128)(2,1)S(1)} %get-tuple-element.90), channel_id=1, source_target_pairs={{0,16},{1,17},{2,18},{3,19},{16,0},{17,1},{18,2},{19,3},{4,20},{5,... | collective-permute-start | bytes 552968 | tf_op jit(solution)/shard_map/ppermute | solution.py:19
  408.7 12.3 %collective-permute-start.20 = (bf16[120,768]{1,0:T(8,128)(2,1)S(1)}, bf16[120,768]{1,0:T(8,128)(2,1)S(1)}, u32[]{:S(2)}, u32[]{:S(2)}) collective-permute-start(bf16[120,768]{1,0:T(8,128)(2,1)S(1)} %get-tuple-element.89), channel_id=1, source_target_pairs={{0,17},{1,16},{2,19},{3,18},{16,1},{17,0},{18,3},{19,2},{4,21},{5,... | collective-permute-start | bytes 552968 | tf_op jit(solution)/shard_map/ppermute | solution.py:19
  413.0 10.8 %collective-permute-start.21 = (bf16[120,768]{1,0:T(8,128)(2,1)S(1)}, bf16[120,768]{1,0:T(8,128)(2,1)S(1)}, u32[]{:S(2)}, u32[]{:S(2)}) collective-permute-start(bf16[120,768]{1,0:T(8,128)(2,1)S(1)} %get-tuple-element.88), channel_id=1, source_target_pairs={{0,18},{1,19},{2,16},{3,17},{16,2},{17,3},{18,0},{19,1},{4,22},{5,... | collective-permute-start | bytes 552968 | tf_op jit(solution)/shard_map/ppermute | solution.py:19
  420.9 7.8 collective-permute-start.22
  423.8 34.0 %collective-permute-start.31 = (bf16[120,768]{1,0:T(8,128)(2,1)}, bf16[120,768]{1,0:T(8,128)(2,1)}, u32[]{:S(2)}, u32[]{:S(2)}) collective-permute-start(bf16[120,768]{1,0:T(8,128)(2,1)} %get-tuple-element.76), channel_id=1, source_target_pairs={{0,2},{1,3},{2,0},{3,1},{16,18},{17,19},{18,16},{19,17},{4,6},{5,7... | collective-permute-start | bytes 552968 | tf_op jit(solution)/shard_map/ppermute | solution.py:19
  428.8 25.6 %collective-permute-start.30 = (bf16[120,768]{1,0:T(8,128)(2,1)}, bf16[120,768]{1,0:T(8,128)(2,1)}, u32[]{:S(2)}, u32[]{:S(2)}) collective-permute-start(bf16[120,768]{1,0:T(8,128)(2,1)} %get-tuple-element.77), channel_id=1, source_target_pairs={{0,1},{1,0},{2,3},{3,2},{16,17},{17,16},{18,19},{19,18},{4,5},{5,4... | collective-permute-start | bytes 552968 | tf_op jit(solution)/shard_map/ppermute | solution.py:19
  455.2 7.0 collective-permute-start.32
  457.8 6.3 collective-permute-start.33
  462.1 32.0 %collective-permute-start.24 = (bf16[120,768]{1,0:T(8,128)(2,1)S(1)}, bf16[120,768]{1,0:T(8,128)(2,1)S(1)}, u32[]{:S(2)}, u32[]{:S(2)}) collective-permute-start(bf16[120,768]{1,0:T(8,128)(2,1)S(1)} %get-tuple-element.84), channel_id=1, source_target_pairs={{0,2},{1,3},{2,0},{3,1},{16,18},{17,19},{18,16},{19,17},{4,6},{5,7... | collective-permute-start | bytes 552968 | tf_op jit(solution)/shard_map/ppermute | solution.py:19
  464.1 30.0 %collective-permute-start.23 = (bf16[120,768]{1,0:T(8,128)(2,1)S(1)}, bf16[120,768]{1,0:T(8,128)(2,1)S(1)}, u32[]{:S(2)}, u32[]{:S(2)}) collective-permute-start(bf16[120,768]{1,0:T(8,128)(2,1)S(1)} %get-tuple-element.85), channel_id=1, source_target_pairs={{0,1},{1,0},{2,3},{3,2},{16,17},{17,16},{18,19},{19,18},{4,5},{5,4... | collective-permute-start | bytes 552968 | tf_op jit(solution)/shard_map/ppermute | solution.py:19
  490.3 45.6 %collective-permute-start.43 = (bf16[120,768]{1,0:T(8,128)(2,1)S(1)}, bf16[120,768]{1,0:T(8,128)(2,1)S(1)}, u32[]{:S(2)}, u32[]{:S(2)}) collective-permute-start(bf16[120,768]{1,0:T(8,128)(2,1)S(1)} %get-tuple-element.63), channel_id=1, source_target_pairs={{0,19},{1,18},{2,17},{3,16},{16,3},{17,2},{18,1},{19,0},{4,23},{5,... | collective-permute-start | bytes 552968 | tf_op jit(solution)/shard_map/ppermute | solution.py:19
  491.0 44.9 %collective-permute-start.42 = (bf16[120,768]{1,0:T(8,128)(2,1)S(1)}, bf16[120,768]{1,0:T(8,128)(2,1)S(1)}, u32[]{:S(2)}, u32[]{:S(2)}) collective-permute-start(bf16[120,768]{1,0:T(8,128)(2,1)S(1)} %get-tuple-element.64), channel_id=1, source_target_pairs={{0,18},{1,19},{2,16},{3,17},{16,2},{17,3},{18,0},{19,1},{4,22},{5,... | collective-permute-start | bytes 552968 | tf_op jit(solution)/shard_map/ppermute | solution.py:19
  492.8 43.1 %collective-permute-start.41 = (bf16[120,768]{1,0:T(8,128)(2,1)S(1)}, bf16[120,768]{1,0:T(8,128)(2,1)S(1)}, u32[]{:S(2)}, u32[]{:S(2)}) collective-permute-start(bf16[120,768]{1,0:T(8,128)(2,1)S(1)} %get-tuple-element.65), channel_id=1, source_target_pairs={{0,17},{1,16},{2,19},{3,18},{16,1},{17,0},{18,3},{19,2},{4,21},{5,... | collective-permute-start | bytes 552968 | tf_op jit(solution)/shard_map/ppermute | solution.py:19
  494.1 11.4 %collective-permute-start.25 = (bf16[120,768]{1,0:T(8,128)(2,1)S(1)}, bf16[120,768]{1,0:T(8,128)(2,1)S(1)}, u32[]{:S(2)}, u32[]{:S(2)}) collective-permute-start(bf16[120,768]{1,0:T(8,128)(2,1)S(1)} %get-tuple-element.83), channel_id=1, source_target_pairs={{0,3},{1,2},{2,1},{3,0},{16,19},{17,18},{18,17},{19,16},{4,7},{5,6... | collective-permute-start | bytes 552968 | tf_op jit(solution)/shard_map/ppermute | solution.py:19
  494.1 15.7 %collective-permute-start.26 = (bf16[120,768]{1,0:T(8,128)(2,1)S(1)}, bf16[120,768]{1,0:T(8,128)(2,1)S(1)}, u32[]{:S(2)}, u32[]{:S(2)}) collective-permute-start(bf16[120,768]{1,0:T(8,128)(2,1)S(1)} %get-tuple-element.82), channel_id=1, source_target_pairs={{0,16},{1,17},{2,18},{3,19},{16,0},{17,1},{18,2},{19,3},{4,20},{5,... | collective-permute-start | bytes 552968 | tf_op jit(solution)/shard_map/ppermute | solution.py:19
  505.5 12.2 %collective-permute-start.27 = (bf16[120,768]{1,0:T(8,128)(2,1)S(1)}, bf16[120,768]{1,0:T(8,128)(2,1)S(1)}, u32[]{:S(2)}, u32[]{:S(2)}) collective-permute-start(bf16[120,768]{1,0:T(8,128)(2,1)S(1)} %get-tuple-element.81), channel_id=1, source_target_pairs={{0,17},{1,16},{2,19},{3,18},{16,1},{17,0},{18,3},{19,2},{4,21},{5,... | collective-permute-start | bytes 552968 | tf_op jit(solution)/shard_map/ppermute | solution.py:19
  509.8 8.8 collective-permute-start.28
  517.7 7.8 collective-permute-start.29
  518.6 10.6 %collective-permute-start.38 = (bf16[120,768]{1,0:T(8,128)(2,1)S(1)}, bf16[120,768]{1,0:T(8,128)(2,1)S(1)}, u32[]{:S(2)}, u32[]{:S(2)}) collective-permute-start(bf16[120,768]{1,0:T(8,128)(2,1)S(1)} %get-tuple-element.68), channel_id=1, source_target_pairs={{0,2},{1,3},{2,0},{3,1},{16,18},{17,19},{18,16},{19,17},{4,6},{5,7... | collective-permute-start | bytes 552968 | tf_op jit(solution)/shard_map/ppermute | solution.py:19
  525.5 3.2 collective-permute-start.37
  528.8 7.0 collective-permute-start.39
  529.3 6.5 collective-permute-start.40
  542.1 11.3 %collective-permute-start.46 = (bf16[768,192]{0,1:T(8,128)(2,1)S(1)}, bf16[768,192]{0,1:T(8,128)(2,1)S(1)}, u32[]{:S(2)}, u32[]{:S(2)}) collective-permute-start(bf16[768,192]{0,1:T(8,128)(2,1)S(1)} %get-tuple-element.104), channel_id=1, source_target_pairs={{0,3},{1,2},{2,1},{3,0},{4,7},{5,6},{6,5},{7,4},{8,11},{9,10},{10,... | collective-permute-start | bytes 884744 | tf_op jit(solution)/shard_map/ppermute | solution.py:19
  544.0 13.8 %collective-permute-start.45 = (bf16[768,192]{0,1:T(8,128)(2,1)S(1)}, bf16[768,192]{0,1:T(8,128)(2,1)S(1)}, u32[]{:S(2)}, u32[]{:S(2)}) collective-permute-start(bf16[768,192]{0,1:T(8,128)(2,1)S(1)} %get-tuple-element.105), channel_id=1, source_target_pairs={{0,2},{1,3},{2,0},{3,1},{4,6},{5,7},{6,4},{7,5},{8,10},{9,11},{10,... | collective-permute-start | bytes 884744 | tf_op jit(solution)/shard_map/ppermute | solution.py:19
  544.1 13.7 %collective-permute-start.44 = (bf16[768,192]{0,1:T(8,128)(2,1)S(1)}, bf16[768,192]{0,1:T(8,128)(2,1)S(1)}, u32[]{:S(2)}, u32[]{:S(2)}) collective-permute-start(bf16[768,192]{0,1:T(8,128)(2,1)S(1)} %get-tuple-element.106), channel_id=1, source_target_pairs={{0,1},{1,0},{2,3},{3,2},{4,5},{5,4},{6,7},{7,6},{8,9},{9,8},{10,11... | collective-permute-start | bytes 884744 | tf_op jit(solution)/shard_map/ppermute | solution.py:19
  553.4 432.2 %reduce-scatter.3.cloned.1.call-start = ((), (), s32[]{:S(2)}) async-start(), calls=%async_computation.4 | async-start | bytes 5898240 | tf_op jit(solution)/shard_map/reduce_scatter | solution.py:236
  714.4 29.0 %collective-permute-start.47 = (bf16[2,6,256,192]{2,3,1,0:T(8,128)(2,1)S(1)}, bf16[2,6,256,192]{2,3,1,0:T(8,128)(2,1)}, u32[]{:S(2)}, u32[]{:S(2)}) collective-permute-start(bf16[2,6,256,192]{2,3,1,0:T(8,128)(2,1)S(1)} %fusion.106), channel_id=1, source_target_pairs={{0,12},{4,0},{8,4},{12,8},{1,13},{5,1},{9,5},{13,9},{2,14},{6,2},{... | collective-permute-start | bytes 3538952 | tf_op jit(solution)/shard_map/ppermute | solution.py:23
  746.7 37.9 %collective-permute-start.48 = (bf16[2,6,256,192]{2,3,1,0:T(8,128)(2,1)}, bf16[2,6,256,192]{2,3,1,0:T(8,128)(2,1)}, u32[]{:S(2)}, u32[]{:S(2)}) collective-permute-start(bf16[2,6,256,192]{2,3,1,0:T(8,128)(2,1)} %fusion.62), channel_id=1, source_target_pairs={{0,12},{4,0},{8,4},{12,8},{1,13},{5,1},{9,5},{13,9},{2,14},{6,2},{... | collective-permute-start | bytes 3538952 | tf_op jit(solution)/shard_map/ppermute | solution.py:23
  786.9 52.9 %collective-permute-start.49 = (bf16[2,6,256,192]{2,3,1,0:T(8,128)(2,1)S(1)}, bf16[2,6,256,192]{2,3,1,0:T(8,128)(2,1)S(1)}, u32[]{:S(2)}, u32[]{:S(2)}) collective-permute-start(bf16[2,6,256,192]{2,3,1,0:T(8,128)(2,1)S(1)} %fusion.64), channel_id=1, source_target_pairs={{0,12},{4,0},{8,4},{12,8},{1,13},{5,1},{9,5},{13,9},{2,14},{6,2},{... | collective-permute-start | bytes 3538952 | tf_op jit(solution)/shard_map/ppermute | solution.py:23
  848.9 24.9 %collective-permute-start.50 = (bf16[2,768,768]{1,2,0:T(8,128)(2,1)}, bf16[2,768,768]{1,2,0:T(8,128)(2,1)}, u32[]{:S(2)}, u32[]{:S(2)}) collective-permute-start(bf16[2,768,768]{1,2,0:T(8,128)(2,1)} %pad_maximum_fusion.9), channel_id=1, source_target_pairs={{0,1},{1,0},{2,3},{3,2},{4,5},{5,4},{6,7},{7,6},{8,9},{9,8},{10,11... | collective-permute-start | bytes 7077896 | tf_op jit(solution)/shard_map/ppermute | solution.py:19
  859.8 11.1 %collective-permute-start.52 = (bf16[2,768,192]{1,2,0:T(8,128)(2,1)S(1)}, bf16[2,768,192]{1,2,0:T(8,128)(2,1)}, u32[]{:S(2)}, u32[]{:S(2)}) collective-permute-start(bf16[2,768,192]{1,2,0:T(8,128)(2,1)S(1)} %pad_maximum_fusion.27), channel_id=1, source_target_pairs={{0,1},{1,0},{2,3},{3,2},{4,5},{5,4},{6,7},{7,6},{8,9},{9,8},{10,11... | collective-permute-start | bytes 1769480 | tf_op jit(solution)/shard_map/ppermute | solution.py:19
  872.2 8.3 collective-permute-start.53
  877.7 28.4 %collective-permute-start.51 = (bf16[1,768,768]{1,2,0:T(8,128)(2,1)}, bf16[1,768,768]{1,2,0:T(8,128)(2,1)}, u32[]{:S(2)}, u32[]{:S(2)}) collective-permute-start(bf16[1,768,768]{1,2,0:T(8,128)(2,1)} %fusion.105), channel_id=1, source_target_pairs={{0,2},{1,3},{2,0},{3,1},{4,6},{5,7},{6,4},{7,5},{8,10},{9,11},{10,... | collective-permute-start | bytes 3538952 | tf_op jit(solution)/shard_map/ppermute | solution.py:19
  914.5 16.1 %collective-permute-start.54 = (bf16[4,96,778]{2,1,0:T(8,128)(2,1)S(1)}, bf16[4,96,778]{2,1,0:T(8,128)(2,1)}, u32[]{:S(2)}, u32[]{:S(2)}) collective-permute-start(bf16[4,96,778]{2,1,0:T(8,128)(2,1)S(1)} %dynamic-slice_bitcast_fusion), channel_id=1, source_target_pairs={{0,16},{16,0},{1,17},{17,1},{2,18},{18,2},{3,19},{19,3},{4,20},{20... | collective-permute-start | bytes 1792520 | tf_op jit(solution)/shard_map/ppermute | solution.py:19
  931.9 37.0 %collective-permute-start.55 = (bf16[96,778]{1,0:T(8,128)(2,1)S(1)}, bf16[96,778]{1,0:T(8,128)(2,1)S(1)}, u32[]{:S(2)}, u32[]{:S(2)}) collective-permute-start(bf16[96,778]{1,0:T(8,128)(2,1)S(1)} %get-tuple-element.113), channel_id=1, source_target_pairs={{0,4},{4,0},{8,12},{12,8},{1,5},{5,1},{9,13},{13,9},{2,6},{6,2},{1... | collective-permute-start | bytes 448136 | tf_op jit(solution)/shard_map/ppermute | solution.py:19
  954.1 14.8 %collective-permute-start.57 = (bf16[96,778]{1,0:T(8,128)(2,1)S(1)}, bf16[96,778]{1,0:T(8,128)(2,1)S(1)}, u32[]{:S(2)}, u32[]{:S(2)}) collective-permute-start(bf16[96,778]{1,0:T(8,128)(2,1)S(1)} %get-tuple-element.114), channel_id=1, source_target_pairs={{0,12},{4,8},{8,4},{12,0},{1,13},{5,9},{9,5},{13,1},{2,14},{6,10},... | collective-permute-start | bytes 448136 | tf_op jit(solution)/shard_map/ppermute | solution.py:19
  961.0 14.0 %collective-permute-start.56 = (bf16[96,778]{1,0:T(8,128)(2,1)S(1)}, bf16[96,778]{1,0:T(8,128)(2,1)S(1)}, u32[]{:S(2)}, u32[]{:S(2)}) collective-permute-start(bf16[96,778]{1,0:T(8,128)(2,1)S(1)} %get-tuple-element.115), channel_id=1, source_target_pairs={{0,8},{4,12},{8,0},{12,4},{1,9},{5,13},{9,1},{13,5},{2,10},{6,14},... | collective-permute-start | bytes 448136 | tf_op jit(solution)/shard_map/ppermute | solution.py:19
  975.1 5.9 collective-permute-start.60
  978.5 2.9 collective-permute-start.59
  (114 other events, 1189.6 us)
Sparse Core Ops, SparseCore 0:
  9.6 100.2 all-gather.2
  123.6 128.9 all-gather.4
  553.5 84.8 reduce-scatter.4
  756.1 123.3 reduce-scatter.2

commit v2 on v1

v2 whole, which is shorter than its diff:
```python
import functools

import jax
import jax.numpy as jnp
from jax import lax
from jax.experimental import pallas as pl
from jax.experimental.pallas import tpu as pltpu
from jax.sharding import PartitionSpec as P

HD = 64
PLEN = 1024
CLEN = 128
CONTS = 8

EPSILON = 1e-06
NEGATIVE = -1e30
F32 = jnp.float32
BF16 = jnp.bfloat16
ROOT = 0.7978845608028654
CUBE = 0.044715
UNITS = 768


def xor_swap(value, axis, size, mask):
    return lax.ppermute(value, axis, [(place, place ^ mask) for place in range(size)])


def ring_step(value, axis, size, shift):
    return lax.ppermute(value, axis, [(place, (place + shift) % size) for place in range(size)])


def pick(stacked, index):
    return lax.dynamic_index_in_dim(stacked, index, 0, keepdims=False)


def xor_gather(value, axis, size, order=None):
    if order is None:
        order = [1 << bit for bit in range(size.bit_length() - 1)]
    have = {0: value}
    for mask in order:
        keys = sorted(have)
        moved = xor_swap(jnp.stack([have[key] for key in keys]), axis, size, mask)
        for place, key in enumerate(keys):
            have[key ^ mask] = moved[place]
    return [have[key] for key in range(size)]


def in_order(pieces, me):
    stacked = jnp.stack(pieces)
    return jnp.stack([pick(stacked, me ^ place) for place in range(len(pieces))])


def xor_exchange(pieces, axis, size):
    return [pieces[0]] + [xor_swap(pieces[mask], axis, size, mask) for mask in range(1, size)]


def rms_unit(values):
    factor = lax.rsqrt(jnp.mean(values * values, axis=-1, keepdims=True) + EPSILON)
    return (values * factor, factor)


def rms_backward(grad_normed, unit_part, factor, gain):
    scaled = grad_normed * gain
    inner = jnp.mean(scaled * unit_part, axis=-1, keepdims=True)
    return (factor * (scaled - unit_part * inner), jnp.sum(grad_normed * unit_part, axis=0))


def dot_last(left, right):
    return lax.dot_general(left, right, (((1,), (1,)), ((), ())), preferred_element_type=F32)

def dot_plain(left, right):
    return lax.dot_general(left, right, (((1,), (0,)), ((), ())), preferred_element_type=F32)

def add_all(parts):
    return functools.reduce(jnp.add, parts)

def key_lanes(rows, width):
    return rows[:, : width + (-width) % 128]

def value_lanes(rows, width):
    return rows[:, width - (-width) % 128 :]

def spread_heads(columns, ahead, behind):
    width, count = columns.shape
    groups = []
    for first in range(0, width, HD):
        pieces = [columns[first : first + HD]]
        above, below = ahead + first, width - first - HD + behind
        if above:
            pieces.insert(0, jnp.zeros((above, count), columns.dtype))
        if below:
            pieces.append(jnp.zeros((below, count), columns.dtype))
        groups.append(jnp.concatenate(pieces, axis=0))
    return jnp.concatenate(groups, axis=1)

def causal(scores, count):
    key_row = lax.broadcasted_iota(jnp.int32, scores.shape, 0)
    query_row = lax.broadcasted_iota(jnp.int32, scores.shape, 1) % count
    return jnp.where(key_row <= query_row, scores, NEGATIVE)

def attend_forward_kernel(prompts, scalars, segments, query, local, *rest):
    remote, (out, lse_prompt, lse_cont) = rest[:-3], rest[-3:]
    width = query.shape[0]
    rows = remote[0].shape[1]
    conts = segments.shape[0]
    clen = (local.shape[0] - prompts * rows) // conts
    pad = (-width) % 128

    def attend(start, count, blocks, mask):
        lanes = pl.ds(start, count)
        spread = spread_heads(query[:, lanes], 0, pad)
        scores = [mask(place, dot_plain(key_lanes(block, width), spread)) for place, block in enumerate(blocks)]
        peak = functools.reduce(jnp.maximum, [jnp.max(part, axis=0, keepdims=True) for part in scores])
        shifted = [jnp.exp(part - peak) for part in scores]
        total = add_all([jnp.sum(part, axis=0, keepdims=True) for part in shifted])
        weights = [part.astype(BF16) for part in shifted]
        flipped = [value_lanes(block, width).T for block in blocks]
        for head in range(width // HD):
            group = slice(head * count, (head + 1) * count)
            part = slice(pad + head * HD, pad + (head + 1) * HD)
            mixed = add_all([dot_plain(flip[part], one[:, group]) for flip, one in zip(flipped, weights)])
            out[head * HD : (head + 1) * HD, lanes] = (mixed / total[:, group]).astype(BF16)
        return peak + jnp.log(total)

    @pl.loop(0, prompts)
    def _(prompt):
        start = pl.multiple_of(prompt * rows, rows)
        blocks = [local[pl.ds(start, rows), :]] + [one[prompt] for one in remote]
        lse_prompt[prompt] = attend(start, rows, blocks,
            lambda place, scores: jnp.where(place <= scalars[0], scores, NEGATIVE) if place else causal(scores, rows))

    @pl.loop(0, conts)
    def _(cont):
        start = pl.multiple_of(prompts * rows + cont * clen, clen)
        segment = segments[cont]
        first = pl.multiple_of(segment * rows, rows)
        blocks = [local[pl.ds(start, clen), :], local[pl.ds(first, rows), :]] + [one[segment] for one in remote]
        lse_cont[cont] = attend(start, clen, blocks, lambda place, scores: scores if place else causal(scores, clen))

def attend_backward_kernel(prompts, scalars, segments, query, grad, lse_prompt, lse_cont, local, *rest):
    places = (len(rest) - 2) // 2 + 1
    remote, (grad_query, grad_local), grad_remote, sums = rest[: places - 1], rest[places - 1 : places + 1], rest[places + 1 : -1], rest[-1]
    width = query.shape[0]
    rows = remote[0].shape[1]
    conts = segments.shape[0]
    clen = (local.shape[0] - prompts * rows) // conts
    pad = (-width) % 128

    def attend(start, count, lse, blocks, mask):
        lanes = pl.ds(start, count)
        query_spread = spread_heads(query[:, lanes], 0, pad)
        grad_spread = spread_heads(grad[:, lanes], pad, 0)
        weights = [jnp.exp(mask(place, dot_plain(key_lanes(block, width), query_spread)) - lse) for place, block in enumerate(blocks)]
        slopes = [dot_plain(value_lanes(block, width), grad_spread) for block in blocks]
        centre = add_all([jnp.sum(part * slope, axis=0, keepdims=True) for part, slope in zip(weights, slopes)])
        grad_scores = [(part * (slope - centre)).astype(BF16) for part, slope in zip(weights, slopes)]
        flipped = [key_lanes(block, width).T for block in blocks]
        for head in range(width // HD):
            group = slice(head * count, (head + 1) * count)
            part = slice(head * HD, (head + 1) * HD)
            mixed = add_all([dot_plain(flip[part], one[:, group]) for flip, one in zip(flipped, grad_scores)])
            grad_query[part, lanes] = (mixed * 0.125).astype(BF16)
        results = []
        for part, one in zip(weights, grad_scores):
            key_part = dot_last(one, query_spread)
            value_part = dot_last(part.astype(BF16), grad_spread)
            if pad:
                edge = width - pad
                results.append(jnp.concatenate([key_part[:, :edge], key_part[:, edge:] + value_part[:, : 2 * pad], value_part[:, 2 * pad :]], axis=1))
            else:
                results.append(jnp.concatenate([key_part, value_part], axis=1))
        return results

    @pl.loop(0, prompts)
    def _(prompt):
        start = pl.multiple_of(prompt * rows, rows)
        blocks = [local[pl.ds(start, rows), :]] + [one[prompt] for one in remote]
        results = attend(start, rows, lse_prompt[prompt], blocks,
            lambda place, scores: jnp.where(place <= scalars[0], scores, NEGATIVE) if place else causal(scores, rows))
        for place in range(places):
            sums[place, prompt] = results[place]

    @pl.loop(0, conts)
    def _(cont):
        start = pl.multiple_of(prompts * rows + cont * clen, clen)
        segment = segments[cont]
        first = pl.multiple_of(segment * rows, rows)
        blocks = [local[pl.ds(start, clen), :], local[pl.ds(first, rows), :]] + [one[segment] for one in remote]
        results = attend(start, clen, lse_cont[cont], blocks, lambda place, scores: scores if place else causal(scores, clen))
        grad_local[pl.ds(start, clen), :] = results[0].astype(BF16)
        for place in range(places):
            sums[place, segment] += results[place + 1]

    @pl.loop(0, prompts)
    def _(prompt):
        grad_local[pl.ds(pl.multiple_of(prompt * rows, rows), rows), :] = sums[0, prompt].astype(BF16)
        for place in range(1, places):
            grad_remote[place - 1][prompt] = sums[place, prompt].astype(BF16)

VM = pl.BlockSpec(memory_space=pltpu.VMEM)
SM = pl.BlockSpec(memory_space=pltpu.SMEM)

def attend_forward(scalars, segments, query, local, remote):
    prompts, rows, _ = remote[0].shape
    conts = segments.shape[0]
    clen = (local.shape[0] - prompts * rows) // conts
    heads = query.shape[0] // HD
    scores = heads * (prompts * rows * (len(remote) + 1) * rows + conts * clen * ((len(remote) + 1) * rows + clen))
    return pl.pallas_call(functools.partial(attend_forward_kernel, prompts),
        out_shape=(jax.ShapeDtypeStruct(query.shape, BF16), jax.ShapeDtypeStruct((prompts, 1, heads * rows), F32), jax.ShapeDtypeStruct((conts, 1, heads * clen), F32)),
        in_specs=[SM, SM] + [VM] * (2 + len(remote)), out_specs=(VM,) * 3,
        compiler_params=pltpu.CompilerParams(vmem_limit_bytes=56 * 2**20),
        cost_estimate=pl.CostEstimate(flops=16 * HD * scores, bytes_accessed=10**7, transcendentals=scores),
    )(scalars, segments, query, local, *remote)

def attend_backward(scalars, segments, query, grad, lse_prompt, lse_cont, local, remote):
    prompts, rows, _ = remote[0].shape
    conts = segments.shape[0]
    clen = (local.shape[0] - prompts * rows) // conts
    heads = query.shape[0] // HD
    scores = heads * (prompts * rows * (len(remote) + 1) * rows + conts * clen * ((len(remote) + 1) * rows + clen))
    shape = lambda value: jax.ShapeDtypeStruct(value.shape, BF16)
    return pl.pallas_call(functools.partial(attend_backward_kernel, prompts),
        out_shape=(shape(query), shape(local)) + tuple(shape(one) for one in remote),
        in_specs=[SM, SM] + [VM] * (5 + len(remote)), out_specs=(VM,) * (2 + len(remote)),
        scratch_shapes=[pltpu.VMEM((len(remote) + 1,) + remote[0].shape, F32)],
        compiler_params=pltpu.CompilerParams(vmem_limit_bytes=60 * 2**20),
        cost_estimate=pl.CostEstimate(flops=40 * HD * scores, bytes_accessed=2 * 10**7, transcendentals=scores),
    )(scalars, segments, query, grad, lse_prompt, lse_cont, local, *remote)


def expert_forward_kernel(rows, up, down, produced, hidden_pre, total):
    step = pl.program_id(0)
    pre = dot_plain(rows[...], up[...])
    hidden_pre[...] = pre
    inner = ROOT * (pre + CUBE * (pre * pre * pre))
    hidden = (0.5 * pre * (1.0 + jnp.tanh(inner))).astype(BF16)
    part = dot_plain(hidden, down[...])
    @pl.when(step == 0)
    def _():
        total[...] = part
    @pl.when(step > 0)
    def _():
        total[...] += part
    @pl.when(step == pl.num_programs(0) - 1)
    def _():
        produced[...] = total[...].astype(BF16)

def expert_backward_kernel(rows, grads, hidden_pre, up, down, rows_grad, grad_up, grad_down, total, rows_flip, grads_flip):
    step = pl.program_id(0)
    @pl.when(step == 0)
    def _():
        rows_flip[...] = rows[...].T
        grads_flip[...] = grads[...].T
    pre = hidden_pre[...]
    square = pre * pre
    bend = jnp.tanh(ROOT * (pre + CUBE * (square * pre)))
    half = 0.5 * (1.0 + bend)
    hidden = (pre * half).astype(BF16)
    slope = half + (0.5 * ROOT) * pre * (1.0 - bend * bend) * (1.0 + (3.0 * CUBE) * square)
    grad_hidden = dot_last(grads[...], down[...])
    grad_pre = (grad_hidden * slope).astype(BF16)
    grad_down[...] = dot_plain(grads_flip[...], hidden).astype(BF16)
    grad_up[...] = dot_plain(rows_flip[...], grad_pre).astype(BF16)
    part = dot_last(grad_pre, up[...])
    @pl.when(step == 0)
    def _():
        total[...] = part
    @pl.when(step > 0)
    def _():
        total[...] += part
    @pl.when(step == pl.num_programs(0) - 1)
    def _():
        rows_grad[...] = total[...].astype(BF16)

def expert_forward(rows, up, down):
    n, width = rows.shape
    units = up.shape[1]
    return pl.pallas_call(expert_forward_kernel, grid=(units // UNITS,),
        in_specs=[pl.BlockSpec((n, width), lambda i: (0, 0)), pl.BlockSpec((width, UNITS), lambda i: (0, i)), pl.BlockSpec((UNITS, width), lambda i: (i, 0))],
        out_specs=(pl.BlockSpec((n, width), lambda i: (0, 0)), pl.BlockSpec((n, UNITS), lambda i: (0, i))),
        out_shape=(jax.ShapeDtypeStruct((n, width), BF16), jax.ShapeDtypeStruct((n, units), F32)),
        scratch_shapes=[pltpu.VMEM((n, width), F32)],
        compiler_params=pltpu.CompilerParams(vmem_limit_bytes=56 * 2**20),
    )(rows, up, down)

def expert_backward(rows, grads, pre, up, down):
    n, width = rows.shape
    units = up.shape[1]
    whole = pl.BlockSpec((n, width), lambda i: (0, 0))
    return pl.pallas_call(expert_backward_kernel, grid=(units // UNITS,),
        in_specs=[whole, whole, pl.BlockSpec((n, UNITS), lambda i: (0, i)), pl.BlockSpec((width, UNITS), lambda i: (0, i)), pl.BlockSpec((UNITS, width), lambda i: (i, 0))],
        out_specs=(whole, pl.BlockSpec((width, UNITS), lambda i: (0, i)), pl.BlockSpec((width, UNITS), lambda i: (0, i))),
        out_shape=(jax.ShapeDtypeStruct((n, width), BF16), jax.ShapeDtypeStruct((width, units), BF16), jax.ShapeDtypeStruct((width, units), BF16)),
        scratch_shapes=[pltpu.VMEM((n, width), F32), pltpu.VMEM((width, n), BF16), pltpu.VMEM((width, n), BF16)],
        compiler_params=pltpu.CompilerParams(vmem_limit_bytes=60 * 2**20),
    )(rows, grads, pre, up, down)


def slot_dispatch(chosen, priority, first, expert_count, capacity):
    tokens = chosen.shape[0]
    expert_range = jnp.arange(expert_count)
    chosen_hot = chosen[:, None] == expert_range[None, :]
    order_hot = (priority[:, None] == jnp.arange(tokens)[None, :]).astype(BF16)
    sorted_hot = jnp.dot(order_hot, chosen_hot.astype(BF16), preferred_element_type=F32)
    places = jnp.arange(tokens)
    before = (places[:, None] > places[None, :]).astype(BF16)
    earlier = jnp.dot(before, sorted_hot.astype(BF16), preferred_element_type=F32)
    sorted_rank = jnp.minimum(jnp.sum(earlier * sorted_hot, axis=1), capacity)
    rank = jnp.einsum(
        "it,i->t", order_hot, sorted_rank.astype(BF16), preferred_element_type=F32
    ).astype(jnp.int32)
    place = jnp.where(rank < capacity, (chosen ^ first) * capacity + rank, -1)
    dispatch = place[:, None] == jnp.arange(expert_count * capacity)[None, :]
    return (chosen_hot, dispatch.astype(BF16))


def shards(
    tokens,
    cotangent,
    gains,
    qkv_weight,
    proj_weight,
    router_weight,
    expert_up,
    expert_down,
    expert_ids,
    slot_order,
    segment_ids,
):
    dp_count, ctx_count, tp_count = (lax.axis_size(name) for name in ("dp", "ctx", "tp"))
    dp_index, ctx_index, tp_index = (lax.axis_index(name) for name in ("dp", "ctx", "tp"))
    group = dp_count * tp_count
    group_index = dp_index * tp_count + tp_index
    tok_dev, width = tokens.shape
    expert_count = router_weight.shape[1]
    capacity = 5 * tok_dev // (4 * expert_count)
    prompt_rows = PLEN // ctx_count
    conts_here = segment_ids.shape[0]
    prompts_here = conts_here * ctx_count // CONTS
    head_rows = prompts_here * prompt_rows
    local_width = qkv_weight.shape[2]
    shard_rows = qkv_weight.shape[1]
    tp_order = [2, 1]

    full_up = lax.all_gather(expert_up, "ctx", axis=2, tiled=True)[0]

    def gather_weights(part):
        by_ctx = in_order(xor_gather(part, "ctx", ctx_count), ctx_index)
        by_dp = in_order(xor_gather(by_ctx, "dp", dp_count), dp_index)
        return by_dp.reshape(dp_count * ctx_count * part.shape[0], part.shape[1])

    full_qkv = gather_weights(qkv_weight.transpose(1, 0, 2).reshape(shard_rows, 3 * local_width))
    proj_router = gather_weights(jnp.concatenate([proj_weight.T, router_weight], axis=1))
    full_router = proj_router[:, local_width:]
    proj_near = jnp.concatenate(
        xor_gather(proj_router[:, :local_width], "tp", tp_count, tp_order), axis=1
    )

    block_rows = in_order(xor_gather(tokens, "tp", tp_count, tp_order), tp_index).reshape(-1, width)
    unit_block, _ = rms_unit(block_rows.astype(F32))
    normed_one = (gains[0] * unit_block).astype(BF16)
    query_weight, pair_weight = full_qkv[:, :local_width], full_qkv[:, local_width:]
    query = (
        jnp.einsum("dc,rd->cr", query_weight, normed_one, preferred_element_type=F32) * 0.125
    ).astype(BF16)
    local = jnp.dot(normed_one, pair_weight, preferred_element_type=F32).astype(BF16)
    ring = [local[:head_rows].reshape(prompts_here, prompt_rows, 2 * local_width)]
    for _ in range(ctx_count - 1):
        ring.append(ring_step(ring[-1], "ctx", ctx_count, 1))
    remote = ring[1:]
    scalars = ctx_index.astype(jnp.int32).reshape(1)
    attended, lse_prompt, lse_cont = attend_forward(scalars, segment_ids, query, local, remote)
    down_after, _ = lax.optimization_barrier((expert_down, remote[-1]))
    full_down = lax.all_gather(down_after, "ctx", axis=1, tiled=True)[0]

    def row_block(columns, k):
        return lax.dynamic_slice_in_dim(columns, (tp_index ^ k) * tok_dev, tok_dev, 1)

    attended_near = jnp.concatenate(
        xor_exchange([row_block(attended, k) for k in range(tp_count)], "tp", tp_count), axis=0
    )
    branch = jnp.einsum("cr,dc->rd", attended_near, proj_near, preferred_element_type=F32)
    tokens_wide = tokens.astype(F32)
    middle = tokens_wide + branch
    unit_two, factor_two = rms_unit(middle)
    normed_two = (gains[1] * unit_two).astype(BF16)
    logits = jnp.dot(normed_two, full_router, preferred_element_type=F32)
    router_probs = jax.nn.softmax(logits, axis=-1)
    chosen_hot, dispatch = slot_dispatch(
        expert_ids[:, 0], slot_order[0], group_index, expert_count, capacity
    )
    gate_value = jnp.sum(jnp.where(chosen_hot, router_probs, 0.0), axis=-1)

    def to_slots(rows):
        return jnp.einsum("tj,td->jd", dispatch, rows, preferred_element_type=F32).astype(BF16)

    def from_slots(rows):
        return jnp.dot(dispatch, rows, preferred_element_type=F32)

    def exchange_slots(rows):
        pieces = rows.reshape(group, -1, width)
        moved = xor_exchange([pieces[k] for k in range(group)], ("dp", "tp"), group)
        return jnp.concatenate(moved, axis=0)

    upstream = cotangent.astype(F32)
    weighted = (gate_value[:, None] * upstream).astype(BF16)
    arrived = exchange_slots(to_slots(normed_two))
    grad_arrived = exchange_slots(to_slots(weighted))
    produced, hidden_pre = expert_forward(arrived, full_up, full_down)
    rows_grad, up_part, down_part = expert_backward(
        arrived, grad_arrived, hidden_pre, full_up, full_down
    )
    routed_rows = from_slots(exchange_slots(produced))
    grad_returned = from_slots(exchange_slots(rows_grad))
    grad_up = lax.psum_scatter(up_part, "ctx", scatter_dimension=1, tiled=True).astype(F32)[None]

    output = (middle + gate_value[:, None] * routed_rows).astype(BF16)
    grad_gate = jnp.sum(upstream * routed_rows, axis=-1)
    grad_logits = (
        (grad_gate * gate_value)[:, None] * (chosen_hot.astype(F32) - router_probs)
    ).astype(BF16)
    router_part = jnp.einsum("td,te->de", normed_two, grad_logits, preferred_element_type=F32)
    grad_second = grad_returned + jnp.einsum(
        "te,de->td", grad_logits, full_router, preferred_element_type=F32
    )
    middle_part, gain_two = rms_backward(grad_second, unit_two, factor_two, gains[1])
    grad_middle = upstream + middle_part
    grad_low = grad_middle.astype(BF16)
    grad_near = jnp.einsum("dc,rd->cr", proj_near, grad_low, preferred_element_type=F32)
    grad_near = grad_near.astype(BF16).reshape(tp_count, local_width, tok_dev)
    grad_rows = xor_exchange([grad_near[k] for k in range(tp_count)], "tp", tp_count)
    grad_rows = jnp.stack(grad_rows)
    grad_attended = jnp.concatenate(
        [pick(grad_rows, tp_index ^ place) for place in range(tp_count)], axis=1
    )
    grad_query, grad_local, *grad_remote = attend_backward(
        scalars, segment_ids, query, grad_attended, lse_prompt, lse_cont, local, remote
    )
    running = grad_remote[-1]
    own_pair = grad_local[:head_rows].reshape(running.shape)
    for before in ([own_pair] + grad_remote[:-1])[::-1]:
        arriving = ring_step(running, "ctx", ctx_count, -1)
        running = (before.astype(F32) + arriving.astype(F32)).astype(BF16)
    down_part, _ = lax.optimization_barrier((down_part, running))
    grad_down = lax.psum_scatter(down_part, "ctx", scatter_dimension=1, tiled=True)
    grad_down = grad_down.T.astype(F32)[None]
    grad_pair = jnp.concatenate(
        [running.reshape(head_rows, 2 * local_width), grad_local[head_rows:]], axis=0
    )
    qkv_part = jnp.concatenate(
        [
            jnp.einsum("rd,cr->dc", normed_one, grad_query, preferred_element_type=F32),
            jnp.einsum("rd,rc->dc", normed_one, grad_pair, preferred_element_type=F32),
        ],
        axis=1,
    )
    pair_blocks = grad_pair.reshape(tp_count, tok_dev, 2 * local_width)
    first_near = [
        jnp.einsum(
            "cr,dc->rd", row_block(grad_query, k), query_weight, preferred_element_type=F32
        )
        + jnp.einsum(
            "rc,dc->rd", pick(pair_blocks, tp_index ^ k), pair_weight, preferred_element_type=F32
        )
        for k in range(tp_count)
    ]

    def scatter_near(pieces, order):
        pieces = dict(enumerate(pieces))
        for mask in order:
            sent = [key for key in sorted(pieces) if key & mask]
            moved = xor_swap(
                jnp.stack([pieces[key].astype(BF16) for key in sent]), "tp", tp_count, mask
            )
            for place, key in enumerate(sent):
                pieces[key ^ mask] = pieces[key ^ mask] + moved[place].astype(F32)
                del pieces[key]
        return pieces[0]

    scatter_order = tp_order[::-1]
    grad_first = scatter_near(first_near, scatter_order)
    unit_one, factor_one = rms_unit(tokens_wide)
    rows_part, gain_one = rms_backward(grad_first, unit_one, factor_one, gains[0])
    grad_tokens = rows_part + grad_middle

    proj_blocks = jnp.einsum("cr,rd->dc", attended_near, grad_low, preferred_element_type=F32)
    proj_part = scatter_near(
        [proj_blocks[:, k * local_width : (k + 1) * local_width] for k in range(tp_count)],
        scatter_order,
    )
    small_part = jnp.concatenate(
        [router_part, jnp.stack([gain_one, gain_two], axis=1)], axis=1
    )
    packed = jnp.concatenate([qkv_part, proj_part, small_part], axis=1)
    packed = packed.reshape(dp_count, ctx_count, shard_rows, -1).astype(BF16)

    def scatter_ordered(values, axis, size, me):
        moved = xor_exchange([pick(values, me ^ k) for k in range(size)], axis, size)
        return sum(piece.astype(F32) for piece in moved)

    summed = scatter_ordered(packed, "dp", dp_count, dp_index).astype(BF16)
    summed = scatter_ordered(summed, "ctx", ctx_count, ctx_index)
    small_sum = summed[:, 4 * local_width :]
    small_all = xor_exchange([small_sum.astype(BF16)] * tp_count, "tp", tp_count)
    small_sum = small_sum + sum(piece.astype(F32) for piece in small_all[1:])
    grad_qkv = summed[:, : 3 * local_width].reshape(shard_rows, 3, local_width).transpose(1, 0, 2)
    grad_proj = summed[:, 3 * local_width : 4 * local_width].T
    grad_router = small_sum[:, :expert_count]
    grad_gains = small_sum[:, expert_count:].T
    return (output, grad_tokens, grad_gains, grad_qkv, grad_proj, grad_router, grad_up, grad_down)


def solution(mesh):
    in_specs = (
        P(("dp", "ctx", "tp"), None),
        P(("dp", "ctx", "tp"), None),
        P(),
        P(None, ("dp", "ctx"), "tp"),
        P("tp", ("dp", "ctx")),
        P(("dp", "ctx"), None),
        P(("dp", "tp"), None, "ctx"),
        P(("dp", "tp"), "ctx", None),
        P(("dp", "ctx", "tp"), None),
        P(("dp", "ctx", "tp"), None),
        P(("dp", "ctx")),
    )
    out_specs = (
        P(("dp", "ctx", "tp"), None),
        P(("dp", "ctx", "tp"), None),
        P(None, ("dp", "ctx")),
        P(None, ("dp", "ctx"), "tp"),
        P("tp", ("dp", "ctx")),
        P(("dp", "ctx"), None),
        P(("dp", "tp"), None, "ctx"),
        P(("dp", "tp"), "ctx", None),
    )
    return jax.shard_map(shards, mesh=mesh, in_specs=in_specs, out_specs=out_specs, check_vma=False)
```

time: 1010 us -> 743 us (0.74)
  matrix products: 252 us -> 50.5 us
  Pallas kernels: 0 us -> 115 us
  other arithmetic: 102 us -> 36.7 us
  local copies, waits for them, and re-layouts: 122 us -> 69 us
  waiting for transfers between devices: 414 us -> 379 us
  starting transfers between devices: 89.1 us -> 65.1 us
    dot_general x29 -> x15, matrix products: 240 us -> 37.5 us  [the longest x4 8.13 us: shards(): jnp.einsum('cr,dc->rd', row_block(grad_query, k), query_weight, preferred...]
    pallas_call x0 -> x4, Pallas kernels: none -> 115 us  [the longest x1 45.1 us: attend_backward(): pl.pallas_call(functools.partial(attend_backward_kernel, prompts), out_sh...]
    ppermute x55, waiting for transfers between devices: 262 us -> 185 us  [xor_swap(): lax.ppermute(value, axis, [(place, place ^ mask) for place in range(size)])]
    ppermute x6, waiting for transfers between devices: 152 us -> 194 us  [ring_step(): lax.ppermute(value, axis, [(place, (place + shift) % size) for place in r...]
    convert_element_type x8 -> x3, other arithmetic: 42.5 us -> 3.31 us  [shards(): running = (before.astype(F32) + arriving.astype(F32)).astype(BF16)]
    ppermute x55, starting transfers between devices: 87.9 us -> 59.3 us  [xor_swap(): lax.ppermute(value, axis, [(place, place ^ mask) for place in range(size)])]
    reduce_sum x2 -> x0, other arithmetic: 19.7 us -> none  [attend_forward(): total = jnp.sum(shifted, axis=-1, keepdims=True)]
    another operation x8 -> x2, local copies, waits for them, and re-layouts: 17.2 us -> 2.77 us  [the longest x3 14.6 us: shards(): jnp.stack(pair_total)]
  transfers between devices with their start and end apart: 65 -> 65, of which waited for: 31 -> 28; matrix products, arithmetic and copies ran while one was open for 44% -> 19% of each run, Pallas kernels for 0% -> 13%
where the time goes in v2:
time: 743 us; the launch traced here: 731 us
  waiting for transfers between devices  379 us (51%)
  Pallas kernels  115 us (15%)
  local copies, waits for them, and re-layouts  69 us (9%)
  starting transfers between devices  65.1 us (9%)
  matrix products  50.5 us (7%)
  other arithmetic  36.7 us (5%)
  between operations  15.5 us (2%)
    ppermute x6, waiting for transfers between devices, ring_step(): lax.ppermute(value, axis, [(place, (place + shift) % size) for place in r...  194 us
    ppermute x55, waiting for transfers between devices, xor_swap(): lax.ppermute(value, axis, [(place, place ^ mask) for place in range(size)])  185 us
    ppermute x55, starting transfers between devices, xor_swap(): lax.ppermute(value, axis, [(place, place ^ mask) for place in range(size)])  59.3 us
    pallas_call x1, Pallas kernels, attend_backward(): pl.pallas_call(functools.partial(attend_backward_kernel, prompts), out_sh...  45.1 us
    unnamed x153, local copies, waits for them, and re-layouts  36.1 us
    pallas_call x1, Pallas kernels, expert_backward(): pl.pallas_call(expert_backward_kernel, grid=(units // UNITS,), in_specs=[...  28.2 us
    pallas_call x1, Pallas kernels, attend_forward(): pl.pallas_call(functools.partial(attend_forward_kernel, prompts), out_sha...  24.9 us
    pallas_call x1, Pallas kernels, expert_forward(): pl.pallas_call(expert_forward_kernel, grid=(units // UNITS,), in_specs=[p...  16.7 us
  transfers between devices with their start and end apart: 65, of which 28 were waited for; matrix products, arithmetic and copies ran while one was open for 19% of the time, Pallas kernels for 13%

profile of v2, /device:TPU:25, one launch (start us, length us, event | category | flops | bytes accessed | tf_op | source)
XLA Modules:
  0.0 730.7 jit_solution(9836804632057222988)
XLA Ops:
  8.5 25.8 %collective-permute-done.3 = bf16[1,768,768]{2,1,0:T(8,128)(2,1)S(1)} collective-permute-done((bf16[1,768,768]{2,1,0:T(8,128)(2,1)}, bf16[1,768,768]{2,1,0:T(8,128)(2,1)S(1)}, u32[]{:S(2)}, u32[]{:S(2)}) %collective-permute-start.3) | collective-permute-done | bytes 1179680 | tf_op jit(solution)/shard_map/ppermute | solution.py:25
  34.3 2.9 pad_maximum_fusion.1
  39.2 5.3 collective-permute-done
  44.7 16.0 %collective-permute-done.1 = bf16[2,96,576]{1,2,0:T(8,128)(2,1)S(1)} collective-permute-done((bf16[2,96,576]{1,2,0:T(8,128)(2,1)S(1)}, bf16[2,96,576]{1,2,0:T(8,128)(2,1)S(1)}, u32[]{:S(2)}, u32[]{:S(2)}) %collective-permute-start.1) | collective-permute-done | bytes 221216 | tf_op jit(solution)/shard_map/ppermute | solution.py:25
  62.8 10.9 %collective-permute-done.2 = bf16[1,4,96,576]{3,2,1,0:T(8,128)(2,1)S(1)} collective-permute-done((bf16[1,4,96,576]{3,2,1,0:T(8,128)(2,1)S(1)}, bf16[1,4,96,576]{3,2,1,0:T(8,128)(2,1)S(1)}, u32[]{:S(2)}, u32[]{:S(2)}) %collective-permute-start.2) | collective-permute-done | bytes 442400 | tf_op jit(solution)/shard_map/ppermute | solution.py:25
  79.9 2.8 maximum_convert_fusion
  84.2 3.0 convolution_convert_fusion.local
  87.5 80.3 %collective-permute-done.5.rest_0_ = bf16[6,256,384]{2,1,0:T(8,128)(2,1)S(1)} collective-permute-done((bf16[6,256,384]{2,1,0:T(8,128)(2,1)S(1)}, bf16[6,256,384]{2,1,0:T(8,128)(2,1)S(1)}, u32[]{:S(2)}, u32[]{:S(2)}) %collective-permute-start.5) | collective-permute-done | bytes 1179680 | tf_op jit(solution)/shard_map/ppermute | solution.py:29
  167.8 31.5 %collective-permute-done.6.rest_1_ = bf16[6,256,384]{2,1,0:T(8,128)(2,1)} collective-permute-done((bf16[6,256,384]{2,1,0:T(8,128)(2,1)S(1)}, bf16[6,256,384]{2,1,0:T(8,128)(2,1)}, u32[]{:S(2)}, u32[]{:S(2)}) %collective-permute-start.6) | collective-permute-done | bytes 1179680 | tf_op jit(solution)/shard_map/ppermute | solution.py:29
  199.3 2.9 collective-permute-start.7
  202.3 25.0 %collective-permute-done.11 = bf16[1,96,200]{1,2,0:T(8,128)(2,1)S(1)} collective-permute-done((bf16[1,96,200]{1,2,0:T(8,128)(2,1)S(1)}, bf16[1,96,200]{1,2,0:T(8,128)(2,1)S(1)}, u32[]{:S(2)}, u32[]{:S(2)}) %collective-permute-start.11) | collective-permute-done | bytes 38432 | tf_op jit(solution)/shard_map/ppermute | solution.py:25
  228.9 2.9 collective-permute-done.12
  234.2 2.5 collective-permute-done.13
  240.1 3.8 collective-permute-done.14
  244.9 5.8 collective-permute-start.15
  250.7 5.5 fusion.2.query
  256.2 24.9 %shard_map.170 = (bf16[192,3072]{1,0:T(8,128)(2,1)}, f32[6,1,768]{2,1,0:T(1,128)}, f32[12,1,384]{2,1,0:T(1,128)}) custom-call(s32[1]{0:T(128)} %bitcast.scalars, s32[12]{0:T(128)} %segments.3, bf16[192,3072]{1,0:T(8,128)(2,1)} %fusion.2.query, bf16[3072,384]{1,0:T(8,128)(2,1)} %copy-done.21, bf16[6,256,384]{2,1,0:T(8,128)(2,1)} %copy-done.59, ...), custom_call_target="tpu_custom_call" | custom-call | flops 10267656192 | bytes 10000000 | tf_op jit(solution)/shard_map/pallas_call | solution.py:209
  281.1 2.4 constant_dynamic-slice_fusion.7
  286.0 2.5 copy.102
  289.6 3.7 collective-permute-done.10
  293.3 5.1 collective-permute-done.9
  298.4 2.4 multiply_reduce_fusion.3
  312.8 2.1 collective-permute-start.35
  320.5 6.6 collective-permute-done.34
  337.6 8.9 %collective-permute-done.20 = bf16[120,768]{1,0:T(8,128)(2,1)S(1)} collective-permute-done((bf16[120,768]{1,0:T(8,128)(2,1)S(1)}, bf16[120,768]{1,0:T(8,128)(2,1)S(1)}, u32[]{:S(2)}, u32[]{:S(2)}) %collective-permute-start.20) | collective-permute-done | bytes 184352 | tf_op jit(solution)/shard_map/ppermute | solution.py:25
  348.6 16.7 %shard_map.171 = (bf16[960,768]{1,0:T(8,128)(2,1)}, f32[960,3072]{1,0:T(8,128)}) custom-call(bf16[960,768]{1,0:T(8,128)(2,1)} %constant_dynamic-update-slice_fusion.rows, bf16[768,3072]{1,0:T(8,128)(2,1)} %bitcast.165, bf16[3072,768]{1,0:T(8,128)(2,1)} %bitcast.167), custom_call_target="tpu_custom_call" | custom-call | tf_op jit(solution)/shard_map/pallas_call | solution.py:279
  365.2 2.6 fusion.116
  368.6 28.2 %shard_map.172 = (bf16[960,768]{1,0:T(8,128)(2,1)}, bf16[768,3072]{1,0:T(8,128)(2,1)}, bf16[768,3072]{1,0:T(8,128)(2,1)}) custom-call(bf16[960,768]{1,0:T(8,128)(2,1)} %constant_dynamic-update-slice_fusion.rows, bf16[960,768]{1,0:T(8,128)(2,1)} %constant_dynamic-update-slice_fusion.14.grads, f32[960,3072]{1,0:T(8,128)} %get-tuple-element.26.hidden_pre, ...), custom_call_target="tpu_custom_call" | custom-call | tf_op jit(solution)/shard_map/pallas_call | solution.py:291
  396.8 2.5 fusion.114
  407.5 7.4 %collective-permute-done.25 = bf16[120,768]{1,0:T(8,128)(2,1)S(1)} collective-permute-done((bf16[120,768]{1,0:T(8,128)(2,1)}, bf16[120,768]{1,0:T(8,128)(2,1)S(1)}, u32[]{:S(2)}, u32[]{:S(2)}) %collective-permute-start.25) | collective-permute-done | bytes 184352 | tf_op jit(solution)/shard_map/ppermute | solution.py:25
  418.2 7.4 %collective-permute-done.27 = bf16[120,768]{1,0:T(8,128)(2,1)S(1)} collective-permute-done((bf16[120,768]{1,0:T(8,128)(2,1)}, bf16[120,768]{1,0:T(8,128)(2,1)S(1)}, u32[]{:S(2)}, u32[]{:S(2)}) %collective-permute-start.27) | collective-permute-done | bytes 184352 | tf_op jit(solution)/shard_map/ppermute | solution.py:25
  428.8 4.2 collective-permute-done.29
  433.7 3.1 fusion.16
  441.0 2.0 collective-permute-start.43
  445.0 4.6 collective-permute-done.43
  449.7 2.3 multiply_reduce_fusion.1
  457.6 6.7 collective-permute-done.45
  464.3 6.9 collective-permute-done.46
  472.6 45.1 %shard_map.173 = (bf16[192,3072]{1,0:T(8,128)(2,1)}, bf16[3072,384]{1,0:T(8,128)(2,1)}, bf16[6,256,384]{2,1,0:T(8,128)(2,1)}, bf16[6,256,384]{2,1,0:T(8,128)(2,1)}, bf16[6,256,384]{2,1,0:T(8,128)(2,1)}) custom-call(s32[1]{0:T(128)} %bitcast.scalars, s32[12]{0:T(128)} %segments.3, bf16[192,3072]{1,0:T(8,128)(2,1)} %fusion.2.query, ...), custom_call_target="tpu_custom_call" | custom-call | flops 25669140480 | bytes 20000000 | tf_op jit(solution)/shard_map/pallas_call | solution.py:223
  517.7 2.3 collective-permute-start.47
  520.0 27.8 %collective-permute-done.47 = bf16[6,256,384]{2,1,0:T(8,128)(2,1)S(1)} collective-permute-done((bf16[6,256,384]{2,1,0:T(8,128)(2,1)}, bf16[6,256,384]{2,1,0:T(8,128)(2,1)S(1)}, u32[]{:S(2)}, u32[]{:S(2)}) %collective-permute-start.47) | collective-permute-done | bytes 1179680 | tf_op jit(solution)/shard_map/ppermute | solution.py:29
  549.7 28.7 %collective-permute-done.48 = bf16[6,256,384]{2,1,0:T(8,128)(2,1)S(1)} collective-permute-done((bf16[6,256,384]{2,1,0:T(8,128)(2,1)S(1)}, bf16[6,256,384]{2,1,0:T(8,128)(2,1)S(1)}, u32[]{:S(2)}, u32[]{:S(2)}) %collective-permute-start.48) | collective-permute-done | bytes 1179680 | tf_op jit(solution)/shard_map/ppermute | solution.py:29
  581.3 25.4 %collective-permute-done.49 = bf16[6,256,384]{2,1,0:T(8,128)(2,1)S(1)} collective-permute-done((bf16[6,256,384]{2,1,0:T(8,128)(2,1)S(1)}, bf16[6,256,384]{2,1,0:T(8,128)(2,1)S(1)}, u32[]{:S(2)}, u32[]{:S(2)}) %collective-permute-start.49) | collective-permute-done | bytes 1179680 | tf_op jit(solution)/shard_map/ppermute | solution.py:29
  615.5 2.3 collective-permute-start.50
  617.8 3.8 fusion.120
  623.8 6.7 copy.113
  636.4 3.0 fusion.39
  640.5 2.2 convolution_convert_fusion.2
  642.9 2.0 fusion.58
  646.8 2.0 fusion.65
  648.8 5.8 fusion.43
  654.6 13.6 %collective-permute-done.51 = bf16[1,768,768]{1,2,0:T(8,128)(2,1)} collective-permute-done((bf16[1,768,768]{1,2,0:T(8,128)(2,1)}, bf16[1,768,768]{1,2,0:T(8,128)(2,1)}, u32[]{:S(2)}, u32[]{:S(2)}) %collective-permute-start.51) | collective-permute-done | bytes 1179680 | tf_op jit(solution)/shard_map/ppermute | solution.py:25
  668.2 4.2 fusion.13
  672.7 2.9 concatenate.53
  676.5 2.4 copy.119
  678.9 13.2 %collective-permute-done.54 = bf16[4,96,778]{2,1,0:T(8,128)(2,1)} collective-permute-done((bf16[4,96,778]{2,1,0:T(8,128)(2,1)S(1)}, bf16[4,96,778]{2,1,0:T(8,128)(2,1)}, u32[]{:S(2)}, u32[]{:S(2)}) %collective-permute-start.54) | collective-permute-done | bytes 597536 | tf_op jit(solution)/shard_map/ppermute | solution.py:25
  693.6 3.5 collective-permute-start.57
  697.0 3.6 fusion.12
  700.7 3.0 copy.120
  703.7 3.3 collective-permute-done.56
  707.1 2.9 collective-permute-start.58
  715.1 2.8 bitcast_convert_fusion
  717.9 2.8 convert_bitcast_fusion
  720.7 3.0 copy.125
  (343 shorter events, 116.9 us)
Async XLA Ops:
  7.2 341.4 %all-gather.3.cloned.1.call-start = ((), (), s32[]{:S(2)}) async-start(), calls=%async_computation.2 | async-start | bytes 5898240 | tf_op jit(solution)/shard_map/all_gather | solution.py:346
  7.2 27.1 %collective-permute-start.3 = (bf16[1,768,768]{2,1,0:T(8,128)(2,1)}, bf16[1,768,768]{2,1,0:T(8,128)(2,1)S(1)}, u32[]{:S(2)}, u32[]{:S(2)}) collective-permute-start(bf16[1,768,768]{2,1,0:T(8,128)(2,1)} %bitcast.169), channel_id=1, source_target_pairs={{0,2},{1,3},{2,0},{3,1},{4,6},{5,7},{6,4},{7,5},{8,10},{9,11},{10,... | collective-permute-start | bytes 3538952 | tf_op jit(solution)/shard_map/ppermute | solution.py:25
  37.2 38.3 %collective-permute-start.4 = (bf16[2,768,768]{2,1,0:T(8,128)(2,1)}, bf16[2,768,768]{2,1,0:T(8,128)(2,1)}, u32[]{:S(2)}, u32[]{:S(2)}) collective-permute-start(bf16[2,768,768]{2,1,0:T(8,128)(2,1)} %pad_maximum_fusion.1), channel_id=1, source_target_pairs={{0,1},{1,0},{2,3},{3,2},{4,5},{5,4},{6,7},{7,6},{8,9},{9,8},{10,11... | collective-permute-start | bytes 7077896 | tf_op jit(solution)/shard_map/ppermute | solution.py:25
  38.9 5.5 collective-permute-start
  44.5 16.1 %collective-permute-start.1 = (bf16[2,96,576]{1,2,0:T(8,128)(2,1)S(1)}, bf16[2,96,576]{1,2,0:T(8,128)(2,1)S(1)}, u32[]{:S(2)}, u32[]{:S(2)}) collective-permute-start(bf16[2,96,576]{1,2,0:T(8,128)(2,1)S(1)} %pad_maximum_fusion.13), channel_id=1, source_target_pairs={{0,8},{4,12},{8,0},{12,4},{1,9},{5,13},{9,1},{13,5},{2,10},{6,14},... | collective-permute-start | bytes 663560 | tf_op jit(solution)/shard_map/ppermute | solution.py:25
  61.3 12.4 %collective-permute-start.2 = (bf16[1,4,96,576]{3,2,1,0:T(8,128)(2,1)S(1)}, bf16[1,4,96,576]{3,2,1,0:T(8,128)(2,1)S(1)}, u32[]{:S(2)}, u32[]{:S(2)}) collective-permute-start(bf16[1,4,96,576]{3,2,1,0:T(8,128)(2,1)S(1)} %copy.98), channel_id=1, source_target_pairs={{0,16},{16,0},{1,17},{17,1},{2,18},{18,2},{3,19},{19,3},{4,20},{20... | collective-permute-start | bytes 1327112 | tf_op jit(solution)/shard_map/ppermute | solution.py:25
  62.6 285.9 %all-gather.5.cloned.1.call-start = ((), (), s32[]{:S(2)}) async-start(), calls=%async_computation.3 | async-start | bytes 5898240 | tf_op jit(solution)/shard_map/all_gather | solution.py:375
  87.4 80.4 %collective-permute-start.5 = (bf16[6,256,384]{2,1,0:T(8,128)(2,1)S(1)}, bf16[6,256,384]{2,1,0:T(8,128)(2,1)S(1)}, u32[]{:S(2)}, u32[]{:S(2)}) collective-permute-start(bf16[6,256,384]{2,1,0:T(8,128)(2,1)S(1)} %bitcast.185), channel_id=1, source_target_pairs={{0,4},{4,8},{8,12},{12,0},{1,5},{5,9},{9,13},{13,1},{2,6},{6,10},{... | collective-permute-start | bytes 3538952 | tf_op jit(solution)/shard_map/ppermute | solution.py:29
  167.8 31.5 %collective-permute-start.6 = (bf16[6,256,384]{2,1,0:T(8,128)(2,1)S(1)}, bf16[6,256,384]{2,1,0:T(8,128)(2,1)}, u32[]{:S(2)}, u32[]{:S(2)}) collective-permute-start(bf16[6,256,384]{2,1,0:T(8,128)(2,1)S(1)} %collective-permute-done.5.rest_0_), channel_id=1, source_target_pairs={{0,4},{4,8},{8,12},{12,0},{1,5},{5,9},{9,13},{13,1},{2,6},{6,10},{... | collective-permute-start | bytes 3538952 | tf_op jit(solution)/shard_map/ppermute | solution.py:29
  199.3 37.6 %collective-permute-start.7 = (bf16[6,256,384]{2,1,0:T(8,128)(2,1)}, bf16[6,256,384]{2,1,0:T(8,128)(2,1)}, u32[]{:S(2)}, u32[]{:S(2)}) collective-permute-start(bf16[6,256,384]{2,1,0:T(8,128)(2,1)} %collective-permute-done.6.rest_1_), channel_id=1, source_target_pairs={{0,4},{4,8},{8,12},{12,0},{1,5},{5,9},{9,13},{13,1},{2,6},{6,10},{... | collective-permute-start | bytes 3538952 | tf_op jit(solution)/shard_map/ppermute | solution.py:29
  202.2 25.1 %collective-permute-start.11 = (bf16[1,96,200]{1,2,0:T(8,128)(2,1)S(1)}, bf16[1,96,200]{1,2,0:T(8,128)(2,1)S(1)}, u32[]{:S(2)}, u32[]{:S(2)}) collective-permute-start(bf16[1,96,200]{1,2,0:T(8,128)(2,1)S(1)} %maximum_bitcast_fusion.2), channel_id=1, source_target_pairs={{0,4},{4,0},{8,12},{12,8},{1,5},{5,1},{9,13},{13,9},{2,6},{6,2},{1... | collective-permute-start | bytes 115208 | tf_op jit(solution)/shard_map/ppermute | solution.py:25
  227.4 4.5 collective-permute-start.12
  232.0 4.7 collective-permute-start.13
  236.9 478.1 %reduce-scatter.3.cloned.1.call-start = ((), (), s32[]{:S(2)}) async-start(), calls=%async_computation.4 | async-start | bytes 5898240 | tf_op jit(solution)/shard_map/reduce_scatter | solution.py:416
  238.4 5.6 collective-permute-start.14
  244.9 43.6 %collective-permute-start.15 = (bf16[2,768,192]{1,2,0:T(8,128)(2,1)}, bf16[2,768,192]{1,2,0:T(8,128)(2,1)}, u32[]{:S(2)}, u32[]{:S(2)}) collective-permute-start(bf16[2,768,192]{1,2,0:T(8,128)(2,1)} %pad_maximum_fusion.10), channel_id=1, source_target_pairs={{0,1},{1,0},{2,3},{3,2},{4,5},{5,4},{6,7},{7,6},{8,9},{9,8},{10,11... | collective-permute-start | bytes 1769480 | tf_op jit(solution)/shard_map/ppermute | solution.py:25
  283.4 9.9 %collective-permute-start.10 = (bf16[192,768]{1,0:T(8,128)(2,1)}, bf16[192,768]{1,0:T(8,128)(2,1)}, u32[]{:S(2)}, u32[]{:S(2)}) collective-permute-start(bf16[192,768]{1,0:T(8,128)(2,1)} %get-tuple-element.129), channel_id=1, source_target_pairs={{0,3},{1,2},{2,1},{3,0},{4,7},{5,6},{6,5},{7,4},{8,11},{9,10},{10,... | collective-permute-start | bytes 884744 | tf_op jit(solution)/shard_map/ppermute | solution.py:25
  284.5 8.8 %collective-permute-start.8 = (bf16[192,768]{1,0:T(8,128)(2,1)}, bf16[192,768]{1,0:T(8,128)(2,1)}, u32[]{:S(2)}, u32[]{:S(2)}) collective-permute-start(bf16[192,768]{1,0:T(8,128)(2,1)} %get-tuple-element.131), channel_id=1, source_target_pairs={{0,1},{1,0},{2,3},{3,2},{4,5},{5,4},{6,7},{7,6},{8,9},{9,8},{10,11... | collective-permute-start | bytes 884744 | tf_op jit(solution)/shard_map/ppermute | solution.py:25
  285.0 13.4 %collective-permute-start.9 = (bf16[192,768]{1,0:T(8,128)(2,1)}, bf16[192,768]{1,0:T(8,128)(2,1)}, u32[]{:S(2)}, u32[]{:S(2)}) collective-permute-start(bf16[192,768]{1,0:T(8,128)(2,1)} %get-tuple-element.130), channel_id=1, source_target_pairs={{0,2},{1,3},{2,0},{3,1},{4,6},{5,7},{6,4},{7,5},{8,10},{9,11},{10,... | collective-permute-start | bytes 884744 | tf_op jit(solution)/shard_map/ppermute | solution.py:25
  305.9 7.0 collective-permute-start.30
  306.9 8.7 %collective-permute-start.31 = (bf16[120,768]{1,0:T(8,128)(2,1)S(1)}, bf16[120,768]{1,0:T(8,128)(2,1)S(1)}, u32[]{:S(2)}, u32[]{:S(2)}) collective-permute-start(bf16[120,768]{1,0:T(8,128)(2,1)S(1)} %get-tuple-element.99), channel_id=1, source_target_pairs={{0,2},{1,3},{2,0},{3,1},{16,18},{17,19},{18,16},{19,17},{4,6},{5,7... | collective-permute-start | bytes 552968 | tf_op jit(solution)/shard_map/ppermute | solution.py:25
  308.1 9.9 %collective-permute-start.32 = (bf16[120,768]{1,0:T(8,128)(2,1)S(1)}, bf16[120,768]{1,0:T(8,128)(2,1)S(1)}, u32[]{:S(2)}, u32[]{:S(2)}) collective-permute-start(bf16[120,768]{1,0:T(8,128)(2,1)S(1)} %get-tuple-element.98), channel_id=1, source_target_pairs={{0,3},{1,2},{2,1},{3,0},{16,19},{17,18},{18,17},{19,16},{4,7},{5,6... | collective-permute-start | bytes 552968 | tf_op jit(solution)/shard_map/ppermute | solution.py:25
  308.5 10.2 %collective-permute-start.33 = (bf16[120,768]{1,0:T(8,128)(2,1)S(1)}, bf16[120,768]{1,0:T(8,128)(2,1)S(1)}, u32[]{:S(2)}, u32[]{:S(2)}) collective-permute-start(bf16[120,768]{1,0:T(8,128)(2,1)S(1)} %get-tuple-element.97), channel_id=1, source_target_pairs={{0,16},{1,17},{2,18},{3,19},{16,0},{17,1},{18,2},{19,3},{4,20},{5,... | collective-permute-start | bytes 552968 | tf_op jit(solution)/shard_map/ppermute | solution.py:25
  309.7 17.4 %collective-permute-start.34 = (bf16[120,768]{1,0:T(8,128)(2,1)S(1)}, bf16[120,768]{1,0:T(8,128)(2,1)S(1)}, u32[]{:S(2)}, u32[]{:S(2)}) collective-permute-start(bf16[120,768]{1,0:T(8,128)(2,1)S(1)} %get-tuple-element.96), channel_id=1, source_target_pairs={{0,17},{1,16},{2,19},{3,18},{16,1},{17,0},{18,3},{19,2},{4,21},{5,... | collective-permute-start | bytes 552968 | tf_op jit(solution)/shard_map/ppermute | solution.py:25
  312.8 15.3 %collective-permute-start.35 = (bf16[120,768]{1,0:T(8,128)(2,1)S(1)}, bf16[120,768]{1,0:T(8,128)(2,1)S(1)}, u32[]{:S(2)}, u32[]{:S(2)}) collective-permute-start(bf16[120,768]{1,0:T(8,128)(2,1)S(1)} %get-tuple-element.95), channel_id=1, source_target_pairs={{0,18},{1,19},{2,16},{3,17},{16,2},{17,3},{18,0},{19,1},{4,22},{5,... | collective-permute-start | bytes 552968 | tf_op jit(solution)/shard_map/ppermute | solution.py:25
  315.6 14.8 %collective-permute-start.36 = (bf16[120,768]{1,0:T(8,128)(2,1)S(1)}, bf16[120,768]{1,0:T(8,128)(2,1)S(1)}, u32[]{:S(2)}, u32[]{:S(2)}) collective-permute-start(bf16[120,768]{1,0:T(8,128)(2,1)S(1)} %get-tuple-element.94), channel_id=1, source_target_pairs={{0,19},{1,18},{2,17},{3,16},{16,3},{17,2},{18,1},{19,0},{4,23},{5,... | collective-permute-start | bytes 552968 | tf_op jit(solution)/shard_map/ppermute | solution.py:25
  318.0 14.4 %collective-permute-start.16 = (bf16[120,768]{1,0:T(8,128)(2,1)S(1)}, bf16[120,768]{1,0:T(8,128)(2,1)S(1)}, u32[]{:S(2)}, u32[]{:S(2)}) collective-permute-start(bf16[120,768]{1,0:T(8,128)(2,1)S(1)} %get-tuple-element.116), channel_id=1, source_target_pairs={{0,1},{1,0},{2,3},{3,2},{16,17},{17,16},{18,19},{19,18},{4,5},{5,4... | collective-permute-start | bytes 552968 | tf_op jit(solution)/shard_map/ppermute | solution.py:25
  318.7 15.6 %collective-permute-start.17 = (bf16[120,768]{1,0:T(8,128)(2,1)S(1)}, bf16[120,768]{1,0:T(8,128)(2,1)S(1)}, u32[]{:S(2)}, u32[]{:S(2)}) collective-permute-start(bf16[120,768]{1,0:T(8,128)(2,1)S(1)} %get-tuple-element.115), channel_id=1, source_target_pairs={{0,2},{1,3},{2,0},{3,1},{16,18},{17,19},{18,16},{19,17},{4,6},{5,7... | collective-permute-start | bytes 552968 | tf_op jit(solution)/shard_map/ppermute | solution.py:25
  327.2 9.0 %collective-permute-start.18 = (bf16[120,768]{1,0:T(8,128)(2,1)S(1)}, bf16[120,768]{1,0:T(8,128)(2,1)S(1)}, u32[]{:S(2)}, u32[]{:S(2)}) collective-permute-start(bf16[120,768]{1,0:T(8,128)(2,1)S(1)} %get-tuple-element.114), channel_id=1, source_target_pairs={{0,3},{1,2},{2,1},{3,0},{16,19},{17,18},{18,17},{19,16},{4,7},{5,6... | collective-permute-start | bytes 552968 | tf_op jit(solution)/shard_map/ppermute | solution.py:25
  328.2 8.7 %collective-permute-start.19 = (bf16[120,768]{1,0:T(8,128)(2,1)S(1)}, bf16[120,768]{1,0:T(8,128)(2,1)S(1)}, u32[]{:S(2)}, u32[]{:S(2)}) collective-permute-start(bf16[120,768]{1,0:T(8,128)(2,1)S(1)} %get-tuple-element.113), channel_id=1, source_target_pairs={{0,16},{1,17},{2,18},{3,19},{16,0},{17,1},{18,2},{19,3},{4,20},{5,... | collective-permute-start | bytes 552968 | tf_op jit(solution)/shard_map/ppermute | solution.py:25
  330.4 16.1 %collective-permute-start.20 = (bf16[120,768]{1,0:T(8,128)(2,1)S(1)}, bf16[120,768]{1,0:T(8,128)(2,1)S(1)}, u32[]{:S(2)}, u32[]{:S(2)}) collective-permute-start(bf16[120,768]{1,0:T(8,128)(2,1)S(1)} %get-tuple-element.112), channel_id=1, source_target_pairs={{0,17},{1,16},{2,19},{3,18},{16,1},{17,0},{18,3},{19,2},{4,21},{5,... | collective-permute-start | bytes 552968 | tf_op jit(solution)/shard_map/ppermute | solution.py:25
  332.4 14.8 %collective-permute-start.21 = (bf16[120,768]{1,0:T(8,128)(2,1)S(1)}, bf16[120,768]{1,0:T(8,128)(2,1)S(1)}, u32[]{:S(2)}, u32[]{:S(2)}) collective-permute-start(bf16[120,768]{1,0:T(8,128)(2,1)S(1)} %get-tuple-element.111), channel_id=1, source_target_pairs={{0,18},{1,19},{2,16},{3,17},{16,2},{17,3},{18,0},{19,1},{4,22},{5,... | collective-permute-start | bytes 552968 | tf_op jit(solution)/shard_map/ppermute | solution.py:25
  334.3 13.6 %collective-permute-start.22 = (bf16[120,768]{1,0:T(8,128)(2,1)S(1)}, bf16[120,768]{1,0:T(8,128)(2,1)S(1)}, u32[]{:S(2)}, u32[]{:S(2)}) collective-permute-start(bf16[120,768]{1,0:T(8,128)(2,1)S(1)} %get-tuple-element.110), channel_id=1, source_target_pairs={{0,19},{1,18},{2,17},{3,16},{16,3},{17,2},{18,1},{19,0},{4,23},{5,... | collective-permute-start | bytes 552968 | tf_op jit(solution)/shard_map/ppermute | solution.py:25
  367.8 34.2 %collective-permute-start.23 = (bf16[120,768]{1,0:T(8,128)(2,1)}, bf16[120,768]{1,0:T(8,128)(2,1)}, u32[]{:S(2)}, u32[]{:S(2)}) collective-permute-start(bf16[120,768]{1,0:T(8,128)(2,1)} %get-tuple-element.108), channel_id=1, source_target_pairs={{0,1},{1,0},{2,3},{3,2},{16,17},{17,16},{18,19},{19,18},{4,5},{5,4... | collective-permute-start | bytes 552968 | tf_op jit(solution)/shard_map/ppermute | solution.py:25
  367.8 36.7 %collective-permute-start.24 = (bf16[120,768]{1,0:T(8,128)(2,1)}, bf16[120,768]{1,0:T(8,128)(2,1)}, u32[]{:S(2)}, u32[]{:S(2)}) collective-permute-start(bf16[120,768]{1,0:T(8,128)(2,1)} %get-tuple-element.107), channel_id=1, source_target_pairs={{0,2},{1,3},{2,0},{3,1},{16,18},{17,19},{18,16},{19,17},{4,6},{5,7... | collective-permute-start | bytes 552968 | tf_op jit(solution)/shard_map/ppermute | solution.py:25
  399.3 39.0 %collective-permute-start.37 = (bf16[120,768]{1,0:T(8,128)(2,1)}, bf16[120,768]{1,0:T(8,128)(2,1)}, u32[]{:S(2)}, u32[]{:S(2)}) collective-permute-start(bf16[120,768]{1,0:T(8,128)(2,1)} %get-tuple-element.92), channel_id=1, source_target_pairs={{0,1},{1,0},{2,3},{3,2},{16,17},{17,16},{18,19},{19,18},{4,5},{5,4... | collective-permute-start | bytes 552968 | tf_op jit(solution)/shard_map/ppermute | solution.py:25
  400.0 40.9 %collective-permute-start.38 = (bf16[120,768]{1,0:T(8,128)(2,1)}, bf16[120,768]{1,0:T(8,128)(2,1)}, u32[]{:S(2)}, u32[]{:S(2)}) collective-permute-start(bf16[120,768]{1,0:T(8,128)(2,1)} %get-tuple-element.91), channel_id=1, source_target_pairs={{0,2},{1,3},{2,0},{3,1},{16,18},{17,19},{18,16},{19,17},{4,6},{5,7... | collective-permute-start | bytes 552968 | tf_op jit(solution)/shard_map/ppermute | solution.py:25
  400.8 43.2 %collective-permute-start.39 = (bf16[120,768]{1,0:T(8,128)(2,1)}, bf16[120,768]{1,0:T(8,128)(2,1)}, u32[]{:S(2)}, u32[]{:S(2)}) collective-permute-start(bf16[120,768]{1,0:T(8,128)(2,1)} %get-tuple-element.90), channel_id=1, source_target_pairs={{0,3},{1,2},{2,1},{3,0},{16,19},{17,18},{18,17},{19,16},{4,7},{5,6... | collective-permute-start | bytes 552968 | tf_op jit(solution)/shard_map/ppermute | solution.py:25
  401.7 316.2 %reduce-scatter.5.cloned.1.call-start = ((), (), s32[]{:S(2)}) async-start(), calls=%async_computation.5 | async-start | bytes 5898240 | tf_op jit(solution)/shard_map/reduce_scatter | solution.py:446
  402.0 12.9 %collective-permute-start.25 = (bf16[120,768]{1,0:T(8,128)(2,1)}, bf16[120,768]{1,0:T(8,128)(2,1)S(1)}, u32[]{:S(2)}, u32[]{:S(2)}) collective-permute-start(bf16[120,768]{1,0:T(8,128)(2,1)} %get-tuple-element.106), channel_id=1, source_target_pairs={{0,3},{1,2},{2,1},{3,0},{16,19},{17,18},{18,17},{19,16},{4,7},{5,6... | collective-permute-start | bytes 552968 | tf_op jit(solution)/shard_map/ppermute | solution.py:25
  404.5 12.0 %collective-permute-start.26 = (bf16[120,768]{1,0:T(8,128)(2,1)}, bf16[120,768]{1,0:T(8,128)(2,1)S(1)}, u32[]{:S(2)}, u32[]{:S(2)}) collective-permute-start(bf16[120,768]{1,0:T(8,128)(2,1)} %get-tuple-element.105), channel_id=1, source_target_pairs={{0,16},{1,17},{2,18},{3,19},{16,0},{17,1},{18,2},{19,3},{4,20},{5,... | collective-permute-start | bytes 552968 | tf_op jit(solution)/shard_map/ppermute | solution.py:25
  414.9 10.7 %collective-permute-start.27 = (bf16[120,768]{1,0:T(8,128)(2,1)}, bf16[120,768]{1,0:T(8,128)(2,1)S(1)}, u32[]{:S(2)}, u32[]{:S(2)}) collective-permute-start(bf16[120,768]{1,0:T(8,128)(2,1)} %get-tuple-element.104), channel_id=1, source_target_pairs={{0,17},{1,16},{2,19},{3,18},{16,1},{17,0},{18,3},{19,2},{4,21},{5,... | collective-permute-start | bytes 552968 | tf_op jit(solution)/shard_map/ppermute | solution.py:25
  416.5 11.0 %collective-permute-start.28 = (bf16[120,768]{1,0:T(8,128)(2,1)}, bf16[120,768]{1,0:T(8,128)(2,1)S(1)}, u32[]{:S(2)}, u32[]{:S(2)}) collective-permute-start(bf16[120,768]{1,0:T(8,128)(2,1)} %get-tuple-element.103), channel_id=1, source_target_pairs={{0,18},{1,19},{2,16},{3,17},{16,2},{17,3},{18,0},{19,1},{4,22},{5,... | collective-permute-start | bytes 552968 | tf_op jit(solution)/shard_map/ppermute | solution.py:25
  425.6 7.4 %collective-permute-start.29 = (bf16[120,768]{1,0:T(8,128)(2,1)}, bf16[120,768]{1,0:T(8,128)(2,1)S(1)}, u32[]{:S(2)}, u32[]{:S(2)}) collective-permute-start(bf16[120,768]{1,0:T(8,128)(2,1)} %get-tuple-element.102), channel_id=1, source_target_pairs={{0,19},{1,18},{2,17},{3,16},{16,3},{17,2},{18,1},{19,0},{4,23},{5,... | collective-permute-start | bytes 552968 | tf_op jit(solution)/shard_map/ppermute | solution.py:25
  427.5 17.4 %collective-permute-start.40 = (bf16[120,768]{1,0:T(8,128)(2,1)S(1)}, bf16[120,768]{1,0:T(8,128)(2,1)S(1)}, u32[]{:S(2)}, u32[]{:S(2)}) collective-permute-start(bf16[120,768]{1,0:T(8,128)(2,1)S(1)} %copy-done.35), channel_id=1, source_target_pairs={{0,16},{1,17},{2,18},{3,19},{16,0},{17,1},{18,2},{19,3},{4,20},{5,... | collective-permute-start | bytes 552968 | tf_op jit(solution)/shard_map/ppermute | solution.py:25
  433.0 11.9 %collective-permute-start.41 = (bf16[120,768]{1,0:T(8,128)(2,1)S(1)}, bf16[120,768]{1,0:T(8,128)(2,1)S(1)}, u32[]{:S(2)}, u32[]{:S(2)}) collective-permute-start(bf16[120,768]{1,0:T(8,128)(2,1)S(1)} %copy-done.34), channel_id=1, source_target_pairs={{0,17},{1,16},{2,19},{3,18},{16,1},{17,0},{18,3},{19,2},{4,21},{5,... | collective-permute-start | bytes 552968 | tf_op jit(solution)/shard_map/ppermute | solution.py:25
  438.3 6.6 collective-permute-start.42
  441.0 8.6 %collective-permute-start.43 = (bf16[120,768]{1,0:T(8,128)(2,1)S(1)}, bf16[120,768]{1,0:T(8,128)(2,1)S(1)}, u32[]{:S(2)}, u32[]{:S(2)}) collective-permute-start(bf16[120,768]{1,0:T(8,128)(2,1)S(1)} %get-tuple-element.86), channel_id=1, source_target_pairs={{0,19},{1,18},{2,17},{3,16},{16,3},{17,2},{18,1},{19,0},{4,23},{5,... | collective-permute-start | bytes 552968 | tf_op jit(solution)/shard_map/ppermute | solution.py:25
  455.8 8.5 %collective-permute-start.45 = (bf16[192,768]{1,0:T(8,128)(2,1)S(1)}, bf16[192,768]{1,0:T(8,128)(2,1)S(1)}, u32[]{:S(2)}, u32[]{:S(2)}) collective-permute-start(bf16[192,768]{1,0:T(8,128)(2,1)S(1)} %get-tuple-element.126), channel_id=1, source_target_pairs={{0,2},{1,3},{2,0},{3,1},{4,6},{5,7},{6,4},{7,5},{8,10},{9,11},{10,... | collective-permute-start | bytes 884744 | tf_op jit(solution)/shard_map/ppermute | solution.py:25
  456.5 14.8 %collective-permute-start.46 = (bf16[192,768]{1,0:T(8,128)(2,1)S(1)}, bf16[192,768]{1,0:T(8,128)(2,1)S(1)}, u32[]{:S(2)}, u32[]{:S(2)}) collective-permute-start(bf16[192,768]{1,0:T(8,128)(2,1)S(1)} %get-tuple-element.125), channel_id=1, source_target_pairs={{0,3},{1,2},{2,1},{3,0},{4,7},{5,6},{6,5},{7,4},{8,11},{9,10},{10,... | collective-permute-start | bytes 884744 | tf_op jit(solution)/shard_map/ppermute | solution.py:25
  517.7 30.1 %collective-permute-start.47 = (bf16[6,256,384]{2,1,0:T(8,128)(2,1)}, bf16[6,256,384]{2,1,0:T(8,128)(2,1)S(1)}, u32[]{:S(2)}, u32[]{:S(2)}) collective-permute-start(bf16[6,256,384]{2,1,0:T(8,128)(2,1)} %get-tuple-element.34), channel_id=1, source_target_pairs={{0,12},{4,0},{8,4},{12,8},{1,13},{5,1},{9,5},{13,9},{2,14},{6,2},{... | collective-permute-start | bytes 3538952 | tf_op jit(solution)/shard_map/ppermute | solution.py:29
  549.5 28.9 %collective-permute-start.48 = (bf16[6,256,384]{2,1,0:T(8,128)(2,1)S(1)}, bf16[6,256,384]{2,1,0:T(8,128)(2,1)S(1)}, u32[]{:S(2)}, u32[]{:S(2)}) collective-permute-start(bf16[6,256,384]{2,1,0:T(8,128)(2,1)S(1)} %add_convert_fusion.3), channel_id=1, source_target_pairs={{0,12},{4,0},{8,4},{12,8},{1,13},{5,1},{9,5},{13,9},{2,14},{6,2},{... | collective-permute-start | bytes 3538952 | tf_op jit(solution)/shard_map/ppermute | solution.py:29
  578.7 28.0 %collective-permute-start.49 = (bf16[6,256,384]{2,1,0:T(8,128)(2,1)S(1)}, bf16[6,256,384]{2,1,0:T(8,128)(2,1)S(1)}, u32[]{:S(2)}, u32[]{:S(2)}) collective-permute-start(bf16[6,256,384]{2,1,0:T(8,128)(2,1)S(1)} %add_convert_fusion.2), channel_id=1, source_target_pairs={{0,12},{4,0},{8,4},{12,8},{1,13},{5,1},{9,5},{13,9},{2,14},{6,2},{... | collective-permute-start | bytes 3538952 | tf_op jit(solution)/shard_map/ppermute | solution.py:29
  615.5 20.9 %collective-permute-start.50 = (bf16[2,768,768]{1,2,0:T(8,128)(2,1)}, bf16[2,768,768]{1,2,0:T(8,128)(2,1)}, u32[]{:S(2)}, u32[]{:S(2)}) collective-permute-start(bf16[2,768,768]{1,2,0:T(8,128)(2,1)} %pad_maximum_fusion.3), channel_id=1, source_target_pairs={{0,1},{1,0},{2,3},{3,2},{4,5},{5,4},{6,7},{7,6},{8,9},{9,8},{10,11... | collective-permute-start | bytes 7077896 | tf_op jit(solution)/shard_map/ppermute | solution.py:25
  622.4 10.4 %collective-permute-start.52 = (bf16[2,768,192]{1,2,0:T(8,128)(2,1)}, bf16[2,768,192]{1,2,0:T(8,128)(2,1)}, u32[]{:S(2)}, u32[]{:S(2)}) collective-permute-start(bf16[2,768,192]{1,2,0:T(8,128)(2,1)} %pad_maximum_fusion.11), channel_id=1, source_target_pairs={{0,1},{1,0},{2,3},{3,2},{4,5},{5,4},{6,7},{7,6},{8,9},{9,8},{10,11... | collective-permute-start | bytes 1769480 | tf_op jit(solution)/shard_map/ppermute | solution.py:25
  634.0 8.8 %collective-permute-start.53 = (bf16[1,768,192]{1,2,0:T(8,128)(2,1)S(1)}, bf16[1,768,192]{1,2,0:T(8,128)(2,1)S(1)}, u32[]{:S(2)}, u32[]{:S(2)}) collective-permute-start(bf16[1,768,192]{1,2,0:T(8,128)(2,1)S(1)} %fusion.81), channel_id=1, source_target_pairs={{0,2},{1,3},{2,0},{3,1},{4,6},{5,7},{6,4},{7,5},{8,10},{9,11},{10,... | collective-permute-start | bytes 884744 | tf_op jit(solution)/shard_map/ppermute | solution.py:25
  639.4 28.8 %collective-permute-start.51 = (bf16[1,768,768]{1,2,0:T(8,128)(2,1)}, bf16[1,768,768]{1,2,0:T(8,128)(2,1)}, u32[]{:S(2)}, u32[]{:S(2)}) collective-permute-start(bf16[1,768,768]{1,2,0:T(8,128)(2,1)} %fusion.39), channel_id=1, source_target_pairs={{0,2},{1,3},{2,0},{3,1},{4,6},{5,7},{6,4},{7,5},{8,10},{9,11},{10,... | collective-permute-start | bytes 3538952 | tf_op jit(solution)/shard_map/ppermute | solution.py:25
  675.7 16.4 %collective-permute-start.54 = (bf16[4,96,778]{2,1,0:T(8,128)(2,1)S(1)}, bf16[4,96,778]{2,1,0:T(8,128)(2,1)}, u32[]{:S(2)}, u32[]{:S(2)}) collective-permute-start(bf16[4,96,778]{2,1,0:T(8,128)(2,1)S(1)} %dynamic-slice_bitcast_fusion), channel_id=1, source_target_pairs={{0,16},{16,0},{1,17},{17,1},{2,18},{18,2},{3,19},{19,3},{4,20},{20... | collective-permute-start | bytes 1792520 | tf_op jit(solution)/shard_map/ppermute | solution.py:25
  693.4 10.3 %collective-permute-start.55 = (bf16[96,778]{1,0:T(8,128)(2,1)S(1)}, bf16[96,778]{1,0:T(8,128)(2,1)S(1)}, u32[]{:S(2)}, u32[]{:S(2)}) collective-permute-start(bf16[96,778]{1,0:T(8,128)(2,1)S(1)} %get-tuple-element.134), channel_id=1, source_target_pairs={{0,4},{4,0},{8,12},{12,8},{1,5},{5,1},{9,13},{13,9},{2,6},{6,2},{1... | collective-permute-start | bytes 448136 | tf_op jit(solution)/shard_map/ppermute | solution.py:25
  693.5 13.6 %collective-permute-start.56 = (bf16[96,778]{1,0:T(8,128)(2,1)S(1)}, bf16[96,778]{1,0:T(8,128)(2,1)S(1)}, u32[]{:S(2)}, u32[]{:S(2)}) collective-permute-start(bf16[96,778]{1,0:T(8,128)(2,1)S(1)} %get-tuple-element.136), channel_id=1, source_target_pairs={{0,8},{4,12},{8,0},{12,4},{1,9},{5,13},{9,1},{13,5},{2,10},{6,14},... | collective-permute-start | bytes 448136 | tf_op jit(solution)/shard_map/ppermute | solution.py:25
  693.6 13.5 %collective-permute-start.57 = (bf16[96,778]{1,0:T(8,128)(2,1)S(1)}, bf16[96,778]{1,0:T(8,128)(2,1)S(1)}, u32[]{:S(2)}, u32[]{:S(2)}) collective-permute-start(bf16[96,778]{1,0:T(8,128)(2,1)S(1)} %get-tuple-element.135), channel_id=1, source_target_pairs={{0,12},{4,8},{8,4},{12,0},{1,13},{5,9},{9,5},{13,1},{2,14},{6,10},... | collective-permute-start | bytes 448136 | tf_op jit(solution)/shard_map/ppermute | solution.py:25
  707.1 6.5 collective-permute-start.58
  710.0 3.6 collective-permute-start.59
  710.2 3.5 collective-permute-start.60
  (61 other events, 1449.5 us)
Sparse Core Ops, SparseCore 0:
  62.8 115.1 all-gather.2
  237.0 92.7 all-gather.4
  401.9 85.8 reduce-scatter.2
  608.2 86.1 reduce-scatter.4

commit v3 on v2

v3 whole, which is shorter than its diff:
```python
import functools

import jax
import jax.numpy as jnp
from jax import lax
from jax.experimental import pallas as pl
from jax.experimental.pallas import tpu as pltpu
from jax.sharding import PartitionSpec as P

HD = 64
PLEN = 1024
CLEN = 128
CONTS = 8
CHUNK = 128
UNITS = 768

EPSILON = 1e-06
NEGATIVE = -1e30
ROOT = 0.7978845608028654
CUBE = 0.044715
F32 = jnp.float32
BF16 = jnp.bfloat16
VM = pl.BlockSpec(memory_space=pltpu.VMEM)
SM = pl.BlockSpec(memory_space=pltpu.SMEM)
ROOM = pltpu.CompilerParams(vmem_limit_bytes=60 * 2**20)


def shape(dims, dtype=BF16):
    return jax.ShapeDtypeStruct(dims, dtype)


def low(value):
    return value.astype(BF16)


def dot_last(left, right):
    return lax.dot_general(left, right, (((1,), (1,)), ((), ())), preferred_element_type=F32)


def dot_plain(left, right):
    return lax.dot_general(left, right, (((1,), (0,)), ((), ())), preferred_element_type=F32)


def add_all(parts):
    return functools.reduce(jnp.add, parts)


def xor_swap(value, axis, size, mask):
    return lax.ppermute(value, axis, [(place, place ^ mask) for place in range(size)])


def ring_step(value, axis, size, shift):
    return lax.ppermute(value, axis, [(place, (place + shift) % size) for place in range(size)])


def pick(stacked, index):
    return lax.dynamic_index_in_dim(stacked, index, 0, keepdims=False)


def xor_gather(value, axis, size, order=None):
    if order is None:
        order = [1 << bit for bit in range(size.bit_length() - 1)]
    have = {0: value}
    for mask in order:
        keys = sorted(have)
        moved = xor_swap(jnp.stack([have[key] for key in keys]), axis, size, mask)
        for place, key in enumerate(keys):
            have[key ^ mask] = moved[place]
    return [have[key] for key in range(size)]


def xor_exchange(pieces, axis, size):
    return [pieces[0]] + [xor_swap(pieces[mask], axis, size, mask) for mask in range(1, size)]


def chunk_list(value, axis):
    return [
        lax.slice_in_dim(value, first, first + CHUNK, axis=axis)
        for first in range(0, value.shape[axis], CHUNK)
    ]


def split_order(value, axis=0):
    parts = chunk_list(value, axis)
    return jnp.concatenate(parts[0::2] + parts[1::2], axis=axis)


def plain_order(value, axis=0):
    parts = chunk_list(value, axis)
    half = len(parts) // 2
    return jnp.concatenate([parts[(at % 2) * half + at // 2] for at in range(2 * half)], axis=axis)


def rms_unit(values):
    factor = lax.rsqrt(jnp.mean(values * values, axis=-1, keepdims=True) + EPSILON)
    return (values * factor, factor)


def rms_backward(grad_normed, unit_part, factor, gain):
    scaled = grad_normed * gain
    inner = jnp.mean(scaled * unit_part, axis=-1, keepdims=True)
    return factor * (scaled - unit_part * inner)


def normalize_kernel(tokens, gains, own, second):
    unit, _ = rms_unit(tokens[...].astype(F32))
    own[...] = split_order(low(gains[0:1, :] * unit))
    second[...] = own[own.shape[0] // 2 :, :]


def normalize(tokens, gains):
    rows, width = tokens.shape
    return pl.pallas_call(
        normalize_kernel,
        out_shape=(shape((rows, width)), shape((rows // 2, width))),
        in_specs=[VM] * 2,
        out_specs=(VM,) * 2,
        compiler_params=ROOM,
        name="normalize",
    )(tokens, gains)


def key_lanes(rows, width):
    return rows[:, : width + (-width) % 128]


def value_lanes(rows, width):
    return rows[:, width - (-width) % 128 :]


def spread_heads(columns, ahead, behind):
    width, count = columns.shape
    groups = []
    for first in range(0, width, HD):
        pieces = [columns[first : first + HD]]
        above, below = ahead + first, width - first - HD + behind
        if above:
            pieces.insert(0, jnp.zeros((above, count), columns.dtype))
        if below:
            pieces.append(jnp.zeros((below, count), columns.dtype))
        groups.append(jnp.concatenate(pieces, axis=0))
    return jnp.concatenate(groups, axis=1)


def causal(scores, count):
    key_row = lax.broadcasted_iota(jnp.int32, scores.shape, 0)
    query_row = lax.broadcasted_iota(jnp.int32, scores.shape, 1) % count
    return jnp.where(key_row <= query_row, scores, NEGATIVE)


def work_items(info, sizes, attend):
    prompts, conts, places, per = sizes
    ctx_index = info[0]

    def prompt_chunks(prompt):
        return [info[1 + prompt * places * per + at] for at in range(places * per)]

    def prompt_mask(scores):
        count = per * CHUNK
        parts = [causal(scores[:count], count)]
        for place in range(1, places):
            part = scores[place * count : (place + 1) * count]
            parts.append(jnp.where(place <= ctx_index, part, NEGATIVE))
        return jnp.concatenate(parts, axis=0)

    def cont_mask(scores):
        return jnp.concatenate([causal(scores[:CLEN], CLEN), scores[CLEN:]], axis=0)

    @pl.loop(0, prompts)
    def _(prompt):
        chunks = prompt_chunks(prompt)
        attend(0, prompt, chunks[:per], chunks, prompt_mask)

    first = 1 + prompts * places * per

    @pl.loop(0, conts)
    def _(cont):
        own = info[first + cont]
        attend(1, cont, [own], [own] + prompt_chunks(info[first + conts + cont]), cont_mask)


def chunk_lanes(chunk):
    return pl.ds(pl.multiple_of(chunk * CHUNK, CHUNK), CHUNK)


def load_lanes(ref, chunks):
    return jnp.concatenate([ref[:, chunk_lanes(chunk)] for chunk in chunks], axis=1)


def attend_forward_kernel(sizes, inputs, info, query_weight, pair_weight, *rest):
    rows, (query, pairs, *outs, lse_prompt, lse_cont, mixed) = rest[:inputs], rest[inputs:]
    lse = (lse_prompt, lse_cont)
    width = query.shape[0]
    pad = (-width) % 128
    query_flip = query_weight[...].T
    at = 0
    for one in rows:
        value = one[...]
        count = value.shape[0]
        pair = low(dot_plain(value, pair_weight[...]))
        pairs[at // CHUNK : (at + count) // CHUNK] = pair.reshape(-1, CHUNK, 2 * width)
        if at < query.shape[1]:
            query[:, at : at + count] = low(dot_last(query_flip, value) * 0.125)
        at += count

    def attend(kind, index, own, chunks, mask):
        count = len(own) * CHUNK
        block = jnp.concatenate([pairs[chunk] for chunk in chunks], axis=0)
        spread = spread_heads(load_lanes(query, own), 0, pad)
        scores = mask(dot_plain(key_lanes(block, width), spread))
        peak = jnp.max(scores, axis=0, keepdims=True)
        shifted = jnp.exp(scores - peak)
        total = jnp.sum(shifted, axis=0, keepdims=True)
        weights = low(shifted)
        flip = value_lanes(block, width).T
        for head in range(width // HD):
            group = slice(head * count, (head + 1) * count)
            part = slice(pad + head * HD, pad + (head + 1) * HD)
            result = low(dot_plain(flip[part], weights[:, group]) / total[:, group])
            for place, chunk in enumerate(own):
                mixed[head * HD : (head + 1) * HD, chunk_lanes(chunk)] = result[
                    :, place * CHUNK : (place + 1) * CHUNK
                ]
        lse[kind][index] = peak + jnp.log(total)

    work_items(info, sizes, attend)
    each = outs[0].shape[1]
    for place, out in enumerate(outs):
        out[...] = mixed[:, place * each : (place + 1) * each]


def attend_backward_kernel(sizes, info, query, lse_prompt, lse_cont, pairs, *rest):
    *grads, grad_query, grad_pairs, grad, sums = rest
    lse = (lse_prompt, lse_cont)
    width = query.shape[0]
    pad = (-width) % 128
    each = grads[0].shape[1]
    for place, one in enumerate(grads):
        grad[:, place * each : (place + 1) * each] = one[...]

    def attend(kind, index, own, chunks, mask):
        count = len(own) * CHUNK
        block = jnp.concatenate([pairs[chunk] for chunk in chunks], axis=0)
        query_spread = spread_heads(load_lanes(query, own), 0, pad)
        grad_spread = spread_heads(load_lanes(grad, own), pad, 0)
        keys = key_lanes(block, width)
        weights = jnp.exp(mask(dot_plain(keys, query_spread)) - lse[kind][index])
        slopes = dot_plain(value_lanes(block, width), grad_spread)
        centre = jnp.sum(weights * slopes, axis=0, keepdims=True)
        grad_scores = low(weights * (slopes - centre))
        flip = keys.T
        for head in range(width // HD):
            group = slice(head * count, (head + 1) * count)
            part = slice(head * HD, (head + 1) * HD)
            result = low(dot_plain(flip[part], grad_scores[:, group]) * 0.125)
            for place, chunk in enumerate(own):
                grad_query[part, chunk_lanes(chunk)] = result[
                    :, place * CHUNK : (place + 1) * CHUNK
                ]
        key_part = dot_last(grad_scores, query_spread)
        value_part = dot_last(low(weights), grad_spread)
        if pad:
            edge = width - pad
            shared = key_part[:, edge:] + value_part[:, : 2 * pad]
            joined = [key_part[:, :edge], shared, value_part[:, 2 * pad :]]
        else:
            joined = [key_part, value_part]
        result = jnp.concatenate(joined, axis=1)
        for place, chunk in enumerate(chunks):
            part = result[place * CHUNK : (place + 1) * CHUNK]
            if kind == 0 or place == 0:
                sums[chunk] = part
            else:
                sums[chunk] += part

    work_items(info, sizes, attend)

    @pl.loop(0, pairs.shape[0], unroll=4)
    def _(chunk):
        grad_pairs[chunk] = low(sums[chunk])


def attend_cost(factor, sizes, heads):
    prompts, conts, places, per = sizes
    scores = heads * places * per * CHUNK * CHUNK * (prompts * per + conts)
    return pl.CostEstimate(flops=factor * HD * scores, bytes_accessed=10**7, transcendentals=scores)


def attend_forward(sizes, info, query_weight, pair_weight, rows, local_rows):
    prompts, conts, places, per = sizes
    width = query_weight.shape[1]
    heads = width // HD
    count = sum(one.shape[0] for one in rows)
    each = local_rows // 4
    return pl.pallas_call(
        functools.partial(attend_forward_kernel, sizes, len(rows)),
        out_shape=(
            shape((width, local_rows)),
            shape((count // CHUNK, CHUNK, 2 * width)),
            *([shape((width, each))] * 4),
            shape((prompts, 1, heads * per * CHUNK), F32),
            shape((conts, 1, heads * CLEN), F32),
        ),
        in_specs=[SM] + [VM] * (2 + len(rows)),
        out_specs=(VM,) * 8,
        scratch_shapes=[pltpu.VMEM((width, local_rows), BF16)],
        compiler_params=ROOM,
        cost_estimate=attend_cost(20, sizes, heads),
        name="attend_forward",
    )(info, query_weight, pair_weight, *rows)


def attend_backward(sizes, info, query, lse_prompt, lse_cont, pairs, grads):
    return pl.pallas_call(
        functools.partial(attend_backward_kernel, sizes),
        out_shape=(shape(query.shape), shape(pairs.shape)),
        in_specs=[SM] + [VM] * (4 + len(grads)),
        out_specs=(VM,) * 2,
        scratch_shapes=[pltpu.VMEM(query.shape, BF16), pltpu.VMEM(pairs.shape, F32)],
        compiler_params=ROOM,
        cost_estimate=attend_cost(40, sizes, query.shape[0] // HD),
        name="attend_backward",
    )(info, query, lse_prompt, lse_cont, pairs, *grads)


def rows_remote_kernel(grad_pairs, pair_weight, keep, send):
    half = grad_pairs.shape[0] // 2
    wide = grad_pairs.shape[2]
    keep[0] = dot_last(grad_pairs[:half].reshape(half * CHUNK, wide), pair_weight[...])
    send[0] = low(dot_last(grad_pairs[half:].reshape(half * CHUNK, wide), pair_weight[...]))


def rows_local_kernel(grad_pairs, grad_query, query_weight, pair_weight, keep, send):
    half = grad_pairs.shape[0] // 2
    wide = grad_pairs.shape[2]
    each = half * CHUNK
    query_rows = grad_query[...].T
    rows = dot_last(grad_pairs[...].reshape(2 * each, wide), pair_weight[...])
    rows = rows + dot_last(query_rows, query_weight[...])
    keep[0] = rows[:each]
    send[0] = low(rows[each:])


def rows_remote(grad_pairs, pair_weight, places, each):
    width = pair_weight.shape[0]
    chunks = 2 * each // CHUNK
    count = places - 1
    return pl.pallas_call(
        rows_remote_kernel,
        grid=(count,),
        in_specs=[
            pl.BlockSpec((chunks,) + grad_pairs.shape[1:], lambda at: (1 + count - at, 0, 0)),
            pl.BlockSpec(pair_weight.shape, lambda at: (0, 0)),
        ],
        out_specs=(
            pl.BlockSpec((1, each, width), lambda at: (at, 0, 0)),
            pl.BlockSpec((1, each, width), lambda at: (at, 0, 0)),
        ),
        out_shape=(shape((count, each, width), F32), shape((count, each, width))),
        compiler_params=ROOM,
        name="rows_remote",
    )(grad_pairs, pair_weight)


def rows_local(grad_pairs, grad_query, query_weight, pair_weight, each):
    width = pair_weight.shape[0]
    chunks = 2 * each // CHUNK
    return pl.pallas_call(
        rows_local_kernel,
        grid=(2,),
        in_specs=[
            pl.BlockSpec((chunks,) + grad_pairs.shape[1:], lambda at: (1 - at, 0, 0)),
            pl.BlockSpec((grad_query.shape[0], 2 * each), lambda at: (0, 1 - at)),
            pl.BlockSpec(query_weight.shape, lambda at: (0, 0)),
            pl.BlockSpec(pair_weight.shape, lambda at: (0, 0)),
        ],
        out_specs=(
            pl.BlockSpec((1, each, width), lambda at: (at, 0, 0)),
            pl.BlockSpec((1, each, width), lambda at: (at, 0, 0)),
        ),
        out_shape=(shape((2, each, width), F32), shape((2, each, width))),
        compiler_params=ROOM,
        name="rows_local",
    )(grad_pairs, grad_query, query_weight, pair_weight)


def qkv_grad_kernel(grad_query, grad_pairs, *rest):
    *rows, out = rest
    width, local_rows = grad_query.shape
    total_query = total_pair = None
    at = 0
    for one in rows:
        value = one[...]
        count = value.shape[0]
        chunks = slice(at // CHUNK, (at + count) // CHUNK)
        part = dot_plain(grad_pairs[chunks].reshape(count, 2 * width).T, value)
        total_pair = part if total_pair is None else total_pair + part
        if at < local_rows:
            part = dot_plain(grad_query[:, at : at + count], value)
            total_query = part if total_query is None else total_query + part
        at += count
    out[...] = low(jnp.concatenate([total_query, total_pair], axis=0).T)


def qkv_grad(grad_query, grad_pairs, rows):
    width = rows[0].shape[1]
    return pl.pallas_call(
        qkv_grad_kernel,
        out_shape=shape((width, 3 * grad_query.shape[0])),
        in_specs=[VM] * (2 + len(rows)),
        out_specs=VM,
        compiler_params=ROOM,
        name="qkv_grad",
    )(grad_query, grad_pairs, *rows)


def final_kernel(first, tokens, gains, grad_middle, kept, beside, across, own, far, out):
    unit, factor = rms_unit(tokens[...].astype(F32))
    rows = kept[0] + beside[0].astype(F32) + across[...].astype(F32)
    ring = jnp.concatenate([own[...], far[...]], axis=0).astype(F32)
    rows = plain_order(rows + jnp.where(first[0] == 0, ring, 0.0))
    out[...] = rms_backward(rows, unit, factor, gains[0:1, :]) + grad_middle[...]


def final_rows(side, tokens, gains, grad_middle, kept, beside, across, own, far):
    rows, width = tokens.shape
    last = pl.BlockSpec((1, rows, width), lambda at: (1, 0, 0))
    half = pl.BlockSpec((rows // 2, width), lambda at: (0, 0))
    whole = pl.BlockSpec((rows, width), lambda at: (0, 0))
    return pl.pallas_call(
        final_kernel,
        grid=(1,),
        in_specs=[
            SM,
            whole,
            pl.BlockSpec(gains.shape, lambda at: (0, 0)),
            whole,
            last,
            last,
            whole,
            half,
            half,
        ],
        out_specs=whole,
        out_shape=shape((rows, width), F32),
        compiler_params=ROOM,
        name="final_rows",
    )(side, tokens, gains, grad_middle, kept, beside, across, own, far)


def slot_places(chosen, priority, first, expert_count, capacity):
    tokens = chosen.shape[0]
    expert_range = jnp.arange(expert_count)
    chosen_hot = low(chosen[:, None] == expert_range[None, :])
    order_hot = low(priority[:, None] == jnp.arange(tokens)[None, :])
    sorted_hot = jnp.dot(order_hot, chosen_hot, preferred_element_type=F32)
    places = jnp.arange(tokens)
    before = low(places[:, None] > places[None, :])
    earlier = jnp.dot(before, low(sorted_hot), preferred_element_type=F32)
    sorted_rank = jnp.minimum(jnp.sum(earlier * sorted_hot, axis=1), capacity)
    rank = jnp.einsum("it,i->t", order_hot, low(sorted_rank), preferred_element_type=F32)
    rank = rank.astype(jnp.int32)
    near = chosen ^ first
    block = (near >> 1) + (near & 1) * (expert_count // 2)
    return jnp.where(rank < capacity, block * capacity + rank, -1)


def softmax_rows(logits):
    shifted = jnp.exp(logits - jnp.max(logits, axis=-1, keepdims=True))
    return shifted / jnp.sum(shifted, axis=-1, keepdims=True)


def one_hot_experts(ids, expert_count):
    return ids == lax.broadcasted_iota(jnp.int32, (ids.shape[0], expert_count), 1)


def middle_kernel(
    parts, tokens, cotangent, gains, router, ids, place_row, *rest
):
    attended, proj = rest[:parts], rest[parts : 2 * parts]
    even_rows, odd_rows, even_grads, odd_grads, middle, normed, probs = rest[2 * parts :]
    mixed = plain_order(jnp.concatenate([one[...] for one in attended], axis=0), 1)
    branch = dot_plain(mixed.T, jnp.concatenate([one[...] for one in proj], axis=0))
    total = tokens[...].astype(F32) + branch
    middle[...] = total
    unit, _ = rms_unit(total)
    normed_rows = low(gains[1:2, :] * unit)
    normed[...] = normed_rows
    chances = softmax_rows(dot_plain(normed_rows, router[...]))
    probs[...] = chances
    hot = one_hot_experts(ids[...], chances.shape[1])
    gate = jnp.sum(jnp.where(hot, chances, 0.0), axis=1, keepdims=True)
    weighted = low(gate * cotangent[...].astype(F32))
    half = even_rows.shape[0]
    for at, (row_slots, grad_slots) in enumerate(((even_rows, even_grads), (odd_rows, odd_grads))):
        slots = at * half + lax.broadcasted_iota(jnp.int32, (half, tokens.shape[0]), 0)
        dispatch = low(slots == place_row[...])
        row_slots[...] = low(dot_plain(dispatch, normed_rows))
        grad_slots[...] = low(dot_plain(dispatch, weighted))


def middle_rows(tokens, cotangent, gains, router, ids, place, slots, attended, proj):
    rows, width = tokens.shape
    half = shape((slots // 2, width))
    return pl.pallas_call(
        functools.partial(middle_kernel, len(attended)),
        out_shape=(
            half,
            half,
            half,
            half,
            shape((rows, width), F32),
            shape((rows, width)),
            shape((rows, router.shape[1]), F32),
        ),
        in_specs=[VM] * (6 + 2 * len(attended)),
        out_specs=(VM,) * 7,
        compiler_params=ROOM,
        name="middle_rows",
    )(tokens, cotangent, gains, router, ids, place[None, :], *attended, *proj)


def gather_slots(refs, capacity):
    own, beside, *pairs = refs
    even = [own[0:capacity, :]] + [pair[0:capacity, :] for pair in pairs]
    odd = [beside[0:capacity, :]] + [pair[capacity:, :] for pair in pairs]
    return jnp.concatenate(even + odd, axis=0)


def combine_kernel(
    parts, moved, capacity, *refs
):
    tokens_in, rest = refs[:8], refs[8:]
    cotangent, gains, router, ids, place_column, middle, normed, probs = tokens_in
    attended, proj, rest = rest[:parts], rest[parts : 2 * parts], rest[2 * parts :]
    row_refs, grad_refs, rest = rest[:moved], rest[moved : 2 * moved], rest[2 * moved :]
    output, grad_middle, *near, proj_keep, proj_send, small = rest
    rows, expert_count = probs.shape
    slots = 2 * (moved - 1) * capacity
    slot_range = lax.broadcasted_iota(jnp.int32, (rows, slots), 1)
    dispatch = low(slot_range == place_column[...])
    routed = dot_plain(dispatch, gather_slots(row_refs, capacity))
    returned = dot_plain(dispatch, gather_slots(grad_refs, capacity))
    chances = probs[...]
    hot = one_hot_experts(ids[...], expert_count)
    gate = jnp.sum(jnp.where(hot, chances, 0.0), axis=1, keepdims=True)
    total = middle[...]
    output[...] = low(total + gate * routed)
    upstream = cotangent[...].astype(F32)
    grad_gate = jnp.sum(upstream * routed, axis=1, keepdims=True)
    grad_logits = low((grad_gate * gate) * (hot.astype(F32) - chances))
    grad_second = returned + dot_last(grad_logits, router[...])
    unit, factor = rms_unit(total)
    gain_two = jnp.sum(grad_second * unit, axis=0, keepdims=True)
    grad_rows = upstream + rms_backward(grad_second, unit, factor, gains[1:2, :])
    grad_middle[...] = grad_rows
    grad_low = split_order(low(grad_rows))
    for place in range(parts):
        near[place][...] = low(dot_last(proj[place][...], grad_low))
        part = dot_plain(attended[place][...], grad_low)
        if place % 2:
            proj_send[place // 2] = low(part)
        else:
            proj_keep[place // 2] = part
    small[0:expert_count, :] = dot_plain(grad_logits.T, normed[...])
    small[expert_count:, :] = jnp.broadcast_to(gain_two, (small.shape[0] - expert_count, rows))


def combine_rows(
    cotangent, gains, router, ids, place, middle, normed, probs, attended, proj, row_slots, grad_slots
):
    rows, width = middle.shape
    capacity = 5 * rows // (4 * router.shape[1])
    local_width = proj[0].shape[0]
    parts = len(proj)
    inputs = [cotangent, gains, router, ids, place[:, None], middle, normed, probs]
    inputs += list(attended) + list(proj) + list(row_slots) + list(grad_slots)
    return pl.pallas_call(
        functools.partial(combine_kernel, parts, len(row_slots), capacity),
        out_shape=(
            shape((rows, width)),
            shape((rows, width), F32),
            *([shape((local_width, rows))] * parts),
            shape((parts // 2, local_width, width), F32),
            shape((parts // 2, local_width, width)),
            shape((router.shape[1] + 8, width), F32),
        ),
        in_specs=[VM] * len(inputs),
        out_specs=(VM,) * (5 + parts),
        compiler_params=ROOM,
        name="combine_rows",
    )(*inputs)


def expert_forward_kernel(moved, capacity, *refs):
    parts, (up, down, even, odd, hidden_pre, rows, total) = refs[:moved], refs[moved:]
    step = pl.program_id(0)

    @pl.when(step == 0)
    def _():
        rows[...] = gather_slots(parts, capacity)

    pre = dot_plain(rows[...], up[...])
    hidden_pre[...] = pre
    inner = ROOT * (pre + CUBE * (pre * pre * pre))
    hidden = low(0.5 * pre * (1.0 + jnp.tanh(inner)))
    part = dot_plain(hidden, down[...])

    @pl.when(step == 0)
    def _():
        total[...] = part

    @pl.when(step > 0)
    def _():
        total[...] += part

    @pl.when(step == pl.num_programs(0) - 1)
    def _():
        half = even.shape[0]
        even[...] = low(total[:half])
        odd[...] = low(total[half:])


def expert_backward_kernel(moved, capacity, *refs):
    row_parts, grad_parts, rest = refs[:moved], refs[moved : 2 * moved], refs[2 * moved :]
    hidden_pre, up, down, even, odd, grad_up, grad_down, total, grads, rows_flip, grads_flip = rest
    step = pl.program_id(0)

    @pl.when(step == 0)
    def _():
        arrived = gather_slots(grad_parts, capacity)
        grads[...] = arrived
        grads_flip[...] = arrived.T
        rows_flip[...] = gather_slots(row_parts, capacity).T

    pre = hidden_pre[...]
    square = pre * pre
    bend = jnp.tanh(ROOT * (pre + CUBE * (square * pre)))
    half = 0.5 * (1.0 + bend)
    hidden = low(pre * half)
    slope = half + (0.5 * ROOT) * pre * (1.0 - bend * bend) * (1.0 + (3.0 * CUBE) * square)
    grad_pre = low(dot_last(grads[...], down[...]) * slope)
    grad_down[...] = low(dot_plain(grads_flip[...], hidden))
    grad_up[...] = low(dot_plain(rows_flip[...], grad_pre))
    part = dot_last(grad_pre, up[...])

    @pl.when(step == 0)
    def _():
        total[...] = part

    @pl.when(step > 0)
    def _():
        total[...] += part

    @pl.when(step == pl.num_programs(0) - 1)
    def _():
        count = even.shape[0]
        even[...] = low(total[:count])
        odd[...] = low(total[count:])


def whole_specs(values):
    return [pl.BlockSpec(value.shape, lambda at: (0, 0)) for value in values]


def expert_forward(parts, up, down):
    width, units = up.shape
    half = parts[1].shape[0]
    capacity = half // (len(parts) - 1)
    block = pl.BlockSpec((half, width), lambda at: (0, 0))
    return pl.pallas_call(
        functools.partial(expert_forward_kernel, len(parts), capacity),
        grid=(units // UNITS,),
        in_specs=whole_specs(parts)
        + [
            pl.BlockSpec((width, UNITS), lambda at: (0, at)),
            pl.BlockSpec((UNITS, width), lambda at: (at, 0)),
        ],
        out_specs=(block, block, pl.BlockSpec((2 * half, UNITS), lambda at: (0, at))),
        out_shape=(shape((half, width)), shape((half, width)), shape((2 * half, units), F32)),
        scratch_shapes=[
            pltpu.VMEM((2 * half, width), BF16),
            pltpu.VMEM((2 * half, width), F32),
        ],
        compiler_params=ROOM,
        cost_estimate=pl.CostEstimate(
            flops=8 * half * width * units,
            bytes_accessed=12 * half * units,
            transcendentals=2 * half * units,
        ),
        name="expert_forward",
    )(*parts, up, down)


def expert_backward(row_parts, grad_parts, hidden_pre, up, down):
    width, units = up.shape
    half = row_parts[1].shape[0]
    capacity = half // (len(row_parts) - 1)
    block = pl.BlockSpec((half, width), lambda at: (0, 0))
    return pl.pallas_call(
        functools.partial(expert_backward_kernel, len(row_parts), capacity),
        grid=(units // UNITS,),
        in_specs=whole_specs(row_parts)
        + whole_specs(grad_parts)
        + [
            pl.BlockSpec((2 * half, UNITS), lambda at: (0, at)),
            pl.BlockSpec((width, UNITS), lambda at: (0, at)),
            pl.BlockSpec((UNITS, width), lambda at: (at, 0)),
        ],
        out_specs=(
            block,
            block,
            pl.BlockSpec((width, UNITS), lambda at: (0, at)),
            pl.BlockSpec((width, UNITS), lambda at: (0, at)),
        ),
        out_shape=(
            shape((half, width)),
            shape((half, width)),
            shape((width, units)),
            shape((width, units)),
        ),
        scratch_shapes=[
            pltpu.VMEM((2 * half, width), F32),
            pltpu.VMEM((2 * half, width), BF16),
            pltpu.VMEM((width, 2 * half), BF16),
            pltpu.VMEM((width, 2 * half), BF16),
        ],
        compiler_params=ROOM,
        cost_estimate=pl.CostEstimate(
            flops=16 * half * width * units,
            bytes_accessed=16 * half * units,
            transcendentals=2 * half * units,
        ),
        name="expert_backward",
    )(*row_parts, *grad_parts, hidden_pre, up, down)


def shards(
    tokens,
    cotangent,
    gains,
    qkv_weight,
    proj_weight,
    router_weight,
    expert_up,
    expert_down,
    expert_ids,
    slot_order,
    segment_ids,
):
    dp_count, ctx_count, tp_count = (lax.axis_size(name) for name in ("dp", "ctx", "tp"))
    dp_index, ctx_index, tp_index = (lax.axis_index(name) for name in ("dp", "ctx", "tp"))
    group = dp_count * tp_count
    group_index = dp_index * tp_count + tp_index
    tok_dev, width = tokens.shape
    half_rows = tok_dev // 2
    expert_count = router_weight.shape[1]
    capacity = 5 * tok_dev // (4 * expert_count)
    slots = expert_count * capacity
    per = PLEN // ctx_count // CHUNK
    conts_here = segment_ids.shape[0]
    prompts_here = conts_here * ctx_count // CONTS
    local_width = qkv_weight.shape[2]
    shard_rows = qkv_weight.shape[1]
    side, core = tp_index >> 1, tp_index & 1

    def across(value):
        return xor_swap(value, "tp", tp_count, 2)

    def beside(value):
        return xor_swap(value, "tp", tp_count, 1)

    full_up = lax.all_gather(expert_up, "ctx", axis=2, tiled=True)[0]

    own, own_second = normalize(tokens, gains)
    far_second = across(own_second)
    carried = jnp.where(side == 0, own[:half_rows], far_second)
    far_first = across(own[:half_rows])
    rows = [own, beside(own), far_first, far_second, beside(far_first), beside(far_second)]
    for _ in range(ctx_count - 1):
        carried = ring_step(carried, "ctx", ctx_count, 1)
        other = across(carried)
        rows += [carried, other, beside(carried), beside(other)]
    down_after, _ = lax.optimization_barrier((expert_down, carried))
    full_down = lax.all_gather(down_after, "ctx", axis=1, tiled=True)[0]

    packed = jnp.concatenate(
        [
            qkv_weight.transpose(1, 0, 2).reshape(shard_rows, 3 * local_width),
            proj_weight.T,
            router_weight,
        ],
        axis=1,
    )
    by_ctx = jnp.stack(xor_exchange([packed] * ctx_count, "ctx", ctx_count))
    by_dp = jnp.stack(xor_gather(by_ctx, "dp", dp_count)).reshape((-1,) + packed.shape)
    shard_index = dp_index * ctx_count + ctx_index
    weights = jnp.concatenate(
        [pick(by_dp, shard_index ^ place) for place in range(dp_count * ctx_count)], axis=0
    )
    query_weight = weights[:, :local_width]
    pair_weight = weights[:, local_width : 3 * local_width]
    router = weights[:, 4 * local_width :]
    proj = xor_gather(weights[:, 3 * local_width : 4 * local_width].T, "tp", tp_count, [2, 1])

    device_chunks = tok_dev // CHUNK

    def split_place(at):
        return (at % 2) * (device_chunks // 2) + at // 2

    at = jnp.arange(prompts_here * per)
    owner, inside = at // device_chunks, at % device_chunks
    local_at = (owner ^ tp_index) * device_chunks + split_place(inside)
    remote_at = ((owner ^ core) * 2 + ((inside % 2) ^ side)) * (device_chunks // 2) + inside // 2
    remote_first = (tp_count + 2 * jnp.arange(ctx_count - 1)) * device_chunks
    prompt_at = jnp.concatenate(
        [
            local_at.reshape(prompts_here, 1, per),
            remote_first[None, :, None] + remote_at.reshape(prompts_here, 1, per),
        ],
        axis=1,
    )
    at = jnp.arange(conts_here)
    cont_at = ((2 + at // device_chunks) ^ tp_index) * device_chunks + split_place(
        at % device_chunks
    )
    info = jnp.concatenate([ctx_index[None], prompt_at.reshape(-1), cont_at, segment_ids])
    info = info.astype(jnp.int32)
    sizes = (prompts_here, conts_here, ctx_count, per)

    query, pairs, *attended, lse_prompt, lse_cont = attend_forward(
        sizes, info, query_weight, pair_weight, rows, tp_count * tok_dev
    )
    attended = xor_exchange(attended, "tp", tp_count)
    place = slot_places(expert_ids[:, 0], slot_order[0], group_index, expert_count, capacity)

    def start_exchange(odd):
        return xor_swap(odd, ("dp", "tp"), group, 1)

    def finish_exchange(even, other):
        moved = [even, other]
        for at in range(1, group // 2):
            block = slice(at * capacity, (at + 1) * capacity)
            pair = jnp.concatenate([even[block], other[block]], axis=0)
            moved.append(xor_swap(pair, ("dp", "tp"), group, 2 * at))
        return moved

    even_rows, odd_rows, even_grads, odd_grads, middle, normed_two, probs = middle_rows(
        tokens, cotangent, gains, router, expert_ids, place, slots, attended, proj
    )
    row_slots = finish_exchange(even_rows, start_exchange(odd_rows))
    other_grads = start_exchange(odd_grads)
    row_slots, even_grads, other_grads = lax.optimization_barrier(
        (row_slots, even_grads, other_grads)
    )
    grad_slots = finish_exchange(even_grads, other_grads)
    even, odd, hidden_pre = expert_forward(row_slots, full_up, full_down)
    even, odd, hidden_pre, grad_slots = lax.optimization_barrier(
        (even, odd, hidden_pre, grad_slots)
    )
    even, other, hidden_pre = lax.optimization_barrier((even, start_exchange(odd), hidden_pre))
    made_slots = finish_exchange(even, other)
    even, odd, grad_up, grad_down = expert_backward(
        row_slots, grad_slots, hidden_pre, full_up, full_down
    )
    even, odd, made_slots = lax.optimization_barrier((even, odd, made_slots))
    back_slots = finish_exchange(even, start_exchange(odd))
    grad_up = lax.psum_scatter(grad_up, "ctx", scatter_dimension=1, tiled=True).astype(F32)[None]
    grad_down = lax.psum_scatter(grad_down, "ctx", scatter_dimension=1, tiled=True)
    grad_down = grad_down.T.astype(F32)[None]

    output, grad_middle, *grad_near, proj_keep, proj_send, small_part = combine_rows(
        cotangent,
        gains,
        router,
        expert_ids,
        place,
        middle,
        normed_two,
        probs,
        attended,
        proj,
        made_slots,
        back_slots,
    )
    grad_query, grad_pairs = attend_backward(
        sizes, info, query, lse_prompt, lse_cont, pairs, xor_exchange(grad_near, "tp", tp_count)
    )

    remote_keep, remote_send = rows_remote(grad_pairs, pair_weight, ctx_count, tok_dev)
    remote_send = beside(remote_send)
    local_keep, local_send = rows_local(
        grad_pairs, grad_query, query_weight, pair_weight, tok_dev
    )
    local_send = beside(local_send)
    pieces = []
    for at in range(ctx_count - 1):
        chip = remote_keep[at] + remote_send[at].astype(F32)
        pieces.append(chip[:half_rows] + across(low(chip[half_rows:])).astype(F32))
    running = low(pieces[0])
    for piece in pieces[1:]:
        running = low(piece + ring_step(running, "ctx", ctx_count, -1).astype(F32))
    running = ring_step(running, "ctx", ctx_count, -1)
    far_rows = across(low(local_keep[0] + local_send[0].astype(F32)))
    grad_tokens = final_rows(
        side.astype(jnp.int32).reshape(1),
        tokens,
        gains,
        grad_middle,
        local_keep,
        local_send,
        far_rows,
        running,
        across(running),
    )

    def scatter_weights(values):
        values = low(values).reshape(dp_count, ctx_count, shard_rows, -1)
        for axis, size, me in (("dp", dp_count, dp_index), ("ctx", ctx_count, ctx_index)):
            moved = xor_exchange([pick(values, me ^ k) for k in range(size)], axis, size)
            values = add_all([piece.astype(F32) for piece in moved])
            if axis == "dp":
                values = low(values)
        return values

    def sum_tp(values):
        moved = xor_exchange([low(values)] * tp_count, "tp", tp_count)
        return values + add_all([piece.astype(F32) for piece in moved[1:]])

    proj_chip = proj_keep + beside(proj_send).astype(F32)
    proj_sum = proj_chip[0] + across(low(proj_chip[1])).astype(F32)
    early = jnp.concatenate([low(proj_sum), low(small_part[: expert_count + 1])], axis=0).T
    early = scatter_weights(early)
    grad_proj = early[:, :local_width].T
    small = sum_tp(early[:, local_width:])
    grad_qkv = scatter_weights(qkv_grad(grad_query, grad_pairs, rows))
    grad_qkv = grad_qkv.reshape(shard_rows, 3, local_width).transpose(1, 0, 2)
    gain_range = lax.dynamic_slice_in_dim(gains[0], shard_index * shard_rows, shard_rows)
    gain_one = sum_tp(jnp.sum(qkv_weight.astype(F32) * grad_qkv, axis=(0, 2))) / gain_range
    grad_router = small[:, :expert_count]
    grad_gains = jnp.stack([gain_one, small[:, expert_count]])
    return (output, grad_tokens, grad_gains, grad_qkv, grad_proj, grad_router, grad_up, grad_down)


def solution(mesh):
    in_specs = (
        P(("dp", "ctx", "tp"), None),
        P(("dp", "ctx", "tp"), None),
        P(),
        P(None, ("dp", "ctx"), "tp"),
        P("tp", ("dp", "ctx")),
        P(("dp", "ctx"), None),
        P(("dp", "tp"), None, "ctx"),
        P(("dp", "tp"), "ctx", None),
        P(("dp", "ctx", "tp"), None),
        P(("dp", "ctx", "tp"), None),
        P(("dp", "ctx")),
    )
    out_specs = (
        P(("dp", "ctx", "tp"), None),
        P(("dp", "ctx", "tp"), None),
        P(None, ("dp", "ctx")),
        P(None, ("dp", "ctx"), "tp"),
        P("tp", ("dp", "ctx")),
        P(("dp", "ctx"), None),
        P(("dp", "tp"), None, "ctx"),
        P(("dp", "tp"), "ctx", None),
    )
    return jax.shard_map(shards, mesh=mesh, in_specs=in_specs, out_specs=out_specs, check_vma=False)
```

time: 743 us -> 632 us (0.85)
  waiting for transfers between devices: 379 us -> 242 us
  Pallas kernels: 115 us -> 190 us
  matrix products: 50.5 us -> 1.61 us
  starting transfers between devices: 65.1 us -> 106 us
  local copies, waits for them, and re-layouts: 69 us -> 44.4 us
  other arithmetic: 36.7 us -> 25 us
    ppermute x6, waiting for transfers between devices: 194 us -> 83.1 us  [ring_step(): lax.ppermute(value, axis, [(place, (place + shift) % size) for place in r...]
    pallas_call x4 -> x11, Pallas kernels: 115 us -> 190 us  [the longest x1 44.6 us: attend_backward(): pl.pallas_call(functools.partial(attend_backward_kernel, sizes), out_shap...]
    dot_general x25 -> x3, matrix products: 50.5 us -> 1.61 us  [the longest x1 0.71 us: slot_places(): sorted_hot = jnp.dot(order_hot, chosen_hot, preferred_element_type=F32)]
    ppermute x55 -> x65, starting transfers between devices: 59.3 us -> 97.3 us  [xor_swap(): lax.ppermute(value, axis, [(place, place ^ mask) for place in range(size)])]
    ppermute x55 -> x65, waiting for transfers between devices: 185 us -> 158 us  [xor_swap(): lax.ppermute(value, axis, [(place, place ^ mask) for place in range(size)])]
    unnamed x153 -> x129, local copies, waits for them, and re-layouts: 36.1 us -> 23.1 us
  transfers between devices with their start and end apart: 65 -> 75, of which waited for: 28 -> 32; matrix products, arithmetic and copies ran while one was open for 19% -> 10% of each run, Pallas kernels for 13% -> 26%
where the time goes in v3:
time: 632 us; the launch traced here: 624 us
  waiting for transfers between devices  242 us (38%)
  Pallas kernels  190 us (30%)
  starting transfers between devices  106 us (17%)
  local copies, waits for them, and re-layouts  44.4 us (7%)
  other arithmetic  25 us (4%)
  between operations  14.9 us (2%)
    ppermute x65, waiting for transfers between devices, xor_swap(): lax.ppermute(value, axis, [(place, place ^ mask) for place in range(size)])  158 us
    ppermute x65, starting transfers between devices, xor_swap(): lax.ppermute(value, axis, [(place, place ^ mask) for place in range(size)])  97.3 us
    ppermute x6, waiting for transfers between devices, ring_step(): lax.ppermute(value, axis, [(place, (place + shift) % size) for place in r...  83.1 us
    pallas_call x1, Pallas kernels, attend_backward(): pl.pallas_call(functools.partial(attend_backward_kernel, sizes), out_shap...  44.6 us
    pallas_call x1, Pallas kernels, attend_forward(): pl.pallas_call(functools.partial(attend_forward_kernel, sizes, len(rows))...  36.3 us
    pallas_call x1, Pallas kernels, expert_backward(): pl.pallas_call(functools.partial(expert_backward_kernel, len(row_parts),...  29.3 us
    unnamed x129, local copies, waits for them, and re-layouts  23.1 us
    pallas_call x1, Pallas kernels, expert_forward(): pl.pallas_call(functools.partial(expert_forward_kernel, len(parts), capac...  16.7 us
  transfers between devices with their start and end apart: 75, of which 32 were waited for; matrix products, arithmetic and copies ran while one was open for 10% of the time, Pallas kernels for 26%

profile of v3, /device:TPU:25, one launch (start us, length us, event | category | flops | bytes accessed | tf_op | source)
XLA Modules:
  0.0 623.9 jit_solution(5710304950630390123)
XLA Ops:
  8.0 2.9 normalize.1
  13.8 2.2 collective-permute-start
  15.9 9.4 %collective-permute-done.6.rest_3_ = bf16[384,768]{1,0:T(8,128)(2,1)S(1)} collective-permute-done((bf16[384,768]{1,0:T(8,128)(2,1)}, bf16[384,768]{1,0:T(8,128)(2,1)S(1)}, u32[]{:S(2)}, u32[]{:S(2)}) %collective-permute-start.6) | collective-permute-done | bytes 589856 | tf_op jit(solution)/shard_map/ppermute | solution.py:49
  25.4 2.4 broadcast_select_fusion
  27.8 14.2 %collective-permute-done.1 = bf16[96,776]{0,1:T(8,128)(2,1)S(1)} collective-permute-done((bf16[96,776]{0,1:T(8,128)(2,1)S(1)}, bf16[96,776]{0,1:T(8,128)(2,1)S(1)}, u32[]{:S(2)}, u32[]{:S(2)}) %collective-permute-start.1) | collective-permute-done | bytes 149024 | tf_op jit(solution)/shard_map/ppermute | solution.py:49
  43.9 31.0 %collective-permute-done.9.rest_6_ = bf16[384,768]{1,0:T(8,128)(2,1)} collective-permute-done((bf16[384,768]{1,0:T(8,128)(2,1)}, bf16[384,768]{1,0:T(8,128)(2,1)}, u32[]{:S(2)}, u32[]{:S(2)}) %collective-permute-start.9) | collective-permute-done | bytes 589856 | tf_op jit(solution)/shard_map/ppermute | solution.py:53
  77.3 1.5 copy.154
  84.4 33.0 %collective-permute-done.13.rest_10_ = bf16[384,768]{1,0:T(8,128)(2,1)} collective-permute-done((bf16[384,768]{1,0:T(8,128)(2,1)}, bf16[384,768]{1,0:T(8,128)(2,1)}, u32[]{:S(2)}, u32[]{:S(2)}) %collective-permute-start.13) | collective-permute-done | bytes 589856 | tf_op jit(solution)/shard_map/ppermute | solution.py:53
  120.3 19.0 %collective-permute-done.17.rest_14_ = bf16[384,768]{1,0:T(8,128)(2,1)} collective-permute-done((bf16[384,768]{1,0:T(8,128)(2,1)}, bf16[384,768]{1,0:T(8,128)(2,1)}, u32[]{:S(2)}, u32[]{:S(2)}) %collective-permute-start.17) | collective-permute-done | bytes 589856 | tf_op jit(solution)/shard_map/ppermute | solution.py:53
  146.7 4.0 collective-permute-done.24
  150.7 10.1 %collective-permute-start.11 = (bf16[384,768]{1,0:T(8,128)(2,1)}, bf16[384,768]{1,0:T(8,128)(2,1)}, u32[]{:S(2)}, u32[]{:S(2)}) collective-permute-start(bf16[384,768]{1,0:T(8,128)(2,1)} %collective-permute-done.9.rest_6_), channel_id=1, source_target_pairs={{0,1},{1,0},{2,3},{3,2},{4,5},{5,4},{6,7},{7,6},{8,9},{9,8},{10,11... | collective-permute-start | bytes 1769480 | tf_op jit(solution)/shard_map/ppermute | solution.py:49
  164.0 8.3 %collective-permute-start.12 = (bf16[384,768]{1,0:T(8,128)(2,1)}, bf16[384,768]{1,0:T(8,128)(2,1)}, u32[]{:S(2)}, u32[]{:S(2)}) collective-permute-start(bf16[384,768]{1,0:T(8,128)(2,1)} %collective-permute-done.10.rest_7_), channel_id=1, source_target_pairs={{0,1},{1,0},{2,3},{3,2},{4,5},{5,4},{6,7},{7,6},{8,9},{9,8},{10,11... | collective-permute-start | bytes 1769480 | tf_op jit(solution)/shard_map/ppermute | solution.py:49
  172.3 4.3 collective-permute-done.14.rest_11_
  176.6 8.3 %collective-permute-start.16 = (bf16[384,768]{1,0:T(8,128)(2,1)}, bf16[384,768]{1,0:T(8,128)(2,1)}, u32[]{:S(2)}, u32[]{:S(2)}) collective-permute-start(bf16[384,768]{1,0:T(8,128)(2,1)} %collective-permute-done.14.rest_11_), channel_id=1, source_target_pairs={{0,1},{1,0},{2,3},{3,2},{4,5},{5,4},{6,7},{7,6},{8,9},{9,8},{10,11... | collective-permute-start | bytes 1769480 | tf_op jit(solution)/shard_map/ppermute | solution.py:49
  184.9 4.3 collective-permute-done.18.rest_15_
  189.3 4.4 collective-permute-start.20
  196.7 36.3 %attend_forward.1 = (bf16[192,3072]{1,0:T(8,128)(2,1)}, bf16[60,128,384]{2,1,0:T(8,128)(2,1)}, bf16[192,768]{1,0:T(8,128)(2,1)}, bf16[192,768]{1,0:T(8,128)(2,1)...) custom-call(s32[73]{0:T(128)} %pad_add_fusion.1.info, ...), custom_call_target="tpu_custom_call" | custom-call | flops 12079595520 | bytes 10000000 | tf_op jit(solution)/shard_map/attend_forward/pallas_call | solution.py:295
  236.8 1.6 slice.233.router.refs_2_
  242.3 6.5 %collective-permute-done.23.rest_3_.refs_11_ = bf16[192,768]{1,0:T(8,128)(2,1)S(1)} collective-permute-done((bf16[192,768]{1,0:T(8,128)(2,1)}, bf16[192,768]{1,0:T(8,128)(2,1)S(1)}, u32[]{:S(2)}, u32[]{:S(2)}) %collective-permute-start.23) | collective-permute-done | bytes 294944 | tf_op jit(solution)/shard_map/ppermute | solution.py:49
  249.5 8.6 %middle_rows.1 = (bf16[480,768]{1,0:T(8,128)(2,1)}, bf16[480,768]{1,0:T(8,128)(2,1)}, bf16[480,768]{1,0:T(8,128)(2,1)}, bf16[480,768]{1,0:T(8,128)(2,1)}, f32[76...) custom-call(bf16[768,768]{1,0:T(8,128)(2,1)} %tokens.5, bf16[768,768]{1,0:T(8,128)(2,1)} %refs_0_.1, ...), custom_call_target="tpu_custom_call" | custom-call | tf_op jit(solution)/shard_map/middle_rows/pallas_call | solution.py:505
  263.5 7.1 %collective-permute-done.27.refs_2_ = bf16[240,768]{1,0:T(8,128)(2,1)S(1)} collective-permute-done((bf16[240,768]{1,0:T(8,128)(2,1)S(1)}, bf16[240,768]{1,0:T(8,128)(2,1)S(1)}, u32[]{:S(2)}, u32[]{:S(2)}) %collective-permute-start.27) | collective-permute-done | bytes 368672 | tf_op jit(solution)/shard_map/ppermute | solution.py:49
  270.7 8.8 %collective-permute-done.29.refs_4_ = bf16[240,768]{1,0:T(8,128)(2,1)S(1)} collective-permute-done((bf16[240,768]{1,0:T(8,128)(2,1)S(1)}, bf16[240,768]{1,0:T(8,128)(2,1)S(1)}, u32[]{:S(2)}, u32[]{:S(2)}) %collective-permute-start.29) | collective-permute-done | bytes 368672 | tf_op jit(solution)/shard_map/ppermute | solution.py:49
  280.9 2.0 collective-permute-start.32
  283.3 16.7 %expert_forward.1 = (bf16[480,768]{1,0:T(8,128)(2,1)}, bf16[480,768]{1,0:T(8,128)(2,1)}, f32[960,3072]{1,0:T(8,128)}) custom-call(bf16[480,768]{1,0:T(8,128)(2,1)} %get-tuple-element.86.refs_0_, bf16[480,768]{1,0:T(8,128)(2,1)} %copy-done.26, bf16[240,768]{1,0:T(8,128)(2,1)} %copy-done.44, bf16[240,768]{1,0:T(8,128)(2,1)} %copy-done.45, ...), custom_call_target="tpu_custom_call" | custom-call | flops 9059696640 | bytes 17694720 | tf_op jit(solution)/shard_map/expert_forward/pallas_call | solution.py:671
  300.1 2.0 collective-permute-start.34
  302.0 2.1 collective-permute-done.34.refs_17_
  304.1 29.3 %expert_backward.1 = (bf16[480,768]{1,0:T(8,128)(2,1)}, bf16[480,768]{1,0:T(8,128)(2,1)}, bf16[768,3072]{1,0:T(8,128)(2,1)}, bf16[768,3072]{1,0:T(8,128)(2,1)}) custom-call(bf16[480,768]{1,0:T(8,128)(2,1)} %get-tuple-element.86.refs_0_, bf16[480,768]{1,0:T(8,128)(2,1)} %copy-done.26, bf16[240,768]{1,0:T(8,128)(2,1)} %copy-done.44, ...), custom_call_target="tpu_custom_call" | custom-call | flops 18119393280 | bytes 23592960 | tf_op jit(solution)/shard_map/expert_backward/pallas_call | solution.py:700
  337.5 6.9 %collective-permute-done.35.refs_18_ = bf16[240,768]{1,0:T(8,128)(2,1)S(1)} collective-permute-done((bf16[240,768]{1,0:T(8,128)(2,1)S(1)}, bf16[240,768]{1,0:T(8,128)(2,1)S(1)}, u32[]{:S(2)}, u32[]{:S(2)}) %collective-permute-start.35) | collective-permute-done | bytes 368672 | tf_op jit(solution)/shard_map/ppermute | solution.py:49
  345.7 7.9 %collective-permute-done.37.refs_20_ = bf16[240,768]{1,0:T(8,128)(2,1)S(1)} collective-permute-done((bf16[240,768]{1,0:T(8,128)(2,1)S(1)}, bf16[240,768]{1,0:T(8,128)(2,1)S(1)}, u32[]{:S(2)}, u32[]{:S(2)}) %collective-permute-start.37) | collective-permute-done | bytes 368672 | tf_op jit(solution)/shard_map/ppermute | solution.py:49
  353.5 1.5 collective-permute-start.38
  355.1 1.8 collective-permute-done.38.refs_22_
  360.9 6.1 collective-permute-done.39.refs_23_
  367.6 8.3 %collective-permute-done.41.refs_25_ = bf16[240,768]{1,0:T(8,128)(2,1)S(1)} collective-permute-done((bf16[240,768]{1,0:T(8,128)(2,1)S(1)}, bf16[240,768]{1,0:T(8,128)(2,1)S(1)}, u32[]{:S(2)}, u32[]{:S(2)}) %collective-permute-start.41) | collective-permute-done | bytes 368672 | tf_op jit(solution)/shard_map/ppermute | solution.py:49
  376.6 15.0 %combine_rows.1 = (bf16[768,768]{1,0:T(8,128)(2,1)}, f32[768,768]{1,0:T(8,128)}, bf16[192,768]{1,0:T(8,128)(2,1)}, bf16[192,768]{1,0:T(8,128)(2,1)}, bf16[192,76...) custom-call(bf16[768,768]{1,0:T(8,128)(2,1)} %refs_0_.1, ...), custom_call_target="tpu_custom_call" | custom-call | tf_op jit(solution)/shard_map/combine_rows/pallas_call | solution.py:578
  394.6 7.1 %collective-permute-done.43.rest_2_ = bf16[192,768]{1,0:T(8,128)(2,1)S(1)} collective-permute-done((bf16[192,768]{1,0:T(8,128)(2,1)}, bf16[192,768]{1,0:T(8,128)(2,1)S(1)}, u32[]{:S(2)}, u32[]{:S(2)}) %collective-permute-start.43) | collective-permute-done | bytes 294944 | tf_op jit(solution)/shard_map/ppermute | solution.py:49
  401.7 6.8 %collective-permute-done.44.rest_3_ = bf16[192,768]{1,0:T(8,128)(2,1)S(1)} collective-permute-done((bf16[192,768]{1,0:T(8,128)(2,1)}, bf16[192,768]{1,0:T(8,128)(2,1)S(1)}, u32[]{:S(2)}, u32[]{:S(2)}) %collective-permute-start.44) | collective-permute-done | bytes 294944 | tf_op jit(solution)/shard_map/ppermute | solution.py:49
  409.2 44.6 %attend_backward.1 = (bf16[192,3072]{1,0:T(8,128)(2,1)}, bf16[60,128,384]{2,1,0:T(8,128)(2,1)}) custom-call(s32[73]{0:T(128)} %pad_add_fusion.1.info, bf16[192,3072]{1,0:T(8,128)(2,1)} %get-tuple-element.119.query, f32[6,1,768]{2,1,0:T(1,128)} %get-tuple-element.120.lse_prompt, f32[12,1,384]{2,1,0:T(1,128)} %get-tuple-element.121.lse_cont, ...), custom_call_target="tpu_custom_call" | custom-call | flops 24159191040 | bytes 10000000 | tf_op jit(solution)/shard_map/attend_backward/pallas_call | solution.py:314
  453.9 7.9 %rows_remote.1 = (f32[3,768,768]{2,1,0:T(8,128)}, bf16[3,768,768]{2,1,0:T(8,128)(2,1)}) custom-call(bf16[60,128,384]{2,1,0:T(8,128)(2,1)} %get-tuple-element.127.grad_pairs, bf16[768,384]{1,0:T(8,128)(2,1)} %slice.235.pair_weight), custom_call_target="tpu_custom_call" | custom-call | tf_op jit(solution)/shard_map/rows_remote/pallas_call | solution.py:348
  463.7 7.7 %rows_local.1 = (f32[2,768,768]{2,1,0:T(8,128)}, bf16[2,768,768]{2,1,0:T(8,128)(2,1)}) custom-call(bf16[60,128,384]{2,1,0:T(8,128)(2,1)} %get-tuple-element.127.grad_pairs, bf16[192,3072]{1,0:T(8,128)(2,1)} %get-tuple-element.128.grad_query, bf16[768,192]{1,0:T(8,128)(2,1)} %get-tuple-element.199.query_weight, bf16[768,384]{1,0:T(8,128)(2,1)} %slice.235.pair_weight), custom_call_target="tpu_custom_call" | custom-call | tf_op jit(solution)/shard_map/rows_local/pallas_call | solution.py:368
  471.5 14.5 %qkv_grad.1 = bf16[768,576]{1,0:T(8,128)(2,1)} custom-call(bf16[192,3072]{1,0:T(8,128)(2,1)} %get-tuple-element.128.grad_query, bf16[60,128,384]{2,1,0:T(8,128)(2,1)} %get-tuple-element.127.grad_pairs, bf16[768,768]{1,0:T(8,128)(2,1)} %get-tuple-element.73.rest_0_, bf16[768,768]{1,0:T(8,128)(2,1)} %collective-permute-done.4.rest_1_, ...), custom_call_target="tpu_custom_call" | custom-call | tf_op jit(solution)/shard_map/qkv_grad/pallas_call | solution.py:407
  485.9 2.1 constant_dynamic-slice_fusion.3
  492.1 8.6 %collective-permute-done.55 = bf16[4,96,576]{2,1,0:T(8,128)(2,1)} collective-permute-done((bf16[4,96,576]{2,1,0:T(8,128)(2,1)}, bf16[4,96,576]{2,1,0:T(8,128)(2,1)}, u32[]{:S(2)}, u32[]{:S(2)}) %collective-permute-start.55) | collective-permute-done | bytes 442400 | tf_op jit(solution)/shard_map/ppermute | solution.py:49
  500.8 2.1 copy.174
  502.9 4.9 convert_add_fusion
  511.7 4.6 collective-permute-start.57
  517.2 4.3 collective-permute-done.50
  523.2 4.4 collective-permute-start.51
  530.3 4.2 collective-permute-done.49
  534.6 4.0 collective-permute-start.56
  539.5 2.6 fusion.8
  546.4 7.0 %collective-permute-start.61 = (bf16[96]{0:T(256)(128)(2,1)S(1)}, bf16[96]{0:T(256)(128)(2,1)S(1)}, u32[]{:S(2)}, u32[]{:S(2)}) collective-permute-start(bf16[96]{0:T(256)(128)(2,1)S(1)} %convert_element_type.200), channel_id=1, source_target_pairs={{0,3},{1,2},{2,1},{3,0},{4,7},{5,6},{6,5},{7,4},{8,11},{9,10},{10,... | collective-permute-start | bytes 584 | tf_op jit(solution)/shard_map/ppermute | solution.py:49
  554.7 3.6 collective-permute-start.59
  559.7 2.2 collective-permute-start.53
  561.9 2.2 fusion.3
  564.4 2.4 collective-permute-start.67
  568.1 6.6 %collective-permute-done.67 = bf16[96,201]{1,0:T(8,128)(2,1)S(1)} collective-permute-done((bf16[96,201]{1,0:T(8,128)(2,1)S(1)}, bf16[96,201]{1,0:T(8,128)(2,1)S(1)}, u32[]{:S(2)}, u32[]{:S(2)}) %collective-permute-start.67) | collective-permute-done | bytes 38624 | tf_op jit(solution)/shard_map/ppermute | solution.py:49
  574.7 6.5 %collective-permute-done.66 = bf16[96,201]{1,0:T(8,128)(2,1)S(1)} collective-permute-done((bf16[96,201]{1,0:T(8,128)(2,1)S(1)}, bf16[96,201]{1,0:T(8,128)(2,1)S(1)}, u32[]{:S(2)}, u32[]{:S(2)}) %collective-permute-start.66) | collective-permute-done | bytes 38624 | tf_op jit(solution)/shard_map/ppermute | solution.py:49
  581.3 1.6 collective-permute-start.70
  585.5 8.6 %collective-permute-done.70 = bf16[96,9]{1,0:T(8,128)(2,1)S(1)} collective-permute-done((bf16[96,9]{1,0:T(8,128)(2,1)S(1)}, bf16[96,9]{1,0:T(8,128)(2,1)S(1)}, u32[]{:S(2)}, u32[]{:S(2)}) %collective-permute-start.70) | collective-permute-done | bytes 1760 | tf_op jit(solution)/shard_map/ppermute | solution.py:49
  595.6 8.7 %collective-permute-done.54.far = bf16[384,768]{1,0:T(8,128)(2,1)} collective-permute-done((bf16[384,768]{1,0:T(8,128)(2,1)S(1)}, bf16[384,768]{1,0:T(8,128)(2,1)}, u32[]{:S(2)}, u32[]{:S(2)}) %collective-permute-start.54) | collective-permute-done | bytes 589856 | tf_op jit(solution)/shard_map/ppermute | solution.py:49
  604.3 6.6 %final_rows.1 = f32[768,768]{1,0:T(8,128)} custom-call(s32[1]{0:T(128)} %bitcast.26.first, bf16[768,768]{1,0:T(8,128)(2,1)} %tokens.5, f32[2,768]{1,0:T(2,128)} %gains.5, f32[768,768]{1,0:T(8,128)} %get-tuple-element.118.grad_middle, f32[2,768,768]{2,1,0:T(8,128)} %get-tuple-element.129.kept, bf16[2,768,768]{2,1,0:T(8,128)(2,1)} %collective-permute-done.45.beside, ...), custom_call_target="tpu_custom_call" | custom-call | tf_op jit(solution)/shard_map/final_rows/pallas_call | solution.py:430
  610.9 1.4 convert_bitcast_fusion
  612.3 2.0 copy.180
  614.3 2.8 bitcast_convert_fusion
  (321 shorter events, 88.3 us)
Async XLA Ops:
  7.2 276.1 %all-gather.3.cloned.1.call-start = ((), (), s32[]{:S(2)}) async-start(), calls=%async_computation.2 | async-start | bytes 5898240 | tf_op jit(solution)/shard_map/all_gather | solution.py:773
  7.9 275.4 %all-gather.5.cloned.1.call-start = ((), (), s32[]{:S(2)}) async-start(), calls=%async_computation.3 | async-start | bytes 5898240 | tf_op jit(solution)/shard_map/all_gather | solution.py:785
  10.9 14.5 %collective-permute-start.6 = (bf16[384,768]{1,0:T(8,128)(2,1)}, bf16[384,768]{1,0:T(8,128)(2,1)S(1)}, u32[]{:S(2)}, u32[]{:S(2)}) collective-permute-start(bf16[384,768]{1,0:T(8,128)(2,1)} %get-tuple-element.74), channel_id=1, source_target_pairs={{0,2},{1,3},{2,0},{3,1},{4,6},{5,7},{6,4},{7,5},{8,10},{9,11},{10,... | collective-permute-start | bytes 1769480 | tf_op jit(solution)/shard_map/ppermute | solution.py:49
  12.3 15.4 %collective-permute-start.2 = (bf16[96,776]{0,1:T(8,128)(2,1)S(1)}, bf16[96,776]{0,1:T(8,128)(2,1)S(1)}, u32[]{:S(2)}, u32[]{:S(2)}) collective-permute-start(bf16[96,776]{0,1:T(8,128)(2,1)S(1)} %get-tuple-element.236), channel_id=1, source_target_pairs={{0,12},{4,8},{8,4},{12,0},{1,13},{5,9},{9,5},{13,1},{2,14},{6,10},... | collective-permute-start | bytes 446984 | tf_op jit(solution)/shard_map/ppermute | solution.py:49
  12.4 29.5 %collective-permute-start.1 = (bf16[96,776]{0,1:T(8,128)(2,1)S(1)}, bf16[96,776]{0,1:T(8,128)(2,1)S(1)}, u32[]{:S(2)}, u32[]{:S(2)}) collective-permute-start(bf16[96,776]{0,1:T(8,128)(2,1)S(1)} %get-tuple-element.236), channel_id=1, source_target_pairs={{0,8},{4,12},{8,0},{12,4},{1,9},{5,13},{9,1},{13,5},{2,10},{6,14},... | collective-permute-start | bytes 446984 | tf_op jit(solution)/shard_map/ppermute | solution.py:49
  13.8 28.2 %collective-permute-start = (bf16[96,776]{0,1:T(8,128)(2,1)S(1)}, bf16[96,776]{0,1:T(8,128)(2,1)S(1)}, u32[]{:S(2)}, u32[]{:S(2)}) collective-permute-start(bf16[96,776]{0,1:T(8,128)(2,1)S(1)} %get-tuple-element.236), channel_id=1, source_target_pairs={{0,4},{4,0},{8,12},{12,8},{1,5},{5,1},{9,13},{13,9},{2,6},{6,2},{1... | collective-permute-start | bytes 446984 | tf_op jit(solution)/shard_map/ppermute | solution.py:49
  27.8 47.2 %collective-permute-start.9 = (bf16[384,768]{1,0:T(8,128)(2,1)}, bf16[384,768]{1,0:T(8,128)(2,1)}, u32[]{:S(2)}, u32[]{:S(2)}) collective-permute-start(bf16[384,768]{1,0:T(8,128)(2,1)} %get-tuple-element.200), channel_id=1, source_target_pairs={{0,4},{4,8},{8,12},{12,0},{1,5},{5,9},{9,13},{13,1},{2,6},{6,10},{... | collective-permute-start | bytes 1769480 | tf_op jit(solution)/shard_map/ppermute | solution.py:53
  42.6 34.7 %collective-permute-start.3 = (bf16[1,4,96,776]{3,2,1,0:T(8,128)(2,1)S(1)}, bf16[1,4,96,776]{3,2,1,0:T(8,128)(2,1)}, u32[]{:S(2)}, u32[]{:S(2)}) collective-permute-start(bf16[1,4,96,776]{3,2,1,0:T(8,128)(2,1)S(1)} %copy.153), channel_id=1, source_target_pairs={{0,16},{16,0},{1,17},{17,1},{2,18},{18,2},{3,19},{19,3},{4,20},{20... | collective-permute-start | bytes 1787912 | tf_op jit(solution)/shard_map/ppermute | solution.py:49
  74.9 42.6 %collective-permute-start.13 = (bf16[384,768]{1,0:T(8,128)(2,1)}, bf16[384,768]{1,0:T(8,128)(2,1)}, u32[]{:S(2)}, u32[]{:S(2)}) collective-permute-start(bf16[384,768]{1,0:T(8,128)(2,1)} %collective-permute-done.9.rest_6_), channel_id=1, source_target_pairs={{0,4},{4,8},{8,12},{12,0},{1,5},{5,9},{9,13},{13,1},{2,6},{6,10},{... | collective-permute-start | bytes 1769480 | tf_op jit(solution)/shard_map/ppermute | solution.py:53
  74.9 86.0 %collective-permute-start.4 = (bf16[768,768]{1,0:T(8,128)(2,1)S(1)}, bf16[768,768]{1,0:T(8,128)(2,1)}, u32[]{:S(2)}, u32[]{:S(2)}) collective-permute-start(bf16[768,768]{1,0:T(8,128)(2,1)S(1)} %copy-done.1), channel_id=1, source_target_pairs={{0,1},{1,0},{2,3},{3,2},{4,5},{5,4},{6,7},{7,6},{8,9},{9,8},{10,11... | collective-permute-start | bytes 3538952 | tf_op jit(solution)/shard_map/ppermute | solution.py:49
  76.2 84.6 %collective-permute-start.5 = (bf16[384,768]{1,0:T(8,128)(2,1)}, bf16[384,768]{1,0:T(8,128)(2,1)}, u32[]{:S(2)}, u32[]{:S(2)}) collective-permute-start(bf16[384,768]{1,0:T(8,128)(2,1)} %get-tuple-element.201), channel_id=1, source_target_pairs={{0,2},{1,3},{2,0},{3,1},{4,6},{5,7},{6,4},{7,5},{8,10},{9,11},{10,... | collective-permute-start | bytes 1769480 | tf_op jit(solution)/shard_map/ppermute | solution.py:49
  76.9 84.2 %collective-permute-start.8 = (bf16[384,768]{1,0:T(8,128)(2,1)S(1)}, bf16[384,768]{1,0:T(8,128)(2,1)}, u32[]{:S(2)}, u32[]{:S(2)}) collective-permute-start(bf16[384,768]{1,0:T(8,128)(2,1)S(1)} %collective-permute-done.6.rest_3_), channel_id=1, source_target_pairs={{0,1},{1,0},{2,3},{3,2},{4,5},{5,4},{6,7},{7,6},{8,9},{9,8},{10,11... | collective-permute-start | bytes 1769480 | tf_op jit(solution)/shard_map/ppermute | solution.py:49
  117.5 21.9 %collective-permute-start.17 = (bf16[384,768]{1,0:T(8,128)(2,1)}, bf16[384,768]{1,0:T(8,128)(2,1)}, u32[]{:S(2)}, u32[]{:S(2)}) collective-permute-start(bf16[384,768]{1,0:T(8,128)(2,1)} %collective-permute-done.13.rest_10_), channel_id=1, source_target_pairs={{0,4},{4,8},{8,12},{12,0},{1,5},{5,9},{9,13},{13,1},{2,6},{6,10},{... | collective-permute-start | bytes 1769480 | tf_op jit(solution)/shard_map/ppermute | solution.py:53
  139.4 471.5 %reduce-scatter.5.cloned.1.call-start = ((), (), s32[]{:S(2)}) async-start(), calls=%async_computation.5 | async-start | bytes 5898240 | tf_op jit(solution)/shard_map/reduce_scatter | solution.py:869
  145.4 18.6 %collective-permute-start.10 = (bf16[384,768]{1,0:T(8,128)(2,1)}, bf16[384,768]{1,0:T(8,128)(2,1)}, u32[]{:S(2)}, u32[]{:S(2)}) collective-permute-start(bf16[384,768]{1,0:T(8,128)(2,1)} %collective-permute-done.9.rest_6_), channel_id=1, source_target_pairs={{0,2},{1,3},{2,0},{3,1},{4,6},{5,7},{6,4},{7,5},{8,10},{9,11},{10,... | collective-permute-start | bytes 1769480 | tf_op jit(solution)/shard_map/ppermute | solution.py:49
  150.7 21.6 %collective-permute-start.11 = (bf16[384,768]{1,0:T(8,128)(2,1)}, bf16[384,768]{1,0:T(8,128)(2,1)}, u32[]{:S(2)}, u32[]{:S(2)}) collective-permute-start(bf16[384,768]{1,0:T(8,128)(2,1)} %collective-permute-done.9.rest_6_), channel_id=1, source_target_pairs={{0,1},{1,0},{2,3},{3,2},{4,5},{5,4},{6,7},{7,6},{8,9},{9,8},{10,11... | collective-permute-start | bytes 1769480 | tf_op jit(solution)/shard_map/ppermute | solution.py:49
  160.9 15.7 %collective-permute-start.14 = (bf16[384,768]{1,0:T(8,128)(2,1)}, bf16[384,768]{1,0:T(8,128)(2,1)}, u32[]{:S(2)}, u32[]{:S(2)}) collective-permute-start(bf16[384,768]{1,0:T(8,128)(2,1)} %collective-permute-done.13.rest_10_), channel_id=1, source_target_pairs={{0,2},{1,3},{2,0},{3,1},{4,6},{5,7},{6,4},{7,5},{8,10},{9,11},{10,... | collective-permute-start | bytes 1769480 | tf_op jit(solution)/shard_map/ppermute | solution.py:49
  161.2 28.1 %collective-permute-start.18 = (bf16[384,768]{1,0:T(8,128)(2,1)}, bf16[384,768]{1,0:T(8,128)(2,1)}, u32[]{:S(2)}, u32[]{:S(2)}) collective-permute-start(bf16[384,768]{1,0:T(8,128)(2,1)} %collective-permute-done.17.rest_14_), channel_id=1, source_target_pairs={{0,2},{1,3},{2,0},{3,1},{4,6},{5,7},{6,4},{7,5},{8,10},{9,11},{10,... | collective-permute-start | bytes 1769480 | tf_op jit(solution)/shard_map/ppermute | solution.py:49
  163.6 33.1 %collective-permute-start.15 = (bf16[384,768]{1,0:T(8,128)(2,1)}, bf16[384,768]{1,0:T(8,128)(2,1)}, u32[]{:S(2)}, u32[]{:S(2)}) collective-permute-start(bf16[384,768]{1,0:T(8,128)(2,1)} %collective-permute-done.13.rest_10_), channel_id=1, source_target_pairs={{0,1},{1,0},{2,3},{3,2},{4,5},{5,4},{6,7},{7,6},{8,9},{9,8},{10,11... | collective-permute-start | bytes 1769480 | tf_op jit(solution)/shard_map/ppermute | solution.py:49
  164.0 32.6 %collective-permute-start.12 = (bf16[384,768]{1,0:T(8,128)(2,1)}, bf16[384,768]{1,0:T(8,128)(2,1)}, u32[]{:S(2)}, u32[]{:S(2)}) collective-permute-start(bf16[384,768]{1,0:T(8,128)(2,1)} %collective-permute-done.10.rest_7_), channel_id=1, source_target_pairs={{0,1},{1,0},{2,3},{3,2},{4,5},{5,4},{6,7},{7,6},{8,9},{9,8},{10,11... | collective-permute-start | bytes 1769480 | tf_op jit(solution)/shard_map/ppermute | solution.py:49
  172.3 24.4 %collective-permute-start.19 = (bf16[384,768]{1,0:T(8,128)(2,1)}, bf16[384,768]{1,0:T(8,128)(2,1)}, u32[]{:S(2)}, u32[]{:S(2)}) collective-permute-start(bf16[384,768]{1,0:T(8,128)(2,1)} %collective-permute-done.17.rest_14_), channel_id=1, source_target_pairs={{0,1},{1,0},{2,3},{3,2},{4,5},{5,4},{6,7},{7,6},{8,9},{9,8},{10,11... | collective-permute-start | bytes 1769480 | tf_op jit(solution)/shard_map/ppermute | solution.py:49
  176.6 20.1 %collective-permute-start.16 = (bf16[384,768]{1,0:T(8,128)(2,1)}, bf16[384,768]{1,0:T(8,128)(2,1)}, u32[]{:S(2)}, u32[]{:S(2)}) collective-permute-start(bf16[384,768]{1,0:T(8,128)(2,1)} %collective-permute-done.14.rest_11_), channel_id=1, source_target_pairs={{0,1},{1,0},{2,3},{3,2},{4,5},{5,4},{6,7},{7,6},{8,9},{9,8},{10,11... | collective-permute-start | bytes 1769480 | tf_op jit(solution)/shard_map/ppermute | solution.py:49
  196.6 43.6 %collective-permute-start.25 = (bf16[2,192,768]{2,1,0:T(8,128)(2,1)S(1)}, bf16[2,192,768]{2,1,0:T(8,128)(2,1)S(1)}, u32[]{:S(2)}, u32[]{:S(2)}) collective-permute-start(bf16[2,192,768]{2,1,0:T(8,128)(2,1)S(1)} %copy.164), channel_id=1, source_target_pairs={{0,1},{1,0},{2,3},{3,2},{4,5},{5,4},{6,7},{7,6},{8,9},{9,8},{10,11... | collective-permute-start | bytes 1769480 | tf_op jit(solution)/shard_map/ppermute | solution.py:49
  233.8 14.9 %collective-permute-start.23 = (bf16[192,768]{1,0:T(8,128)(2,1)}, bf16[192,768]{1,0:T(8,128)(2,1)S(1)}, u32[]{:S(2)}, u32[]{:S(2)}) collective-permute-start(bf16[192,768]{1,0:T(8,128)(2,1)} %get-tuple-element.78), channel_id=1, source_target_pairs={{0,3},{1,2},{2,1},{3,0},{4,7},{5,6},{6,5},{7,4},{8,11},{9,10},{10,... | collective-permute-start | bytes 884744 | tf_op jit(solution)/shard_map/ppermute | solution.py:49
  260.6 10.0 %collective-permute-start.27 = (bf16[240,768]{1,0:T(8,128)(2,1)S(1)}, bf16[240,768]{1,0:T(8,128)(2,1)S(1)}, u32[]{:S(2)}, u32[]{:S(2)}) collective-permute-start(bf16[240,768]{1,0:T(8,128)(2,1)S(1)} %pad_maximum_fusion.2), channel_id=1, source_target_pairs={{0,2},{1,3},{2,0},{3,1},{16,18},{17,19},{18,16},{19,17},{4,6},{5,7... | collective-permute-start | bytes 1105928 | tf_op jit(solution)/shard_map/ppermute | solution.py:49
  261.0 9.7 %collective-permute-start.28 = (bf16[240,768]{1,0:T(8,128)(2,1)S(1)}, bf16[240,768]{1,0:T(8,128)(2,1)S(1)}, u32[]{:S(2)}, u32[]{:S(2)}) collective-permute-start(bf16[240,768]{1,0:T(8,128)(2,1)S(1)} %pad_maximum_fusion.3), channel_id=1, source_target_pairs={{0,16},{1,17},{2,18},{3,19},{16,0},{17,1},{18,2},{19,3},{4,20},{5,... | collective-permute-start | bytes 1105928 | tf_op jit(solution)/shard_map/ppermute | solution.py:49
  262.4 17.2 %collective-permute-start.29 = (bf16[240,768]{1,0:T(8,128)(2,1)S(1)}, bf16[240,768]{1,0:T(8,128)(2,1)S(1)}, u32[]{:S(2)}, u32[]{:S(2)}) collective-permute-start(bf16[240,768]{1,0:T(8,128)(2,1)S(1)} %pad_maximum_fusion.4), channel_id=1, source_target_pairs={{0,18},{1,19},{2,16},{3,17},{16,2},{17,3},{18,0},{19,1},{4,22},{5,... | collective-permute-start | bytes 1105928 | tf_op jit(solution)/shard_map/ppermute | solution.py:49
  280.4 19.6 %collective-permute-start.31 = (bf16[240,768]{1,0:T(8,128)(2,1)S(1)}, bf16[240,768]{1,0:T(8,128)(2,1)S(1)}, u32[]{:S(2)}, u32[]{:S(2)}) collective-permute-start(bf16[240,768]{1,0:T(8,128)(2,1)S(1)} %pad_maximum_fusion.5), channel_id=1, source_target_pairs={{0,2},{1,3},{2,0},{3,1},{16,18},{17,19},{18,16},{19,17},{4,6},{5,7... | collective-permute-start | bytes 1105928 | tf_op jit(solution)/shard_map/ppermute | solution.py:49
  280.9 19.2 %collective-permute-start.32 = (bf16[240,768]{1,0:T(8,128)(2,1)S(1)}, bf16[240,768]{1,0:T(8,128)(2,1)S(1)}, u32[]{:S(2)}, u32[]{:S(2)}) collective-permute-start(bf16[240,768]{1,0:T(8,128)(2,1)S(1)} %pad_maximum_fusion.6), channel_id=1, source_target_pairs={{0,16},{1,17},{2,18},{3,19},{16,0},{17,1},{18,2},{19,3},{4,20},{5,... | collective-permute-start | bytes 1105928 | tf_op jit(solution)/shard_map/ppermute | solution.py:49
  282.9 17.1 %collective-permute-start.33 = (bf16[240,768]{1,0:T(8,128)(2,1)S(1)}, bf16[240,768]{1,0:T(8,128)(2,1)S(1)}, u32[]{:S(2)}, u32[]{:S(2)}) collective-permute-start(bf16[240,768]{1,0:T(8,128)(2,1)S(1)} %pad_maximum_fusion.7), channel_id=1, source_target_pairs={{0,18},{1,19},{2,16},{3,17},{16,2},{17,3},{18,0},{19,1},{4,22},{5,... | collective-permute-start | bytes 1105928 | tf_op jit(solution)/shard_map/ppermute | solution.py:49
  333.4 280.9 %reduce-scatter.3.cloned.1.call-start = ((), (), s32[]{:S(2)}) async-start(), calls=%async_computation.4 | async-start | bytes 5898240 | tf_op jit(solution)/shard_map/reduce_scatter | solution.py:868
  334.6 9.9 %collective-permute-start.35 = (bf16[240,768]{1,0:T(8,128)(2,1)S(1)}, bf16[240,768]{1,0:T(8,128)(2,1)S(1)}, u32[]{:S(2)}, u32[]{:S(2)}) collective-permute-start(bf16[240,768]{1,0:T(8,128)(2,1)S(1)} %pad_maximum_fusion.8), channel_id=1, source_target_pairs={{0,2},{1,3},{2,0},{3,1},{16,18},{17,19},{18,16},{19,17},{4,6},{5,7... | collective-permute-start | bytes 1105928 | tf_op jit(solution)/shard_map/ppermute | solution.py:49
  336.0 9.6 %collective-permute-start.36 = (bf16[240,768]{1,0:T(8,128)(2,1)S(1)}, bf16[240,768]{1,0:T(8,128)(2,1)S(1)}, u32[]{:S(2)}, u32[]{:S(2)}) collective-permute-start(bf16[240,768]{1,0:T(8,128)(2,1)S(1)} %pad_maximum_fusion.9), channel_id=1, source_target_pairs={{0,16},{1,17},{2,18},{3,19},{16,0},{17,1},{18,2},{19,3},{4,20},{5,... | collective-permute-start | bytes 1105928 | tf_op jit(solution)/shard_map/ppermute | solution.py:49
  337.4 16.1 %collective-permute-start.37 = (bf16[240,768]{1,0:T(8,128)(2,1)S(1)}, bf16[240,768]{1,0:T(8,128)(2,1)S(1)}, u32[]{:S(2)}, u32[]{:S(2)}) collective-permute-start(bf16[240,768]{1,0:T(8,128)(2,1)S(1)} %pad_maximum_fusion.10), channel_id=1, source_target_pairs={{0,18},{1,19},{2,16},{3,17},{16,2},{17,3},{18,0},{19,1},{4,22},{5,... | collective-permute-start | bytes 1105928 | tf_op jit(solution)/shard_map/ppermute | solution.py:49
  357.0 10.0 %collective-permute-start.39 = (bf16[240,768]{1,0:T(8,128)(2,1)S(1)}, bf16[240,768]{1,0:T(8,128)(2,1)S(1)}, u32[]{:S(2)}, u32[]{:S(2)}) collective-permute-start(bf16[240,768]{1,0:T(8,128)(2,1)S(1)} %pad_maximum_fusion.11), channel_id=1, source_target_pairs={{0,2},{1,3},{2,0},{3,1},{16,18},{17,19},{18,16},{19,17},{4,6},{5,7... | collective-permute-start | bytes 1105928 | tf_op jit(solution)/shard_map/ppermute | solution.py:49
  357.9 9.6 %collective-permute-start.40 = (bf16[240,768]{1,0:T(8,128)(2,1)S(1)}, bf16[240,768]{1,0:T(8,128)(2,1)S(1)}, u32[]{:S(2)}, u32[]{:S(2)}) collective-permute-start(bf16[240,768]{1,0:T(8,128)(2,1)S(1)} %pad_maximum_fusion.12), channel_id=1, source_target_pairs={{0,16},{1,17},{2,18},{3,19},{16,0},{17,1},{18,2},{19,3},{4,20},{5,... | collective-permute-start | bytes 1105928 | tf_op jit(solution)/shard_map/ppermute | solution.py:49
  358.8 17.1 %collective-permute-start.41 = (bf16[240,768]{1,0:T(8,128)(2,1)S(1)}, bf16[240,768]{1,0:T(8,128)(2,1)S(1)}, u32[]{:S(2)}, u32[]{:S(2)}) collective-permute-start(bf16[240,768]{1,0:T(8,128)(2,1)S(1)} %pad_maximum_fusion.13), channel_id=1, source_target_pairs={{0,18},{1,19},{2,16},{3,17},{16,2},{17,3},{18,0},{19,1},{4,22},{5,... | collective-permute-start | bytes 1105928 | tf_op jit(solution)/shard_map/ppermute | solution.py:49
  393.6 14.9 %collective-permute-start.44 = (bf16[192,768]{1,0:T(8,128)(2,1)}, bf16[192,768]{1,0:T(8,128)(2,1)S(1)}, u32[]{:S(2)}, u32[]{:S(2)}) collective-permute-start(bf16[192,768]{1,0:T(8,128)(2,1)} %get-tuple-element.126), channel_id=1, source_target_pairs={{0,3},{1,2},{2,1},{3,0},{4,7},{5,6},{6,5},{7,4},{8,11},{9,10},{10,... | collective-permute-start | bytes 884744 | tf_op jit(solution)/shard_map/ppermute | solution.py:49
  461.8 41.1 %collective-permute-start.47 = (bf16[3,768,768]{2,1,0:T(8,128)(2,1)}, bf16[3,768,768]{2,1,0:T(8,128)(2,1)}, u32[]{:S(2)}, u32[]{:S(2)}) collective-permute-start(bf16[3,768,768]{2,1,0:T(8,128)(2,1)} %get-tuple-element.132), channel_id=1, source_target_pairs={{0,1},{1,0},{2,3},{3,2},{4,5},{5,4},{6,7},{7,6},{8,9},{9,8},{10,11... | collective-permute-start | bytes 10616840 | tf_op jit(solution)/shard_map/ppermute | solution.py:49
  461.8 28.2 %collective-permute-start.62 = (bf16[2,192,768]{2,1,0:T(8,128)(2,1)S(1)}, bf16[2,192,768]{2,1,0:T(8,128)(2,1)S(1)}, u32[]{:S(2)}, u32[]{:S(2)}) collective-permute-start(bf16[2,192,768]{2,1,0:T(8,128)(2,1)S(1)} %copy-done.43), channel_id=1, source_target_pairs={{0,1},{1,0},{2,3},{3,2},{4,5},{5,4},{6,7},{7,6},{8,9},{9,8},{10,11... | collective-permute-start | bytes 1769480 | tf_op jit(solution)/shard_map/ppermute | solution.py:49
  471.4 90.5 %collective-permute-start.45 = (bf16[2,768,768]{2,1,0:T(8,128)(2,1)}, bf16[2,768,768]{2,1,0:T(8,128)(2,1)}, u32[]{:S(2)}, u32[]{:S(2)}) collective-permute-start(bf16[2,768,768]{2,1,0:T(8,128)(2,1)} %get-tuple-element.130), channel_id=1, source_target_pairs={{0,1},{1,0},{2,3},{3,2},{4,5},{5,4},{6,7},{7,6},{8,9},{9,8},{10,11... | collective-permute-start | bytes 7077896 | tf_op jit(solution)/shard_map/ppermute | solution.py:49
  488.1 12.7 %collective-permute-start.55 = (bf16[4,96,576]{2,1,0:T(8,128)(2,1)}, bf16[4,96,576]{2,1,0:T(8,128)(2,1)}, u32[]{:S(2)}, u32[]{:S(2)}) collective-permute-start(bf16[4,96,576]{2,1,0:T(8,128)(2,1)} %get-tuple-element.203), channel_id=1, source_target_pairs={{0,16},{16,0},{1,17},{17,1},{2,18},{18,2},{3,19},{19,3},{4,20},{20... | collective-permute-start | bytes 1327112 | tf_op jit(solution)/shard_map/ppermute | solution.py:49
  490.9 32.3 %collective-permute-start.63 = (bf16[192,768]{1,0:T(8,128)(2,1)}, bf16[192,768]{1,0:T(8,128)(2,1)}, u32[]{:S(2)}, u32[]{:S(2)}) collective-permute-start(bf16[192,768]{1,0:T(8,128)(2,1)} %fusion.24), channel_id=1, source_target_pairs={{0,2},{1,3},{2,0},{3,1},{4,6},{5,7},{6,4},{7,5},{8,10},{9,11},{10,... | collective-permute-start | bytes 884744 | tf_op jit(solution)/shard_map/ppermute | solution.py:49
  507.9 13.7 %collective-permute-start.50 = (bf16[384,768]{1,0:T(8,128)(2,1)S(1)}, bf16[384,768]{1,0:T(8,128)(2,1)S(1)}, u32[]{:S(2)}, u32[]{:S(2)}) collective-permute-start(bf16[384,768]{1,0:T(8,128)(2,1)S(1)} %fusion.20), channel_id=1, source_target_pairs={{0,2},{1,3},{2,0},{3,1},{4,6},{5,7},{6,4},{7,5},{8,10},{9,11},{10,... | collective-permute-start | bytes 1769480 | tf_op jit(solution)/shard_map/ppermute | solution.py:49
  510.9 31.3 %collective-permute-start.58 = (bf16[96,576]{0,1:T(8,128)(2,1)}, bf16[96,576]{0,1:T(8,128)(2,1)}, u32[]{:S(2)}, u32[]{:S(2)}) collective-permute-start(bf16[96,576]{0,1:T(8,128)(2,1)} %get-tuple-element.229), channel_id=1, source_target_pairs={{0,12},{4,8},{8,4},{12,0},{1,13},{5,9},{9,5},{13,1},{2,14},{6,10},... | collective-permute-start | bytes 331784 | tf_op jit(solution)/shard_map/ppermute | solution.py:49
  511.7 31.7 %collective-permute-start.57 = (bf16[96,576]{0,1:T(8,128)(2,1)}, bf16[96,576]{0,1:T(8,128)(2,1)}, u32[]{:S(2)}, u32[]{:S(2)}) collective-permute-start(bf16[96,576]{0,1:T(8,128)(2,1)} %get-tuple-element.230), channel_id=1, source_target_pairs={{0,8},{4,12},{8,0},{12,4},{1,9},{5,13},{9,1},{13,5},{2,10},{6,14},... | collective-permute-start | bytes 331784 | tf_op jit(solution)/shard_map/ppermute | solution.py:49
  521.5 13.0 %collective-permute-start.49 = (bf16[384,768]{1,0:T(8,128)(2,1)}, bf16[384,768]{1,0:T(8,128)(2,1)}, u32[]{:S(2)}, u32[]{:S(2)}) collective-permute-start(bf16[384,768]{1,0:T(8,128)(2,1)} %fusion.19), channel_id=1, source_target_pairs={{0,2},{1,3},{2,0},{3,1},{4,6},{5,7},{6,4},{7,5},{8,10},{9,11},{10,... | collective-permute-start | bytes 1769480 | tf_op jit(solution)/shard_map/ppermute | solution.py:49
  523.2 15.4 %collective-permute-start.51 = (bf16[384,768]{1,0:T(8,128)(2,1)}, bf16[384,768]{1,0:T(8,128)(2,1)}, u32[]{:S(2)}, u32[]{:S(2)}) collective-permute-start(bf16[384,768]{1,0:T(8,128)(2,1)} %fusion.5), channel_id=1, source_target_pairs={{0,12},{4,0},{8,4},{12,8},{1,13},{5,1},{9,5},{13,9},{2,14},{6,2},{... | collective-permute-start | bytes 1769480 | tf_op jit(solution)/shard_map/ppermute | solution.py:53
  534.6 9.8 %collective-permute-start.56 = (bf16[96,576]{0,1:T(8,128)(2,1)S(1)}, bf16[96,576]{0,1:T(8,128)(2,1)S(1)}, u32[]{:S(2)}, u32[]{:S(2)}) collective-permute-start(bf16[96,576]{0,1:T(8,128)(2,1)S(1)} %copy-done.34), channel_id=1, source_target_pairs={{0,4},{4,0},{8,12},{12,8},{1,5},{5,1},{9,13},{13,9},{2,6},{6,2},{1... | collective-permute-start | bytes 331784 | tf_op jit(solution)/shard_map/ppermute | solution.py:49
  538.6 15.0 %collective-permute-start.64 = (bf16[4,96,201]{2,1,0:T(8,128)(2,1)S(1)}, bf16[4,96,201]{2,1,0:T(8,128)(2,1)}, u32[]{:S(2)}, u32[]{:S(2)}) collective-permute-start(bf16[4,96,201]{2,1,0:T(8,128)(2,1)S(1)} %bitcast.145), channel_id=1, source_target_pairs={{0,16},{16,0},{1,17},{17,1},{2,18},{18,2},{3,19},{19,3},{4,20},{20... | collective-permute-start | bytes 463112 | tf_op jit(solution)/shard_map/ppermute | solution.py:49
  542.2 12.5 %collective-permute-start.48 = (bf16[384,768]{1,0:T(8,128)(2,1)}, bf16[384,768]{1,0:T(8,128)(2,1)}, u32[]{:S(2)}, u32[]{:S(2)}) collective-permute-start(bf16[384,768]{1,0:T(8,128)(2,1)} %fusion.18), channel_id=1, source_target_pairs={{0,2},{1,3},{2,0},{3,1},{4,6},{5,7},{6,4},{7,5},{8,10},{9,11},{10,... | collective-permute-start | bytes 1769480 | tf_op jit(solution)/shard_map/ppermute | solution.py:49
  543.4 14.8 %collective-permute-start.52 = (bf16[384,768]{1,0:T(8,128)(2,1)}, bf16[384,768]{1,0:T(8,128)(2,1)}, u32[]{:S(2)}, u32[]{:S(2)}) collective-permute-start(bf16[384,768]{1,0:T(8,128)(2,1)} %fusion.8), channel_id=1, source_target_pairs={{0,12},{4,0},{8,4},{12,8},{1,13},{5,1},{9,5},{13,9},{2,14},{6,2},{... | collective-permute-start | bytes 1769480 | tf_op jit(solution)/shard_map/ppermute | solution.py:53
  546.4 18.0 %collective-permute-start.61 = (bf16[96]{0:T(256)(128)(2,1)S(1)}, bf16[96]{0:T(256)(128)(2,1)S(1)}, u32[]{:S(2)}, u32[]{:S(2)}) collective-permute-start(bf16[96]{0:T(256)(128)(2,1)S(1)} %convert_element_type.200), channel_id=1, source_target_pairs={{0,3},{1,2},{2,1},{3,0},{4,7},{5,6},{6,5},{7,4},{8,11},{9,10},{10,... | collective-permute-start | bytes 584 | tf_op jit(solution)/shard_map/ppermute | solution.py:49
  553.6 13.2 %collective-permute-start.60 = (bf16[96]{0:T(256)(128)(2,1)S(1)}, bf16[96]{0:T(256)(128)(2,1)S(1)}, u32[]{:S(2)}, u32[]{:S(2)}) collective-permute-start(bf16[96]{0:T(256)(128)(2,1)S(1)} %convert_element_type.200), channel_id=1, source_target_pairs={{0,2},{1,3},{2,0},{3,1},{4,6},{5,7},{6,4},{7,5},{8,10},{9,11},{10,... | collective-permute-start | bytes 584 | tf_op jit(solution)/shard_map/ppermute | solution.py:49
  554.7 12.2 %collective-permute-start.59 = (bf16[96]{0:T(256)(128)(2,1)S(1)}, bf16[96]{0:T(256)(128)(2,1)S(1)}, u32[]{:S(2)}, u32[]{:S(2)}) collective-permute-start(bf16[96]{0:T(256)(128)(2,1)S(1)} %convert_element_type.200), channel_id=1, source_target_pairs={{0,1},{1,0},{2,3},{3,2},{4,5},{5,4},{6,7},{7,6},{8,9},{9,8},{10,11... | collective-permute-start | bytes 584 | tf_op jit(solution)/shard_map/ppermute | solution.py:49
  559.7 23.8 %collective-permute-start.53 = (bf16[384,768]{1,0:T(8,128)(2,1)S(1)}, bf16[384,768]{1,0:T(8,128)(2,1)S(1)}, u32[]{:S(2)}, u32[]{:S(2)}) collective-permute-start(bf16[384,768]{1,0:T(8,128)(2,1)S(1)} %fusion.11), channel_id=1, source_target_pairs={{0,12},{4,0},{8,4},{12,8},{1,13},{5,1},{9,5},{13,9},{2,14},{6,2},{... | collective-permute-start | bytes 1769480 | tf_op jit(solution)/shard_map/ppermute | solution.py:53
  564.1 31.5 %collective-permute-start.46 = (bf16[768,768]{1,0:T(8,128)(2,1)S(1)}, bf16[768,768]{1,0:T(8,128)(2,1)S(1)}, u32[]{:S(2)}, u32[]{:S(2)}) collective-permute-start(bf16[768,768]{1,0:T(8,128)(2,1)S(1)} %fusion.3), channel_id=1, source_target_pairs={{0,2},{1,3},{2,0},{3,1},{4,6},{5,7},{6,4},{7,5},{8,10},{9,11},{10,... | collective-permute-start | bytes 3538952 | tf_op jit(solution)/shard_map/ppermute | solution.py:49
  564.4 10.3 %collective-permute-start.67 = (bf16[96,201]{1,0:T(8,128)(2,1)S(1)}, bf16[96,201]{1,0:T(8,128)(2,1)S(1)}, u32[]{:S(2)}, u32[]{:S(2)}) collective-permute-start(bf16[96,201]{1,0:T(8,128)(2,1)S(1)} %get-tuple-element.238), channel_id=1, source_target_pairs={{0,12},{4,8},{8,4},{12,0},{1,13},{5,9},{9,5},{13,1},{2,14},{6,10},... | collective-permute-start | bytes 115784 | tf_op jit(solution)/shard_map/ppermute | solution.py:49
  566.9 14.3 %collective-permute-start.66 = (bf16[96,201]{1,0:T(8,128)(2,1)S(1)}, bf16[96,201]{1,0:T(8,128)(2,1)S(1)}, u32[]{:S(2)}, u32[]{:S(2)}) collective-permute-start(bf16[96,201]{1,0:T(8,128)(2,1)S(1)} %get-tuple-element.239), channel_id=1, source_target_pairs={{0,8},{4,12},{8,0},{12,4},{1,9},{5,13},{9,1},{13,5},{2,10},{6,14},... | collective-permute-start | bytes 115784 | tf_op jit(solution)/shard_map/ppermute | solution.py:49
  566.9 14.3 %collective-permute-start.65 = (bf16[96,201]{1,0:T(8,128)(2,1)S(1)}, bf16[96,201]{1,0:T(8,128)(2,1)S(1)}, u32[]{:S(2)}, u32[]{:S(2)}) collective-permute-start(bf16[96,201]{1,0:T(8,128)(2,1)S(1)} %get-tuple-element.237), channel_id=1, source_target_pairs={{0,4},{4,0},{8,12},{12,8},{1,5},{5,1},{9,13},{13,9},{2,6},{6,2},{1... | collective-permute-start | bytes 115784 | tf_op jit(solution)/shard_map/ppermute | solution.py:49
  581.3 12.7 %collective-permute-start.70 = (bf16[96,9]{1,0:T(8,128)(2,1)S(1)}, bf16[96,9]{1,0:T(8,128)(2,1)S(1)}, u32[]{:S(2)}, u32[]{:S(2)}) collective-permute-start(bf16[96,9]{1,0:T(8,128)(2,1)S(1)} %slice.319), channel_id=1, source_target_pairs={{0,3},{1,2},{2,1},{3,0},{4,7},{5,6},{6,5},{7,4},{8,11},{9,10},{10,... | collective-permute-start | bytes 5192 | tf_op jit(solution)/shard_map/ppermute | solution.py:49
  582.9 11.1 %collective-permute-start.69 = (bf16[96,9]{1,0:T(8,128)(2,1)S(1)}, bf16[96,9]{1,0:T(8,128)(2,1)S(1)}, u32[]{:S(2)}, u32[]{:S(2)}) collective-permute-start(bf16[96,9]{1,0:T(8,128)(2,1)S(1)} %slice.319), channel_id=1, source_target_pairs={{0,2},{1,3},{2,0},{3,1},{4,6},{5,7},{6,4},{7,5},{8,10},{9,11},{10,... | collective-permute-start | bytes 5192 | tf_op jit(solution)/shard_map/ppermute | solution.py:49
  583.2 10.9 %collective-permute-start.68 = (bf16[96,9]{1,0:T(8,128)(2,1)S(1)}, bf16[96,9]{1,0:T(8,128)(2,1)S(1)}, u32[]{:S(2)}, u32[]{:S(2)}) collective-permute-start(bf16[96,9]{1,0:T(8,128)(2,1)S(1)} %slice.319), channel_id=1, source_target_pairs={{0,1},{1,0},{2,3},{3,2},{4,5},{5,4},{6,7},{7,6},{8,9},{9,8},{10,11... | collective-permute-start | bytes 5192 | tf_op jit(solution)/shard_map/ppermute | solution.py:49
  583.5 20.8 %collective-permute-start.54 = (bf16[384,768]{1,0:T(8,128)(2,1)S(1)}, bf16[384,768]{1,0:T(8,128)(2,1)}, u32[]{:S(2)}, u32[]{:S(2)}) collective-permute-start(bf16[384,768]{1,0:T(8,128)(2,1)S(1)} %collective-permute-done.53.own), channel_id=1, source_target_pairs={{0,2},{1,3},{2,0},{3,1},{4,6},{5,7},{6,4},{7,5},{8,10},{9,11},{10,... | collective-permute-start | bytes 1769480 | tf_op jit(solution)/shard_map/ppermute | solution.py:49
  (65 other events, 804.9 us)
Sparse Core Ops, SparseCore 0:
  9.6 127.8 all-gather.2
  139.5 93.0 all-gather.4
  333.5 88.7 reduce-scatter.4
  424.5 85.7 reduce-scatter.2

commit v4 on v3

v4 whole, which is shorter than its diff:
```python
import functools

import jax
import jax.numpy as jnp
from jax import lax
from jax.experimental import pallas as pl
from jax.experimental.pallas import tpu as pltpu
from jax.sharding import PartitionSpec as P

HD = 64
PLEN = 1024
CLEN = 128
CONTS = 8
CHUNK = 128
UNITS = 768

EPSILON = 1e-06
NEGATIVE = -1e30
ROOT = 0.7978845608028654
CUBE = 0.044715
F32 = jnp.float32
BF16 = jnp.bfloat16
VM = pl.BlockSpec(memory_space=pltpu.VMEM)
SM = pl.BlockSpec(memory_space=pltpu.SMEM)
ROOM = pltpu.CompilerParams(vmem_limit_bytes=60 * 2**20)


def shape(dims, dtype=BF16):
    return jax.ShapeDtypeStruct(dims, dtype)


def low(value):
    return value.astype(BF16)


def dot_last(left, right):
    return lax.dot_general(left, right, (((1,), (1,)), ((), ())), preferred_element_type=F32)


def dot_plain(left, right):
    return lax.dot_general(left, right, (((1,), (0,)), ((), ())), preferred_element_type=F32)


def add_all(parts):
    return functools.reduce(jnp.add, parts)


def xor_swap(value, axis, size, mask):
    return lax.ppermute(value, axis, [(place, place ^ mask) for place in range(size)])


def ring_step(value, axis, size, shift):
    return lax.ppermute(value, axis, [(place, (place + shift) % size) for place in range(size)])


def pick(stacked, index):
    return lax.dynamic_index_in_dim(stacked, index, 0, keepdims=False)


def xor_gather(value, axis, size, order=None):
    if order is None:
        order = [1 << bit for bit in range(size.bit_length() - 1)]
    have = {0: value}
    for mask in order:
        keys = sorted(have)
        moved = xor_swap(jnp.stack([have[key] for key in keys]), axis, size, mask)
        for place, key in enumerate(keys):
            have[key ^ mask] = moved[place]
    return [have[key] for key in range(size)]


def xor_exchange(pieces, axis, size):
    return [pieces[0]] + [xor_swap(pieces[mask], axis, size, mask) for mask in range(1, size)]


def chunk_list(value, axis):
    return [
        lax.slice_in_dim(value, first, first + CHUNK, axis=axis)
        for first in range(0, value.shape[axis], CHUNK)
    ]


def split_order(value, axis=0):
    parts = chunk_list(value, axis)
    return jnp.concatenate(parts[0::2] + parts[1::2], axis=axis)


def plain_order(value, axis=0):
    parts = chunk_list(value, axis)
    half = len(parts) // 2
    return jnp.concatenate([parts[(at % 2) * half + at // 2] for at in range(2 * half)], axis=axis)


def rms_unit(values):
    factor = lax.rsqrt(jnp.mean(values * values, axis=-1, keepdims=True) + EPSILON)
    return (values * factor, factor)


def rms_backward(grad_normed, unit_part, factor, gain):
    scaled = grad_normed * gain
    inner = jnp.mean(scaled * unit_part, axis=-1, keepdims=True)
    return factor * (scaled - unit_part * inner)


def normalize_kernel(tokens, gains, own, second):
    unit, _ = rms_unit(tokens[...].astype(F32))
    own[...] = split_order(low(gains[0:1, :] * unit))
    second[...] = own[own.shape[0] // 2 :, :]


def normalize(tokens, gains):
    rows, width = tokens.shape
    return pl.pallas_call(
        normalize_kernel,
        out_shape=(shape((rows, width)), shape((rows // 2, width))),
        in_specs=[VM] * 2,
        out_specs=(VM,) * 2,
        compiler_params=ROOM,
        name="normalize",
    )(tokens, gains)


def key_lanes(rows, width):
    return rows[:, : width + (-width) % 128]


def value_lanes(rows, width):
    return rows[:, width - (-width) % 128 :]


def spread_heads(columns, ahead, behind):
    width, count = columns.shape
    groups = []
    for first in range(0, width, HD):
        pieces = [columns[first : first + HD]]
        above, below = ahead + first, width - first - HD + behind
        if above:
            pieces.insert(0, jnp.zeros((above, count), columns.dtype))
        if below:
            pieces.append(jnp.zeros((below, count), columns.dtype))
        groups.append(jnp.concatenate(pieces, axis=0))
    return jnp.concatenate(groups, axis=1)


def causal(scores, count):
    key_row = lax.broadcasted_iota(jnp.int32, scores.shape, 0)
    query_row = lax.broadcasted_iota(jnp.int32, scores.shape, 1) % count
    return jnp.where(key_row <= query_row, scores, NEGATIVE)


def work_items(info, sizes, attend):
    prompts, conts, places, per = sizes
    ctx_index = info[0]

    def prompt_chunks(prompt):
        first = 1 + prompt * 2 * per
        return [info[first + at] for at in range(per)], [info[first + per + at] for at in range(per)]

    def prompt_mask(scores):
        count = per * CHUNK
        parts = [causal(scores[:count], count)]
        for place in range(1, places):
            part = scores[place * count : (place + 1) * count]
            parts.append(jnp.where(place <= ctx_index, part, NEGATIVE))
        return jnp.concatenate(parts, axis=0)

    def cont_mask(scores):
        return jnp.concatenate([causal(scores[:CLEN], CLEN), scores[CLEN:]], axis=0)

    @pl.loop(0, prompts)
    def _(prompt):
        own, far = prompt_chunks(prompt)
        attend(0, prompt, own, own, far, prompt_mask)

    first = 1 + prompts * 2 * per

    @pl.loop(0, conts)
    def _(cont):
        own = [info[first + cont]]
        near, far = prompt_chunks(info[first + conts + cont])
        attend(1, cont, own, own + near, far, cont_mask)


def chunk_lanes(chunk):
    return pl.ds(pl.multiple_of(chunk * CHUNK, CHUNK), CHUNK)


def load_lanes(ref, chunks):
    return jnp.concatenate([ref[:, chunk_lanes(chunk)] for chunk in chunks], axis=1)


def project_local_kernel(query_weight, pair_weight, *rest):
    *rows, query, pairs = rest
    width = query.shape[0]
    query_flip = query_weight[...].T
    at = 0
    for one in rows:
        value = one[...]
        count = value.shape[0]
        pair = low(dot_plain(value, pair_weight[...]))
        pairs[at // CHUNK : (at + count) // CHUNK] = pair.reshape(-1, CHUNK, 2 * width)
        query[:, at : at + count] = low(dot_last(query_flip, value) * 0.125)
        at += count


def project_remote_kernel(pair_weight, *rest):
    *rows, pairs = rest
    at = 0
    for one in rows:
        count = one.shape[0]
        pair = low(dot_plain(one[...], pair_weight[...]))
        pairs[at // CHUNK : (at + count) // CHUNK] = pair.reshape(-1, CHUNK, pairs.shape[2])
        at += count


def project_local(query_weight, pair_weight, rows):
    count = sum(one.shape[0] for one in rows)
    wide = pair_weight.shape[1]
    return pl.pallas_call(
        project_local_kernel,
        out_shape=(shape((query_weight.shape[1], count)), shape((count // CHUNK, CHUNK, wide))),
        in_specs=[VM] * (2 + len(rows)),
        out_specs=(VM,) * 2,
        compiler_params=ROOM,
        cost_estimate=pl.CostEstimate(
            flops=3 * count * pair_weight.size, bytes_accessed=10**7, transcendentals=0
        ),
        name="project_local",
    )(query_weight, pair_weight, *rows)


def project_remote(pair_weight, rows):
    count = sum(one.shape[0] for one in rows)
    return pl.pallas_call(
        project_remote_kernel,
        out_shape=shape((count // CHUNK, CHUNK, pair_weight.shape[1])),
        in_specs=[VM] * (1 + len(rows)),
        out_specs=VM,
        compiler_params=ROOM,
        cost_estimate=pl.CostEstimate(
            flops=2 * count * pair_weight.size, bytes_accessed=4 * 10**6, transcendentals=0
        ),
        name="project_remote",
    )(pair_weight, *rows)


def load_block(local, remote, near, far):
    blocks = [local[chunk] for chunk in near]
    blocks += [one[chunk] for one in remote for chunk in far]
    return jnp.concatenate(blocks, axis=0)


def attend_forward_kernel(sizes, info, query, local, *rest):
    remote, (*outs, lse_prompt, lse_cont, mixed) = rest[: sizes[2] - 1], rest[sizes[2] - 1 :]
    lse = (lse_prompt, lse_cont)
    width = query.shape[0]
    pad = (-width) % 128

    def attend(kind, index, own, near, far, mask):
        count = len(own) * CHUNK
        block = load_block(local, remote, near, far)
        spread = spread_heads(load_lanes(query, own), 0, pad)
        scores = mask(dot_plain(key_lanes(block, width), spread))
        peak = jnp.max(scores, axis=0, keepdims=True)
        shifted = jnp.exp(scores - peak)
        total = jnp.sum(shifted, axis=0, keepdims=True)
        weights = low(shifted)
        flip = value_lanes(block, width).T
        for head in range(width // HD):
            group = slice(head * count, (head + 1) * count)
            part = slice(pad + head * HD, pad + (head + 1) * HD)
            result = low(dot_plain(flip[part], weights[:, group]) / total[:, group])
            for place, chunk in enumerate(own):
                mixed[head * HD : (head + 1) * HD, chunk_lanes(chunk)] = result[
                    :, place * CHUNK : (place + 1) * CHUNK
                ]
        lse[kind][index] = peak + jnp.log(total)

    work_items(info, sizes, attend)
    each = outs[0].shape[1]
    for place, out in enumerate(outs):
        out[...] = mixed[:, place * each : (place + 1) * each]


def attend_backward_kernel(sizes, info, query, lse_prompt, lse_cont, local, *rest):
    count_remote = sizes[2] - 1
    remote, rest = rest[:count_remote], rest[count_remote:]
    query_weight, pair_weight, *grads = rest[:6]
    grad_query, grad_local, *rest, grad, sum_local, sum_remote = rest[6:]
    grad_remote, rest = rest[:count_remote], rest[count_remote:]
    *rest, keep_local, send_local = rest
    keep_remote, send_remote = rest[: len(rest) // 2], rest[len(rest) // 2 :]
    lse = (lse_prompt, lse_cont)
    width = query.shape[0]
    pad = (-width) % 128
    each = grads[0].shape[1]
    for place, one in enumerate(grads):
        grad[:, place * each : (place + 1) * each] = one[...]

    def attend(kind, index, own, near, far, mask):
        count = len(own) * CHUNK
        block = load_block(local, remote, near, far)
        query_spread = spread_heads(load_lanes(query, own), 0, pad)
        grad_spread = spread_heads(load_lanes(grad, own), pad, 0)
        keys = key_lanes(block, width)
        weights = jnp.exp(mask(dot_plain(keys, query_spread)) - lse[kind][index])
        slopes = dot_plain(value_lanes(block, width), grad_spread)
        centre = jnp.sum(weights * slopes, axis=0, keepdims=True)
        grad_scores = low(weights * (slopes - centre))
        flip = keys.T
        for head in range(width // HD):
            group = slice(head * count, (head + 1) * count)
            part = slice(head * HD, (head + 1) * HD)
            result = low(dot_plain(flip[part], grad_scores[:, group]) * 0.125)
            for place, chunk in enumerate(own):
                grad_query[part, chunk_lanes(chunk)] = result[
                    :, place * CHUNK : (place + 1) * CHUNK
                ]
        key_part = dot_last(grad_scores, query_spread)
        value_part = dot_last(low(weights), grad_spread)
        if pad:
            edge = width - pad
            shared = key_part[:, edge:] + value_part[:, : 2 * pad]
            joined = [key_part[:, :edge], shared, value_part[:, 2 * pad :]]
        else:
            joined = [key_part, value_part]
        result = jnp.concatenate(joined, axis=1)
        spots = [(sum_local, chunk) for chunk in near]
        spots += [(sum_remote.at[place], chunk) for place in range(count_remote) for chunk in far]
        for at, (sums, chunk) in enumerate(spots):
            part = result[at * CHUNK : (at + 1) * CHUNK]
            if kind == 0 or at == 0:
                sums[chunk] = part
            else:
                sums[chunk] += part

    work_items(info, sizes, attend)

    half = remote[0].shape[0] // 2
    for place in range(count_remote):
        for side, outs in enumerate((keep_remote, send_remote)):
            chunks = slice(side * half, (side + 1) * half)
            part = low(sum_remote[place, chunks])
            grad_remote[place][chunks] = part
            if outs:
                flat = part.reshape(half * CHUNK, 2 * width)
                outs[place][...] = low(dot_last(flat, pair_weight[...]))
    for at, out in enumerate((keep_local.at[1], send_local.at[1], keep_local.at[0], send_local.at[0])):
        chunks = slice(at * half, (at + 1) * half)
        part = low(sum_local[chunks])
        grad_local[chunks] = part
        flat = part.reshape(half * CHUNK, 2 * width)
        part = grad_query[:, at * each : (at + 1) * each].T
        out[...] = low(dot_last(flat, pair_weight[...]) + dot_last(part, query_weight[...]))


def attend_cost(factor, sizes, heads):
    prompts, conts, places, per = sizes
    scores = heads * places * per * CHUNK * CHUNK * (prompts * per + conts)
    return pl.CostEstimate(flops=factor * HD * scores, bytes_accessed=10**7, transcendentals=scores)


def attend_forward(sizes, info, query, local, remote):
    prompts, conts, places, per = sizes
    width, local_rows = query.shape
    heads = width // HD
    return pl.pallas_call(
        functools.partial(attend_forward_kernel, sizes),
        out_shape=(
            *([shape((width, local_rows // 4))] * 4),
            shape((prompts, 1, heads * per * CHUNK), F32),
            shape((conts, 1, heads * CLEN), F32),
        ),
        in_specs=[SM] + [VM] * (2 + len(remote)),
        out_specs=(VM,) * 6,
        scratch_shapes=[pltpu.VMEM((width, local_rows), BF16)],
        compiler_params=ROOM,
        cost_estimate=attend_cost(16, sizes, heads),
        name="attend_forward",
    )(info, query, local, *remote)


def attend_backward(
    sizes, info, query, lse_prompt, lse_cont, local, remote, query_weight, pair_weight, grads
):
    pairs = [local] + list(remote)
    remote_rows = 2 * len(remote) if len(remote) <= 4 else 0
    each = shape((grads[0].shape[1], query_weight.shape[0]))
    both = shape((2,) + each.shape)
    count = len(remote)
    return pl.pallas_call(
        functools.partial(attend_backward_kernel, sizes),
        out_shape=(
            shape(query.shape),
            *(shape(one.shape) for one in pairs),
            *([each] * remote_rows),
            both,
            both,
        ),
        in_specs=[SM] + [VM] * (5 + len(pairs) + len(grads)),
        out_specs=(VM,) * (3 + len(pairs) + remote_rows),
        scratch_shapes=[
            pltpu.VMEM(query.shape, BF16),
            pltpu.VMEM(local.shape, F32),
            pltpu.VMEM((count,) + remote[0].shape, F32),
        ],
        compiler_params=ROOM,
        cost_estimate=attend_cost(40, sizes, query.shape[0] // HD),
        name="attend_backward",
    )(info, query, lse_prompt, lse_cont, *pairs, query_weight, pair_weight, *grads)


def rows_remote_kernel(grad_pairs, pair_weight, keep, send):
    half = grad_pairs.shape[0] // 2
    wide = grad_pairs.shape[2]
    send[...] = low(dot_last(grad_pairs[half:].reshape(half * CHUNK, wide), pair_weight[...]))
    keep[...] = low(dot_last(grad_pairs[:half].reshape(half * CHUNK, wide), pair_weight[...]))


def rows_remote(grad_pairs, pair_weight):
    dims = (grad_pairs.shape[0] // 2 * CHUNK, pair_weight.shape[0])
    return pl.pallas_call(
        rows_remote_kernel,
        in_specs=[VM] * 2,
        out_specs=(VM,) * 2,
        out_shape=(shape(dims), shape(dims)),
        compiler_params=ROOM,
        cost_estimate=pl.CostEstimate(
            flops=4 * dims[0] * pair_weight.size, bytes_accessed=6 * 10**6, transcendentals=0
        ),
        name="rows_remote",
    )(grad_pairs, pair_weight)


def qkv_grad_kernel(places, grad_query, *rest):
    pairs, rows, out = rest[:places], rest[places:-1], rest[-1]
    width, local_rows = grad_query.shape
    total_query = total_pair = None
    spots = [(pair, at) for pair in pairs for at in range(0, pair.shape[0] * CHUNK, CHUNK)]
    first = 0
    for one in rows:
        value = one[...]
        count = value.shape[0]
        pair, at = spots[first // CHUNK]
        chunks = slice(at // CHUNK, (at + count) // CHUNK)
        part = dot_plain(pair[chunks].reshape(count, 2 * width).T, value)
        total_pair = part if total_pair is None else total_pair + part
        if first < local_rows:
            part = dot_plain(grad_query[:, first : first + count], value)
            total_query = part if total_query is None else total_query + part
        first += count
    out[...] = low(jnp.concatenate([total_query, total_pair], axis=0).T)


def qkv_grad(grad_query, pairs, rows):
    width = rows[0].shape[1]
    count = sum(one.shape[0] for one in rows)
    return pl.pallas_call(
        functools.partial(qkv_grad_kernel, len(pairs)),
        out_shape=shape((width, 3 * grad_query.shape[0])),
        in_specs=[VM] * (1 + len(pairs) + len(rows)),
        out_specs=VM,
        compiler_params=ROOM,
        cost_estimate=pl.CostEstimate(
            flops=6 * count * width * grad_query.shape[0],
            bytes_accessed=2 * 10**7,
            transcendentals=0,
        ),
        name="qkv_grad",
    )(grad_query, *pairs, *rows)


def final_kernel(first, tokens, gains, grad_middle, kept, beside, across, own, far, out):
    unit, factor = rms_unit(tokens[...].astype(F32))
    rows = kept[0].astype(F32) + beside[0].astype(F32) + across[...].astype(F32)
    ring = jnp.concatenate([own[...], far[...]], axis=0).astype(F32)
    rows = plain_order(rows + jnp.where(first[0] == 0, ring, 0.0))
    out[...] = rms_backward(rows, unit, factor, gains[0:1, :]) + grad_middle[...]


def final_rows(side, tokens, gains, grad_middle, kept, beside, across, own, far):
    rows, width = tokens.shape
    last = pl.BlockSpec((1, rows, width), lambda at: (1, 0, 0))
    half = pl.BlockSpec((rows // 2, width), lambda at: (0, 0))
    whole = pl.BlockSpec((rows, width), lambda at: (0, 0))
    return pl.pallas_call(
        final_kernel,
        grid=(1,),
        in_specs=[
            SM,
            whole,
            pl.BlockSpec(gains.shape, lambda at: (0, 0)),
            whole,
            last,
            last,
            whole,
            half,
            half,
        ],
        out_specs=whole,
        out_shape=shape((rows, width), F32),
        compiler_params=ROOM,
        name="final_rows",
    )(side, tokens, gains, grad_middle, kept, beside, across, own, far)


def slot_places(chosen, priority, first, expert_count, capacity):
    tokens = chosen.shape[0]
    expert_range = jnp.arange(expert_count)
    chosen_hot = low(chosen[:, None] == expert_range[None, :])
    order_hot = low(priority[:, None] == jnp.arange(tokens)[None, :])
    sorted_hot = jnp.dot(order_hot, chosen_hot, preferred_element_type=F32)
    places = jnp.arange(tokens)
    before = low(places[:, None] > places[None, :])
    earlier = jnp.dot(before, low(sorted_hot), preferred_element_type=F32)
    sorted_rank = jnp.minimum(jnp.sum(earlier * sorted_hot, axis=1), capacity)
    rank = jnp.einsum("it,i->t", order_hot, low(sorted_rank), preferred_element_type=F32)
    rank = rank.astype(jnp.int32)
    near = chosen ^ first
    block = (near >> 1) + (near & 1) * (expert_count // 2)
    return jnp.where(rank < capacity, block * capacity + rank, -1)


def softmax_rows(logits):
    shifted = jnp.exp(logits - jnp.max(logits, axis=-1, keepdims=True))
    return shifted / jnp.sum(shifted, axis=-1, keepdims=True)


def one_hot_experts(ids, expert_count):
    return ids == lax.broadcasted_iota(jnp.int32, (ids.shape[0], expert_count), 1)


def middle_kernel(
    parts, tokens, cotangent, gains, router, ids, place_row, *rest
):
    attended, proj = rest[:parts], rest[parts : 2 * parts]
    even_rows, odd_rows, even_grads, odd_grads, middle, normed, probs = rest[2 * parts :]
    mixed = plain_order(jnp.concatenate([one[...] for one in attended], axis=0), 1)
    branch = dot_plain(mixed.T, jnp.concatenate([one[...] for one in proj], axis=0))
    total = tokens[...].astype(F32) + branch
    middle[...] = total
    unit, _ = rms_unit(total)
    normed_rows = low(gains[1:2, :] * unit)
    normed[...] = normed_rows
    chances = softmax_rows(dot_plain(normed_rows, router[...]))
    probs[...] = chances
    hot = one_hot_experts(ids[...], chances.shape[1])
    gate = jnp.sum(jnp.where(hot, chances, 0.0), axis=1, keepdims=True)
    weighted = low(gate * cotangent[...].astype(F32))
    half = even_rows.shape[0]
    for at, (row_slots, grad_slots) in enumerate(((even_rows, even_grads), (odd_rows, odd_grads))):
        slots = at * half + lax.broadcasted_iota(jnp.int32, (half, tokens.shape[0]), 0)
        dispatch = low(slots == place_row[...])
        row_slots[...] = low(dot_plain(dispatch, normed_rows))
        grad_slots[...] = low(dot_plain(dispatch, weighted))


def middle_rows(tokens, cotangent, gains, router, ids, place, slots, attended, proj):
    rows, width = tokens.shape
    half = shape((slots // 2, width))
    return pl.pallas_call(
        functools.partial(middle_kernel, len(attended)),
        out_shape=(
            half,
            half,
            half,
            half,
            shape((rows, width), F32),
            shape((rows, width)),
            shape((rows, router.shape[1]), F32),
        ),
        in_specs=[VM] * (6 + 2 * len(attended)),
        out_specs=(VM,) * 7,
        compiler_params=ROOM,
        name="middle_rows",
    )(tokens, cotangent, gains, router, ids, place[None, :], *attended, *proj)


def gather_slots(refs, capacity):
    own, beside, *pairs = refs
    even = [own[0:capacity, :]] + [pair[0:capacity, :] for pair in pairs]
    odd = [beside[0:capacity, :]] + [pair[capacity:, :] for pair in pairs]
    return jnp.concatenate(even + odd, axis=0)


def made_kernel(
    capacity, cotangent, ids, place_column, middle, normed, probs, *rest
):
    *row_refs, output, grad_logits, grad_router = rest
    rows, expert_count = probs.shape
    slots = 2 * row_refs[1].shape[0]
    slot_range = lax.broadcasted_iota(jnp.int32, (rows, slots), 1)
    dispatch = low(slot_range == place_column[...])
    routed = dot_plain(dispatch, gather_slots(row_refs, capacity))
    chances = probs[...]
    hot = one_hot_experts(ids[...], expert_count)
    gate = jnp.sum(jnp.where(hot, chances, 0.0), axis=1, keepdims=True)
    output[...] = low(middle[...] + gate * routed)
    grad_gate = jnp.sum(cotangent[...].astype(F32) * routed, axis=1, keepdims=True)
    logits = low((grad_gate * gate) * (hot.astype(F32) - chances))
    grad_logits[...] = logits
    grad_router[...] = dot_plain(logits.T, normed[...])


def made_rows(cotangent, ids, place, middle, normed, probs, row_slots):
    rows, width = middle.shape
    expert_count = probs.shape[1]
    capacity = row_slots[1].shape[0] // (len(row_slots) - 1)
    inputs = [cotangent, ids, place[:, None], middle, normed, probs, *row_slots]
    return pl.pallas_call(
        functools.partial(made_kernel, capacity),
        out_shape=(
            shape((rows, width)),
            shape((rows, expert_count)),
            shape((expert_count, width), F32),
        ),
        in_specs=[VM] * len(inputs),
        out_specs=(VM,) * 3,
        compiler_params=ROOM,
        name="made_rows",
    )(*inputs)


def back_kernel(
    parts, capacity, cotangent, gains, router, place_column, middle, grad_logits, *rest
):
    proj, rest = rest[:parts], rest[parts:]
    *grad_refs, grad_middle, grad_split, gain_two = rest[: -parts]
    near = rest[-parts:]
    rows = middle.shape[0]
    slots = 2 * grad_refs[1].shape[0]
    slot_range = lax.broadcasted_iota(jnp.int32, (rows, slots), 1)
    dispatch = low(slot_range == place_column[...])
    grad_second = dot_plain(dispatch, gather_slots(grad_refs, capacity))
    grad_second = grad_second + dot_last(grad_logits[...], router[...])
    unit, factor = rms_unit(middle[...])
    total = cotangent[...].astype(F32) + rms_backward(grad_second, unit, factor, gains[1:2, :])
    grad_low = split_order(low(total))
    for place in range(parts):
        near[place][...] = low(dot_last(proj[place][...], grad_low))
    grad_middle[...] = total
    grad_split[...] = grad_low
    summed = jnp.sum(grad_second * unit, axis=0, keepdims=True)
    gain_two[...] = jnp.broadcast_to(summed, gain_two.shape)


def back_rows(cotangent, gains, router, place, middle, grad_logits, proj, grad_slots):
    rows, width = middle.shape
    parts = len(proj)
    capacity = grad_slots[1].shape[0] // (len(grad_slots) - 1)
    inputs = [cotangent, gains, router, place[:, None], middle, grad_logits, *proj, *grad_slots]
    return pl.pallas_call(
        functools.partial(back_kernel, parts, capacity),
        out_shape=(
            shape((rows, width), F32),
            shape((rows, width)),
            shape((8, width), F32),
            *([shape((proj[0].shape[0], rows))] * parts),
        ),
        in_specs=[VM] * len(inputs),
        out_specs=(VM,) * (3 + parts),
        compiler_params=ROOM,
        name="back_rows",
    )(*inputs)


def proj_grad_kernel(grad_rows, *rest):
    *attended, keep, send = rest
    for place, one in enumerate(attended):
        part = dot_plain(one[...], grad_rows[...])
        if place % 2:
            send[place // 2] = low(part)
        else:
            keep[place // 2] = part


def proj_grad(grad_rows, attended):
    dims = (len(attended) // 2, attended[0].shape[0], grad_rows.shape[1])
    return pl.pallas_call(
        proj_grad_kernel,
        out_shape=(shape(dims, F32), shape(dims)),
        in_specs=[VM] * (1 + len(attended)),
        out_specs=(VM,) * 2,
        compiler_params=ROOM,
        name="proj_grad",
    )(grad_rows, *attended)


def expert_up_kernel(capacity, *refs):
    *parts, up, hidden, slope, rows_flip, rows = refs

    @pl.when(pl.program_id(0) == 0)
    def _():
        arrived = gather_slots(parts, capacity)
        rows[...] = arrived
        rows_flip[...] = arrived.T

    pre = dot_plain(rows[...], up[...])
    square = pre * pre
    bend = jnp.tanh(ROOT * (pre + CUBE * (square * pre)))
    half = 0.5 * (1.0 + bend)
    hidden[...] = low(pre * half)
    bent = (0.5 * ROOT) * pre * (1.0 - bend * bend) * (1.0 + (3.0 * CUBE) * square)
    slope[...] = low(half + bent)


def expert_out_kernel(hidden, down, even, odd, total):
    step = pl.program_id(0)
    part = dot_plain(hidden[...], down[...])

    @pl.when(step == 0)
    def _():
        total[...] = part

    @pl.when(step > 0)
    def _():
        total[...] += part

    @pl.when(step == pl.num_programs(0) - 1)
    def _():
        half = even.shape[0]
        even[...] = low(total[:half])
        odd[...] = low(total[half:])


def expert_down_kernel(capacity, *refs):
    *parts, hidden, grad_down, grads, grads_flip = refs

    @pl.when(pl.program_id(0) == 0)
    def _():
        arrived = gather_slots(parts, capacity)
        grads[...] = arrived
        grads_flip[...] = arrived.T

    grad_down[...] = low(dot_plain(grads_flip[...], hidden[...]))


def expert_back_kernel(grads, slope, rows_flip, up, down, even, odd, grad_up, total):
    step = pl.program_id(0)
    grad_pre = low(dot_last(grads[...], down[...]) * slope[...].astype(F32))
    grad_up[...] = low(dot_plain(rows_flip[...], grad_pre))
    part = dot_last(grad_pre, up[...])

    @pl.when(step == 0)
    def _():
        total[...] = part

    @pl.when(step > 0)
    def _():
        total[...] += part

    @pl.when(step == pl.num_programs(0) - 1)
    def _():
        half = even.shape[0]
        even[...] = low(total[:half])
        odd[...] = low(total[half:])


def whole_spec(dims):
    return pl.BlockSpec(dims, lambda at: (0, 0))


def column_spec(rows):
    return pl.BlockSpec((rows, UNITS), lambda at: (0, at))


def row_spec(width):
    return pl.BlockSpec((UNITS, width), lambda at: (at, 0))


def expert_cost(products, slots, width, units):
    return pl.CostEstimate(
        flops=2 * products * slots * width * units,
        bytes_accessed=4 * slots * units + 2 * products * width * units,
        transcendentals=slots * units,
    )


def expert_hidden(parts, up):
    width, units = up.shape
    half = parts[1].shape[0]
    slots = 2 * half
    return pl.pallas_call(
        functools.partial(expert_up_kernel, half // (len(parts) - 1)),
        grid=(units // UNITS,),
        in_specs=[whole_spec(one.shape) for one in parts] + [column_spec(width)],
        out_specs=(column_spec(slots), column_spec(slots), whole_spec((width, slots))),
        out_shape=(shape((slots, units)), shape((slots, units)), shape((width, slots))),
        scratch_shapes=[pltpu.VMEM((slots, width), BF16)],
        compiler_params=ROOM,
        cost_estimate=expert_cost(1, slots, width, units),
        name="expert_hidden",
    )(*parts, up)


def expert_out(hidden, down):
    slots, units = hidden.shape
    width = down.shape[1]
    block = whole_spec((slots // 2, width))
    return pl.pallas_call(
        expert_out_kernel,
        grid=(units // UNITS,),
        in_specs=[column_spec(slots), row_spec(width)],
        out_specs=(block, block),
        out_shape=(shape((slots // 2, width)), shape((slots // 2, width))),
        scratch_shapes=[pltpu.VMEM((slots, width), F32)],
        compiler_params=ROOM,
        cost_estimate=expert_cost(1, slots, width, units),
        name="expert_out",
    )(hidden, down)


def expert_down_grad(parts, hidden):
    slots, units = hidden.shape
    half, width = parts[1].shape
    return pl.pallas_call(
        functools.partial(expert_down_kernel, half // (len(parts) - 1)),
        grid=(units // UNITS,),
        in_specs=[whole_spec(one.shape) for one in parts] + [column_spec(slots)],
        out_specs=(column_spec(width), whole_spec((slots, width))),
        out_shape=(shape((width, units)), shape((slots, width))),
        scratch_shapes=[pltpu.VMEM((width, slots), BF16)],
        compiler_params=ROOM,
        cost_estimate=expert_cost(1, slots, width, units),
        name="expert_down_grad",
    )(*parts, hidden)


def expert_back(grads, slope, rows_flip, up, down):
    slots, units = slope.shape
    width = grads.shape[1]
    block = whole_spec((slots // 2, width))
    return pl.pallas_call(
        expert_back_kernel,
        grid=(units // UNITS,),
        in_specs=[
            whole_spec(grads.shape),
            column_spec(slots),
            whole_spec(rows_flip.shape),
            column_spec(width),
            row_spec(width),
        ],
        out_specs=(block, block, column_spec(width)),
        out_shape=(
            shape((slots // 2, width)),
            shape((slots // 2, width)),
            shape((width, units)),
        ),
        scratch_shapes=[pltpu.VMEM((slots, width), F32)],
        compiler_params=ROOM,
        cost_estimate=expert_cost(3, slots, width, units),
        name="expert_back",
    )(grads, slope, rows_flip, up, down)


def shards(
    tokens,
    cotangent,
    gains,
    qkv_weight,
    proj_weight,
    router_weight,
    expert_up,
    expert_down,
    expert_ids,
    slot_order,
    segment_ids,
):
    dp_count, ctx_count, tp_count = (lax.axis_size(name) for name in ("dp", "ctx", "tp"))
    dp_index, ctx_index, tp_index = (lax.axis_index(name) for name in ("dp", "ctx", "tp"))
    group = dp_count * tp_count
    group_index = dp_index * tp_count + tp_index
    tok_dev, width = tokens.shape
    half_rows = tok_dev // 2
    expert_count = router_weight.shape[1]
    capacity = 5 * tok_dev // (4 * expert_count)
    slots = expert_count * capacity
    per = PLEN // ctx_count // CHUNK
    conts_here = segment_ids.shape[0]
    prompts_here = conts_here * ctx_count // CONTS
    local_width = qkv_weight.shape[2]
    shard_rows = qkv_weight.shape[1]
    side, core = tp_index >> 1, tp_index & 1

    def across(value):
        return xor_swap(value, "tp", tp_count, 2)

    def beside(value):
        return xor_swap(value, "tp", tp_count, 1)

    packed = jnp.concatenate(
        [
            qkv_weight.transpose(1, 0, 2).reshape(shard_rows, 3 * local_width),
            proj_weight.T,
            router_weight,
        ],
        axis=1,
    )
    by_ctx = xor_exchange([packed] * ctx_count, "ctx", ctx_count)
    own, own_second = normalize(tokens, gains)
    far_second = across(own_second)
    carried = jnp.where(side == 0, own[:half_rows], far_second)
    by_ctx, carried = lax.optimization_barrier((by_ctx, carried))
    by_dp = xor_gather(jnp.stack(by_ctx), "dp", dp_count)
    far_first = across(own[:half_rows])
    arrived = ring_step(carried, "ctx", ctx_count, 1)
    arrived, far_first, by_dp = lax.optimization_barrier((arrived, far_first, by_dp))
    rows = [own, beside(own), far_first, far_second, beside(far_first), beside(far_second)]
    local_count = len(rows)

    by_dp = jnp.stack(by_dp).reshape((-1,) + packed.shape)
    shard_index = dp_index * ctx_count + ctx_index
    weights = jnp.concatenate(
        [pick(by_dp, shard_index ^ place) for place in range(dp_count * ctx_count)], axis=0
    )
    query_weight = weights[:, :local_width]
    pair_weight = weights[:, local_width : 3 * local_width]
    router = weights[:, 4 * local_width :]

    query, local = project_local(query_weight, pair_weight, rows)
    remote = []
    blocks = []
    for place in range(1, ctx_count):
        other = across(arrived)
        if place < ctx_count - 1:
            following = ring_step(arrived, "ctx", ctx_count, 1)
            if place == 1:
                expert_up, expert_down, following = lax.optimization_barrier(
                    (expert_up, expert_down, following)
                )
                full_up = lax.all_gather(expert_up, "ctx", axis=2, tiled=True)[0]
                full_down = lax.all_gather(expert_down, "ctx", axis=1, tiled=True)[0]
            if place == ctx_count - 2:
                following, query, local = lax.optimization_barrier((following, query, local))
            following, other = lax.optimization_barrier((following, other))
        blocks.append([arrived, other, beside(arrived), beside(other)])
        arrived = following
    rows += [one for block in blocks for one in block]
    remote = [project_remote(pair_weight, block) for block in blocks]
    proj_part, _ = lax.optimization_barrier(
        (weights[:, 3 * local_width : 4 * local_width].T, blocks[-1][1])
    )
    proj = xor_gather(proj_part, "tp", tp_count, [2, 1])

    device_chunks = tok_dev // CHUNK

    def split_place(at):
        return (at % 2) * (device_chunks // 2) + at // 2

    at = jnp.arange(prompts_here * per)
    owner, inside = at // device_chunks, at % device_chunks
    local_at = (owner ^ tp_index) * device_chunks + split_place(inside)
    remote_at = ((owner ^ core) * 2 + ((inside % 2) ^ side)) * (device_chunks // 2) + inside // 2
    prompt_at = jnp.concatenate(
        [local_at.reshape(prompts_here, per), remote_at.reshape(prompts_here, per)], axis=1
    )
    at = jnp.arange(conts_here)
    cont_at = ((2 + at // device_chunks) ^ tp_index) * device_chunks + split_place(
        at % device_chunks
    )
    info = jnp.concatenate([ctx_index[None], prompt_at.reshape(-1), cont_at, segment_ids])
    info = info.astype(jnp.int32)
    sizes = (prompts_here, conts_here, ctx_count, per)

    *attended, lse_prompt, lse_cont = attend_forward(sizes, info, query, local, remote)
    attended = xor_exchange(attended, "tp", tp_count)
    place = slot_places(expert_ids[:, 0], slot_order[0], group_index, expert_count, capacity)

    def start_exchange(odd):
        return xor_swap(odd, ("dp", "tp"), group, 1)

    def finish_exchange(even, other):
        moved = [even, other]
        for at in range(1, group // 2):
            block = slice(at * capacity, (at + 1) * capacity)
            pair = jnp.concatenate([even[block], other[block]], axis=0)
            moved.append(xor_swap(pair, ("dp", "tp"), group, 2 * at))
        return moved

    even_rows, odd_rows, even_grads, odd_grads, middle, normed_two, probs = middle_rows(
        tokens, cotangent, gains, router, expert_ids, place, slots, attended, proj
    )
    row_slots = finish_exchange(even_rows, start_exchange(odd_rows))
    other_grads = start_exchange(odd_grads)
    row_slots, even_grads, other_grads = lax.optimization_barrier(
        (row_slots, even_grads, other_grads)
    )
    grad_slots = finish_exchange(even_grads, other_grads)
    hidden, slope, rows_flip = expert_hidden(row_slots, full_up)
    grad_down, arrived_grads = expert_down_grad(grad_slots, hidden)
    hidden, arrived_grads = lax.optimization_barrier((hidden, arrived_grads))
    even, odd = expert_out(hidden, full_down)
    even, other, slope = lax.optimization_barrier((even, start_exchange(odd), slope))
    made_slots = finish_exchange(even, other)
    even, odd, grad_up = expert_back(arrived_grads, slope, rows_flip, full_up, full_down)
    even, odd, made_slots, grad_up = lax.optimization_barrier((even, odd, made_slots, grad_up))
    back_slots = finish_exchange(even, start_exchange(odd))
    grad_down = lax.psum_scatter(grad_down, "ctx", scatter_dimension=1, tiled=True)
    grad_down = grad_down.T.astype(F32)[None]
    grad_up = lax.psum_scatter(grad_up, "ctx", scatter_dimension=1, tiled=True).astype(F32)[None]

    output, grad_logits, router_part = made_rows(
        cotangent, expert_ids, place, middle, normed_two, probs, made_slots
    )
    grad_middle, grad_split, gain_two, *grad_near = back_rows(
        cotangent, gains, router, place, middle, grad_logits, proj, back_slots
    )
    grad_near = xor_exchange(grad_near, "tp", tp_count)
    proj_keep, proj_send = proj_grad(grad_split, attended)
    proj_chip = proj_keep + beside(proj_send).astype(F32)
    proj_message = low(proj_chip[1])
    grad_near, proj_message = lax.optimization_barrier((grad_near, proj_message))
    grad_query, grad_local, *grads = attend_backward(
        sizes,
        info,
        query,
        lse_prompt,
        lse_cont,
        local,
        remote,
        query_weight,
        pair_weight,
        grad_near,
    )
    count = ctx_count - 1
    grad_remote, (*remote_rows, local_keep, local_send) = grads[:count], grads[count:]
    if remote_rows:
        remote_rows = list(zip(remote_rows[:count], remote_rows[count:]))
    else:
        remote_rows = [rows_remote(one, pair_weight) for one in grad_remote]

    pieces = []
    messages = []
    for keep, send in remote_rows[::-1]:
        chip = keep.astype(F32) + beside(send).astype(F32)
        messages.append(low(chip[half_rows:]))
        pieces.append(chip[:half_rows])
    local_send, proj_message, messages = lax.optimization_barrier(
        (local_send, proj_message, messages)
    )
    pieces = [piece + across(message).astype(F32) for piece, message in zip(pieces, messages)]
    running = low(pieces[0])
    local_send = beside(local_send)
    far_message = low(local_keep[0].astype(F32) + local_send[0].astype(F32))
    far_rows = across(far_message)
    proj_far = across(proj_message)
    grad_pairs, running, far_message = lax.optimization_barrier(
        ([grad_local, *grad_remote], running, far_message)
    )
    qkv_part = qkv_grad(grad_query, grad_pairs, rows)
    moved = ring_step(running, "ctx", ctx_count, -1)
    moved, proj_far, qkv_part = lax.optimization_barrier((moved, proj_far, qkv_part))

    proj_sum = proj_chip[0] + proj_far.astype(F32)
    early = jnp.concatenate([low(proj_sum), low(router_part), low(gain_two[:1])], axis=0).T
    packed = jnp.concatenate([qkv_part, early], axis=1)
    packed = packed.reshape(dp_count, ctx_count, shard_rows, -1)

    def scatter_sum(values, axis, size, me):
        parts = xor_exchange([pick(values, me ^ k) for k in range(size)], axis, size)
        return add_all([piece.astype(F32) for piece in parts])

    for piece in pieces[1:-1]:
        moved = ring_step(low(piece + moved.astype(F32)), "ctx", ctx_count, -1)
    summed = low(scatter_sum(packed, "dp", dp_count, dp_index))
    moved, summed, far_rows = lax.optimization_barrier((moved, summed, far_rows))
    running = low(pieces[-1] + moved.astype(F32))
    hops = [[], []]
    for ctx_from in range(ctx_count):
        for tp_from in range(tp_count):
            target = (ctx_from - 1) % ctx_count * tp_count + (tp_from & 1)
            hops[tp_from >> 1].append((ctx_from * tp_count + tp_from, target))
    own_rows, other_rows = (lax.ppermute(running, ("ctx", "tp"), hop) for hop in hops)
    summed = scatter_sum(summed, "ctx", ctx_count, ctx_index)
    other_rows, grad_up, grad_down = lax.optimization_barrier((other_rows, grad_up, grad_down))
    grad_tokens = final_rows(
        side.astype(jnp.int32).reshape(1),
        tokens,
        gains,
        grad_middle,
        local_keep,
        local_send,
        far_rows,
        own_rows,
        other_rows,
    )

    def sum_tp(values):
        moved = xor_exchange([low(values)] * tp_count, "tp", tp_count)
        return values + add_all([piece.astype(F32) for piece in moved[1:]])

    qkv_width = 3 * local_width
    grad_qkv = summed[:, :qkv_width].reshape(shard_rows, 3, local_width).transpose(1, 0, 2)
    grad_proj = summed[:, qkv_width : qkv_width + local_width].T
    gain_range = lax.dynamic_slice_in_dim(gains[0], shard_index * shard_rows, shard_rows)
    gain_one = jnp.sum(qkv_weight.astype(F32) * grad_qkv, axis=(0, 2))
    small = sum_tp(jnp.concatenate([summed[:, qkv_width + local_width :], gain_one[:, None]], axis=1))
    grad_router = small[:, :expert_count]
    grad_gains = jnp.stack([small[:, expert_count + 1] / gain_range, small[:, expert_count]])
    return (output, grad_tokens, grad_gains, grad_qkv, grad_proj, grad_router, grad_up, grad_down)


def solution(mesh):
    in_specs = (
        P(("dp", "ctx", "tp"), None),
        P(("dp", "ctx", "tp"), None),
        P(),
        P(None, ("dp", "ctx"), "tp"),
        P("tp", ("dp", "ctx")),
        P(("dp", "ctx"), None),
        P(("dp", "tp"), None, "ctx"),
        P(("dp", "tp"), "ctx", None),
        P(("dp", "ctx", "tp"), None),
        P(("dp", "ctx", "tp"), None),
        P(("dp", "ctx")),
    )
    out_specs = (
        P(("dp", "ctx", "tp"), None),
        P(("dp", "ctx", "tp"), None),
        P(None, ("dp", "ctx")),
        P(None, ("dp", "ctx"), "tp"),
        P("tp", ("dp", "ctx")),
        P(("dp", "ctx"), None),
        P(("dp", "tp"), None, "ctx"),
        P(("dp", "tp"), "ctx", None),
    )
    return jax.shard_map(shards, mesh=mesh, in_specs=in_specs, out_specs=out_specs, check_vma=False)
```

time: 632 us -> 546 us (0.86)
  the two profiles are of different devices: /device:TPU:25 before, /device:TPU:0 now
where the time goes in v4:
time: 546 us; the launch traced here: 541 us
  Pallas kernels  204 us (37%)
  waiting for transfers between devices  164 us (30%)
  starting transfers between devices  90.2 us (17%)
  local copies, waits for them, and re-layouts  41 us (8%)
  other arithmetic  24.5 us (4%)
  between operations  14.9 us (3%)
    ppermute x59, waiting for transfers between devices, xor_swap(): lax.ppermute(value, axis, [(place, place ^ mask) for place in range(size)])  122 us
    pallas_call x1, Pallas kernels, attend_backward(): pl.pallas_call(functools.partial(attend_backward_kernel, sizes), out_shap...  52.6 us
    ppermute x59, starting transfers between devices, xor_swap(): lax.ppermute(value, axis, [(place, place ^ mask) for place in range(size)])  47.4 us
    ppermute x5, waiting for transfers between devices, ring_step(): lax.ppermute(value, axis, [(place, (place + shift) % size) for place in r...  33.7 us
    ppermute x5, starting transfers between devices, ring_step(): lax.ppermute(value, axis, [(place, (place + shift) % size) for place in r...  31.6 us
    pallas_call x1, Pallas kernels, attend_forward(): pl.pallas_call(functools.partial(attend_forward_kernel, sizes), out_shape...  25 us
    pallas_call x1, Pallas kernels, expert_back(): pl.pallas_call(expert_back_kernel, grid=(units // UNITS,), in_specs=[whol...  21.1 us
    unnamed x98, local copies, waits for them, and re-layouts  16.8 us
  transfers between devices with their start and end apart: 70, of which 27 were waited for; matrix products, arithmetic and copies ran while one was open for 10% of the time, Pallas kernels for 36%

profile of v4, /device:TPU:0, one launch (start us, length us, event | category | flops | bytes accessed | tf_op | source)
XLA Modules:
  0.0 540.5 jit_solution(1558028932257965712)
XLA Ops:
  7.2 3.0 normalize.1
  10.2 2.9 collective-permute-start.3
  14.3 1.6 collective-permute-start
  15.9 2.6 collective-permute-start.1
  18.7 8.1 %collective-permute-done.3.rest_3_.rest_7_ = bf16[384,768]{1,0:T(8,128)(2,1)} collective-permute-done((bf16[384,768]{1,0:T(8,128)(2,1)}, bf16[384,768]{1,0:T(8,128)(2,1)}, u32[]{:S(2)}, u32[]{:S(2)}) %collective-permute-start.3) | collective-permute-done | bytes 589856 | tf_op jit(solution)/shard_map/ppermute | solution.py:49
  26.8 2.0 fusion.39
  28.7 4.5 collective-permute-done.1
  33.8 1.6 collective-permute-start.6
  35.4 15.7 %collective-permute-start.4 = (bf16[384,768]{1,0:T(8,128)(2,1)}, bf16[384,768]{1,0:T(8,128)(2,1)}, u32[]{:S(2)}, u32[]{:S(2)}) collective-permute-start(bf16[384,768]{1,0:T(8,128)(2,1)} %get-tuple-element.126), channel_id=1, source_target_pairs={{0,4},{4,8},{8,12},{12,0},{1,5},{5,9},{9,13},{13,1},{2,6},{6,10},{... | collective-permute-start | bytes 1769480 | tf_op jit(solution)/shard_map/ppermute | solution.py:53
  52.1 7.8 %collective-permute-done.4.rest_0_.rest_10_ = bf16[384,768]{1,0:T(8,128)(2,1)} collective-permute-done((bf16[384,768]{1,0:T(8,128)(2,1)}, bf16[384,768]{1,0:T(8,128)(2,1)}, u32[]{:S(2)}, u32[]{:S(2)}) %collective-permute-start.4) | collective-permute-done | bytes 589856 | tf_op jit(solution)/shard_map/ppermute | solution.py:53
  61.2 3.7 collective-permute-start.7
  64.9 8.3 %collective-permute-done.7.rest_0_.rest_14_ = bf16[384,768]{1,0:T(8,128)(2,1)} collective-permute-done((bf16[384,768]{1,0:T(8,128)(2,1)}, bf16[384,768]{1,0:T(8,128)(2,1)}, u32[]{:S(2)}, u32[]{:S(2)}) %collective-permute-start.7) | collective-permute-done | bytes 589856 | tf_op jit(solution)/shard_map/ppermute | solution.py:53
  78.0 13.0 %collective-permute-done.8.rest_1_.rest_11_ = bf16[384,768]{1,0:T(8,128)(2,1)} collective-permute-done((bf16[384,768]{1,0:T(8,128)(2,1)}, bf16[384,768]{1,0:T(8,128)(2,1)}, u32[]{:S(2)}, u32[]{:S(2)}) %collective-permute-start.8) | collective-permute-done | bytes 589856 | tf_op jit(solution)/shard_map/ppermute | solution.py:49
  90.9 2.4 collective-permute-start.9
  95.9 8.3 %project_local.1 = (bf16[192,3072]{1,0:T(8,128)(2,1)}, bf16[24,128,384]{2,1,0:T(8,128)(2,1)}) custom-call(bf16[768,192]{1,0:T(8,128)(2,1)} %get-tuple-element.291.query_weight.rest_3_, bf16[768,384]{1,0:T(8,128)(2,1)} %slice.204.pair_weight.rest_4_, bf16[768,768]{1,0:T(8,128)(2,1)} %get-tuple-element.124.rest_0_.rest_4_, ...), custom_call_target="tpu_custom_call" | custom-call | flops 2717908992 | bytes 10000000 | tf_op jit(solution)/shard_map/project_local/pallas_call | solution.py:219
  104.1 17.6 %collective-permute-done.9.rest_0_.rest_18_ = bf16[384,768]{1,0:T(8,128)(2,1)S(1)} collective-permute-done((bf16[384,768]{1,0:T(8,128)(2,1)}, bf16[384,768]{1,0:T(8,128)(2,1)S(1)}, u32[]{:S(2)}, u32[]{:S(2)}) %collective-permute-start.9) | collective-permute-done | bytes 589856 | tf_op jit(solution)/shard_map/ppermute | solution.py:53
  124.6 10.9 %collective-permute-done.18.rest_1_.rest_19_ = bf16[384,768]{1,0:T(8,128)(2,1)} collective-permute-done((bf16[384,768]{1,0:T(8,128)(2,1)S(1)}, bf16[384,768]{1,0:T(8,128)(2,1)}, u32[]{:S(2)}, u32[]{:S(2)}) %collective-permute-start.18) | collective-permute-done | bytes 589856 | tf_op jit(solution)/shard_map/ppermute | solution.py:49
  137.3 4.2 project_remote.3.rest_0_
  141.5 4.2 project_remote.4.rest_1_
  145.7 2.0 collective-permute-done.24
  149.0 4.2 project_remote.5.rest_2_
  153.2 25.0 %attend_forward.1 = (bf16[192,768]{1,0:T(8,128)(2,1)}, bf16[192,768]{1,0:T(8,128)(2,1)}, bf16[192,768]{1,0:T(8,128)(2,1)}, bf16[192,768]{1,0:T(8,128)(2,1)}, f32...) custom-call(s32[49]{0:T(128)} %pad_add_fusion.1.info, bf16[192,3072]{1,0:T(8,128)(2,1)} %get-tuple-element.139.query, ...), custom_call_target="tpu_custom_call" | custom-call | flops 9663676416 | bytes 10000000 | tf_op jit(solution)/shard_map/attend_forward/pallas_call | solution.py:367
  184.1 2.0 slice_bitcast_fusion.2
  186.1 2.7 collective-permute-done.22.rest_2_
  188.8 4.5 collective-permute-done.23.rest_3_
  194.1 8.6 %middle_rows.1 = (bf16[480,768]{1,0:T(8,128)(2,1)}, bf16[480,768]{1,0:T(8,128)(2,1)}, bf16[480,768]{1,0:T(8,128)(2,1)}, bf16[480,768]{1,0:T(8,128)(2,1)}, f32[76...) custom-call(bf16[768,768]{1,0:T(8,128)(2,1)} %tokens.5, bf16[768,768]{1,0:T(8,128)(2,1)} %cotangent.5, ...), custom_call_target="tpu_custom_call" | custom-call | tf_op jit(solution)/shard_map/middle_rows/pallas_call | solution.py:561
  206.7 3.0 collective-permute-start.29
  209.7 7.7 %collective-permute-done.27.refs_2_ = bf16[240,768]{1,0:T(8,128)(2,1)S(1)} collective-permute-done((bf16[240,768]{1,0:T(8,128)(2,1)S(1)}, bf16[240,768]{1,0:T(8,128)(2,1)S(1)}, u32[]{:S(2)}, u32[]{:S(2)}) %collective-permute-start.27) | collective-permute-done | bytes 368672 | tf_op jit(solution)/shard_map/ppermute | solution.py:49
  217.4 7.7 %collective-permute-done.28.refs_3_ = bf16[240,768]{1,0:T(8,128)(2,1)S(1)} collective-permute-done((bf16[240,768]{1,0:T(8,128)(2,1)S(1)}, bf16[240,768]{1,0:T(8,128)(2,1)S(1)}, u32[]{:S(2)}, u32[]{:S(2)}) %collective-permute-start.28) | collective-permute-done | bytes 368672 | tf_op jit(solution)/shard_map/ppermute | solution.py:49
  227.9 1.8 collective-permute-start.33
  229.6 14.0 %expert_hidden.1 = (bf16[960,3072]{1,0:T(8,128)(2,1)}, bf16[960,3072]{1,0:T(8,128)(2,1)}, bf16[768,960]{1,0:T(8,128)(2,1)}) custom-call(bf16[480,768]{1,0:T(8,128)(2,1)} %get-tuple-element.157.refs_0_, bf16[480,768]{1,0:T(8,128)(2,1)} %copy-done.20, bf16[240,768]{1,0:T(8,128)(2,1)} %copy-done.32, bf16[240,768]{1,0:T(8,128)(2,1)} %copy-done.33, ...), custom_call_target="tpu_custom_call" | custom-call | flops 4529848320 | bytes 16515072 | tf_op jit(solution)/shard_map/expert_hidden/pallas_call | solution.py:783
  245.9 9.8 %expert_down_grad.1 = (bf16[768,3072]{1,0:T(8,128)(2,1)}, bf16[960,768]{1,0:T(8,128)(2,1)}) custom-call(bf16[480,768]{1,0:T(8,128)(2,1)} %get-tuple-element.164.refs_0_, bf16[480,768]{1,0:T(8,128)(2,1)} %copy-done.19, bf16[240,768]{1,0:T(8,128)(2,1)} %copy-done.35, bf16[240,768]{1,0:T(8,128)(2,1)} %copy-done.36, bf16[240,768]{1,0:T(8,128)(2,1)} %copy-done.37, ...), custom_call_target="tpu_custom_call" | custom-call | flops 4529848320 | bytes 16515072 | tf_op jit(solution)/shard_map/expert_down_grad/pallas_call | solution.py:816
  255.7 8.6 %all-gather.5.cloned.1.call-done = bf16[1,3072,768]{2,1,0:T(8,128)(2,1)} async-done(((bf16[1,768,768]{2,1,0:T(8,128)(2,1)}), bf16[1,3072,768]{2,1,0:T(8,128)(2,1)}) %all-gather.5.cloned.1.call-update) | async-done | bytes 4718608 | tf_op jit(solution)/shard_map/all_gather | solution.py:932
  264.4 9.7 %expert_out.1 = (bf16[480,768]{1,0:T(8,128)(2,1)}, bf16[480,768]{1,0:T(8,128)(2,1)}) custom-call(bf16[960,3072]{1,0:T(8,128)(2,1)} %get-tuple-element.168.refs_5_.hidden, bf16[3072,768]{1,0:T(8,128)(2,1)} %bitcast.107), custom_call_target="tpu_custom_call" | custom-call | flops 4529848320 | bytes 16515072 | tf_op jit(solution)/shard_map/expert_out/pallas_call | solution.py:800
  274.1 2.4 collective-permute-done.34.rest_1_
  281.1 21.1 %expert_back.1 = (bf16[480,768]{1,0:T(8,128)(2,1)}, bf16[480,768]{1,0:T(8,128)(2,1)}, bf16[768,3072]{1,0:T(8,128)(2,1)}) custom-call(bf16[960,768]{1,0:T(8,128)(2,1)} %get-tuple-element.167.grads, bf16[960,3072]{1,0:T(8,128)(2,1)} %get-tuple-element.173.slope, bf16[768,960]{1,0:T(8,128)(2,1)} %get-tuple-element.174.rows_flip, bf16[768,3072]{1,0:T(8,128)(2,1)} %bitcast.106, ...), custom_call_target="tpu_custom_call" | custom-call | flops 13589544960 | bytes 25952256 | tf_op jit(solution)/shard_map/expert_back/pallas_call | solution.py:833
  304.8 1.6 collective-permute-start.39
  309.5 6.1 %made_rows.1 = (bf16[768,768]{1,0:T(8,128)(2,1)}, bf16[768,8]{1,0:T(8,128)(2,1)}, f32[8,768]{1,0:T(8,128)}) custom-call(bf16[768,768]{1,0:T(8,128)(2,1)} %cotangent.5, s32[768,1]{1,0:T(8,128)} %copy.141.ids, s32[768,1]{1,0:T(8,128)} %broadcast_in_dim.45.place_column, f32[768,768]{1,0:T(8,128)} %get-tuple-element.150.middle, ...), custom_call_target="tpu_custom_call" | custom-call | tf_op jit(solution)/shard_map/made_rows/pallas_call | solution.py:610
  316.3 8.4 %collective-permute-done.40.rest_7_ = bf16[240,768]{1,0:T(8,128)(2,1)S(1)} collective-permute-done((bf16[240,768]{1,0:T(8,128)(2,1)S(1)}, bf16[240,768]{1,0:T(8,128)(2,1)S(1)}, u32[]{:S(2)}, u32[]{:S(2)}) %collective-permute-start.40) | collective-permute-done | bytes 368672 | tf_op jit(solution)/shard_map/ppermute | solution.py:49
  325.6 8.7 %back_rows.1 = (f32[768,768]{1,0:T(8,128)}, bf16[768,768]{1,0:T(8,128)(2,1)}, f32[8,768]{1,0:T(8,128)}, bf16[192,768]{1,0:T(8,128)(2,1)}, bf16[192,768]{1,0:T(8,...) custom-call(bf16[768,768]{1,0:T(8,128)(2,1)} %cotangent.5, f32[2,768]{1,0:T(2,128)} %gains.7, ...), custom_call_target="tpu_custom_call" | custom-call | tf_op jit(solution)/shard_map/back_rows/pallas_call | solution.py:652
  334.3 3.8 proj_grad.1
  344.9 3.9 collective-permute-done.43.rest_7_
  348.8 4.4 collective-permute-done.44.rest_8_
  353.2 52.6 %attend_backward.1 = (bf16[192,3072]{1,0:T(8,128)(2,1)}, bf16[24,128,384]{2,1,0:T(8,128)(2,1)}, bf16[12,128,384]{2,1,0:T(8,128)(2,1)}, bf16[12,128,384]{2,1,0:T(...) custom-call(s32[49]{0:T(128)} %pad_add_fusion.1.info, ...), custom_call_target="tpu_custom_call" | custom-call | flops 24159191040 | bytes 10000000 | tf_op jit(solution)/shard_map/attend_backward/pallas_call | solution.py:391
  407.0 2.2 collective-permute-done.46
  409.2 1.6 convert_add_fusion.2
  413.3 2.0 copy-done.11
  421.1 12.2 %collective-permute-done.51 = bf16[384,768]{1,0:T(8,128)(2,1)} collective-permute-done((bf16[384,768]{1,0:T(8,128)(2,1)}, bf16[384,768]{1,0:T(8,128)(2,1)}, u32[]{:S(2)}, u32[]{:S(2)}) %collective-permute-start.51) | collective-permute-done | bytes 589856 | tf_op jit(solution)/shard_map/ppermute | solution.py:49
  433.3 2.4 fusion.7
  435.7 2.7 fusion.4
  439.4 8.8 %collective-permute-start.52 = (bf16[384,768]{1,0:T(8,128)(2,1)}, bf16[384,768]{1,0:T(8,128)(2,1)}, u32[]{:S(2)}, u32[]{:S(2)}) collective-permute-start(bf16[384,768]{1,0:T(8,128)(2,1)} %fusion.7), channel_id=1, source_target_pairs={{0,12},{4,0},{8,4},{12,8},{1,13},{5,1},{9,5},{13,9},{2,14},{6,2},{... | collective-permute-start | bytes 1769480 | tf_op jit(solution)/shard_map/ppermute | solution.py:53
  448.2 14.4 %qkv_grad.1 = bf16[768,576]{1,0:T(8,128)(2,1)} custom-call(bf16[192,3072]{1,0:T(8,128)(2,1)} %get-tuple-element.221.grad_query, bf16[24,128,384]{2,1,0:T(8,128)(2,1)} %get-tuple-element.222.rest_0_, bf16[12,128,384]{2,1,0:T(8,128)(2,1)} %get-tuple-element.223.rest_1_, bf16[12,128,384]{2,1,0:T(8,128)(2,1)} %get-tuple-element.224.rest_2_, ...), custom_call_target="tpu_custom_call" | custom-call | flops 6794772480 | bytes 20000000 | tf_op jit(solution)/shard_map/qkv_grad/pallas_call | solution.py:458
  466.7 2.3 fusion.9
  472.2 9.0 %collective-permute-done.55 = bf16[4,96,777]{2,1,0:T(8,128)(2,1)} collective-permute-done((bf16[4,96,777]{2,1,0:T(8,128)(2,1)}, bf16[4,96,777]{2,1,0:T(8,128)(2,1)}, u32[]{:S(2)}, u32[]{:S(2)}) %collective-permute-start.55) | collective-permute-done | bytes 596768 | tf_op jit(solution)/shard_map/ppermute | solution.py:49
  481.2 2.3 copy.151
  485.0 2.8 collective-permute-start.62
  487.7 1.7 collective-permute-start.60
  489.4 2.1 collective-permute-done.57
  492.9 9.8 %collective-permute-start.58 = (bf16[384,768]{1,0:T(8,128)(2,1)S(1)}, bf16[384,768]{1,0:T(8,128)(2,1)}, u32[]{:S(2)}, u32[]{:S(2)}) collective-permute-start(bf16[384,768]{1,0:T(8,128)(2,1)S(1)} %fusion.6), channel_id=1, source_target_pairs={{0,12},{1,13},{4,0},{5,1},{8,4},{9,5},{12,8},{13,9},{16,28},{17,29... | collective-permute-start | bytes 1769480 | tf_op jit(solution)/shard_map/ppermute | solution.py:1073
  504.4 1.6 collective-permute-start.65
  509.0 11.0 %collective-permute-done.64 = bf16[96,10]{0,1:T(8,128)(2,1)S(1)} collective-permute-done((bf16[96,10]{0,1:T(8,128)(2,1)S(1)}, bf16[96,10]{0,1:T(8,128)(2,1)S(1)}, u32[]{:S(2)}, u32[]{:S(2)}) %collective-permute-start.64) | collective-permute-done | bytes 1952 | tf_op jit(solution)/shard_map/ppermute | solution.py:49
  522.7 2.8 bitcast_convert_fusion
  525.6 1.9 copy.154
  527.5 6.3 %final_rows.1 = f32[768,768]{1,0:T(8,128)} custom-call(s32[1]{0:T(128)} %bitcast.28.first, bf16[768,768]{1,0:T(8,128)(2,1)} %tokens.5, f32[2,768]{1,0:T(2,128)} %gains.7, f32[768,768]{1,0:T(8,128)} %get-tuple-element.189.grad_middle, bf16[2,768,768]{2,1,0:T(8,128)(2,1)} %get-tuple-element.203.kept, bf16[2,768,768]{2,1,0:T(8,128)(2,1)} %collective-permute-done.49.beside, ...), custom_call_target="tpu_custom_call" | custom-call | tf_op jit(solution)/shard_map/final_rows/pallas_call | solution.py:486
  (287 shorter events, 79.1 us)
Async XLA Ops:
  7.2 222.4 %all-gather.3.cloned.1.call-start = ((), (), s32[]{:S(2)}) async-start(), calls=%async_computation.2 | async-start | bytes 5898240 | tf_op jit(solution)/shard_map/all_gather | solution.py:931
  10.2 16.6 %collective-permute-start.3 = (bf16[384,768]{1,0:T(8,128)(2,1)}, bf16[384,768]{1,0:T(8,128)(2,1)}, u32[]{:S(2)}, u32[]{:S(2)}) collective-permute-start(bf16[384,768]{1,0:T(8,128)(2,1)} %get-tuple-element.125), channel_id=1, source_target_pairs={{0,2},{1,3},{2,0},{3,1},{4,6},{5,7},{6,4},{7,5},{8,10},{9,11},{10,... | collective-permute-start | bytes 1769480 | tf_op jit(solution)/shard_map/ppermute | solution.py:49
  14.3 14.5 %collective-permute-start = (bf16[96,776]{0,1:T(8,128)(2,1)S(1)}, bf16[96,776]{0,1:T(8,128)(2,1)S(1)}, u32[]{:S(2)}, u32[]{:S(2)}) collective-permute-start(bf16[96,776]{0,1:T(8,128)(2,1)S(1)} %pad_maximum_fusion.16), channel_id=1, source_target_pairs={{0,4},{4,0},{8,12},{12,8},{1,5},{5,1},{9,13},{13,9},{2,6},{6,2},{1... | collective-permute-start | bytes 446984 | tf_op jit(solution)/shard_map/ppermute | solution.py:49
  15.9 17.3 %collective-permute-start.1 = (bf16[96,776]{0,1:T(8,128)(2,1)S(1)}, bf16[96,776]{0,1:T(8,128)(2,1)S(1)}, u32[]{:S(2)}, u32[]{:S(2)}) collective-permute-start(bf16[96,776]{0,1:T(8,128)(2,1)S(1)} %pad_maximum_fusion.16), channel_id=1, source_target_pairs={{0,8},{4,12},{8,0},{12,4},{1,9},{5,13},{9,1},{13,5},{2,10},{6,14},... | collective-permute-start | bytes 446984 | tf_op jit(solution)/shard_map/ppermute | solution.py:49
  18.5 14.7 %collective-permute-start.2 = (bf16[96,776]{0,1:T(8,128)(2,1)S(1)}, bf16[96,776]{0,1:T(8,128)(2,1)S(1)}, u32[]{:S(2)}, u32[]{:S(2)}) collective-permute-start(bf16[96,776]{0,1:T(8,128)(2,1)S(1)} %pad_maximum_fusion.16), channel_id=1, source_target_pairs={{0,12},{4,8},{8,4},{12,0},{1,13},{5,9},{9,5},{13,1},{2,14},{6,10},... | collective-permute-start | bytes 446984 | tf_op jit(solution)/shard_map/ppermute | solution.py:49
  33.8 17.9 %collective-permute-start.6 = (bf16[1,4,96,776]{3,2,1,0:T(8,128)(2,1)S(1)}, bf16[1,4,96,776]{3,2,1,0:T(8,128)(2,1)S(1)}, u32[]{:S(2)}, u32[]{:S(2)}) collective-permute-start(bf16[1,4,96,776]{3,2,1,0:T(8,128)(2,1)S(1)} %copy.127), channel_id=1, source_target_pairs={{0,16},{16,0},{1,17},{17,1},{2,18},{18,2},{3,19},{19,3},{4,20},{20... | collective-permute-start | bytes 1787912 | tf_op jit(solution)/shard_map/ppermute | solution.py:49
  35.4 24.5 %collective-permute-start.4 = (bf16[384,768]{1,0:T(8,128)(2,1)}, bf16[384,768]{1,0:T(8,128)(2,1)}, u32[]{:S(2)}, u32[]{:S(2)}) collective-permute-start(bf16[384,768]{1,0:T(8,128)(2,1)} %get-tuple-element.126), channel_id=1, source_target_pairs={{0,4},{4,8},{8,12},{12,0},{1,5},{5,9},{9,13},{13,1},{2,6},{6,10},{... | collective-permute-start | bytes 1769480 | tf_op jit(solution)/shard_map/ppermute | solution.py:53
  51.2 10.0 %collective-permute-start.5 = (bf16[384,768]{1,0:T(8,128)(2,1)S(1)}, bf16[384,768]{1,0:T(8,128)(2,1)}, u32[]{:S(2)}, u32[]{:S(2)}) collective-permute-start(bf16[384,768]{1,0:T(8,128)(2,1)S(1)} %get-tuple-element.292), channel_id=1, source_target_pairs={{0,2},{1,3},{2,0},{3,1},{4,6},{5,7},{6,4},{7,5},{8,10},{9,11},{10,... | collective-permute-start | bytes 1769480 | tf_op jit(solution)/shard_map/ppermute | solution.py:49
  61.2 12.0 %collective-permute-start.7 = (bf16[384,768]{1,0:T(8,128)(2,1)}, bf16[384,768]{1,0:T(8,128)(2,1)}, u32[]{:S(2)}, u32[]{:S(2)}) collective-permute-start(bf16[384,768]{1,0:T(8,128)(2,1)} %collective-permute-done.4.rest_0_.rest_10_), channel_id=1, source_target_pairs={{0,4},{4,8},{8,12},{12,0},{1,5},{5,9},{9,13},{13,1},{2,6},{6,10},{... | collective-permute-start | bytes 1769480 | tf_op jit(solution)/shard_map/ppermute | solution.py:53
  73.2 191.2 %all-gather.5.cloned.1.call-start = ((), (), s32[]{:S(2)}) async-start(), calls=%async_computation.3 | async-start | bytes 5898240 | tf_op jit(solution)/shard_map/all_gather | solution.py:932
  73.2 22.6 %collective-permute-start.10 = (bf16[768,768]{1,0:T(8,128)(2,1)}, bf16[768,768]{1,0:T(8,128)(2,1)}, u32[]{:S(2)}, u32[]{:S(2)}) collective-permute-start(bf16[768,768]{1,0:T(8,128)(2,1)} %get-tuple-element.124.rest_0_.rest_4_), channel_id=1, source_target_pairs={{0,1},{1,0},{2,3},{3,2},{4,5},{5,4},{6,7},{7,6},{8,9},{9,8},{10,11... | collective-permute-start | bytes 3538952 | tf_op jit(solution)/shard_map/ppermute | solution.py:49
  74.8 21.1 %collective-permute-start.12 = (bf16[384,768]{1,0:T(8,128)(2,1)}, bf16[384,768]{1,0:T(8,128)(2,1)}, u32[]{:S(2)}, u32[]{:S(2)}) collective-permute-start(bf16[384,768]{1,0:T(8,128)(2,1)} %collective-permute-done.3.rest_3_.rest_7_), channel_id=1, source_target_pairs={{0,1},{1,0},{2,3},{3,2},{4,5},{5,4},{6,7},{7,6},{8,9},{9,8},{10,11... | collective-permute-start | bytes 1769480 | tf_op jit(solution)/shard_map/ppermute | solution.py:49
  75.3 15.6 %collective-permute-start.8 = (bf16[384,768]{1,0:T(8,128)(2,1)}, bf16[384,768]{1,0:T(8,128)(2,1)}, u32[]{:S(2)}, u32[]{:S(2)}) collective-permute-start(bf16[384,768]{1,0:T(8,128)(2,1)} %collective-permute-done.4.rest_0_.rest_10_), channel_id=1, source_target_pairs={{0,2},{1,3},{2,0},{3,1},{4,6},{5,7},{6,4},{7,5},{8,10},{9,11},{10,... | collective-permute-start | bytes 1769480 | tf_op jit(solution)/shard_map/ppermute | solution.py:49
  77.4 18.4 %collective-permute-start.11 = (bf16[384,768]{1,0:T(8,128)(2,1)}, bf16[384,768]{1,0:T(8,128)(2,1)}, u32[]{:S(2)}, u32[]{:S(2)}) collective-permute-start(bf16[384,768]{1,0:T(8,128)(2,1)} %collective-permute-done.5.rest_2_.rest_6_), channel_id=1, source_target_pairs={{0,1},{1,0},{2,3},{3,2},{4,5},{5,4},{6,7},{7,6},{8,9},{9,8},{10,11... | collective-permute-start | bytes 1769480 | tf_op jit(solution)/shard_map/ppermute | solution.py:49
  77.7 443.5 %reduce-scatter.5.cloned.1.call-start = ((), (), s32[]{:S(2)}) async-start(), calls=%async_computation.5 | async-start | bytes 5898240 | tf_op jit(solution)/shard_map/reduce_scatter | solution.py:998
  90.9 30.8 %collective-permute-start.9 = (bf16[384,768]{1,0:T(8,128)(2,1)}, bf16[384,768]{1,0:T(8,128)(2,1)S(1)}, u32[]{:S(2)}, u32[]{:S(2)}) collective-permute-start(bf16[384,768]{1,0:T(8,128)(2,1)} %collective-permute-done.7.rest_0_.rest_14_), channel_id=1, source_target_pairs={{0,4},{4,8},{8,12},{12,0},{1,5},{5,9},{9,13},{13,1},{2,6},{6,10},{... | collective-permute-start | bytes 1769480 | tf_op jit(solution)/shard_map/ppermute | solution.py:53
  93.3 28.4 %collective-permute-start.15 = (bf16[384,768]{1,0:T(8,128)(2,1)}, bf16[384,768]{1,0:T(8,128)(2,1)S(1)}, u32[]{:S(2)}, u32[]{:S(2)}) collective-permute-start(bf16[384,768]{1,0:T(8,128)(2,1)} %collective-permute-done.7.rest_0_.rest_14_), channel_id=1, source_target_pairs={{0,2},{1,3},{2,0},{3,1},{4,6},{5,7},{6,4},{7,5},{8,10},{9,11},{10,... | collective-permute-start | bytes 1769480 | tf_op jit(solution)/shard_map/ppermute | solution.py:49
  95.8 28.3 %collective-permute-start.13 = (bf16[384,768]{1,0:T(8,128)(2,1)}, bf16[384,768]{1,0:T(8,128)(2,1)}, u32[]{:S(2)}, u32[]{:S(2)}) collective-permute-start(bf16[384,768]{1,0:T(8,128)(2,1)} %collective-permute-done.4.rest_0_.rest_10_), channel_id=1, source_target_pairs={{0,1},{1,0},{2,3},{3,2},{4,5},{5,4},{6,7},{7,6},{8,9},{9,8},{10,11... | collective-permute-start | bytes 1769480 | tf_op jit(solution)/shard_map/ppermute | solution.py:49
  121.7 13.7 %collective-permute-start.18 = (bf16[384,768]{1,0:T(8,128)(2,1)S(1)}, bf16[384,768]{1,0:T(8,128)(2,1)}, u32[]{:S(2)}, u32[]{:S(2)}) collective-permute-start(bf16[384,768]{1,0:T(8,128)(2,1)S(1)} %collective-permute-done.9.rest_0_.rest_18_), channel_id=1, source_target_pairs={{0,2},{1,3},{2,0},{3,1},{4,6},{5,7},{6,4},{7,5},{8,10},{9,11},{10,... | collective-permute-start | bytes 1769480 | tf_op jit(solution)/shard_map/ppermute | solution.py:49
  123.4 12.8 %collective-permute-start.14 = (bf16[384,768]{1,0:T(8,128)(2,1)}, bf16[384,768]{1,0:T(8,128)(2,1)}, u32[]{:S(2)}, u32[]{:S(2)}) collective-permute-start(bf16[384,768]{1,0:T(8,128)(2,1)} %collective-permute-done.8.rest_1_.rest_11_), channel_id=1, source_target_pairs={{0,1},{1,0},{2,3},{3,2},{4,5},{5,4},{6,7},{7,6},{8,9},{9,8},{10,11... | collective-permute-start | bytes 1769480 | tf_op jit(solution)/shard_map/ppermute | solution.py:49
  123.5 18.1 %collective-permute-start.16 = (bf16[384,768]{1,0:T(8,128)(2,1)}, bf16[384,768]{1,0:T(8,128)(2,1)}, u32[]{:S(2)}, u32[]{:S(2)}) collective-permute-start(bf16[384,768]{1,0:T(8,128)(2,1)} %collective-permute-done.7.rest_0_.rest_14_), channel_id=1, source_target_pairs={{0,1},{1,0},{2,3},{3,2},{4,5},{5,4},{6,7},{7,6},{8,9},{9,8},{10,11... | collective-permute-start | bytes 1769480 | tf_op jit(solution)/shard_map/ppermute | solution.py:49
  123.9 17.6 %collective-permute-start.17 = (bf16[384,768]{1,0:T(8,128)(2,1)S(1)}, bf16[384,768]{1,0:T(8,128)(2,1)}, u32[]{:S(2)}, u32[]{:S(2)}) collective-permute-start(bf16[384,768]{1,0:T(8,128)(2,1)S(1)} %collective-permute-done.15.rest_1_.rest_15_), channel_id=1, source_target_pairs={{0,1},{1,0},{2,3},{3,2},{4,5},{5,4},{6,7},{7,6},{8,9},{9,8},{10,11... | collective-permute-start | bytes 1769480 | tf_op jit(solution)/shard_map/ppermute | solution.py:49
  124.1 24.8 %collective-permute-start.19 = (bf16[384,768]{1,0:T(8,128)(2,1)S(1)}, bf16[384,768]{1,0:T(8,128)(2,1)}, u32[]{:S(2)}, u32[]{:S(2)}) collective-permute-start(bf16[384,768]{1,0:T(8,128)(2,1)S(1)} %collective-permute-done.9.rest_0_.rest_18_), channel_id=1, source_target_pairs={{0,1},{1,0},{2,3},{3,2},{4,5},{5,4},{6,7},{7,6},{8,9},{9,8},{10,11... | collective-permute-start | bytes 1769480 | tf_op jit(solution)/shard_map/ppermute | solution.py:49
  135.5 13.5 %collective-permute-start.20 = (bf16[384,768]{1,0:T(8,128)(2,1)}, bf16[384,768]{1,0:T(8,128)(2,1)}, u32[]{:S(2)}, u32[]{:S(2)}) collective-permute-start(bf16[384,768]{1,0:T(8,128)(2,1)} %collective-permute-done.18.rest_1_.rest_19_), channel_id=1, source_target_pairs={{0,1},{1,0},{2,3},{3,2},{4,5},{5,4},{6,7},{7,6},{8,9},{9,8},{10,11... | collective-permute-start | bytes 1769480 | tf_op jit(solution)/shard_map/ppermute | solution.py:49
  136.2 11.5 %collective-permute-start.24 = (bf16[1,192,768]{1,2,0:T(8,128)(2,1)S(1)}, bf16[1,192,768]{1,2,0:T(8,128)(2,1)S(1)}, u32[]{:S(2)}, u32[]{:S(2)}) collective-permute-start(bf16[1,192,768]{1,2,0:T(8,128)(2,1)S(1)} %bitcast.90), channel_id=1, source_target_pairs={{0,2},{1,3},{2,0},{3,1},{4,6},{5,7},{6,4},{7,5},{8,10},{9,11},{10,... | collective-permute-start | bytes 884744 | tf_op jit(solution)/shard_map/ppermute | solution.py:49
  149.0 35.2 %collective-permute-start.25 = (bf16[2,192,768]{2,1,0:T(8,128)(2,1)}, bf16[2,192,768]{2,1,0:T(8,128)(2,1)}, u32[]{:S(2)}, u32[]{:S(2)}) collective-permute-start(bf16[2,192,768]{2,1,0:T(8,128)(2,1)} %copy.137), channel_id=1, source_target_pairs={{0,1},{1,0},{2,3},{3,2},{4,5},{5,4},{6,7},{7,6},{8,9},{9,8},{10,11... | collective-permute-start | bytes 1769480 | tf_op jit(solution)/shard_map/ppermute | solution.py:49
  178.2 7.9 %collective-permute-start.21 = (bf16[192,768]{1,0:T(8,128)(2,1)}, bf16[192,768]{1,0:T(8,128)(2,1)S(1)}, u32[]{:S(2)}, u32[]{:S(2)}) collective-permute-start(bf16[192,768]{1,0:T(8,128)(2,1)} %get-tuple-element.146), channel_id=1, source_target_pairs={{0,1},{1,0},{2,3},{3,2},{4,5},{5,4},{6,7},{7,6},{8,9},{9,8},{10,11... | collective-permute-start | bytes 884744 | tf_op jit(solution)/shard_map/ppermute | solution.py:49
  178.7 10.1 %collective-permute-start.22 = (bf16[192,768]{1,0:T(8,128)(2,1)}, bf16[192,768]{1,0:T(8,128)(2,1)S(1)}, u32[]{:S(2)}, u32[]{:S(2)}) collective-permute-start(bf16[192,768]{1,0:T(8,128)(2,1)} %get-tuple-element.147), channel_id=1, source_target_pairs={{0,2},{1,3},{2,0},{3,1},{4,6},{5,7},{6,4},{7,5},{8,10},{9,11},{10,... | collective-permute-start | bytes 884744 | tf_op jit(solution)/shard_map/ppermute | solution.py:49
  179.2 14.1 %collective-permute-start.23 = (bf16[192,768]{1,0:T(8,128)(2,1)}, bf16[192,768]{1,0:T(8,128)(2,1)S(1)}, u32[]{:S(2)}, u32[]{:S(2)}) collective-permute-start(bf16[192,768]{1,0:T(8,128)(2,1)} %get-tuple-element.148), channel_id=1, source_target_pairs={{0,3},{1,2},{2,1},{3,0},{4,7},{5,6},{6,5},{7,4},{8,11},{9,10},{10,... | collective-permute-start | bytes 884744 | tf_op jit(solution)/shard_map/ppermute | solution.py:49
  203.8 5.9 %collective-permute-start.30 = (bf16[480,768]{1,0:T(8,128)(2,1)}, bf16[480,768]{1,0:T(8,128)(2,1)S(1)}, u32[]{:S(2)}, u32[]{:S(2)}) collective-permute-start(bf16[480,768]{1,0:T(8,128)(2,1)} %get-tuple-element.156), channel_id=1, source_target_pairs={{0,1},{1,0},{2,3},{3,2},{16,17},{17,16},{18,19},{19,18},{4,5},{5,4... | collective-permute-start | bytes 2211848 | tf_op jit(solution)/shard_map/ppermute | solution.py:49
  205.9 11.5 %collective-permute-start.27 = (bf16[240,768]{1,0:T(8,128)(2,1)S(1)}, bf16[240,768]{1,0:T(8,128)(2,1)S(1)}, u32[]{:S(2)}, u32[]{:S(2)}) collective-permute-start(bf16[240,768]{1,0:T(8,128)(2,1)S(1)} %pad_maximum_fusion.4), channel_id=1, source_target_pairs={{0,2},{1,3},{2,0},{3,1},{16,18},{17,19},{18,16},{19,17},{4,6},{5,7... | collective-permute-start | bytes 1105928 | tf_op jit(solution)/shard_map/ppermute | solution.py:49
  206.5 18.5 %collective-permute-start.28 = (bf16[240,768]{1,0:T(8,128)(2,1)S(1)}, bf16[240,768]{1,0:T(8,128)(2,1)S(1)}, u32[]{:S(2)}, u32[]{:S(2)}) collective-permute-start(bf16[240,768]{1,0:T(8,128)(2,1)S(1)} %pad_maximum_fusion.5), channel_id=1, source_target_pairs={{0,16},{1,17},{2,18},{3,19},{16,0},{17,1},{18,2},{19,3},{4,20},{5,... | collective-permute-start | bytes 1105928 | tf_op jit(solution)/shard_map/ppermute | solution.py:49
  206.7 18.4 %collective-permute-start.29 = (bf16[240,768]{1,0:T(8,128)(2,1)S(1)}, bf16[240,768]{1,0:T(8,128)(2,1)S(1)}, u32[]{:S(2)}, u32[]{:S(2)}) collective-permute-start(bf16[240,768]{1,0:T(8,128)(2,1)S(1)} %pad_maximum_fusion.6), channel_id=1, source_target_pairs={{0,18},{1,19},{2,16},{3,17},{16,2},{17,3},{18,0},{19,1},{4,22},{5,... | collective-permute-start | bytes 1105928 | tf_op jit(solution)/shard_map/ppermute | solution.py:49
  225.9 17.7 %collective-permute-start.31 = (bf16[240,768]{1,0:T(8,128)(2,1)S(1)}, bf16[240,768]{1,0:T(8,128)(2,1)S(1)}, u32[]{:S(2)}, u32[]{:S(2)}) collective-permute-start(bf16[240,768]{1,0:T(8,128)(2,1)S(1)} %pad_maximum_fusion.7), channel_id=1, source_target_pairs={{0,2},{1,3},{2,0},{3,1},{16,18},{17,19},{18,16},{19,17},{4,6},{5,7... | collective-permute-start | bytes 1105928 | tf_op jit(solution)/shard_map/ppermute | solution.py:49
  227.5 17.5 %collective-permute-start.32 = (bf16[240,768]{1,0:T(8,128)(2,1)S(1)}, bf16[240,768]{1,0:T(8,128)(2,1)S(1)}, u32[]{:S(2)}, u32[]{:S(2)}) collective-permute-start(bf16[240,768]{1,0:T(8,128)(2,1)S(1)} %pad_maximum_fusion.8), channel_id=1, source_target_pairs={{0,16},{1,17},{2,18},{3,19},{16,0},{17,1},{18,2},{19,3},{4,20},{5,... | collective-permute-start | bytes 1105928 | tf_op jit(solution)/shard_map/ppermute | solution.py:49
  227.9 17.1 %collective-permute-start.33 = (bf16[240,768]{1,0:T(8,128)(2,1)S(1)}, bf16[240,768]{1,0:T(8,128)(2,1)S(1)}, u32[]{:S(2)}, u32[]{:S(2)}) collective-permute-start(bf16[240,768]{1,0:T(8,128)(2,1)S(1)} %pad_maximum_fusion.9), channel_id=1, source_target_pairs={{0,18},{1,19},{2,16},{3,17},{16,2},{17,3},{18,0},{19,1},{4,22},{5,... | collective-permute-start | bytes 1105928 | tf_op jit(solution)/shard_map/ppermute | solution.py:49
  255.7 267.0 %reduce-scatter.3.cloned.1.call-start = ((), (), s32[]{:S(2)}) async-start(), calls=%async_computation.4 | async-start | bytes 5898240 | tf_op jit(solution)/shard_map/reduce_scatter | solution.py:1000
  277.4 24.7 %collective-permute-start.35 = (bf16[240,768]{1,0:T(8,128)(2,1)S(1)}, bf16[240,768]{1,0:T(8,128)(2,1)S(1)}, u32[]{:S(2)}, u32[]{:S(2)}) collective-permute-start(bf16[240,768]{1,0:T(8,128)(2,1)S(1)} %pad_maximum_fusion.10), channel_id=1, source_target_pairs={{0,2},{1,3},{2,0},{3,1},{16,18},{17,19},{18,16},{19,17},{4,6},{5,7... | collective-permute-start | bytes 1105928 | tf_op jit(solution)/shard_map/ppermute | solution.py:49
  278.9 23.2 %collective-permute-start.36 = (bf16[240,768]{1,0:T(8,128)(2,1)S(1)}, bf16[240,768]{1,0:T(8,128)(2,1)S(1)}, u32[]{:S(2)}, u32[]{:S(2)}) collective-permute-start(bf16[240,768]{1,0:T(8,128)(2,1)S(1)} %pad_maximum_fusion.11), channel_id=1, source_target_pairs={{0,16},{1,17},{2,18},{3,19},{16,0},{17,1},{18,2},{19,3},{4,20},{5,... | collective-permute-start | bytes 1105928 | tf_op jit(solution)/shard_map/ppermute | solution.py:49
  280.5 21.7 %collective-permute-start.37 = (bf16[240,768]{1,0:T(8,128)(2,1)S(1)}, bf16[240,768]{1,0:T(8,128)(2,1)S(1)}, u32[]{:S(2)}, u32[]{:S(2)}) collective-permute-start(bf16[240,768]{1,0:T(8,128)(2,1)S(1)} %pad_maximum_fusion.12), channel_id=1, source_target_pairs={{0,18},{1,19},{2,16},{3,17},{16,2},{17,3},{18,0},{19,1},{4,22},{5,... | collective-permute-start | bytes 1105928 | tf_op jit(solution)/shard_map/ppermute | solution.py:49
  304.8 11.5 %collective-permute-start.39 = (bf16[240,768]{1,0:T(8,128)(2,1)S(1)}, bf16[240,768]{1,0:T(8,128)(2,1)S(1)}, u32[]{:S(2)}, u32[]{:S(2)}) collective-permute-start(bf16[240,768]{1,0:T(8,128)(2,1)S(1)} %pad_maximum_fusion.13), channel_id=1, source_target_pairs={{0,2},{1,3},{2,0},{3,1},{16,18},{17,19},{18,16},{19,17},{4,6},{5,7... | collective-permute-start | bytes 1105928 | tf_op jit(solution)/shard_map/ppermute | solution.py:49
  306.4 18.3 %collective-permute-start.40 = (bf16[240,768]{1,0:T(8,128)(2,1)S(1)}, bf16[240,768]{1,0:T(8,128)(2,1)S(1)}, u32[]{:S(2)}, u32[]{:S(2)}) collective-permute-start(bf16[240,768]{1,0:T(8,128)(2,1)S(1)} %pad_maximum_fusion.14), channel_id=1, source_target_pairs={{0,16},{1,17},{2,18},{3,19},{16,0},{17,1},{18,2},{19,3},{4,20},{5,... | collective-permute-start | bytes 1105928 | tf_op jit(solution)/shard_map/ppermute | solution.py:49
  308.0 16.7 %collective-permute-start.41 = (bf16[240,768]{1,0:T(8,128)(2,1)S(1)}, bf16[240,768]{1,0:T(8,128)(2,1)S(1)}, u32[]{:S(2)}, u32[]{:S(2)}) collective-permute-start(bf16[240,768]{1,0:T(8,128)(2,1)S(1)} %pad_maximum_fusion.15), channel_id=1, source_target_pairs={{0,18},{1,19},{2,16},{3,17},{16,2},{17,3},{18,0},{19,1},{4,22},{5,... | collective-permute-start | bytes 1105928 | tf_op jit(solution)/shard_map/ppermute | solution.py:49
  338.1 6.8 %collective-permute-start.42 = (bf16[192,768]{1,0:T(8,128)(2,1)}, bf16[192,768]{1,0:T(8,128)(2,1)}, u32[]{:S(2)}, u32[]{:S(2)}) collective-permute-start(bf16[192,768]{1,0:T(8,128)(2,1)} %get-tuple-element.193), channel_id=1, source_target_pairs={{0,1},{1,0},{2,3},{3,2},{4,5},{5,4},{6,7},{7,6},{8,9},{9,8},{10,11... | collective-permute-start | bytes 884744 | tf_op jit(solution)/shard_map/ppermute | solution.py:49
  338.6 10.2 %collective-permute-start.43 = (bf16[192,768]{1,0:T(8,128)(2,1)}, bf16[192,768]{1,0:T(8,128)(2,1)}, u32[]{:S(2)}, u32[]{:S(2)}) collective-permute-start(bf16[192,768]{1,0:T(8,128)(2,1)} %get-tuple-element.194), channel_id=1, source_target_pairs={{0,2},{1,3},{2,0},{3,1},{4,6},{5,7},{6,4},{7,5},{8,10},{9,11},{10,... | collective-permute-start | bytes 884744 | tf_op jit(solution)/shard_map/ppermute | solution.py:49
  339.6 13.6 %collective-permute-start.44 = (bf16[192,768]{1,0:T(8,128)(2,1)S(1)}, bf16[192,768]{1,0:T(8,128)(2,1)}, u32[]{:S(2)}, u32[]{:S(2)}) collective-permute-start(bf16[192,768]{1,0:T(8,128)(2,1)S(1)} %copy-done.38), channel_id=1, source_target_pairs={{0,3},{1,2},{2,1},{3,0},{4,7},{5,6},{6,5},{7,4},{8,11},{9,10},{10,... | collective-permute-start | bytes 884744 | tf_op jit(solution)/shard_map/ppermute | solution.py:49
  406.5 5.1 collective-permute-start.47
  406.6 6.7 %collective-permute-start.48 = (bf16[768,768]{1,0:T(8,128)(2,1)}, bf16[768,768]{1,0:T(8,128)(2,1)S(1)}, u32[]{:S(2)}, u32[]{:S(2)}) collective-permute-start(bf16[768,768]{1,0:T(8,128)(2,1)} %get-tuple-element.211), channel_id=1, source_target_pairs={{0,1},{1,0},{2,3},{3,2},{4,5},{5,4},{6,7},{7,6},{8,9},{9,8},{10,11... | collective-permute-start | bytes 3538952 | tf_op jit(solution)/shard_map/ppermute | solution.py:49
  416.5 19.2 %collective-permute-start.49 = (bf16[2,768,768]{2,1,0:T(8,128)(2,1)}, bf16[2,768,768]{2,1,0:T(8,128)(2,1)}, u32[]{:S(2)}, u32[]{:S(2)}) collective-permute-start(bf16[2,768,768]{2,1,0:T(8,128)(2,1)} %get-tuple-element.212), channel_id=1, source_target_pairs={{0,1},{1,0},{2,3},{3,2},{4,5},{5,4},{6,7},{7,6},{8,9},{9,8},{10,11... | collective-permute-start | bytes 7077896 | tf_op jit(solution)/shard_map/ppermute | solution.py:49
  416.8 16.5 %collective-permute-start.51 = (bf16[384,768]{1,0:T(8,128)(2,1)}, bf16[384,768]{1,0:T(8,128)(2,1)}, u32[]{:S(2)}, u32[]{:S(2)}) collective-permute-start(bf16[384,768]{1,0:T(8,128)(2,1)} %slice.268), channel_id=1, source_target_pairs={{0,2},{1,3},{2,0},{3,1},{4,6},{5,7},{6,4},{7,5},{8,10},{9,11},{10,... | collective-permute-start | bytes 1769480 | tf_op jit(solution)/shard_map/ppermute | solution.py:49
  419.0 43.6 %collective-permute-start.53 = (bf16[192,768]{0,1:T(8,128)(2,1)}, bf16[192,768]{0,1:T(8,128)(2,1)S(1)}, u32[]{:S(2)}, u32[]{:S(2)}) collective-permute-start(bf16[192,768]{0,1:T(8,128)(2,1)} %fusion.19), channel_id=1, source_target_pairs={{0,2},{1,3},{2,0},{3,1},{4,6},{5,7},{6,4},{7,5},{8,10},{9,11},{10,... | collective-permute-start | bytes 884744 | tf_op jit(solution)/shard_map/ppermute | solution.py:49
  420.1 45.9 %collective-permute-start.50 = (bf16[384,768]{1,0:T(8,128)(2,1)S(1)}, bf16[384,768]{1,0:T(8,128)(2,1)}, u32[]{:S(2)}, u32[]{:S(2)}) collective-permute-start(bf16[384,768]{1,0:T(8,128)(2,1)S(1)} %slice.267), channel_id=1, source_target_pairs={{0,2},{1,3},{2,0},{3,1},{4,6},{5,7},{6,4},{7,5},{8,10},{9,11},{10,... | collective-permute-start | bytes 1769480 | tf_op jit(solution)/shard_map/ppermute | solution.py:49
  438.4 46.5 %collective-permute-start.56 = (bf16[768,768]{1,0:T(8,128)(2,1)}, bf16[768,768]{1,0:T(8,128)(2,1)}, u32[]{:S(2)}, u32[]{:S(2)}) collective-permute-start(bf16[768,768]{1,0:T(8,128)(2,1)} %fusion.4), channel_id=1, source_target_pairs={{0,2},{1,3},{2,0},{3,1},{4,6},{5,7},{6,4},{7,5},{8,10},{9,11},{10,... | collective-permute-start | bytes 3538952 | tf_op jit(solution)/shard_map/ppermute | solution.py:49
  439.4 23.3 %collective-permute-start.52 = (bf16[384,768]{1,0:T(8,128)(2,1)}, bf16[384,768]{1,0:T(8,128)(2,1)}, u32[]{:S(2)}, u32[]{:S(2)}) collective-permute-start(bf16[384,768]{1,0:T(8,128)(2,1)} %fusion.7), channel_id=1, source_target_pairs={{0,12},{4,0},{8,4},{12,8},{1,13},{5,1},{9,5},{13,9},{2,14},{6,2},{... | collective-permute-start | bytes 1769480 | tf_op jit(solution)/shard_map/ppermute | solution.py:53
  465.7 15.5 %collective-permute-start.55 = (bf16[4,96,777]{2,1,0:T(8,128)(2,1)}, bf16[4,96,777]{2,1,0:T(8,128)(2,1)}, u32[]{:S(2)}, u32[]{:S(2)}) collective-permute-start(bf16[4,96,777]{2,1,0:T(8,128)(2,1)} %get-tuple-element.289), channel_id=1, source_target_pairs={{0,16},{16,0},{1,17},{17,1},{2,18},{18,2},{3,19},{19,3},{4,20},{20... | collective-permute-start | bytes 1790216 | tf_op jit(solution)/shard_map/ppermute | solution.py:49
  468.9 16.0 %collective-permute-start.54 = (bf16[384,768]{1,0:T(8,128)(2,1)}, bf16[384,768]{1,0:T(8,128)(2,1)}, u32[]{:S(2)}, u32[]{:S(2)}) collective-permute-start(bf16[384,768]{1,0:T(8,128)(2,1)} %fusion.9), channel_id=1, source_target_pairs={{0,12},{4,0},{8,4},{12,8},{1,13},{5,1},{9,5},{13,9},{2,14},{6,2},{... | collective-permute-start | bytes 1769480 | tf_op jit(solution)/shard_map/ppermute | solution.py:53
  469.8 21.7 %collective-permute-start.57 = (bf16[384,768]{1,0:T(8,128)(2,1)}, bf16[384,768]{1,0:T(8,128)(2,1)}, u32[]{:S(2)}, u32[]{:S(2)}) collective-permute-start(bf16[384,768]{1,0:T(8,128)(2,1)} %slice.266), channel_id=1, source_target_pairs={{0,2},{1,3},{2,0},{3,1},{4,6},{5,7},{6,4},{7,5},{8,10},{9,11},{10,... | collective-permute-start | bytes 1769480 | tf_op jit(solution)/shard_map/ppermute | solution.py:49
  485.0 19.1 %collective-permute-start.62 = (bf16[96,777]{0,1:T(8,128)(2,1)S(1)}, bf16[96,777]{0,1:T(8,128)(2,1)S(1)}, u32[]{:S(2)}, u32[]{:S(2)}) collective-permute-start(bf16[96,777]{0,1:T(8,128)(2,1)S(1)} %get-tuple-element.295), channel_id=1, source_target_pairs={{0,12},{4,8},{8,4},{12,0},{1,13},{5,9},{9,5},{13,1},{2,14},{6,10},... | collective-permute-start | bytes 447560 | tf_op jit(solution)/shard_map/ppermute | solution.py:49
  487.7 16.4 %collective-permute-start.61 = (bf16[96,777]{0,1:T(8,128)(2,1)S(1)}, bf16[96,777]{0,1:T(8,128)(2,1)S(1)}, u32[]{:S(2)}, u32[]{:S(2)}) collective-permute-start(bf16[96,777]{0,1:T(8,128)(2,1)S(1)} %get-tuple-element.296), channel_id=1, source_target_pairs={{0,8},{4,12},{8,0},{12,4},{1,9},{5,13},{9,1},{13,5},{2,10},{6,14},... | collective-permute-start | bytes 447560 | tf_op jit(solution)/shard_map/ppermute | solution.py:49
  487.7 16.4 %collective-permute-start.60 = (bf16[96,777]{0,1:T(8,128)(2,1)S(1)}, bf16[96,777]{0,1:T(8,128)(2,1)S(1)}, u32[]{:S(2)}, u32[]{:S(2)}) collective-permute-start(bf16[96,777]{0,1:T(8,128)(2,1)S(1)} %get-tuple-element.294), channel_id=1, source_target_pairs={{0,4},{4,0},{8,12},{12,8},{1,5},{5,1},{9,13},{13,9},{2,6},{6,2},{1... | collective-permute-start | bytes 447560 | tf_op jit(solution)/shard_map/ppermute | solution.py:49
  492.9 34.6 %collective-permute-start.58 = (bf16[384,768]{1,0:T(8,128)(2,1)S(1)}, bf16[384,768]{1,0:T(8,128)(2,1)}, u32[]{:S(2)}, u32[]{:S(2)}) collective-permute-start(bf16[384,768]{1,0:T(8,128)(2,1)S(1)} %fusion.6), channel_id=1, source_target_pairs={{0,12},{1,13},{4,0},{5,1},{8,4},{9,5},{12,8},{13,9},{16,28},{17,29... | collective-permute-start | bytes 1769480 | tf_op jit(solution)/shard_map/ppermute | solution.py:1073
  502.8 22.8 %collective-permute-start.59 = (bf16[384,768]{1,0:T(8,128)(2,1)S(1)}, bf16[384,768]{1,0:T(8,128)(2,1)}, u32[]{:S(2)}, u32[]{:S(2)}) collective-permute-start(bf16[384,768]{1,0:T(8,128)(2,1)S(1)} %fusion.6), channel_id=1, source_target_pairs={{2,12},{3,13},{6,0},{7,1},{10,4},{11,5},{14,8},{15,9},{18,28},{19,... | collective-permute-start | bytes 1769480 | tf_op jit(solution)/shard_map/ppermute | solution.py:1073
  505.9 14.0 %collective-permute-start.64 = (bf16[96,10]{0,1:T(8,128)(2,1)S(1)}, bf16[96,10]{0,1:T(8,128)(2,1)S(1)}, u32[]{:S(2)}, u32[]{:S(2)}) collective-permute-start(bf16[96,10]{0,1:T(8,128)(2,1)S(1)} %fusion.22), channel_id=1, source_target_pairs={{0,2},{1,3},{2,0},{3,1},{4,6},{5,7},{6,4},{7,5},{8,10},{9,11},{10,... | collective-permute-start | bytes 5768 | tf_op jit(solution)/shard_map/ppermute | solution.py:49
  507.4 12.6 %collective-permute-start.63 = (bf16[96,10]{0,1:T(8,128)(2,1)S(1)}, bf16[96,10]{0,1:T(8,128)(2,1)S(1)}, u32[]{:S(2)}, u32[]{:S(2)}) collective-permute-start(bf16[96,10]{0,1:T(8,128)(2,1)S(1)} %fusion.22), channel_id=1, source_target_pairs={{0,1},{1,0},{2,3},{3,2},{4,5},{5,4},{6,7},{7,6},{8,9},{9,8},{10,11... | collective-permute-start | bytes 5768 | tf_op jit(solution)/shard_map/ppermute | solution.py:49
  (46 other events, 296.1 us)
Sparse Core Ops, SparseCore 0:
  73.3 101.4 all-gather.2
  176.4 87.8 all-gather.4
  266.7 88.0 reduce-scatter.4
  356.9 85.7 reduce-scatter.2

commit v5 on v4

--- a/solution.py
+++ b/solution.py
@@ -167,14 +167,14 @@
     def cont_mask(scores):
         return jnp.concatenate([causal(scores[:CLEN], CLEN), scores[CLEN:]], axis=0)
 
-    @pl.loop(0, prompts)
+    @pl.loop(0, prompts, unroll=2)
     def _(prompt):
         own, far = prompt_chunks(prompt)
         attend(0, prompt, own, own, far, prompt_mask)
 
     first = 1 + prompts * 2 * per
 
-    @pl.loop(0, conts)
+    @pl.loop(0, conts, unroll=2)
     def _(cont):
         own = [info[first + cont]]
         near, far = prompt_chunks(info[first + conts + cont])
@@ -285,8 +285,9 @@
 def attend_backward_kernel(sizes, info, query, lse_prompt, lse_cont, local, *rest):
     count_remote = sizes[2] - 1
     remote, rest = rest[:count_remote], rest[count_remote:]
-    query_weight, pair_weight, *grads = rest[:6]
-    grad_query, grad_local, *rest, grad, sum_local, sum_remote = rest[6:]
+    query_weight, pair_weight, *rest = rest
+    grads, mixed, rest = rest[:4], rest[4:8], rest[8:]
+    grad_query, grad_local, *rest, grad, centre, sum_local, sum_remote = rest
     grad_remote, rest = rest[:count_remote], rest[count_remote:]
     *rest, keep_local, send_local = rest
     keep_remote, send_remote = rest[: len(rest) // 2], rest[len(rest) // 2 :]
@@ -294,8 +295,14 @@
     width = query.shape[0]
     pad = (-width) % 128
     each = grads[0].shape[1]
-    for place, one in enumerate(grads):
-        grad[:, place * each : (place + 1) * each] = one[...]
+    for place, (one, result) in enumerate(zip(grads, mixed)):
+        columns = slice(place * each, (place + 1) * each)
+        grad[:, columns] = one[...]
+        product = one[...].astype(F32) * result[...].astype(F32)
+        for head in range(width // HD):
+            centre[head : head + 1, columns] = jnp.sum(
+                product[head * HD : (head + 1) * HD], axis=0, keepdims=True
+            )
 
     def attend(kind, index, own, near, far, mask):
         count = len(own) * CHUNK
@@ -305,8 +312,9 @@
         keys = key_lanes(block, width)
         weights = jnp.exp(mask(dot_plain(keys, query_spread)) - lse[kind][index])
         slopes = dot_plain(value_lanes(block, width), grad_spread)
-        centre = jnp.sum(weights * slopes, axis=0, keepdims=True)
-        grad_scores = low(weights * (slopes - centre))
+        middle = load_lanes(centre, own)
+        middle = jnp.concatenate([middle[head : head + 1] for head in range(width // HD)], axis=1)
+        grad_scores = low(weights * (slopes - middle))
         flip = keys.T
         for head in range(width // HD):
             group = slice(head * count, (head + 1) * count)
@@ -381,7 +389,7 @@
 
 
 def attend_backward(
-    sizes, info, query, lse_prompt, lse_cont, local, remote, query_weight, pair_weight, grads
+    sizes, info, query, lse_prompt, lse_cont, local, remote, query_weight, pair_weight, grads, mixed
 ):
     pairs = [local] + list(remote)
     remote_rows = 2 * len(remote) if len(remote) <= 4 else 0
@@ -397,17 +405,18 @@
             both,
             both,
         ),
-        in_specs=[SM] + [VM] * (5 + len(pairs) + len(grads)),
+        in_specs=[SM] + [VM] * (5 + len(pairs) + 2 * len(grads)),
         out_specs=(VM,) * (3 + len(pairs) + remote_rows),
         scratch_shapes=[
             pltpu.VMEM(query.shape, BF16),
+            pltpu.VMEM((8, query.shape[1]), F32),
             pltpu.VMEM(local.shape, F32),
             pltpu.VMEM((count,) + remote[0].shape, F32),
         ],
         compiler_params=ROOM,
         cost_estimate=attend_cost(40, sizes, query.shape[0] // HD),
         name="attend_backward",
-    )(info, query, lse_prompt, lse_cont, *pairs, query_weight, pair_weight, *grads)
+    )(info, query, lse_prompt, lse_cont, *pairs, query_weight, pair_weight, *grads, *mixed)
 
 
 def rows_remote_kernel(grad_pairs, pair_weight, keep, send):
@@ -470,15 +479,16 @@
     )(grad_query, *pairs, *rows)
 
 
-def final_kernel(first, tokens, gains, grad_middle, kept, beside, across, own, far, out):
+def final_kernel(first, tokens, gains, grad_middle, kept, beside, one, two, own, far, out):
     unit, factor = rms_unit(tokens[...].astype(F32))
-    rows = kept[0].astype(F32) + beside[0].astype(F32) + across[...].astype(F32)
+    across = jnp.concatenate([one[one.shape[0] + two.shape[0] - kept.shape[1] :, :], two[...]], axis=0)
+    rows = kept[0].astype(F32) + beside[0].astype(F32) + across.astype(F32)
     ring = jnp.concatenate([own[...], far[...]], axis=0).astype(F32)
     rows = plain_order(rows + jnp.where(first[0] == 0, ring, 0.0))
     out[...] = rms_backward(rows, unit, factor, gains[0:1, :]) + grad_middle[...]
 
 
-def final_rows(side, tokens, gains, grad_middle, kept, beside, across, own, far):
+def final_rows(side, tokens, gains, grad_middle, kept, beside, one, two, own, far):
     rows, width = tokens.shape
     last = pl.BlockSpec((1, rows, width), lambda at: (1, 0, 0))
     half = pl.BlockSpec((rows // 2, width), lambda at: (0, 0))
@@ -493,7 +503,8 @@
             whole,
             last,
             last,
-            whole,
+            pl.BlockSpec(one.shape, lambda at: (0, 0)),
+            pl.BlockSpec(two.shape, lambda at: (0, 0)),
             half,
             half,
         ],
@@ -501,7 +512,7 @@
         out_shape=shape((rows, width), F32),
         compiler_params=ROOM,
         name="final_rows",
-    )(side, tokens, gains, grad_middle, kept, beside, across, own, far)
+    )(side, tokens, gains, grad_middle, kept, beside, one, two, own, far)
 
 
 def slot_places(chosen, priority, first, expert_count, capacity):
@@ -704,23 +715,16 @@
     slope[...] = low(half + bent)
 
 
-def expert_out_kernel(hidden, down, even, odd, total):
-    step = pl.program_id(0)
-    part = dot_plain(hidden[...], down[...])
-
-    @pl.when(step == 0)
+def expert_out_kernel(hidden, down, even, odd):
+    part = low(dot_plain(hidden[...], down[...]))
+
+    @pl.when(pl.program_id(0) < 2)
     def _():
-        total[...] = part
-
-    @pl.when(step > 0)
+        even[...] = part
+
+    @pl.when(pl.program_id(0) >= 2)
     def _():
-        total[...] += part
-
-    @pl.when(step == pl.num_programs(0) - 1)
-    def _():
-        half = even.shape[0]
-        even[...] = low(total[:half])
-        odd[...] = low(total[half:])
+        odd[...] = part
 
 
 def expert_down_kernel(capacity, *refs):
@@ -796,14 +800,18 @@
 def expert_out(hidden, down):
     slots, units = hidden.shape
     width = down.shape[1]
-    block = whole_spec((slots // 2, width))
     return pl.pallas_call(
         expert_out_kernel,
-        grid=(units // UNITS,),
-        in_specs=[column_spec(slots), row_spec(width)],
-        out_specs=(block, block),
+        grid=(4,),
+        in_specs=[
+            pl.BlockSpec((slots // 4, units), lambda at: (at, 0)),
+            pl.BlockSpec((units, width), lambda at: (0, 0), pipeline_mode=pl.Buffered(1)),
+        ],
+        out_specs=(
+            pl.BlockSpec((slots // 4, width), lambda at: (jnp.minimum(at, 1), 0)),
+            pl.BlockSpec((slots // 4, width), lambda at: (jnp.maximum(at - 2, 0), 0)),
+        ),
         out_shape=(shape((slots // 2, width)), shape((slots // 2, width))),
-        scratch_shapes=[pltpu.VMEM((slots, width), F32)],
         compiler_params=ROOM,
         cost_estimate=expert_cost(1, slots, width, units),
         name="expert_out",
@@ -963,6 +971,7 @@
     sizes = (prompts_here, conts_here, ctx_count, per)
 
     *attended, lse_prompt, lse_cont = attend_forward(sizes, info, query, local, remote)
+    mixed = attended
     attended = xor_exchange(attended, "tp", tp_count)
     place = slot_places(expert_ids[:, 0], slot_order[0], group_index, expert_count, capacity)
 
@@ -1007,9 +1016,7 @@
     )
     grad_near = xor_exchange(grad_near, "tp", tp_count)
     proj_keep, proj_send = proj_grad(grad_split, attended)
-    proj_chip = proj_keep + beside(proj_send).astype(F32)
-    proj_message = low(proj_chip[1])
-    grad_near, proj_message = lax.optimization_barrier((grad_near, proj_message))
+    grad_near, proj_keep, proj_send = lax.optimization_barrier((grad_near, proj_keep, proj_send))
     grad_query, grad_local, *grads = attend_backward(
         sizes,
         info,
@@ -1021,6 +1028,7 @@
         query_weight,
         pair_weight,
         grad_near,
+        mixed,
     )
     count = ctx_count - 1
     grad_remote, (*remote_rows, local_keep, local_send) = grads[:count], grads[count:]
@@ -1029,42 +1037,56 @@
     else:
         remote_rows = [rows_remote(one, pair_weight) for one in grad_remote]
 
-    pieces = []
-    messages = []
-    for keep, send in remote_rows[::-1]:
+    remote_rows = remote_rows[::-1]
+
+    def chip_rows(keep, send):
         chip = keep.astype(F32) + beside(send).astype(F32)
-        messages.append(low(chip[half_rows:]))
-        pieces.append(chip[:half_rows])
-    local_send, proj_message, messages = lax.optimization_barrier(
-        (local_send, proj_message, messages)
-    )
-    pieces = [piece + across(message).astype(F32) for piece, message in zip(pieces, messages)]
-    running = low(pieces[0])
-    local_send = beside(local_send)
-    far_message = low(local_keep[0].astype(F32) + local_send[0].astype(F32))
-    far_rows = across(far_message)
-    proj_far = across(proj_message)
-    grad_pairs, running, far_message = lax.optimization_barrier(
-        ([grad_local, *grad_remote], running, far_message)
-    )
-    qkv_part = qkv_grad(grad_query, grad_pairs, rows)
-    moved = ring_step(running, "ctx", ctx_count, -1)
-    moved, proj_far, qkv_part = lax.optimization_barrier((moved, proj_far, qkv_part))
-
-    proj_sum = proj_chip[0] + proj_far.astype(F32)
-    early = jnp.concatenate([low(proj_sum), low(router_part), low(gain_two[:1])], axis=0).T
-    packed = jnp.concatenate([qkv_part, early], axis=1)
-    packed = packed.reshape(dp_count, ctx_count, shard_rows, -1)
+        return chip[:half_rows], low(chip[half_rows:])
 
     def scatter_sum(values, axis, size, me):
         parts = xor_exchange([pick(values, me ^ k) for k in range(size)], axis, size)
         return add_all([piece.astype(F32) for piece in parts])
 
-    for piece in pieces[1:-1]:
-        moved = ring_step(low(piece + moved.astype(F32)), "ctx", ctx_count, -1)
-    summed = low(scatter_sum(packed, "dp", dp_count, dp_index))
-    moved, summed, far_rows = lax.optimization_barrier((moved, summed, far_rows))
-    running = low(pieces[-1] + moved.astype(F32))
+    piece, message = chip_rows(*remote_rows[0])
+    following = chip_rows(*remote_rows[1])
+    near = across(message)
+    grad_pairs, message = lax.optimization_barrier(([grad_local, *grad_remote], message))
+    qkv_part = qkv_grad(grad_query, grad_pairs, rows)
+    near, qkv_part, following, local_send, proj_send, remote_rows[2:] = lax.optimization_barrier(
+        (near, qkv_part, following, local_send, proj_send, remote_rows[2:])
+    )
+    running = low(piece + near.astype(F32))
+    for place in range(1, count):
+        piece, message = following
+        message, running = lax.optimization_barrier((message, running))
+        moved = ring_step(running, "ctx", ctx_count, -1)
+        near = across(message)
+        if place < count - 1:
+            following = chip_rows(*remote_rows[place + 1])
+        if place == 1:
+            local_send = beside(local_send)
+            far_message = low(local_keep[0].astype(F32) + local_send[0].astype(F32))
+            first_rows = (tok_dev - local_width) // 2
+            proj_chip = proj_keep + beside(proj_send).astype(F32)
+            far_first = jnp.concatenate([low(proj_chip[1]), far_message[:first_rows]], axis=0)
+            near, far_first = lax.optimization_barrier((near, far_first))
+            far_first = across(far_first)
+            moved, near, far_first, following = lax.optimization_barrier(
+                (moved, near, far_first, following)
+            )
+            proj_sum = proj_chip[0] + far_first[:local_width].astype(F32)
+            early = jnp.concatenate([low(proj_sum), low(router_part), low(gain_two[:1])], axis=0)
+            packed = jnp.concatenate([qkv_part, early.T], axis=1)
+            packed = packed.reshape(dp_count, ctx_count, shard_rows, -1)
+        if place == count - 1:
+            summed = low(scatter_sum(packed, "dp", dp_count, dp_index))
+            near, far_second = lax.optimization_barrier((near, far_message[first_rows:]))
+            far_second = across(far_second)
+            moved, near, summed, grad_up, grad_down = lax.optimization_barrier(
+                (moved, near, summed, grad_up, grad_down)
+            )
+        running = low(piece + near.astype(F32) + moved.astype(F32))
+    running, summed = lax.optimization_barrier((running, summed))
     hops = [[], []]
     for ctx_from in range(ctx_count):
         for tp_from in range(tp_count):
@@ -1072,7 +1094,6 @@
             hops[tp_from >> 1].append((ctx_from * tp_count + tp_from, target))
     own_rows, other_rows = (lax.ppermute(running, ("ctx", "tp"), hop) for hop in hops)
     summed = scatter_sum(summed, "ctx", ctx_count, ctx_index)
-    other_rows, grad_up, grad_down = lax.optimization_barrier((other_rows, grad_up, grad_down))
     grad_tokens = final_rows(
         side.astype(jnp.int32).reshape(1),
         tokens,
@@ -1080,21 +1101,21 @@
         grad_middle,
         local_keep,
         local_send,
-        far_rows,
+        far_first,
+        far_second,
         own_rows,
         other_rows,
     )
-
-    def sum_tp(values):
-        moved = xor_exchange([low(values)] * tp_count, "tp", tp_count)
-        return values + add_all([piece.astype(F32) for piece in moved[1:]])
 
     qkv_width = 3 * local_width
     grad_qkv = summed[:, :qkv_width].reshape(shard_rows, 3, local_width).transpose(1, 0, 2)
     grad_proj = summed[:, qkv_width : qkv_width + local_width].T
     gain_range = lax.dynamic_slice_in_dim(gains[0], shard_index * shard_rows, shard_rows)
     gain_one = jnp.sum(qkv_weight.astype(F32) * grad_qkv, axis=(0, 2))
-    small = sum_tp(jnp.concatenate([summed[:, qkv_width + local_width :], gain_one[:, None]], axis=1))
+    small = jnp.concatenate([summed[:, qkv_width + local_width :], gain_one[:, None]], axis=1)
+    parts = xor_exchange([low(small)] * tp_count, "tp", tp_count)
+    parts, grad_tokens = lax.optimization_barrier((parts, grad_tokens))
+    small = small + add_all([part.astype(F32) for part in parts[1:]])
     grad_router = small[:, :expert_count]
     grad_gains = jnp.stack([small[:, expert_count + 1] / gain_range, small[:, expert_count]])
     return (output, grad_tokens, grad_gains, grad_qkv, grad_proj, grad_router, grad_up, grad_down)

time: 546 us -> 542 us (level)
  the two profiles are of different devices: /device:TPU:0 before, /device:TPU:25 now
where the time goes in v5:
time: 542 us; the launch traced here: 537 us
  Pallas kernels  197 us (36%)
  waiting for transfers between devices  180 us (33%)
  starting transfers between devices  79.6 us (15%)
  local copies, waits for them, and re-layouts  37.3 us (7%)
  other arithmetic  25.8 us (5%)
  between operations  15.1 us (3%)
    ppermute x59, waiting for transfers between devices, xor_swap(): lax.ppermute(value, axis, [(place, place ^ mask) for place in range(size)])  123 us
    ppermute x59, starting transfers between devices, xor_swap(): lax.ppermute(value, axis, [(place, place ^ mask) for place in range(size)])  73.7 us
    ppermute x5, waiting for transfers between devices, ring_step(): lax.ppermute(value, axis, [(place, (place + shift) % size) for place in r...  57.5 us
    pallas_call x1, Pallas kernels, attend_backward(): pl.pallas_call(functools.partial(attend_backward_kernel, sizes), out_shap...  47.1 us
    pallas_call x1, Pallas kernels, attend_forward(): pl.pallas_call(functools.partial(attend_forward_kernel, sizes), out_shape...  22.8 us
    pallas_call x1, Pallas kernels, expert_back(): pl.pallas_call(expert_back_kernel, grid=(units // UNITS,), in_specs=[whol...  21.2 us
    unnamed x106, local copies, waits for them, and re-layouts  17.2 us
    pallas_call x1, Pallas kernels, qkv_grad(): pl.pallas_call(functools.partial(qkv_grad_kernel, len(pairs)), out_shape=...  14.9 us
  transfers between devices with their start and end apart: 70, of which 27 were waited for; matrix products, arithmetic and copies ran while one was open for 10% of the time, Pallas kernels for 36%

profile of v5, /device:TPU:25, one launch (start us, length us, event | category | flops | bytes accessed | tf_op | source)
XLA Modules:
  0.0 536.6 jit_solution(3802787186331728231)
XLA Ops:
  7.2 3.0 normalize.1
  12.9 3.3 collective-permute-start.2
  16.2 8.6 %collective-permute-done.3.rest_3_.rest_7_ = bf16[384,768]{1,0:T(8,128)(2,1)} collective-permute-done((bf16[384,768]{1,0:T(8,128)(2,1)}, bf16[384,768]{1,0:T(8,128)(2,1)}, u32[]{:S(2)}, u32[]{:S(2)}) %collective-permute-start.3) | collective-permute-done | bytes 589856 | tf_op jit(solution)/shard_map/ppermute | solution.py:49
  24.7 2.0 fusion.34
  28.6 2.0 collective-permute-start.4
  30.8 9.1 %collective-permute-done.6 = bf16[1,4,96,776]{3,2,1,0:T(8,128)(2,1)S(1)} collective-permute-done((bf16[1,4,96,776]{3,2,1,0:T(8,128)(2,1)S(1)}, bf16[1,4,96,776]{3,2,1,0:T(8,128)(2,1)S(1)}, u32[]{:S(2)}, u32[]{:S(2)}) %collective-permute-start.6) | collective-permute-done | bytes 596000 | tf_op jit(solution)/shard_map/ppermute | solution.py:49
  40.3 5.4 %collective-permute-done.4.rest_0_.rest_10_ = bf16[384,768]{1,0:T(8,128)(2,1)} collective-permute-done((bf16[384,768]{1,0:T(8,128)(2,1)}, bf16[384,768]{1,0:T(8,128)(2,1)}, u32[]{:S(2)}, u32[]{:S(2)}) %collective-permute-start.4) | collective-permute-done | bytes 589856 | tf_op jit(solution)/shard_map/ppermute | solution.py:53
  45.7 10.2 %collective-permute-done.7.rest_0_.rest_14_ = bf16[384,768]{1,0:T(8,128)(2,1)} collective-permute-done((bf16[384,768]{1,0:T(8,128)(2,1)}, bf16[384,768]{1,0:T(8,128)(2,1)}, u32[]{:S(2)}, u32[]{:S(2)}) %collective-permute-start.7) | collective-permute-done | bytes 589856 | tf_op jit(solution)/shard_map/ppermute | solution.py:53
  56.0 16.2 %collective-permute-start.10 = (bf16[768,768]{1,0:T(8,128)(2,1)}, bf16[768,768]{1,0:T(8,128)(2,1)}, u32[]{:S(2)}, u32[]{:S(2)}) collective-permute-start(bf16[768,768]{1,0:T(8,128)(2,1)} %get-tuple-element.142.rest_0_.rest_4_), channel_id=1, source_target_pairs={{0,1},{1,0},{2,3},{3,2},{4,5},{5,4},{6,7},{7,6},{8,9},{9,8},{10,11... | collective-permute-start | bytes 3538952 | tf_op jit(solution)/shard_map/ppermute | solution.py:49
  76.8 11.7 %collective-permute-done.8.rest_1_.rest_11_ = bf16[384,768]{1,0:T(8,128)(2,1)} collective-permute-done((bf16[384,768]{1,0:T(8,128)(2,1)}, bf16[384,768]{1,0:T(8,128)(2,1)}, u32[]{:S(2)}, u32[]{:S(2)}) %collective-permute-start.8) | collective-permute-done | bytes 589856 | tf_op jit(solution)/shard_map/ppermute | solution.py:49
  91.3 1.8 collective-permute-start.13
  93.1 8.3 %project_local.1 = (bf16[192,3072]{1,0:T(8,128)(2,1)}, bf16[24,128,384]{2,1,0:T(8,128)(2,1)}) custom-call(bf16[768,192]{1,0:T(8,128)(2,1)} %get-tuple-element.319.query_weight.rest_3_, bf16[768,384]{1,0:T(8,128)(2,1)} %slice.224.pair_weight.rest_4_, bf16[768,768]{1,0:T(8,128)(2,1)} %get-tuple-element.142.rest_0_.rest_4_, ...), custom_call_target="tpu_custom_call" | custom-call | flops 2717908992 | bytes 10000000 | tf_op jit(solution)/shard_map/project_local/pallas_call | solution.py:219
  101.4 30.8 %collective-permute-done.9.rest_0_.rest_18_ = bf16[384,768]{1,0:T(8,128)(2,1)S(1)} collective-permute-done((bf16[384,768]{1,0:T(8,128)(2,1)}, bf16[384,768]{1,0:T(8,128)(2,1)S(1)}, u32[]{:S(2)}, u32[]{:S(2)}) %collective-permute-start.9) | collective-permute-done | bytes 589856 | tf_op jit(solution)/shard_map/ppermute | solution.py:53
  134.9 12.1 %collective-permute-done.18.rest_1_.rest_19_ = bf16[384,768]{1,0:T(8,128)(2,1)} collective-permute-done((bf16[384,768]{1,0:T(8,128)(2,1)S(1)}, bf16[384,768]{1,0:T(8,128)(2,1)}, u32[]{:S(2)}, u32[]{:S(2)}) %collective-permute-start.18) | collective-permute-done | bytes 589856 | tf_op jit(solution)/shard_map/ppermute | solution.py:49
  149.4 4.2 project_remote.3.rest_0_
  153.7 4.2 project_remote.4.rest_1_
  157.8 1.9 collective-permute-done.24
  161.7 4.2 project_remote.5.rest_2_
  165.9 22.8 %attend_forward.1 = (bf16[192,768]{1,0:T(8,128)(2,1)}, bf16[192,768]{1,0:T(8,128)(2,1)}, bf16[192,768]{1,0:T(8,128)(2,1)}, bf16[192,768]{1,0:T(8,128)(2,1)}, f32...) custom-call(s32[49]{0:T(128)} %pad_add_fusion.1.info, bf16[192,3072]{1,0:T(8,128)(2,1)} %get-tuple-element.157.query, ...), custom_call_target="tpu_custom_call" | custom-call | flops 9663676416 | bytes 10000000 | tf_op jit(solution)/shard_map/attend_forward/pallas_call | solution.py:375
  188.8 2.1 collective-permute-start.23
  194.8 1.9 slice_bitcast_fusion.4
  197.3 7.2 %collective-permute-done.23.rest_3_ = bf16[192,768]{1,0:T(8,128)(2,1)S(1)} collective-permute-done((bf16[192,768]{1,0:T(8,128)(2,1)}, bf16[192,768]{1,0:T(8,128)(2,1)S(1)}, u32[]{:S(2)}, u32[]{:S(2)}) %collective-permute-start.23) | collective-permute-done | bytes 294944 | tf_op jit(solution)/shard_map/ppermute | solution.py:49
  205.2 8.6 %middle_rows.1 = (bf16[480,768]{1,0:T(8,128)(2,1)}, bf16[480,768]{1,0:T(8,128)(2,1)}, bf16[480,768]{1,0:T(8,128)(2,1)}, bf16[480,768]{1,0:T(8,128)(2,1)}, f32[76...) custom-call(bf16[768,768]{1,0:T(8,128)(2,1)} %tokens.5, bf16[768,768]{1,0:T(8,128)(2,1)} %cotangent.5, ...), custom_call_target="tpu_custom_call" | custom-call | tf_op jit(solution)/shard_map/middle_rows/pallas_call | solution.py:572
  217.1 2.1 collective-permute-start.29
  219.2 7.3 %collective-permute-done.27.refs_2_ = bf16[240,768]{1,0:T(8,128)(2,1)S(1)} collective-permute-done((bf16[240,768]{1,0:T(8,128)(2,1)S(1)}, bf16[240,768]{1,0:T(8,128)(2,1)S(1)}, u32[]{:S(2)}, u32[]{:S(2)}) %collective-permute-start.27) | collective-permute-done | bytes 368672 | tf_op jit(solution)/shard_map/ppermute | solution.py:49
  226.5 7.7 %collective-permute-done.28.refs_3_ = bf16[240,768]{1,0:T(8,128)(2,1)S(1)} collective-permute-done((bf16[240,768]{1,0:T(8,128)(2,1)S(1)}, bf16[240,768]{1,0:T(8,128)(2,1)S(1)}, u32[]{:S(2)}, u32[]{:S(2)}) %collective-permute-start.28) | collective-permute-done | bytes 368672 | tf_op jit(solution)/shard_map/ppermute | solution.py:49
  237.9 14.4 %expert_hidden.1 = (bf16[960,3072]{1,0:T(8,128)(2,1)}, bf16[960,3072]{1,0:T(8,128)(2,1)}, bf16[768,960]{1,0:T(8,128)(2,1)}) custom-call(bf16[480,768]{1,0:T(8,128)(2,1)} %get-tuple-element.175.refs_0_, bf16[480,768]{1,0:T(8,128)(2,1)} %copy-done.22, bf16[240,768]{1,0:T(8,128)(2,1)} %copy-done.34, bf16[240,768]{1,0:T(8,128)(2,1)} %copy-done.35, ...), custom_call_target="tpu_custom_call" | custom-call | flops 4529848320 | bytes 16515072 | tf_op jit(solution)/shard_map/expert_hidden/pallas_call | solution.py:787
  254.1 9.8 %expert_down_grad.1 = (bf16[768,3072]{1,0:T(8,128)(2,1)}, bf16[960,768]{1,0:T(8,128)(2,1)}) custom-call(bf16[480,768]{1,0:T(8,128)(2,1)} %get-tuple-element.182.refs_0_, bf16[480,768]{1,0:T(8,128)(2,1)} %copy-done.21, bf16[240,768]{1,0:T(8,128)(2,1)} %copy-done.37, bf16[240,768]{1,0:T(8,128)(2,1)} %copy-done.38, bf16[240,768]{1,0:T(8,128)(2,1)} %copy-done.39, ...), custom_call_target="tpu_custom_call" | custom-call | flops 4529848320 | bytes 16515072 | tf_op jit(solution)/shard_map/expert_down_grad/pallas_call | solution.py:824
  264.0 9.3 %expert_out.1 = (bf16[480,768]{1,0:T(8,128)(2,1)}, bf16[480,768]{1,0:T(8,128)(2,1)}) custom-call(bf16[960,3072]{1,0:T(8,128)(2,1)} %get-tuple-element.186.refs_5_.hidden, bf16[3072,768]{1,0:T(8,128)(2,1)} %bitcast.109), custom_call_target="tpu_custom_call" | custom-call | flops 4529848320 | bytes 16515072 | tf_op jit(solution)/shard_map/expert_out/pallas_call | solution.py:803
  273.3 2.6 collective-permute-start.34
  275.9 2.1 collective-permute-done.34.rest_1_
  279.9 1.8 collective-permute-start.37
  281.7 21.2 %expert_back.1 = (bf16[480,768]{1,0:T(8,128)(2,1)}, bf16[480,768]{1,0:T(8,128)(2,1)}, bf16[768,3072]{1,0:T(8,128)(2,1)}) custom-call(bf16[960,768]{1,0:T(8,128)(2,1)} %get-tuple-element.185.grads, bf16[960,3072]{1,0:T(8,128)(2,1)} %get-tuple-element.191.slope, bf16[768,960]{1,0:T(8,128)(2,1)} %get-tuple-element.192.rows_flip, bf16[768,3072]{1,0:T(8,128)(2,1)} %bitcast.108, ...), custom_call_target="tpu_custom_call" | custom-call | flops 13589544960 | bytes 25952256 | tf_op jit(solution)/shard_map/expert_back/pallas_call | solution.py:841
  307.6 1.8 collective-permute-start.41
  310.3 6.2 %made_rows.1 = (bf16[768,768]{1,0:T(8,128)(2,1)}, bf16[768,8]{1,0:T(8,128)(2,1)}, f32[8,768]{1,0:T(8,128)}) custom-call(bf16[768,768]{1,0:T(8,128)(2,1)} %cotangent.5, s32[768,1]{1,0:T(8,128)} %copy.103.ids, s32[768,1]{1,0:T(8,128)} %broadcast_in_dim.45.place_column, f32[768,768]{1,0:T(8,128)} %get-tuple-element.168.middle, ...), custom_call_target="tpu_custom_call" | custom-call | tf_op jit(solution)/shard_map/made_rows/pallas_call | solution.py:621
  316.6 7.1 %collective-permute-done.41.rest_8_ = bf16[240,768]{1,0:T(8,128)(2,1)S(1)} collective-permute-done((bf16[240,768]{1,0:T(8,128)(2,1)S(1)}, bf16[240,768]{1,0:T(8,128)(2,1)S(1)}, u32[]{:S(2)}, u32[]{:S(2)}) %collective-permute-start.41) | collective-permute-done | bytes 368672 | tf_op jit(solution)/shard_map/ppermute | solution.py:49
  324.5 8.6 %back_rows.1 = (f32[768,768]{1,0:T(8,128)}, bf16[768,768]{1,0:T(8,128)(2,1)}, f32[8,768]{1,0:T(8,128)}, bf16[192,768]{1,0:T(8,128)(2,1)}, bf16[192,768]{1,0:T(8,...) custom-call(bf16[768,768]{1,0:T(8,128)(2,1)} %cotangent.5, f32[2,768]{1,0:T(2,128)} %gains.7, ...), custom_call_target="tpu_custom_call" | custom-call | tf_op jit(solution)/shard_map/back_rows/pallas_call | solution.py:663
  333.1 2.0 collective-permute-start.42
  336.8 3.9 proj_grad.1
  340.7 3.3 collective-permute-done.43.rest_7_
  343.9 6.4 %collective-permute-done.44.rest_8_ = bf16[192,768]{1,0:T(8,128)(2,1)S(1)} collective-permute-done((bf16[192,768]{1,0:T(8,128)(2,1)}, bf16[192,768]{1,0:T(8,128)(2,1)S(1)}, u32[]{:S(2)}, u32[]{:S(2)}) %collective-permute-start.44) | collective-permute-done | bytes 294944 | tf_op jit(solution)/shard_map/ppermute | solution.py:49
  351.0 47.1 %attend_backward.1 = (bf16[192,3072]{1,0:T(8,128)(2,1)}, bf16[24,128,384]{2,1,0:T(8,128)(2,1)}, bf16[12,128,384]{2,1,0:T(8,128)(2,1)}, bf16[12,128,384]{2,1,0:T(...) custom-call(s32[49]{0:T(128)} %pad_add_fusion.1.info, ...), custom_call_target="tpu_custom_call" | custom-call | flops 24159191040 | bytes 10000000 | tf_op jit(solution)/shard_map/attend_backward/pallas_call | solution.py:399
  398.7 2.5 collective-permute-done.47
  401.2 1.6 convert_add_fusion.1
  405.2 1.5 collective-permute-start.46
  406.7 14.9 %qkv_grad.1 = bf16[768,576]{1,0:T(8,128)(2,1)} custom-call(bf16[192,3072]{1,0:T(8,128)(2,1)} %get-tuple-element.222.grad_query, bf16[24,128,384]{2,1,0:T(8,128)(2,1)} %get-tuple-element.227.rest_0_, bf16[12,128,384]{2,1,0:T(8,128)(2,1)} %get-tuple-element.228.rest_1_, bf16[12,128,384]{2,1,0:T(8,128)(2,1)} %get-tuple-element.229.rest_2_, ...), custom_call_target="tpu_custom_call" | custom-call | flops 6794772480 | bytes 20000000 | tf_op jit(solution)/shard_map/qkv_grad/pallas_call | solution.py:467
  422.3 2.0 fusion.4
  425.4 2.8 collective-permute-done.50
  430.7 8.0 %collective-permute-done.49 = bf16[384,768]{1,0:T(8,128)(2,1)S(1)} collective-permute-done((bf16[384,768]{1,0:T(8,128)(2,1)S(1)}, bf16[384,768]{1,0:T(8,128)(2,1)S(1)}, u32[]{:S(2)}, u32[]{:S(2)}) %collective-permute-start.49) | collective-permute-done | bytes 589856 | tf_op jit(solution)/shard_map/ppermute | solution.py:49
  440.6 1.9 convert_add_fusion
  444.1 11.1 %collective-permute-done.48 = bf16[384,768]{1,0:T(8,128)(2,1)} collective-permute-done((bf16[384,768]{1,0:T(8,128)(2,1)}, bf16[384,768]{1,0:T(8,128)(2,1)}, u32[]{:S(2)}, u32[]{:S(2)}) %collective-permute-start.48) | collective-permute-done | bytes 589856 | tf_op jit(solution)/shard_map/ppermute | solution.py:53
  455.2 1.5 collective-permute-done.52.one
  456.9 1.5 pad_maximum_fusion.1
  459.8 2.1 add_convert_fusion.2
  463.4 11.6 %collective-permute-done.55 = bf16[384,768]{1,0:T(8,128)(2,1)} collective-permute-done((bf16[384,768]{1,0:T(8,128)(2,1)}, bf16[384,768]{1,0:T(8,128)(2,1)}, u32[]{:S(2)}, u32[]{:S(2)}) %collective-permute-start.55) | collective-permute-done | bytes 589856 | tf_op jit(solution)/shard_map/ppermute | solution.py:49
  476.6 1.4 convert_bitcast_fusion
  478.1 2.9 bitcast_convert_fusion
  481.0 2.3 add_convert_fusion.1
  484.5 3.1 collective-permute-start.57
  488.7 1.9 collective-permute-start.64
  490.6 2.0 copy.113
  493.9 8.5 %collective-permute-done.58 = bf16[96,777]{0,1:T(8,128)(2,1)} collective-permute-done((bf16[96,777]{0,1:T(8,128)(2,1)S(1)}, bf16[96,777]{0,1:T(8,128)(2,1)}, u32[]{:S(2)}, u32[]{:S(2)}) %collective-permute-start.58) | collective-permute-done | bytes 149216 | tf_op jit(solution)/shard_map/ppermute | solution.py:49
  503.8 14.1 %collective-permute-start.60 = (bf16[96,10]{0,1:T(8,128)(2,1)S(1)}, bf16[96,10]{0,1:T(8,128)(2,1)S(1)}, u32[]{:S(2)}, u32[]{:S(2)}) collective-permute-start(bf16[96,10]{0,1:T(8,128)(2,1)S(1)} %fusion.17), channel_id=1, source_target_pairs={{0,1},{1,0},{2,3},{3,2},{4,5},{5,4},{6,7},{7,6},{8,9},{9,8},{10,11... | collective-permute-start | bytes 5768 | tf_op jit(solution)/shard_map/ppermute | solution.py:49
  522.0 6.4 %final_rows.1 = f32[768,768]{1,0:T(8,128)} custom-call(s32[1]{0:T(128)} %bitcast.46.first, bf16[768,768]{1,0:T(8,128)(2,1)} %tokens.5, f32[2,768]{1,0:T(2,128)} %gains.7, f32[768,768]{1,0:T(8,128)} %get-tuple-element.267.grad_middle, bf16[2,768,768]{2,1,0:T(8,128)(2,1)} %get-tuple-element.243.kept, bf16[2,768,768]{2,1,0:T(8,128)(2,1)} %copy-done.3, ...), custom_call_target="tpu_custom_call" | custom-call | tf_op jit(solution)/shard_map/final_rows/pallas_call | solution.py:496
  (299 shorter events, 70.0 us)
Async XLA Ops:
  7.2 230.7 %all-gather.3.cloned.1.call-start = ((), (), s32[]{:S(2)}) async-start(), calls=%async_computation.2 | async-start | bytes 5898240 | tf_op jit(solution)/shard_map/all_gather | solution.py:939
  10.2 14.5 %collective-permute-start.3 = (bf16[384,768]{1,0:T(8,128)(2,1)}, bf16[384,768]{1,0:T(8,128)(2,1)}, u32[]{:S(2)}, u32[]{:S(2)}) collective-permute-start(bf16[384,768]{1,0:T(8,128)(2,1)} %get-tuple-element.143), channel_id=1, source_target_pairs={{0,2},{1,3},{2,0},{3,1},{4,6},{5,7},{6,4},{7,5},{8,10},{9,11},{10,... | collective-permute-start | bytes 1769480 | tf_op jit(solution)/shard_map/ppermute | solution.py:49
  12.6 14.1 %collective-permute-start = (bf16[96,776]{0,1:T(8,128)(2,1)S(1)}, bf16[96,776]{0,1:T(8,128)(2,1)S(1)}, u32[]{:S(2)}, u32[]{:S(2)}) collective-permute-start(bf16[96,776]{0,1:T(8,128)(2,1)S(1)} %pad_maximum_fusion.17), channel_id=1, source_target_pairs={{0,4},{4,0},{8,12},{12,8},{1,5},{5,1},{9,13},{13,9},{2,6},{6,2},{1... | collective-permute-start | bytes 446984 | tf_op jit(solution)/shard_map/ppermute | solution.py:49
  12.8 13.9 %collective-permute-start.1 = (bf16[96,776]{0,1:T(8,128)(2,1)S(1)}, bf16[96,776]{0,1:T(8,128)(2,1)S(1)}, u32[]{:S(2)}, u32[]{:S(2)}) collective-permute-start(bf16[96,776]{0,1:T(8,128)(2,1)S(1)} %pad_maximum_fusion.17), channel_id=1, source_target_pairs={{0,8},{4,12},{8,0},{12,4},{1,9},{5,13},{9,1},{13,5},{2,10},{6,14},... | collective-permute-start | bytes 446984 | tf_op jit(solution)/shard_map/ppermute | solution.py:49
  12.9 13.8 %collective-permute-start.2 = (bf16[96,776]{0,1:T(8,128)(2,1)S(1)}, bf16[96,776]{0,1:T(8,128)(2,1)S(1)}, u32[]{:S(2)}, u32[]{:S(2)}) collective-permute-start(bf16[96,776]{0,1:T(8,128)(2,1)S(1)} %pad_maximum_fusion.17), channel_id=1, source_target_pairs={{0,12},{4,8},{8,4},{12,0},{1,13},{5,9},{9,5},{13,1},{2,14},{6,10},... | collective-permute-start | bytes 446984 | tf_op jit(solution)/shard_map/ppermute | solution.py:49
  27.3 12.6 %collective-permute-start.6 = (bf16[1,4,96,776]{3,2,1,0:T(8,128)(2,1)S(1)}, bf16[1,4,96,776]{3,2,1,0:T(8,128)(2,1)S(1)}, u32[]{:S(2)}, u32[]{:S(2)}) collective-permute-start(bf16[1,4,96,776]{3,2,1,0:T(8,128)(2,1)S(1)} %copy.89), channel_id=1, source_target_pairs={{0,16},{16,0},{1,17},{17,1},{2,18},{18,2},{3,19},{19,3},{4,20},{20... | collective-permute-start | bytes 1787912 | tf_op jit(solution)/shard_map/ppermute | solution.py:49
  28.6 17.1 %collective-permute-start.4 = (bf16[384,768]{1,0:T(8,128)(2,1)}, bf16[384,768]{1,0:T(8,128)(2,1)}, u32[]{:S(2)}, u32[]{:S(2)}) collective-permute-start(bf16[384,768]{1,0:T(8,128)(2,1)} %get-tuple-element.144), channel_id=1, source_target_pairs={{0,4},{4,8},{8,12},{12,0},{1,5},{5,9},{9,13},{13,1},{2,6},{6,10},{... | collective-permute-start | bytes 1769480 | tf_op jit(solution)/shard_map/ppermute | solution.py:53
  30.6 15.2 %collective-permute-start.5 = (bf16[384,768]{1,0:T(8,128)(2,1)S(1)}, bf16[384,768]{1,0:T(8,128)(2,1)}, u32[]{:S(2)}, u32[]{:S(2)}) collective-permute-start(bf16[384,768]{1,0:T(8,128)(2,1)S(1)} %get-tuple-element.320), channel_id=1, source_target_pairs={{0,2},{1,3},{2,0},{3,1},{4,6},{5,7},{6,4},{7,5},{8,10},{9,11},{10,... | collective-permute-start | bytes 1769480 | tf_op jit(solution)/shard_map/ppermute | solution.py:49
  45.7 10.2 %collective-permute-start.7 = (bf16[384,768]{1,0:T(8,128)(2,1)}, bf16[384,768]{1,0:T(8,128)(2,1)}, u32[]{:S(2)}, u32[]{:S(2)}) collective-permute-start(bf16[384,768]{1,0:T(8,128)(2,1)} %collective-permute-done.4.rest_0_.rest_10_), channel_id=1, source_target_pairs={{0,4},{4,8},{8,12},{12,0},{1,5},{5,9},{9,13},{13,1},{2,6},{6,10},{... | collective-permute-start | bytes 1769480 | tf_op jit(solution)/shard_map/ppermute | solution.py:53
  55.9 208.1 %all-gather.5.cloned.1.call-start = ((), (), s32[]{:S(2)}) async-start(), calls=%async_computation.3 | async-start | bytes 5898240 | tf_op jit(solution)/shard_map/all_gather | solution.py:940
  56.0 35.3 %collective-permute-start.10 = (bf16[768,768]{1,0:T(8,128)(2,1)}, bf16[768,768]{1,0:T(8,128)(2,1)}, u32[]{:S(2)}, u32[]{:S(2)}) collective-permute-start(bf16[768,768]{1,0:T(8,128)(2,1)} %get-tuple-element.142.rest_0_.rest_4_), channel_id=1, source_target_pairs={{0,1},{1,0},{2,3},{3,2},{4,5},{5,4},{6,7},{7,6},{8,9},{9,8},{10,11... | collective-permute-start | bytes 3538952 | tf_op jit(solution)/shard_map/ppermute | solution.py:49
  73.6 19.5 %collective-permute-start.12 = (bf16[384,768]{1,0:T(8,128)(2,1)}, bf16[384,768]{1,0:T(8,128)(2,1)}, u32[]{:S(2)}, u32[]{:S(2)}) collective-permute-start(bf16[384,768]{1,0:T(8,128)(2,1)} %collective-permute-done.3.rest_3_.rest_7_), channel_id=1, source_target_pairs={{0,1},{1,0},{2,3},{3,2},{4,5},{5,4},{6,7},{7,6},{8,9},{9,8},{10,11... | collective-permute-start | bytes 1769480 | tf_op jit(solution)/shard_map/ppermute | solution.py:49
  73.8 14.8 %collective-permute-start.8 = (bf16[384,768]{1,0:T(8,128)(2,1)}, bf16[384,768]{1,0:T(8,128)(2,1)}, u32[]{:S(2)}, u32[]{:S(2)}) collective-permute-start(bf16[384,768]{1,0:T(8,128)(2,1)} %collective-permute-done.4.rest_0_.rest_10_), channel_id=1, source_target_pairs={{0,2},{1,3},{2,0},{3,1},{4,6},{5,7},{6,4},{7,5},{8,10},{9,11},{10,... | collective-permute-start | bytes 1769480 | tf_op jit(solution)/shard_map/ppermute | solution.py:49
  75.6 17.5 %collective-permute-start.11 = (bf16[384,768]{1,0:T(8,128)(2,1)}, bf16[384,768]{1,0:T(8,128)(2,1)}, u32[]{:S(2)}, u32[]{:S(2)}) collective-permute-start(bf16[384,768]{1,0:T(8,128)(2,1)} %collective-permute-done.5.rest_2_.rest_6_), channel_id=1, source_target_pairs={{0,1},{1,0},{2,3},{3,2},{4,5},{5,4},{6,7},{7,6},{8,9},{9,8},{10,11... | collective-permute-start | bytes 1769480 | tf_op jit(solution)/shard_map/ppermute | solution.py:49
  76.6 400.0 %reduce-scatter.5.cloned.1.call-start = ((), (), s32[]{:S(2)}) async-start(), calls=%async_computation.5 | async-start | bytes 5898240 | tf_op jit(solution)/shard_map/reduce_scatter | solution.py:1007
  88.6 43.7 %collective-permute-start.9 = (bf16[384,768]{1,0:T(8,128)(2,1)}, bf16[384,768]{1,0:T(8,128)(2,1)S(1)}, u32[]{:S(2)}, u32[]{:S(2)}) collective-permute-start(bf16[384,768]{1,0:T(8,128)(2,1)} %collective-permute-done.7.rest_0_.rest_14_), channel_id=1, source_target_pairs={{0,4},{4,8},{8,12},{12,0},{1,5},{5,9},{9,13},{13,1},{2,6},{6,10},{... | collective-permute-start | bytes 1769480 | tf_op jit(solution)/shard_map/ppermute | solution.py:53
  89.0 43.2 %collective-permute-start.15 = (bf16[384,768]{1,0:T(8,128)(2,1)}, bf16[384,768]{1,0:T(8,128)(2,1)S(1)}, u32[]{:S(2)}, u32[]{:S(2)}) collective-permute-start(bf16[384,768]{1,0:T(8,128)(2,1)} %collective-permute-done.7.rest_0_.rest_14_), channel_id=1, source_target_pairs={{0,2},{1,3},{2,0},{3,1},{4,6},{5,7},{6,4},{7,5},{8,10},{9,11},{10,... | collective-permute-start | bytes 1769480 | tf_op jit(solution)/shard_map/ppermute | solution.py:49
  91.3 43.5 %collective-permute-start.13 = (bf16[384,768]{1,0:T(8,128)(2,1)}, bf16[384,768]{1,0:T(8,128)(2,1)}, u32[]{:S(2)}, u32[]{:S(2)}) collective-permute-start(bf16[384,768]{1,0:T(8,128)(2,1)} %collective-permute-done.4.rest_0_.rest_10_), channel_id=1, source_target_pairs={{0,1},{1,0},{2,3},{3,2},{4,5},{5,4},{6,7},{7,6},{8,9},{9,8},{10,11... | collective-permute-start | bytes 1769480 | tf_op jit(solution)/shard_map/ppermute | solution.py:49
  132.2 14.7 %collective-permute-start.18 = (bf16[384,768]{1,0:T(8,128)(2,1)S(1)}, bf16[384,768]{1,0:T(8,128)(2,1)}, u32[]{:S(2)}, u32[]{:S(2)}) collective-permute-start(bf16[384,768]{1,0:T(8,128)(2,1)S(1)} %collective-permute-done.9.rest_0_.rest_18_), channel_id=1, source_target_pairs={{0,2},{1,3},{2,0},{3,1},{4,6},{5,7},{6,4},{7,5},{8,10},{9,11},{10,... | collective-permute-start | bytes 1769480 | tf_op jit(solution)/shard_map/ppermute | solution.py:49
  133.4 15.5 %collective-permute-start.14 = (bf16[384,768]{1,0:T(8,128)(2,1)}, bf16[384,768]{1,0:T(8,128)(2,1)}, u32[]{:S(2)}, u32[]{:S(2)}) collective-permute-start(bf16[384,768]{1,0:T(8,128)(2,1)} %collective-permute-done.8.rest_1_.rest_11_), channel_id=1, source_target_pairs={{0,1},{1,0},{2,3},{3,2},{4,5},{5,4},{6,7},{7,6},{8,9},{9,8},{10,11... | collective-permute-start | bytes 1769480 | tf_op jit(solution)/shard_map/ppermute | solution.py:49
  134.2 19.5 %collective-permute-start.16 = (bf16[384,768]{1,0:T(8,128)(2,1)}, bf16[384,768]{1,0:T(8,128)(2,1)}, u32[]{:S(2)}, u32[]{:S(2)}) collective-permute-start(bf16[384,768]{1,0:T(8,128)(2,1)} %collective-permute-done.7.rest_0_.rest_14_), channel_id=1, source_target_pairs={{0,1},{1,0},{2,3},{3,2},{4,5},{5,4},{6,7},{7,6},{8,9},{9,8},{10,11... | collective-permute-start | bytes 1769480 | tf_op jit(solution)/shard_map/ppermute | solution.py:49
  134.3 19.4 %collective-permute-start.17 = (bf16[384,768]{1,0:T(8,128)(2,1)S(1)}, bf16[384,768]{1,0:T(8,128)(2,1)}, u32[]{:S(2)}, u32[]{:S(2)}) collective-permute-start(bf16[384,768]{1,0:T(8,128)(2,1)S(1)} %collective-permute-done.15.rest_1_.rest_15_), channel_id=1, source_target_pairs={{0,1},{1,0},{2,3},{3,2},{4,5},{5,4},{6,7},{7,6},{8,9},{9,8},{10,11... | collective-permute-start | bytes 1769480 | tf_op jit(solution)/shard_map/ppermute | solution.py:49
  134.8 26.9 %collective-permute-start.19 = (bf16[384,768]{1,0:T(8,128)(2,1)S(1)}, bf16[384,768]{1,0:T(8,128)(2,1)}, u32[]{:S(2)}, u32[]{:S(2)}) collective-permute-start(bf16[384,768]{1,0:T(8,128)(2,1)S(1)} %collective-permute-done.9.rest_0_.rest_18_), channel_id=1, source_target_pairs={{0,1},{1,0},{2,3},{3,2},{4,5},{5,4},{6,7},{7,6},{8,9},{9,8},{10,11... | collective-permute-start | bytes 1769480 | tf_op jit(solution)/shard_map/ppermute | solution.py:49
  147.0 14.7 %collective-permute-start.20 = (bf16[384,768]{1,0:T(8,128)(2,1)}, bf16[384,768]{1,0:T(8,128)(2,1)}, u32[]{:S(2)}, u32[]{:S(2)}) collective-permute-start(bf16[384,768]{1,0:T(8,128)(2,1)} %collective-permute-done.18.rest_1_.rest_19_), channel_id=1, source_target_pairs={{0,1},{1,0},{2,3},{3,2},{4,5},{5,4},{6,7},{7,6},{8,9},{9,8},{10,11... | collective-permute-start | bytes 1769480 | tf_op jit(solution)/shard_map/ppermute | solution.py:49
  148.9 10.9 %collective-permute-start.24 = (bf16[1,192,768]{1,2,0:T(8,128)(2,1)S(1)}, bf16[1,192,768]{1,2,0:T(8,128)(2,1)S(1)}, u32[]{:S(2)}, u32[]{:S(2)}) collective-permute-start(bf16[1,192,768]{1,2,0:T(8,128)(2,1)S(1)} %bitcast.92), channel_id=1, source_target_pairs={{0,2},{1,3},{2,0},{3,1},{4,6},{5,7},{6,4},{7,5},{8,10},{9,11},{10,... | collective-permute-start | bytes 884744 | tf_op jit(solution)/shard_map/ppermute | solution.py:49
  161.0 33.9 %collective-permute-start.25 = (bf16[2,192,768]{2,1,0:T(8,128)(2,1)}, bf16[2,192,768]{2,1,0:T(8,128)(2,1)}, u32[]{:S(2)}, u32[]{:S(2)}) collective-permute-start(bf16[2,192,768]{2,1,0:T(8,128)(2,1)} %copy.99), channel_id=1, source_target_pairs={{0,1},{1,0},{2,3},{3,2},{4,5},{5,4},{6,7},{7,6},{8,9},{9,8},{10,11... | collective-permute-start | bytes 1769480 | tf_op jit(solution)/shard_map/ppermute | solution.py:49
  188.7 8.1 %collective-permute-start.21 = (bf16[192,768]{1,0:T(8,128)(2,1)}, bf16[192,768]{1,0:T(8,128)(2,1)S(1)}, u32[]{:S(2)}, u32[]{:S(2)}) collective-permute-start(bf16[192,768]{1,0:T(8,128)(2,1)} %get-tuple-element.164.rest_10_), channel_id=1, source_target_pairs={{0,1},{1,0},{2,3},{3,2},{4,5},{5,4},{6,7},{7,6},{8,9},{9,8},{10,11... | collective-permute-start | bytes 884744 | tf_op jit(solution)/shard_map/ppermute | solution.py:49
  188.7 8.5 %collective-permute-start.22 = (bf16[192,768]{1,0:T(8,128)(2,1)}, bf16[192,768]{1,0:T(8,128)(2,1)S(1)}, u32[]{:S(2)}, u32[]{:S(2)}) collective-permute-start(bf16[192,768]{1,0:T(8,128)(2,1)} %get-tuple-element.165.rest_11_), channel_id=1, source_target_pairs={{0,2},{1,3},{2,0},{3,1},{4,6},{5,7},{6,4},{7,5},{8,10},{9,11},{10,... | collective-permute-start | bytes 884744 | tf_op jit(solution)/shard_map/ppermute | solution.py:49
  188.8 15.7 %collective-permute-start.23 = (bf16[192,768]{1,0:T(8,128)(2,1)}, bf16[192,768]{1,0:T(8,128)(2,1)S(1)}, u32[]{:S(2)}, u32[]{:S(2)}) collective-permute-start(bf16[192,768]{1,0:T(8,128)(2,1)} %get-tuple-element.166.rest_12_), channel_id=1, source_target_pairs={{0,3},{1,2},{2,1},{3,0},{4,7},{5,6},{6,5},{7,4},{8,11},{9,10},{10,... | collective-permute-start | bytes 884744 | tf_op jit(solution)/shard_map/ppermute | solution.py:49
  216.3 10.2 %collective-permute-start.27 = (bf16[240,768]{1,0:T(8,128)(2,1)S(1)}, bf16[240,768]{1,0:T(8,128)(2,1)S(1)}, u32[]{:S(2)}, u32[]{:S(2)}) collective-permute-start(bf16[240,768]{1,0:T(8,128)(2,1)S(1)} %pad_maximum_fusion.5), channel_id=1, source_target_pairs={{0,2},{1,3},{2,0},{3,1},{16,18},{17,19},{18,16},{19,17},{4,6},{5,7... | collective-permute-start | bytes 1105928 | tf_op jit(solution)/shard_map/ppermute | solution.py:49
  216.4 17.8 %collective-permute-start.28 = (bf16[240,768]{1,0:T(8,128)(2,1)S(1)}, bf16[240,768]{1,0:T(8,128)(2,1)S(1)}, u32[]{:S(2)}, u32[]{:S(2)}) collective-permute-start(bf16[240,768]{1,0:T(8,128)(2,1)S(1)} %pad_maximum_fusion.6), channel_id=1, source_target_pairs={{0,16},{1,17},{2,18},{3,19},{16,0},{17,1},{18,2},{19,3},{4,20},{5,... | collective-permute-start | bytes 1105928 | tf_op jit(solution)/shard_map/ppermute | solution.py:49
  217.1 17.2 %collective-permute-start.29 = (bf16[240,768]{1,0:T(8,128)(2,1)S(1)}, bf16[240,768]{1,0:T(8,128)(2,1)S(1)}, u32[]{:S(2)}, u32[]{:S(2)}) collective-permute-start(bf16[240,768]{1,0:T(8,128)(2,1)S(1)} %pad_maximum_fusion.7), channel_id=1, source_target_pairs={{0,18},{1,19},{2,16},{3,17},{16,2},{17,3},{18,0},{19,1},{4,22},{5,... | collective-permute-start | bytes 1105928 | tf_op jit(solution)/shard_map/ppermute | solution.py:49
  235.1 17.2 %collective-permute-start.31 = (bf16[240,768]{1,0:T(8,128)(2,1)S(1)}, bf16[240,768]{1,0:T(8,128)(2,1)S(1)}, u32[]{:S(2)}, u32[]{:S(2)}) collective-permute-start(bf16[240,768]{1,0:T(8,128)(2,1)S(1)} %pad_maximum_fusion.8), channel_id=1, source_target_pairs={{0,2},{1,3},{2,0},{3,1},{16,18},{17,19},{18,16},{19,17},{4,6},{5,7... | collective-permute-start | bytes 1105928 | tf_op jit(solution)/shard_map/ppermute | solution.py:49
  236.5 15.8 %collective-permute-start.32 = (bf16[240,768]{1,0:T(8,128)(2,1)S(1)}, bf16[240,768]{1,0:T(8,128)(2,1)S(1)}, u32[]{:S(2)}, u32[]{:S(2)}) collective-permute-start(bf16[240,768]{1,0:T(8,128)(2,1)S(1)} %pad_maximum_fusion.9), channel_id=1, source_target_pairs={{0,16},{1,17},{2,18},{3,19},{16,0},{17,1},{18,2},{19,3},{4,20},{5,... | collective-permute-start | bytes 1105928 | tf_op jit(solution)/shard_map/ppermute | solution.py:49
  236.7 16.7 %collective-permute-start.33 = (bf16[240,768]{1,0:T(8,128)(2,1)S(1)}, bf16[240,768]{1,0:T(8,128)(2,1)S(1)}, u32[]{:S(2)}, u32[]{:S(2)}) collective-permute-start(bf16[240,768]{1,0:T(8,128)(2,1)S(1)} %pad_maximum_fusion.10), channel_id=1, source_target_pairs={{0,18},{1,19},{2,16},{3,17},{16,2},{17,3},{18,0},{19,1},{4,22},{5,... | collective-permute-start | bytes 1105928 | tf_op jit(solution)/shard_map/ppermute | solution.py:49
  264.0 214.1 %reduce-scatter.3.cloned.1.call-start = ((), (), s32[]{:S(2)}) async-start(), calls=%async_computation.4 | async-start | bytes 5898240 | tf_op jit(solution)/shard_map/reduce_scatter | solution.py:1009
  278.9 24.1 %collective-permute-start.35 = (bf16[240,768]{1,0:T(8,128)(2,1)S(1)}, bf16[240,768]{1,0:T(8,128)(2,1)S(1)}, u32[]{:S(2)}, u32[]{:S(2)}) collective-permute-start(bf16[240,768]{1,0:T(8,128)(2,1)S(1)} %pad_maximum_fusion.11), channel_id=1, source_target_pairs={{0,2},{1,3},{2,0},{3,1},{16,18},{17,19},{18,16},{19,17},{4,6},{5,7... | collective-permute-start | bytes 1105928 | tf_op jit(solution)/shard_map/ppermute | solution.py:49
  278.9 24.0 %collective-permute-start.36 = (bf16[240,768]{1,0:T(8,128)(2,1)S(1)}, bf16[240,768]{1,0:T(8,128)(2,1)S(1)}, u32[]{:S(2)}, u32[]{:S(2)}) collective-permute-start(bf16[240,768]{1,0:T(8,128)(2,1)S(1)} %pad_maximum_fusion.12), channel_id=1, source_target_pairs={{0,16},{1,17},{2,18},{3,19},{16,0},{17,1},{18,2},{19,3},{4,20},{5,... | collective-permute-start | bytes 1105928 | tf_op jit(solution)/shard_map/ppermute | solution.py:49
  279.9 23.0 %collective-permute-start.37 = (bf16[240,768]{1,0:T(8,128)(2,1)S(1)}, bf16[240,768]{1,0:T(8,128)(2,1)S(1)}, u32[]{:S(2)}, u32[]{:S(2)}) collective-permute-start(bf16[240,768]{1,0:T(8,128)(2,1)S(1)} %pad_maximum_fusion.13), channel_id=1, source_target_pairs={{0,18},{1,19},{2,16},{3,17},{16,2},{17,3},{18,0},{19,1},{4,22},{5,... | collective-permute-start | bytes 1105928 | tf_op jit(solution)/shard_map/ppermute | solution.py:49
  306.4 10.0 %collective-permute-start.39 = (bf16[240,768]{1,0:T(8,128)(2,1)S(1)}, bf16[240,768]{1,0:T(8,128)(2,1)S(1)}, u32[]{:S(2)}, u32[]{:S(2)}) collective-permute-start(bf16[240,768]{1,0:T(8,128)(2,1)S(1)} %pad_maximum_fusion.14), channel_id=1, source_target_pairs={{0,2},{1,3},{2,0},{3,1},{16,18},{17,19},{18,16},{19,17},{4,6},{5,7... | collective-permute-start | bytes 1105928 | tf_op jit(solution)/shard_map/ppermute | solution.py:49
  306.6 10.0 %collective-permute-start.40 = (bf16[240,768]{1,0:T(8,128)(2,1)S(1)}, bf16[240,768]{1,0:T(8,128)(2,1)S(1)}, u32[]{:S(2)}, u32[]{:S(2)}) collective-permute-start(bf16[240,768]{1,0:T(8,128)(2,1)S(1)} %pad_maximum_fusion.15), channel_id=1, source_target_pairs={{0,16},{1,17},{2,18},{3,19},{16,0},{17,1},{18,2},{19,3},{4,20},{5,... | collective-permute-start | bytes 1105928 | tf_op jit(solution)/shard_map/ppermute | solution.py:49
  307.6 16.1 %collective-permute-start.41 = (bf16[240,768]{1,0:T(8,128)(2,1)S(1)}, bf16[240,768]{1,0:T(8,128)(2,1)S(1)}, u32[]{:S(2)}, u32[]{:S(2)}) collective-permute-start(bf16[240,768]{1,0:T(8,128)(2,1)S(1)} %pad_maximum_fusion.16), channel_id=1, source_target_pairs={{0,18},{1,19},{2,16},{3,17},{16,2},{17,3},{18,0},{19,1},{4,22},{5,... | collective-permute-start | bytes 1105928 | tf_op jit(solution)/shard_map/ppermute | solution.py:49
  333.1 7.6 %collective-permute-start.42 = (bf16[192,768]{1,0:T(8,128)(2,1)}, bf16[192,768]{1,0:T(8,128)(2,1)S(1)}, u32[]{:S(2)}, u32[]{:S(2)}) collective-permute-start(bf16[192,768]{1,0:T(8,128)(2,1)} %get-tuple-element.210), channel_id=1, source_target_pairs={{0,1},{1,0},{2,3},{3,2},{4,5},{5,4},{6,7},{7,6},{8,9},{9,8},{10,11... | collective-permute-start | bytes 884744 | tf_op jit(solution)/shard_map/ppermute | solution.py:49
  335.1 8.9 %collective-permute-start.43 = (bf16[192,768]{1,0:T(8,128)(2,1)}, bf16[192,768]{1,0:T(8,128)(2,1)S(1)}, u32[]{:S(2)}, u32[]{:S(2)}) collective-permute-start(bf16[192,768]{1,0:T(8,128)(2,1)} %get-tuple-element.211), channel_id=1, source_target_pairs={{0,2},{1,3},{2,0},{3,1},{4,6},{5,7},{6,4},{7,5},{8,10},{9,11},{10,... | collective-permute-start | bytes 884744 | tf_op jit(solution)/shard_map/ppermute | solution.py:49
  336.5 13.8 %collective-permute-start.44 = (bf16[192,768]{1,0:T(8,128)(2,1)}, bf16[192,768]{1,0:T(8,128)(2,1)S(1)}, u32[]{:S(2)}, u32[]{:S(2)}) collective-permute-start(bf16[192,768]{1,0:T(8,128)(2,1)} %get-tuple-element.212), channel_id=1, source_target_pairs={{0,3},{1,2},{2,1},{3,0},{4,7},{5,6},{6,5},{7,4},{8,11},{9,10},{10,... | collective-permute-start | bytes 884744 | tf_op jit(solution)/shard_map/ppermute | solution.py:49
  405.2 16.4 %collective-permute-start.46 = (bf16[384,768]{1,0:T(8,128)(2,1)S(1)}, bf16[384,768]{1,0:T(8,128)(2,1)}, u32[]{:S(2)}, u32[]{:S(2)}) collective-permute-start(bf16[384,768]{1,0:T(8,128)(2,1)S(1)} %slice.283), channel_id=1, source_target_pairs={{0,2},{1,3},{2,0},{3,1},{4,6},{5,7},{6,4},{7,5},{8,10},{9,11},{10,... | collective-permute-start | bytes 1769480 | tf_op jit(solution)/shard_map/ppermute | solution.py:49
  421.6 6.8 %collective-permute-start.51 = (bf16[2,768,768]{2,1,0:T(8,128)(2,1)}, bf16[2,768,768]{2,1,0:T(8,128)(2,1)S(1)}, u32[]{:S(2)}, u32[]{:S(2)}) collective-permute-start(bf16[2,768,768]{2,1,0:T(8,128)(2,1)} %get-tuple-element.244), channel_id=1, source_target_pairs={{0,1},{1,0},{2,3},{3,2},{4,5},{5,4},{6,7},{7,6},{8,9},{9,8},{10,11... | collective-permute-start | bytes 7077896 | tf_op jit(solution)/shard_map/ppermute | solution.py:49
  422.2 6.1 %collective-permute-start.50 = (bf16[2,192,768]{2,1,0:T(8,128)(2,1)}, bf16[2,192,768]{2,1,0:T(8,128)(2,1)S(1)}, u32[]{:S(2)}, u32[]{:S(2)}) collective-permute-start(bf16[2,192,768]{2,1,0:T(8,128)(2,1)} %get-tuple-element.242), channel_id=1, source_target_pairs={{0,1},{1,0},{2,3},{3,2},{4,5},{5,4},{6,7},{7,6},{8,9},{9,8},{10,11... | collective-permute-start | bytes 1769480 | tf_op jit(solution)/shard_map/ppermute | solution.py:49
  424.3 14.5 %collective-permute-start.49 = (bf16[384,768]{1,0:T(8,128)(2,1)S(1)}, bf16[384,768]{1,0:T(8,128)(2,1)S(1)}, u32[]{:S(2)}, u32[]{:S(2)}) collective-permute-start(bf16[384,768]{1,0:T(8,128)(2,1)S(1)} %slice.282), channel_id=1, source_target_pairs={{0,2},{1,3},{2,0},{3,1},{4,6},{5,7},{6,4},{7,5},{8,10},{9,11},{10,... | collective-permute-start | bytes 1769480 | tf_op jit(solution)/shard_map/ppermute | solution.py:49
  424.6 16.0 %collective-permute-start.53 = (bf16[768,768]{1,0:T(8,128)(2,1)}, bf16[768,768]{1,0:T(8,128)(2,1)}, u32[]{:S(2)}, u32[]{:S(2)}) collective-permute-start(bf16[768,768]{1,0:T(8,128)(2,1)} %get-tuple-element.248), channel_id=1, source_target_pairs={{0,1},{1,0},{2,3},{3,2},{4,5},{5,4},{6,7},{7,6},{8,9},{9,8},{10,11... | collective-permute-start | bytes 3538952 | tf_op jit(solution)/shard_map/ppermute | solution.py:49
  439.6 17.0 %collective-permute-start.52 = (bf16[480,768]{1,0:T(8,128)(2,1)}, bf16[480,768]{1,0:T(8,128)(2,1)S(1)}, u32[]{:S(2)}, u32[]{:S(2)}) collective-permute-start(bf16[480,768]{1,0:T(8,128)(2,1)} %pad_maximum_fusion.4), channel_id=1, source_target_pairs={{0,2},{1,3},{2,0},{3,1},{4,6},{5,7},{6,4},{7,5},{8,10},{9,11},{10,... | collective-permute-start | bytes 2211848 | tf_op jit(solution)/shard_map/ppermute | solution.py:49
  439.9 15.3 %collective-permute-start.48 = (bf16[384,768]{1,0:T(8,128)(2,1)}, bf16[384,768]{1,0:T(8,128)(2,1)}, u32[]{:S(2)}, u32[]{:S(2)}) collective-permute-start(bf16[384,768]{1,0:T(8,128)(2,1)} %fusion.4), channel_id=1, source_target_pairs={{0,12},{4,0},{8,4},{12,8},{1,13},{5,1},{9,5},{13,9},{2,14},{6,2},{... | collective-permute-start | bytes 1769480 | tf_op jit(solution)/shard_map/ppermute | solution.py:53
  458.5 16.5 %collective-permute-start.56 = (bf16[4,96,777]{2,1,0:T(8,128)(2,1)S(1)}, bf16[4,96,777]{2,1,0:T(8,128)(2,1)S(1)}, u32[]{:S(2)}, u32[]{:S(2)}) collective-permute-start(bf16[4,96,777]{2,1,0:T(8,128)(2,1)S(1)} %get-tuple-element.317), channel_id=1, source_target_pairs={{0,16},{16,0},{1,17},{17,1},{2,18},{18,2},{3,19},{19,3},{4,20},{20... | collective-permute-start | bytes 1790216 | tf_op jit(solution)/shard_map/ppermute | solution.py:49
  461.9 13.0 %collective-permute-start.55 = (bf16[384,768]{1,0:T(8,128)(2,1)}, bf16[384,768]{1,0:T(8,128)(2,1)}, u32[]{:S(2)}, u32[]{:S(2)}) collective-permute-start(bf16[384,768]{1,0:T(8,128)(2,1)} %slice.281), channel_id=1, source_target_pairs={{0,2},{1,3},{2,0},{3,1},{4,6},{5,7},{6,4},{7,5},{8,10},{9,11},{10,... | collective-permute-start | bytes 1769480 | tf_op jit(solution)/shard_map/ppermute | solution.py:49
  463.0 18.1 %collective-permute-start.54 = (bf16[384,768]{1,0:T(8,128)(2,1)}, bf16[384,768]{1,0:T(8,128)(2,1)}, u32[]{:S(2)}, u32[]{:S(2)}) collective-permute-start(bf16[384,768]{1,0:T(8,128)(2,1)} %add_convert_fusion.2), channel_id=1, source_target_pairs={{0,12},{4,0},{8,4},{12,8},{1,13},{5,1},{9,5},{13,9},{2,14},{6,2},{... | collective-permute-start | bytes 1769480 | tf_op jit(solution)/shard_map/ppermute | solution.py:53
  474.9 44.1 %collective-permute-start.63 = (bf16[480,768]{1,0:T(8,128)(2,1)}, bf16[480,768]{1,0:T(8,128)(2,1)}, u32[]{:S(2)}, u32[]{:S(2)}) collective-permute-start(bf16[480,768]{1,0:T(8,128)(2,1)} %slice_bitcast_fusion), channel_id=1, source_target_pairs={{0,2},{1,3},{2,0},{3,1},{4,6},{5,7},{6,4},{7,5},{8,10},{9,11},{10,... | collective-permute-start | bytes 2211848 | tf_op jit(solution)/shard_map/ppermute | solution.py:49
  484.1 8.5 %collective-permute-start.59 = (bf16[96,777]{0,1:T(8,128)(2,1)}, bf16[96,777]{0,1:T(8,128)(2,1)}, u32[]{:S(2)}, u32[]{:S(2)}) collective-permute-start(bf16[96,777]{0,1:T(8,128)(2,1)} %get-tuple-element.323), channel_id=1, source_target_pairs={{0,12},{4,8},{8,4},{12,0},{1,13},{5,9},{9,5},{13,1},{2,14},{6,10},... | collective-permute-start | bytes 447560 | tf_op jit(solution)/shard_map/ppermute | solution.py:49
  484.1 18.3 %collective-permute-start.58 = (bf16[96,777]{0,1:T(8,128)(2,1)S(1)}, bf16[96,777]{0,1:T(8,128)(2,1)}, u32[]{:S(2)}, u32[]{:S(2)}) collective-permute-start(bf16[96,777]{0,1:T(8,128)(2,1)S(1)} %get-tuple-element.324), channel_id=1, source_target_pairs={{0,8},{4,12},{8,0},{12,4},{1,9},{5,13},{9,1},{13,5},{2,10},{6,14},... | collective-permute-start | bytes 447560 | tf_op jit(solution)/shard_map/ppermute | solution.py:49
  484.5 17.8 %collective-permute-start.57 = (bf16[96,777]{0,1:T(8,128)(2,1)S(1)}, bf16[96,777]{0,1:T(8,128)(2,1)}, u32[]{:S(2)}, u32[]{:S(2)}) collective-permute-start(bf16[96,777]{0,1:T(8,128)(2,1)S(1)} %get-tuple-element.322), channel_id=1, source_target_pairs={{0,4},{4,0},{8,12},{12,8},{1,5},{5,1},{9,13},{13,9},{2,6},{6,2},{1... | collective-permute-start | bytes 447560 | tf_op jit(solution)/shard_map/ppermute | solution.py:49
  488.7 32.4 %collective-permute-start.64 = (bf16[384,768]{1,0:T(8,128)(2,1)S(1)}, bf16[384,768]{1,0:T(8,128)(2,1)}, u32[]{:S(2)}, u32[]{:S(2)}) collective-permute-start(bf16[384,768]{1,0:T(8,128)(2,1)S(1)} %copy-done.16), channel_id=1, source_target_pairs={{0,12},{1,13},{4,0},{5,1},{8,4},{9,5},{12,8},{13,9},{16,28},{17,29... | collective-permute-start | bytes 1769480 | tf_op jit(solution)/shard_map/ppermute | solution.py:1095
  492.6 28.6 %collective-permute-start.65 = (bf16[384,768]{1,0:T(8,128)(2,1)S(1)}, bf16[384,768]{1,0:T(8,128)(2,1)S(1)}, u32[]{:S(2)}, u32[]{:S(2)}) collective-permute-start(bf16[384,768]{1,0:T(8,128)(2,1)S(1)} %copy-done.16), channel_id=1, source_target_pairs={{2,12},{3,13},{6,0},{7,1},{10,4},{11,5},{14,8},{15,9},{18,28},{19,... | collective-permute-start | bytes 1769480 | tf_op jit(solution)/shard_map/ppermute | solution.py:1095
  503.8 24.5 %collective-permute-start.60 = (bf16[96,10]{0,1:T(8,128)(2,1)S(1)}, bf16[96,10]{0,1:T(8,128)(2,1)S(1)}, u32[]{:S(2)}, u32[]{:S(2)}) collective-permute-start(bf16[96,10]{0,1:T(8,128)(2,1)S(1)} %fusion.17), channel_id=1, source_target_pairs={{0,1},{1,0},{2,3},{3,2},{4,5},{5,4},{6,7},{7,6},{8,9},{9,8},{10,11... | collective-permute-start | bytes 5768 | tf_op jit(solution)/shard_map/ppermute | solution.py:49
  517.9 10.5 %collective-permute-start.61 = (bf16[96,10]{0,1:T(8,128)(2,1)S(1)}, bf16[96,10]{0,1:T(8,128)(2,1)S(1)}, u32[]{:S(2)}, u32[]{:S(2)}) collective-permute-start(bf16[96,10]{0,1:T(8,128)(2,1)S(1)} %fusion.17), channel_id=1, source_target_pairs={{0,2},{1,3},{2,0},{3,1},{4,6},{5,7},{6,4},{7,5},{8,10},{9,11},{10,... | collective-permute-start | bytes 5768 | tf_op jit(solution)/shard_map/ppermute | solution.py:49
  519.1 9.3 %collective-permute-start.62 = (bf16[96,10]{0,1:T(8,128)(2,1)S(1)}, bf16[96,10]{0,1:T(8,128)(2,1)S(1)}, u32[]{:S(2)}, u32[]{:S(2)}) collective-permute-start(bf16[96,10]{0,1:T(8,128)(2,1)S(1)} %fusion.17), channel_id=1, source_target_pairs={{0,3},{1,2},{2,1},{3,0},{4,7},{5,6},{6,5},{7,4},{8,11},{9,10},{10,... | collective-permute-start | bytes 5768 | tf_op jit(solution)/shard_map/ppermute | solution.py:49
  (52 other events, 320.5 us)
Sparse Core Ops, SparseCore 0:
  56.1 114.3 all-gather.2
  172.1 87.9 all-gather.4
  264.1 86.1 reduce-scatter.4
  352.4 85.7 reduce-scatter.2

commit v6 on v5

--- a/solution.py
+++ b/solution.py
@@ -739,11 +739,11 @@
     grad_down[...] = low(dot_plain(grads_flip[...], hidden[...]))
 
 
-def expert_back_kernel(grads, slope, rows_flip, up, down, even, odd, grad_up, total):
+def expert_back_kernel(grads, slope, up, down, even, odd, grad_pre, total):
     step = pl.program_id(0)
-    grad_pre = low(dot_last(grads[...], down[...]) * slope[...].astype(F32))
-    grad_up[...] = low(dot_plain(rows_flip[...], grad_pre))
-    part = dot_last(grad_pre, up[...])
+    inner = low(dot_last(grads[...], down[...]) * slope[...].astype(F32))
+    grad_pre[...] = inner
+    part = dot_last(inner, up[...])
 
     @pl.when(step == 0)
     def _():
@@ -834,7 +834,7 @@
     )(*parts, hidden)
 
 
-def expert_back(grads, slope, rows_flip, up, down):
+def expert_back(grads, slope, up, down):
     slots, units = slope.shape
     width = grads.shape[1]
     block = whole_spec((slots // 2, width))
@@ -844,21 +844,39 @@
         in_specs=[
             whole_spec(grads.shape),
             column_spec(slots),
-            whole_spec(rows_flip.shape),
             column_spec(width),
             row_spec(width),
         ],
-        out_specs=(block, block, column_spec(width)),
+        out_specs=(block, block, column_spec(slots)),
         out_shape=(
             shape((slots // 2, width)),
             shape((slots // 2, width)),
-            shape((width, units)),
+            shape((slots, units)),
         ),
         scratch_shapes=[pltpu.VMEM((slots, width), F32)],
         compiler_params=ROOM,
-        cost_estimate=expert_cost(3, slots, width, units),
+        cost_estimate=expert_cost(2, slots, width, units),
         name="expert_back",
-    )(grads, slope, rows_flip, up, down)
+    )(grads, slope, up, down)
+
+
+def expert_up_grad_kernel(rows_flip, grad_pre, grad_up):
+    grad_up[...] = low(dot_plain(rows_flip[...], grad_pre[...]))
+
+
+def expert_up_grad(rows_flip, grad_pre):
+    slots, units = grad_pre.shape
+    width = rows_flip.shape[0]
+    return pl.pallas_call(
+        expert_up_grad_kernel,
+        grid=(units // UNITS,),
+        in_specs=[whole_spec(rows_flip.shape), column_spec(slots)],
+        out_specs=column_spec(width),
+        out_shape=shape((width, units)),
+        compiler_params=ROOM,
+        cost_estimate=expert_cost(1, slots, width, units),
+        name="expert_up_grad",
+    )(rows_flip, grad_pre)
 
 
 def shards(
@@ -1001,12 +1019,12 @@
     even, odd = expert_out(hidden, full_down)
     even, other, slope = lax.optimization_barrier((even, start_exchange(odd), slope))
     made_slots = finish_exchange(even, other)
-    even, odd, grad_up = expert_back(arrived_grads, slope, rows_flip, full_up, full_down)
-    even, odd, made_slots, grad_up = lax.optimization_barrier((even, odd, made_slots, grad_up))
+    even, odd, grad_pre = expert_back(arrived_grads, slope, full_up, full_down)
+    even, odd, made_slots, grad_pre = lax.optimization_barrier((even, odd, made_slots, grad_pre))
     back_slots = finish_exchange(even, start_exchange(odd))
     grad_down = lax.psum_scatter(grad_down, "ctx", scatter_dimension=1, tiled=True)
     grad_down = grad_down.T.astype(F32)[None]
-    grad_up = lax.psum_scatter(grad_up, "ctx", scatter_dimension=1, tiled=True).astype(F32)[None]
+    grad_up = expert_up_grad(rows_flip, grad_pre)
 
     output, grad_logits, router_part = made_rows(
         cotangent, expert_ids, place, middle, normed_two, probs, made_slots
@@ -1016,7 +1034,10 @@
     )
     grad_near = xor_exchange(grad_near, "tp", tp_count)
     proj_keep, proj_send = proj_grad(grad_split, attended)
-    grad_near, proj_keep, proj_send = lax.optimization_barrier((grad_near, proj_keep, proj_send))
+    grad_near, proj_keep, proj_send, grad_up = lax.optimization_barrier(
+        (grad_near, proj_keep, proj_send, grad_up)
+    )
+    grad_up = lax.psum_scatter(grad_up, "ctx", scatter_dimension=1, tiled=True).astype(F32)[None]
     grad_query, grad_local, *grads = attend_backward(
         sizes,
         info,

time: 542 us -> 531 us (0.980)
  waiting for transfers between devices: 180 us -> 171 us
  starting transfers between devices: 79.6 us -> 72.4 us
    ppermute x59, starting transfers between devices: 73.7 us -> 60 us  [xor_swap(): lax.ppermute(value, axis, [(place, place ^ mask) for place in range(size)])]
    ppermute x5, waiting for transfers between devices: 57.5 us -> 46.3 us  [ring_step(): lax.ppermute(value, axis, [(place, (place + shift) % size) for place in r...]
    pallas_call x0 -> x1, Pallas kernels: none -> 9.33 us  [expert_up_grad(): pl.pallas_call(expert_up_grad_kernel, grid=(units // UNITS,), in_specs=[w...]
    ppermute x5, starting transfers between devices: 2.44 us -> 8.16 us  [ring_step(): lax.ppermute(value, axis, [(place, (place + shift) % size) for place in r...]
    unnamed x106 -> x104, local copies, waits for them, and re-layouts: 17.2 us -> 16.3 us
  transfers between devices with their start and end apart: 70 -> 70, of which waited for: 27 -> 26; matrix products, arithmetic and copies ran while one was open for 10% -> 10% of each run, Pallas kernels for 36% -> 38%
where the time goes in v6:
time: 531 us; the launch traced here: 526 us
  Pallas kernels  202 us (38%)
  waiting for transfers between devices  171 us (32%)
  starting transfers between devices  72.4 us (14%)
  local copies, waits for them, and re-layouts  37.7 us (7%)
  other arithmetic  26 us (5%)
  between operations  14.9 us (3%)
    ppermute x59, waiting for transfers between devices, xor_swap(): lax.ppermute(value, axis, [(place, place ^ mask) for place in range(size)])  125 us
    ppermute x59, starting transfers between devices, xor_swap(): lax.ppermute(value, axis, [(place, place ^ mask) for place in range(size)])  60 us
    pallas_call x1, Pallas kernels, attend_backward(): pl.pallas_call(functools.partial(attend_backward_kernel, sizes), out_shap...  47.3 us
    ppermute x5, waiting for transfers between devices, ring_step(): lax.ppermute(value, axis, [(place, (place + shift) % size) for place in r...  46.3 us
    pallas_call x1, Pallas kernels, attend_forward(): pl.pallas_call(functools.partial(attend_forward_kernel, sizes), out_shape...  23.1 us
    pallas_call x1, Pallas kernels, expert_back(): pl.pallas_call(expert_back_kernel, grid=(units // UNITS,), in_specs=[whol...  16.5 us
    unnamed x104, local copies, waits for them, and re-layouts  16.3 us
    pallas_call x1, Pallas kernels, qkv_grad(): pl.pallas_call(functools.partial(qkv_grad_kernel, len(pairs)), out_shape=...  14.8 us
  transfers between devices with their start and end apart: 70, of which 26 were waited for; matrix products, arithmetic and copies ran while one was open for 10% of the time, Pallas kernels for 38%

profile of v6, /device:TPU:25, one launch (start us, length us, event | category | flops | bytes accessed | tf_op | source)
XLA Modules:
  0.0 525.7 jit_solution(18079038941052336269)
XLA Ops:
  7.2 3.0 normalize.1
  14.0 2.2 collective-permute-start
  16.2 8.6 %collective-permute-done.3.rest_3_.rest_7_ = bf16[384,768]{1,0:T(8,128)(2,1)} collective-permute-done((bf16[384,768]{1,0:T(8,128)(2,1)}, bf16[384,768]{1,0:T(8,128)(2,1)}, u32[]{:S(2)}, u32[]{:S(2)}) %collective-permute-start.3) | collective-permute-done | bytes 589856 | tf_op jit(solution)/shard_map/ppermute | solution.py:49
  24.7 2.0 fusion.34
  26.7 4.1 collective-permute-done.1
  32.7 1.5 collective-permute-start.4
  34.5 12.1 %collective-permute-done.6 = bf16[1,4,96,776]{3,2,1,0:T(8,128)(2,1)S(1)} collective-permute-done((bf16[1,4,96,776]{3,2,1,0:T(8,128)(2,1)S(1)}, bf16[1,4,96,776]{3,2,1,0:T(8,128)(2,1)S(1)}, u32[]{:S(2)}, u32[]{:S(2)}) %collective-permute-start.6) | collective-permute-done | bytes 596000 | tf_op jit(solution)/shard_map/ppermute | solution.py:49
  47.2 2.3 collective-permute-start.7
  49.5 10.3 %collective-permute-done.7.rest_0_.rest_14_ = bf16[384,768]{1,0:T(8,128)(2,1)} collective-permute-done((bf16[384,768]{1,0:T(8,128)(2,1)}, bf16[384,768]{1,0:T(8,128)(2,1)}, u32[]{:S(2)}, u32[]{:S(2)}) %collective-permute-start.7) | collective-permute-done | bytes 589856 | tf_op jit(solution)/shard_map/ppermute | solution.py:53
  59.9 3.6 collective-permute-start.10
  68.1 11.7 %collective-permute-done.8.rest_1_.rest_11_ = bf16[384,768]{1,0:T(8,128)(2,1)} collective-permute-done((bf16[384,768]{1,0:T(8,128)(2,1)}, bf16[384,768]{1,0:T(8,128)(2,1)}, u32[]{:S(2)}, u32[]{:S(2)}) %collective-permute-start.8) | collective-permute-done | bytes 589856 | tf_op jit(solution)/shard_map/ppermute | solution.py:49
  80.1 4.3 collective-permute-start.9
  86.4 1.8 collective-permute-start.13
  88.2 8.3 %project_local.1 = (bf16[192,3072]{1,0:T(8,128)(2,1)}, bf16[24,128,384]{2,1,0:T(8,128)(2,1)}) custom-call(bf16[768,192]{1,0:T(8,128)(2,1)} %get-tuple-element.321.query_weight.rest_3_, bf16[768,384]{1,0:T(8,128)(2,1)} %slice.224.pair_weight.rest_4_, bf16[768,768]{1,0:T(8,128)(2,1)} %get-tuple-element.143.rest_0_.rest_4_, ...), custom_call_target="tpu_custom_call" | custom-call | flops 2717908992 | bytes 10000000 | tf_op jit(solution)/shard_map/project_local/pallas_call | solution.py:219
  96.5 24.8 %collective-permute-done.9.rest_0_.rest_18_ = bf16[384,768]{1,0:T(8,128)(2,1)S(1)} collective-permute-done((bf16[384,768]{1,0:T(8,128)(2,1)}, bf16[384,768]{1,0:T(8,128)(2,1)S(1)}, u32[]{:S(2)}, u32[]{:S(2)}) %collective-permute-start.9) | collective-permute-done | bytes 589856 | tf_op jit(solution)/shard_map/ppermute | solution.py:53
  123.6 4.6 collective-permute-start.14
  128.9 3.4 collective-permute-done.18.rest_1_.rest_19_
  132.3 5.0 collective-permute-start.20
  139.7 4.2 project_remote.3.rest_0_
  143.9 4.2 project_remote.4.rest_1_
  150.8 4.2 project_remote.5.rest_2_
  155.0 23.1 %attend_forward.1 = (bf16[192,768]{1,0:T(8,128)(2,1)}, bf16[192,768]{1,0:T(8,128)(2,1)}, bf16[192,768]{1,0:T(8,128)(2,1)}, bf16[192,768]{1,0:T(8,128)(2,1)}, f32...) custom-call(s32[49]{0:T(128)} %pad_add_fusion.1.info, bf16[192,3072]{1,0:T(8,128)(2,1)} %get-tuple-element.158.query, ...), custom_call_target="tpu_custom_call" | custom-call | flops 9663676416 | bytes 10000000 | tf_op jit(solution)/shard_map/attend_forward/pallas_call | solution.py:375
  184.3 1.9 slice_bitcast_fusion.4
  186.7 7.2 %collective-permute-done.23.rest_3_ = bf16[192,768]{1,0:T(8,128)(2,1)S(1)} collective-permute-done((bf16[192,768]{1,0:T(8,128)(2,1)}, bf16[192,768]{1,0:T(8,128)(2,1)S(1)}, u32[]{:S(2)}, u32[]{:S(2)}) %collective-permute-start.23) | collective-permute-done | bytes 294944 | tf_op jit(solution)/shard_map/ppermute | solution.py:49
  194.6 8.6 %middle_rows.1 = (bf16[480,768]{1,0:T(8,128)(2,1)}, bf16[480,768]{1,0:T(8,128)(2,1)}, bf16[480,768]{1,0:T(8,128)(2,1)}, bf16[480,768]{1,0:T(8,128)(2,1)}, f32[76...) custom-call(bf16[768,768]{1,0:T(8,128)(2,1)} %tokens.5, bf16[768,768]{1,0:T(8,128)(2,1)} %cotangent.5, ...), custom_call_target="tpu_custom_call" | custom-call | tf_op jit(solution)/shard_map/middle_rows/pallas_call | solution.py:572
  208.7 7.3 %collective-permute-done.27.refs_2_ = bf16[240,768]{1,0:T(8,128)(2,1)S(1)} collective-permute-done((bf16[240,768]{1,0:T(8,128)(2,1)S(1)}, bf16[240,768]{1,0:T(8,128)(2,1)S(1)}, u32[]{:S(2)}, u32[]{:S(2)}) %collective-permute-start.27) | collective-permute-done | bytes 368672 | tf_op jit(solution)/shard_map/ppermute | solution.py:49
  217.1 7.3 %collective-permute-done.29.refs_4_ = bf16[240,768]{1,0:T(8,128)(2,1)S(1)} collective-permute-done((bf16[240,768]{1,0:T(8,128)(2,1)S(1)}, bf16[240,768]{1,0:T(8,128)(2,1)S(1)}, u32[]{:S(2)}, u32[]{:S(2)}) %collective-permute-start.29) | collective-permute-done | bytes 368672 | tf_op jit(solution)/shard_map/ppermute | solution.py:49
  228.2 14.2 %expert_hidden.1 = (bf16[960,3072]{1,0:T(8,128)(2,1)}, bf16[960,3072]{1,0:T(8,128)(2,1)}, bf16[768,960]{1,0:T(8,128)(2,1)}) custom-call(bf16[480,768]{1,0:T(8,128)(2,1)} %get-tuple-element.176.refs_0_, bf16[480,768]{1,0:T(8,128)(2,1)} %copy-done.21, bf16[240,768]{1,0:T(8,128)(2,1)} %copy-done.33, bf16[240,768]{1,0:T(8,128)(2,1)} %copy-done.34, ...), custom_call_target="tpu_custom_call" | custom-call | flops 4529848320 | bytes 16515072 | tf_op jit(solution)/shard_map/expert_hidden/pallas_call | solution.py:787
  243.5 9.8 %expert_down_grad.1 = (bf16[768,3072]{1,0:T(8,128)(2,1)}, bf16[960,768]{1,0:T(8,128)(2,1)}) custom-call(bf16[480,768]{1,0:T(8,128)(2,1)} %get-tuple-element.183.refs_0_, bf16[480,768]{1,0:T(8,128)(2,1)} %copy-done.20, bf16[240,768]{1,0:T(8,128)(2,1)} %copy-done.36, bf16[240,768]{1,0:T(8,128)(2,1)} %copy-done.37, bf16[240,768]{1,0:T(8,128)(2,1)} %copy-done.38, ...), custom_call_target="tpu_custom_call" | custom-call | flops 4529848320 | bytes 16515072 | tf_op jit(solution)/shard_map/expert_down_grad/pallas_call | solution.py:824
  253.4 9.4 %expert_out.1 = (bf16[480,768]{1,0:T(8,128)(2,1)}, bf16[480,768]{1,0:T(8,128)(2,1)}) custom-call(bf16[960,3072]{1,0:T(8,128)(2,1)} %get-tuple-element.187.refs_5_.hidden, bf16[3072,768]{1,0:T(8,128)(2,1)} %bitcast.109), custom_call_target="tpu_custom_call" | custom-call | flops 4529848320 | bytes 16515072 | tf_op jit(solution)/shard_map/expert_out/pallas_call | solution.py:803
  262.8 3.3 collective-permute-start.34
  266.2 2.1 collective-permute-done.34.rest_1_
  268.2 1.4 fusion.37
  270.5 2.1 collective-permute-start.37
  272.6 16.5 %expert_back.1 = (bf16[480,768]{1,0:T(8,128)(2,1)}, bf16[480,768]{1,0:T(8,128)(2,1)}, bf16[960,3072]{1,0:T(8,128)(2,1)}) custom-call(bf16[960,768]{1,0:T(8,128)(2,1)} %get-tuple-element.186.grads, bf16[960,3072]{1,0:T(8,128)(2,1)} %get-tuple-element.192.slope, bf16[768,3072]{1,0:T(8,128)(2,1)} %bitcast.108, bf16[3072,768]{1,0:T(8,128)(2,1)} %bitcast.110), custom_call_target="tpu_custom_call" | custom-call | flops 9059696640 | bytes 21233664 | tf_op jit(solution)/shard_map/expert_back/pallas_call | solution.py:841
  293.4 2.1 collective-permute-start.41
  296.4 6.1 %made_rows.1 = (bf16[768,768]{1,0:T(8,128)(2,1)}, bf16[768,8]{1,0:T(8,128)(2,1)}, f32[8,768]{1,0:T(8,128)}) custom-call(bf16[768,768]{1,0:T(8,128)(2,1)} %cotangent.5, s32[768,1]{1,0:T(8,128)} %copy.103.ids, s32[768,1]{1,0:T(8,128)} %broadcast_in_dim.45.place_column, f32[768,768]{1,0:T(8,128)} %get-tuple-element.169.middle, ...), custom_call_target="tpu_custom_call" | custom-call | tf_op jit(solution)/shard_map/made_rows/pallas_call | solution.py:621
  302.6 7.8 %collective-permute-done.41.rest_8_ = bf16[240,768]{1,0:T(8,128)(2,1)S(1)} collective-permute-done((bf16[240,768]{1,0:T(8,128)(2,1)S(1)}, bf16[240,768]{1,0:T(8,128)(2,1)S(1)}, u32[]{:S(2)}, u32[]{:S(2)}) %collective-permute-start.41) | collective-permute-done | bytes 368672 | tf_op jit(solution)/shard_map/ppermute | solution.py:49
  311.2 8.7 %back_rows.1 = (f32[768,768]{1,0:T(8,128)}, bf16[768,768]{1,0:T(8,128)(2,1)}, f32[8,768]{1,0:T(8,128)}, bf16[192,768]{1,0:T(8,128)(2,1)}, bf16[192,768]{1,0:T(8,...) custom-call(bf16[768,768]{1,0:T(8,128)(2,1)} %cotangent.5, f32[2,768]{1,0:T(2,128)} %gains.7, ...), custom_call_target="tpu_custom_call" | custom-call | tf_op jit(solution)/shard_map/back_rows/pallas_call | solution.py:663
  321.2 1.6 collective-permute-start.43
  322.9 9.3 %expert_up_grad.1 = bf16[768,3072]{1,0:T(8,128)(2,1)} custom-call(bf16[768,960]{1,0:T(8,128)(2,1)} %get-tuple-element.216.rows_flip, bf16[960,3072]{1,0:T(8,128)(2,1)} %get-tuple-element.217.grad_pre), custom_call_target="tpu_custom_call" | custom-call | flops 4529848320 | bytes 16515072 | tf_op jit(solution)/shard_map/expert_up_grad/pallas_call | solution.py:870
  332.2 3.8 proj_grad.1
  337.6 47.3 %attend_backward.1 = (bf16[192,3072]{1,0:T(8,128)(2,1)}, bf16[24,128,384]{2,1,0:T(8,128)(2,1)}, bf16[12,128,384]{2,1,0:T(8,128)(2,1)}, bf16[12,128,384]{2,1,0:T(...) custom-call(s32[49]{0:T(128)} %pad_add_fusion.1.info, ...), custom_call_target="tpu_custom_call" | custom-call | flops 24159191040 | bytes 10000000 | tf_op jit(solution)/shard_map/attend_backward/pallas_call | solution.py:399
  385.6 2.5 collective-permute-done.47
  388.1 1.6 convert_add_fusion.1
  392.2 1.6 collective-permute-start.46
  393.8 14.8 %qkv_grad.1 = bf16[768,576]{1,0:T(8,128)(2,1)} custom-call(bf16[192,3072]{1,0:T(8,128)(2,1)} %get-tuple-element.224.grad_query, bf16[24,128,384]{2,1,0:T(8,128)(2,1)} %get-tuple-element.229.rest_0_, bf16[12,128,384]{2,1,0:T(8,128)(2,1)} %get-tuple-element.230.rest_1_, bf16[12,128,384]{2,1,0:T(8,128)(2,1)} %get-tuple-element.231.rest_2_, ...), custom_call_target="tpu_custom_call" | custom-call | flops 6794772480 | bytes 20000000 | tf_op jit(solution)/shard_map/qkv_grad/pallas_call | solution.py:467
  409.1 2.0 fusion.4
  412.4 2.6 collective-permute-done.50
  417.6 8.2 %collective-permute-done.49 = bf16[384,768]{1,0:T(8,128)(2,1)S(1)} collective-permute-done((bf16[384,768]{1,0:T(8,128)(2,1)S(1)}, bf16[384,768]{1,0:T(8,128)(2,1)S(1)}, u32[]{:S(2)}, u32[]{:S(2)}) %collective-permute-start.49) | collective-permute-done | bytes 589856 | tf_op jit(solution)/shard_map/ppermute | solution.py:49
  427.8 1.9 convert_add_fusion
  431.3 11.1 %collective-permute-done.48 = bf16[384,768]{1,0:T(8,128)(2,1)} collective-permute-done((bf16[384,768]{1,0:T(8,128)(2,1)}, bf16[384,768]{1,0:T(8,128)(2,1)}, u32[]{:S(2)}, u32[]{:S(2)}) %collective-permute-start.48) | collective-permute-done | bytes 589856 | tf_op jit(solution)/shard_map/ppermute | solution.py:53
  444.1 1.5 pad_maximum_fusion.1
  447.0 2.1 add_convert_fusion.2
  450.8 11.6 %collective-permute-done.55 = bf16[384,768]{1,0:T(8,128)(2,1)} collective-permute-done((bf16[384,768]{1,0:T(8,128)(2,1)}, bf16[384,768]{1,0:T(8,128)(2,1)}, u32[]{:S(2)}, u32[]{:S(2)}) %collective-permute-start.55) | collective-permute-done | bytes 589856 | tf_op jit(solution)/shard_map/ppermute | solution.py:49
  464.1 1.4 convert_bitcast_fusion
  465.5 2.9 bitcast_convert_fusion
  468.5 2.3 add_convert_fusion.1
  471.5 2.6 collective-permute-start.58
  476.6 2.0 copy.113
  478.5 2.8 collective-permute-start.64
  481.3 21.5 %collective-permute-done.58 = bf16[96,777]{0,1:T(8,128)(2,1)} collective-permute-done((bf16[96,777]{0,1:T(8,128)(2,1)S(1)}, bf16[96,777]{0,1:T(8,128)(2,1)}, u32[]{:S(2)}, u32[]{:S(2)}) %collective-permute-start.58) | collective-permute-done | bytes 149216 | tf_op jit(solution)/shard_map/ppermute | solution.py:49
  504.3 4.2 collective-permute-start.62
  511.3 6.4 %final_rows.1 = f32[768,768]{1,0:T(8,128)} custom-call(s32[1]{0:T(128)} %bitcast.46.first, bf16[768,768]{1,0:T(8,128)(2,1)} %tokens.5, f32[2,768]{1,0:T(2,128)} %gains.7, f32[768,768]{1,0:T(8,128)} %get-tuple-element.269.grad_middle, bf16[2,768,768]{2,1,0:T(8,128)(2,1)} %get-tuple-element.245.kept, bf16[2,768,768]{2,1,0:T(8,128)(2,1)} %copy-done.3, ...), custom_call_target="tpu_custom_call" | custom-call | tf_op jit(solution)/shard_map/final_rows/pallas_call | solution.py:496
  (298 shorter events, 75.9 us)
Async XLA Ops:
  7.2 221.1 %all-gather.3.cloned.1.call-start = ((), (), s32[]{:S(2)}) async-start(), calls=%async_computation.2 | async-start | bytes 5898240 | tf_op jit(solution)/shard_map/all_gather | solution.py:957
  10.2 14.5 %collective-permute-start.3 = (bf16[384,768]{1,0:T(8,128)(2,1)}, bf16[384,768]{1,0:T(8,128)(2,1)}, u32[]{:S(2)}, u32[]{:S(2)}) collective-permute-start(bf16[384,768]{1,0:T(8,128)(2,1)} %get-tuple-element.144), channel_id=1, source_target_pairs={{0,2},{1,3},{2,0},{3,1},{4,6},{5,7},{6,4},{7,5},{8,10},{9,11},{10,... | collective-permute-start | bytes 1769480 | tf_op jit(solution)/shard_map/ppermute | solution.py:49
  12.6 14.1 %collective-permute-start.2 = (bf16[96,776]{0,1:T(8,128)(2,1)S(1)}, bf16[96,776]{0,1:T(8,128)(2,1)S(1)}, u32[]{:S(2)}, u32[]{:S(2)}) collective-permute-start(bf16[96,776]{0,1:T(8,128)(2,1)S(1)} %pad_maximum_fusion.17), channel_id=1, source_target_pairs={{0,12},{4,8},{8,4},{12,0},{1,13},{5,9},{9,5},{13,1},{2,14},{6,10},... | collective-permute-start | bytes 446984 | tf_op jit(solution)/shard_map/ppermute | solution.py:49
  12.6 18.1 %collective-permute-start.1 = (bf16[96,776]{0,1:T(8,128)(2,1)S(1)}, bf16[96,776]{0,1:T(8,128)(2,1)S(1)}, u32[]{:S(2)}, u32[]{:S(2)}) collective-permute-start(bf16[96,776]{0,1:T(8,128)(2,1)S(1)} %pad_maximum_fusion.17), channel_id=1, source_target_pairs={{0,8},{4,12},{8,0},{12,4},{1,9},{5,13},{9,1},{13,5},{2,10},{6,14},... | collective-permute-start | bytes 446984 | tf_op jit(solution)/shard_map/ppermute | solution.py:49
  14.0 16.8 %collective-permute-start = (bf16[96,776]{0,1:T(8,128)(2,1)S(1)}, bf16[96,776]{0,1:T(8,128)(2,1)S(1)}, u32[]{:S(2)}, u32[]{:S(2)}) collective-permute-start(bf16[96,776]{0,1:T(8,128)(2,1)S(1)} %pad_maximum_fusion.17), channel_id=1, source_target_pairs={{0,4},{4,0},{8,12},{12,8},{1,5},{5,1},{9,13},{13,9},{2,6},{6,2},{1... | collective-permute-start | bytes 446984 | tf_op jit(solution)/shard_map/ppermute | solution.py:49
  31.4 15.2 %collective-permute-start.6 = (bf16[1,4,96,776]{3,2,1,0:T(8,128)(2,1)S(1)}, bf16[1,4,96,776]{3,2,1,0:T(8,128)(2,1)S(1)}, u32[]{:S(2)}, u32[]{:S(2)}) collective-permute-start(bf16[1,4,96,776]{3,2,1,0:T(8,128)(2,1)S(1)} %copy.89), channel_id=1, source_target_pairs={{0,16},{16,0},{1,17},{17,1},{2,18},{18,2},{3,19},{19,3},{4,20},{20... | collective-permute-start | bytes 1787912 | tf_op jit(solution)/shard_map/ppermute | solution.py:49
  32.7 14.3 %collective-permute-start.4 = (bf16[384,768]{1,0:T(8,128)(2,1)}, bf16[384,768]{1,0:T(8,128)(2,1)}, u32[]{:S(2)}, u32[]{:S(2)}) collective-permute-start(bf16[384,768]{1,0:T(8,128)(2,1)} %get-tuple-element.145), channel_id=1, source_target_pairs={{0,4},{4,8},{8,12},{12,0},{1,5},{5,9},{9,13},{13,1},{2,6},{6,10},{... | collective-permute-start | bytes 1769480 | tf_op jit(solution)/shard_map/ppermute | solution.py:53
  34.2 13.0 %collective-permute-start.5 = (bf16[384,768]{1,0:T(8,128)(2,1)S(1)}, bf16[384,768]{1,0:T(8,128)(2,1)}, u32[]{:S(2)}, u32[]{:S(2)}) collective-permute-start(bf16[384,768]{1,0:T(8,128)(2,1)S(1)} %get-tuple-element.322), channel_id=1, source_target_pairs={{0,2},{1,3},{2,0},{3,1},{4,6},{5,7},{6,4},{7,5},{8,10},{9,11},{10,... | collective-permute-start | bytes 1769480 | tf_op jit(solution)/shard_map/ppermute | solution.py:49
  47.2 12.6 %collective-permute-start.7 = (bf16[384,768]{1,0:T(8,128)(2,1)}, bf16[384,768]{1,0:T(8,128)(2,1)}, u32[]{:S(2)}, u32[]{:S(2)}) collective-permute-start(bf16[384,768]{1,0:T(8,128)(2,1)} %collective-permute-done.4.rest_0_.rest_10_), channel_id=1, source_target_pairs={{0,4},{4,8},{8,12},{12,0},{1,5},{5,9},{9,13},{13,1},{2,6},{6,10},{... | collective-permute-start | bytes 1769480 | tf_op jit(solution)/shard_map/ppermute | solution.py:53
  59.9 193.5 %all-gather.5.cloned.1.call-start = ((), (), s32[]{:S(2)}) async-start(), calls=%async_computation.3 | async-start | bytes 5898240 | tf_op jit(solution)/shard_map/all_gather | solution.py:958
  59.9 28.3 %collective-permute-start.10 = (bf16[768,768]{1,0:T(8,128)(2,1)}, bf16[768,768]{1,0:T(8,128)(2,1)}, u32[]{:S(2)}, u32[]{:S(2)}) collective-permute-start(bf16[768,768]{1,0:T(8,128)(2,1)} %get-tuple-element.143.rest_0_.rest_4_), channel_id=1, source_target_pairs={{0,1},{1,0},{2,3},{3,2},{4,5},{5,4},{6,7},{7,6},{8,9},{9,8},{10,11... | collective-permute-start | bytes 3538952 | tf_op jit(solution)/shard_map/ppermute | solution.py:49
  64.9 21.4 %collective-permute-start.12 = (bf16[384,768]{1,0:T(8,128)(2,1)}, bf16[384,768]{1,0:T(8,128)(2,1)}, u32[]{:S(2)}, u32[]{:S(2)}) collective-permute-start(bf16[384,768]{1,0:T(8,128)(2,1)} %collective-permute-done.3.rest_3_.rest_7_), channel_id=1, source_target_pairs={{0,1},{1,0},{2,3},{3,2},{4,5},{5,4},{6,7},{7,6},{8,9},{9,8},{10,11... | collective-permute-start | bytes 1769480 | tf_op jit(solution)/shard_map/ppermute | solution.py:49
  65.1 14.8 %collective-permute-start.8 = (bf16[384,768]{1,0:T(8,128)(2,1)}, bf16[384,768]{1,0:T(8,128)(2,1)}, u32[]{:S(2)}, u32[]{:S(2)}) collective-permute-start(bf16[384,768]{1,0:T(8,128)(2,1)} %collective-permute-done.4.rest_0_.rest_10_), channel_id=1, source_target_pairs={{0,2},{1,3},{2,0},{3,1},{4,6},{5,7},{6,4},{7,5},{8,10},{9,11},{10,... | collective-permute-start | bytes 1769480 | tf_op jit(solution)/shard_map/ppermute | solution.py:49
  66.9 21.3 %collective-permute-start.11 = (bf16[384,768]{1,0:T(8,128)(2,1)}, bf16[384,768]{1,0:T(8,128)(2,1)}, u32[]{:S(2)}, u32[]{:S(2)}) collective-permute-start(bf16[384,768]{1,0:T(8,128)(2,1)} %collective-permute-done.5.rest_2_.rest_6_), channel_id=1, source_target_pairs={{0,1},{1,0},{2,3},{3,2},{4,5},{5,4},{6,7},{7,6},{8,9},{9,8},{10,11... | collective-permute-start | bytes 1769480 | tf_op jit(solution)/shard_map/ppermute | solution.py:49
  67.9 396.2 %reduce-scatter.5.cloned.1.call-start = ((), (), s32[]{:S(2)}) async-start(), calls=%async_computation.5 | async-start | bytes 5898240 | tf_op jit(solution)/shard_map/reduce_scatter | solution.py:1025
  79.9 41.5 %collective-permute-start.15 = (bf16[384,768]{1,0:T(8,128)(2,1)}, bf16[384,768]{1,0:T(8,128)(2,1)S(1)}, u32[]{:S(2)}, u32[]{:S(2)}) collective-permute-start(bf16[384,768]{1,0:T(8,128)(2,1)} %collective-permute-done.7.rest_0_.rest_14_), channel_id=1, source_target_pairs={{0,2},{1,3},{2,0},{3,1},{4,6},{5,7},{6,4},{7,5},{8,10},{9,11},{10,... | collective-permute-start | bytes 1769480 | tf_op jit(solution)/shard_map/ppermute | solution.py:49
  80.1 41.2 %collective-permute-start.9 = (bf16[384,768]{1,0:T(8,128)(2,1)}, bf16[384,768]{1,0:T(8,128)(2,1)S(1)}, u32[]{:S(2)}, u32[]{:S(2)}) collective-permute-start(bf16[384,768]{1,0:T(8,128)(2,1)} %collective-permute-done.7.rest_0_.rest_14_), channel_id=1, source_target_pairs={{0,4},{4,8},{8,12},{12,0},{1,5},{5,9},{9,13},{13,1},{2,6},{6,10},{... | collective-permute-start | bytes 1769480 | tf_op jit(solution)/shard_map/ppermute | solution.py:53
  86.4 42.5 %collective-permute-start.13 = (bf16[384,768]{1,0:T(8,128)(2,1)}, bf16[384,768]{1,0:T(8,128)(2,1)}, u32[]{:S(2)}, u32[]{:S(2)}) collective-permute-start(bf16[384,768]{1,0:T(8,128)(2,1)} %collective-permute-done.4.rest_0_.rest_10_), channel_id=1, source_target_pairs={{0,1},{1,0},{2,3},{3,2},{4,5},{5,4},{6,7},{7,6},{8,9},{9,8},{10,11... | collective-permute-start | bytes 1769480 | tf_op jit(solution)/shard_map/ppermute | solution.py:49
  121.3 10.9 %collective-permute-start.18 = (bf16[384,768]{1,0:T(8,128)(2,1)S(1)}, bf16[384,768]{1,0:T(8,128)(2,1)}, u32[]{:S(2)}, u32[]{:S(2)}) collective-permute-start(bf16[384,768]{1,0:T(8,128)(2,1)S(1)} %collective-permute-done.9.rest_0_.rest_18_), channel_id=1, source_target_pairs={{0,2},{1,3},{2,0},{3,1},{4,6},{5,7},{6,4},{7,5},{8,10},{9,11},{10,... | collective-permute-start | bytes 1769480 | tf_op jit(solution)/shard_map/ppermute | solution.py:49
  123.6 14.4 %collective-permute-start.14 = (bf16[384,768]{1,0:T(8,128)(2,1)}, bf16[384,768]{1,0:T(8,128)(2,1)}, u32[]{:S(2)}, u32[]{:S(2)}) collective-permute-start(bf16[384,768]{1,0:T(8,128)(2,1)} %collective-permute-done.8.rest_1_.rest_11_), channel_id=1, source_target_pairs={{0,1},{1,0},{2,3},{3,2},{4,5},{5,4},{6,7},{7,6},{8,9},{9,8},{10,11... | collective-permute-start | bytes 1769480 | tf_op jit(solution)/shard_map/ppermute | solution.py:49
  128.2 15.7 %collective-permute-start.16 = (bf16[384,768]{1,0:T(8,128)(2,1)}, bf16[384,768]{1,0:T(8,128)(2,1)}, u32[]{:S(2)}, u32[]{:S(2)}) collective-permute-start(bf16[384,768]{1,0:T(8,128)(2,1)} %collective-permute-done.7.rest_0_.rest_14_), channel_id=1, source_target_pairs={{0,1},{1,0},{2,3},{3,2},{4,5},{5,4},{6,7},{7,6},{8,9},{9,8},{10,11... | collective-permute-start | bytes 1769480 | tf_op jit(solution)/shard_map/ppermute | solution.py:49
  128.3 15.6 %collective-permute-start.17 = (bf16[384,768]{1,0:T(8,128)(2,1)S(1)}, bf16[384,768]{1,0:T(8,128)(2,1)}, u32[]{:S(2)}, u32[]{:S(2)}) collective-permute-start(bf16[384,768]{1,0:T(8,128)(2,1)S(1)} %collective-permute-done.15.rest_1_.rest_15_), channel_id=1, source_target_pairs={{0,1},{1,0},{2,3},{3,2},{4,5},{5,4},{6,7},{7,6},{8,9},{9,8},{10,11... | collective-permute-start | bytes 1769480 | tf_op jit(solution)/shard_map/ppermute | solution.py:49
  128.8 22.0 %collective-permute-start.19 = (bf16[384,768]{1,0:T(8,128)(2,1)S(1)}, bf16[384,768]{1,0:T(8,128)(2,1)}, u32[]{:S(2)}, u32[]{:S(2)}) collective-permute-start(bf16[384,768]{1,0:T(8,128)(2,1)S(1)} %collective-permute-done.9.rest_0_.rest_18_), channel_id=1, source_target_pairs={{0,1},{1,0},{2,3},{3,2},{4,5},{5,4},{6,7},{7,6},{8,9},{9,8},{10,11... | collective-permute-start | bytes 1769480 | tf_op jit(solution)/shard_map/ppermute | solution.py:49
  132.3 18.5 %collective-permute-start.20 = (bf16[384,768]{1,0:T(8,128)(2,1)}, bf16[384,768]{1,0:T(8,128)(2,1)}, u32[]{:S(2)}, u32[]{:S(2)}) collective-permute-start(bf16[384,768]{1,0:T(8,128)(2,1)} %collective-permute-done.18.rest_1_.rest_19_), channel_id=1, source_target_pairs={{0,1},{1,0},{2,3},{3,2},{4,5},{5,4},{6,7},{7,6},{8,9},{9,8},{10,11... | collective-permute-start | bytes 1769480 | tf_op jit(solution)/shard_map/ppermute | solution.py:49
  138.0 10.9 %collective-permute-start.24 = (bf16[1,192,768]{1,2,0:T(8,128)(2,1)S(1)}, bf16[1,192,768]{1,2,0:T(8,128)(2,1)S(1)}, u32[]{:S(2)}, u32[]{:S(2)}) collective-permute-start(bf16[1,192,768]{1,2,0:T(8,128)(2,1)S(1)} %bitcast.92), channel_id=1, source_target_pairs={{0,2},{1,3},{2,0},{3,1},{4,6},{5,7},{6,4},{7,5},{8,10},{9,11},{10,... | collective-permute-start | bytes 884744 | tf_op jit(solution)/shard_map/ppermute | solution.py:49
  150.1 34.2 %collective-permute-start.25 = (bf16[2,192,768]{2,1,0:T(8,128)(2,1)}, bf16[2,192,768]{2,1,0:T(8,128)(2,1)}, u32[]{:S(2)}, u32[]{:S(2)}) collective-permute-start(bf16[2,192,768]{2,1,0:T(8,128)(2,1)} %copy.99), channel_id=1, source_target_pairs={{0,1},{1,0},{2,3},{3,2},{4,5},{5,4},{6,7},{7,6},{8,9},{9,8},{10,11... | collective-permute-start | bytes 1769480 | tf_op jit(solution)/shard_map/ppermute | solution.py:49
  178.1 8.1 %collective-permute-start.21 = (bf16[192,768]{1,0:T(8,128)(2,1)}, bf16[192,768]{1,0:T(8,128)(2,1)S(1)}, u32[]{:S(2)}, u32[]{:S(2)}) collective-permute-start(bf16[192,768]{1,0:T(8,128)(2,1)} %get-tuple-element.165.rest_10_), channel_id=1, source_target_pairs={{0,1},{1,0},{2,3},{3,2},{4,5},{5,4},{6,7},{7,6},{8,9},{9,8},{10,11... | collective-permute-start | bytes 884744 | tf_op jit(solution)/shard_map/ppermute | solution.py:49
  178.1 8.5 %collective-permute-start.22 = (bf16[192,768]{1,0:T(8,128)(2,1)}, bf16[192,768]{1,0:T(8,128)(2,1)S(1)}, u32[]{:S(2)}, u32[]{:S(2)}) collective-permute-start(bf16[192,768]{1,0:T(8,128)(2,1)} %get-tuple-element.166.rest_11_), channel_id=1, source_target_pairs={{0,2},{1,3},{2,0},{3,1},{4,6},{5,7},{6,4},{7,5},{8,10},{9,11},{10,... | collective-permute-start | bytes 884744 | tf_op jit(solution)/shard_map/ppermute | solution.py:49
  179.3 14.6 %collective-permute-start.23 = (bf16[192,768]{1,0:T(8,128)(2,1)}, bf16[192,768]{1,0:T(8,128)(2,1)S(1)}, u32[]{:S(2)}, u32[]{:S(2)}) collective-permute-start(bf16[192,768]{1,0:T(8,128)(2,1)} %get-tuple-element.167.rest_12_), channel_id=1, source_target_pairs={{0,3},{1,2},{2,1},{3,0},{4,7},{5,6},{6,5},{7,4},{8,11},{9,10},{10,... | collective-permute-start | bytes 884744 | tf_op jit(solution)/shard_map/ppermute | solution.py:49
  205.7 10.2 %collective-permute-start.27 = (bf16[240,768]{1,0:T(8,128)(2,1)S(1)}, bf16[240,768]{1,0:T(8,128)(2,1)S(1)}, u32[]{:S(2)}, u32[]{:S(2)}) collective-permute-start(bf16[240,768]{1,0:T(8,128)(2,1)S(1)} %pad_maximum_fusion.5), channel_id=1, source_target_pairs={{0,2},{1,3},{2,0},{3,1},{16,18},{17,19},{18,16},{19,17},{4,6},{5,7... | collective-permute-start | bytes 1105928 | tf_op jit(solution)/shard_map/ppermute | solution.py:49
  206.9 10.2 %collective-permute-start.28 = (bf16[240,768]{1,0:T(8,128)(2,1)S(1)}, bf16[240,768]{1,0:T(8,128)(2,1)S(1)}, u32[]{:S(2)}, u32[]{:S(2)}) collective-permute-start(bf16[240,768]{1,0:T(8,128)(2,1)S(1)} %pad_maximum_fusion.6), channel_id=1, source_target_pairs={{0,16},{1,17},{2,18},{3,19},{16,0},{17,1},{18,2},{19,3},{4,20},{5,... | collective-permute-start | bytes 1105928 | tf_op jit(solution)/shard_map/ppermute | solution.py:49
  208.0 16.5 %collective-permute-start.29 = (bf16[240,768]{1,0:T(8,128)(2,1)S(1)}, bf16[240,768]{1,0:T(8,128)(2,1)S(1)}, u32[]{:S(2)}, u32[]{:S(2)}) collective-permute-start(bf16[240,768]{1,0:T(8,128)(2,1)S(1)} %pad_maximum_fusion.7), channel_id=1, source_target_pairs={{0,18},{1,19},{2,16},{3,17},{16,2},{17,3},{18,0},{19,1},{4,22},{5,... | collective-permute-start | bytes 1105928 | tf_op jit(solution)/shard_map/ppermute | solution.py:49
  225.3 17.1 %collective-permute-start.31 = (bf16[240,768]{1,0:T(8,128)(2,1)S(1)}, bf16[240,768]{1,0:T(8,128)(2,1)S(1)}, u32[]{:S(2)}, u32[]{:S(2)}) collective-permute-start(bf16[240,768]{1,0:T(8,128)(2,1)S(1)} %pad_maximum_fusion.8), channel_id=1, source_target_pairs={{0,2},{1,3},{2,0},{3,1},{16,18},{17,19},{18,16},{19,17},{4,6},{5,7... | collective-permute-start | bytes 1105928 | tf_op jit(solution)/shard_map/ppermute | solution.py:49
  226.6 15.9 %collective-permute-start.32 = (bf16[240,768]{1,0:T(8,128)(2,1)S(1)}, bf16[240,768]{1,0:T(8,128)(2,1)S(1)}, u32[]{:S(2)}, u32[]{:S(2)}) collective-permute-start(bf16[240,768]{1,0:T(8,128)(2,1)S(1)} %pad_maximum_fusion.9), channel_id=1, source_target_pairs={{0,16},{1,17},{2,18},{3,19},{16,0},{17,1},{18,2},{19,3},{4,20},{5,... | collective-permute-start | bytes 1105928 | tf_op jit(solution)/shard_map/ppermute | solution.py:49
  227.3 15.2 %collective-permute-start.33 = (bf16[240,768]{1,0:T(8,128)(2,1)S(1)}, bf16[240,768]{1,0:T(8,128)(2,1)S(1)}, u32[]{:S(2)}, u32[]{:S(2)}) collective-permute-start(bf16[240,768]{1,0:T(8,128)(2,1)S(1)} %pad_maximum_fusion.10), channel_id=1, source_target_pairs={{0,18},{1,19},{2,16},{3,17},{16,2},{17,3},{18,0},{19,1},{4,22},{5,... | collective-permute-start | bytes 1105928 | tf_op jit(solution)/shard_map/ppermute | solution.py:49
  253.3 212.2 %reduce-scatter.3.cloned.1.call-start = ((), (), s32[]{:S(2)}) async-start(), calls=%async_computation.4 | async-start | bytes 5898240 | tf_op jit(solution)/shard_map/reduce_scatter | solution.py:1040
  269.7 19.4 %collective-permute-start.35 = (bf16[240,768]{1,0:T(8,128)(2,1)S(1)}, bf16[240,768]{1,0:T(8,128)(2,1)S(1)}, u32[]{:S(2)}, u32[]{:S(2)}) collective-permute-start(bf16[240,768]{1,0:T(8,128)(2,1)S(1)} %pad_maximum_fusion.11), channel_id=1, source_target_pairs={{0,2},{1,3},{2,0},{3,1},{16,18},{17,19},{18,16},{19,17},{4,6},{5,7... | collective-permute-start | bytes 1105928 | tf_op jit(solution)/shard_map/ppermute | solution.py:49
  269.8 19.3 %collective-permute-start.36 = (bf16[240,768]{1,0:T(8,128)(2,1)S(1)}, bf16[240,768]{1,0:T(8,128)(2,1)S(1)}, u32[]{:S(2)}, u32[]{:S(2)}) collective-permute-start(bf16[240,768]{1,0:T(8,128)(2,1)S(1)} %pad_maximum_fusion.12), channel_id=1, source_target_pairs={{0,16},{1,17},{2,18},{3,19},{16,0},{17,1},{18,2},{19,3},{4,20},{5,... | collective-permute-start | bytes 1105928 | tf_op jit(solution)/shard_map/ppermute | solution.py:49
  270.5 18.6 %collective-permute-start.37 = (bf16[240,768]{1,0:T(8,128)(2,1)S(1)}, bf16[240,768]{1,0:T(8,128)(2,1)S(1)}, u32[]{:S(2)}, u32[]{:S(2)}) collective-permute-start(bf16[240,768]{1,0:T(8,128)(2,1)S(1)} %pad_maximum_fusion.13), channel_id=1, source_target_pairs={{0,18},{1,19},{2,16},{3,17},{16,2},{17,3},{18,0},{19,1},{4,22},{5,... | collective-permute-start | bytes 1105928 | tf_op jit(solution)/shard_map/ppermute | solution.py:49
  292.6 10.0 %collective-permute-start.39 = (bf16[240,768]{1,0:T(8,128)(2,1)S(1)}, bf16[240,768]{1,0:T(8,128)(2,1)S(1)}, u32[]{:S(2)}, u32[]{:S(2)}) collective-permute-start(bf16[240,768]{1,0:T(8,128)(2,1)S(1)} %pad_maximum_fusion.14), channel_id=1, source_target_pairs={{0,2},{1,3},{2,0},{3,1},{16,18},{17,19},{18,16},{19,17},{4,6},{5,7... | collective-permute-start | bytes 1105928 | tf_op jit(solution)/shard_map/ppermute | solution.py:49
  292.7 9.9 %collective-permute-start.40 = (bf16[240,768]{1,0:T(8,128)(2,1)S(1)}, bf16[240,768]{1,0:T(8,128)(2,1)S(1)}, u32[]{:S(2)}, u32[]{:S(2)}) collective-permute-start(bf16[240,768]{1,0:T(8,128)(2,1)S(1)} %pad_maximum_fusion.15), channel_id=1, source_target_pairs={{0,16},{1,17},{2,18},{3,19},{16,0},{17,1},{18,2},{19,3},{4,20},{5,... | collective-permute-start | bytes 1105928 | tf_op jit(solution)/shard_map/ppermute | solution.py:49
  293.4 17.0 %collective-permute-start.41 = (bf16[240,768]{1,0:T(8,128)(2,1)S(1)}, bf16[240,768]{1,0:T(8,128)(2,1)S(1)}, u32[]{:S(2)}, u32[]{:S(2)}) collective-permute-start(bf16[240,768]{1,0:T(8,128)(2,1)S(1)} %pad_maximum_fusion.16), channel_id=1, source_target_pairs={{0,18},{1,19},{2,16},{3,17},{16,2},{17,3},{18,0},{19,1},{4,22},{5,... | collective-permute-start | bytes 1105928 | tf_op jit(solution)/shard_map/ppermute | solution.py:49
  319.9 16.1 %collective-permute-start.42 = (bf16[192,768]{1,0:T(8,128)(2,1)}, bf16[192,768]{1,0:T(8,128)(2,1)S(1)}, u32[]{:S(2)}, u32[]{:S(2)}) collective-permute-start(bf16[192,768]{1,0:T(8,128)(2,1)} %get-tuple-element.210), channel_id=1, source_target_pairs={{0,1},{1,0},{2,3},{3,2},{4,5},{5,4},{6,7},{7,6},{8,9},{9,8},{10,11... | collective-permute-start | bytes 884744 | tf_op jit(solution)/shard_map/ppermute | solution.py:49
  321.2 14.9 %collective-permute-start.43 = (bf16[192,768]{1,0:T(8,128)(2,1)}, bf16[192,768]{1,0:T(8,128)(2,1)S(1)}, u32[]{:S(2)}, u32[]{:S(2)}) collective-permute-start(bf16[192,768]{1,0:T(8,128)(2,1)} %get-tuple-element.211), channel_id=1, source_target_pairs={{0,2},{1,3},{2,0},{3,1},{4,6},{5,7},{6,4},{7,5},{8,10},{9,11},{10,... | collective-permute-start | bytes 884744 | tf_op jit(solution)/shard_map/ppermute | solution.py:49
  322.7 14.2 %collective-permute-start.44 = (bf16[192,768]{1,0:T(8,128)(2,1)}, bf16[192,768]{1,0:T(8,128)(2,1)S(1)}, u32[]{:S(2)}, u32[]{:S(2)}) collective-permute-start(bf16[192,768]{1,0:T(8,128)(2,1)} %get-tuple-element.212), channel_id=1, source_target_pairs={{0,3},{1,2},{2,1},{3,0},{4,7},{5,6},{6,5},{7,4},{8,11},{9,10},{10,... | collective-permute-start | bytes 884744 | tf_op jit(solution)/shard_map/ppermute | solution.py:49
  385.1 6.1 %collective-permute-start.45 = (bf16[768,768]{1,0:T(8,128)(2,1)}, bf16[768,768]{1,0:T(8,128)(2,1)S(1)}, u32[]{:S(2)}, u32[]{:S(2)}) collective-permute-start(bf16[768,768]{1,0:T(8,128)(2,1)} %get-tuple-element.223), channel_id=1, source_target_pairs={{0,1},{1,0},{2,3},{3,2},{4,5},{5,4},{6,7},{7,6},{8,9},{9,8},{10,11... | collective-permute-start | bytes 3538952 | tf_op jit(solution)/shard_map/ppermute | solution.py:49
  392.2 16.4 %collective-permute-start.46 = (bf16[384,768]{1,0:T(8,128)(2,1)S(1)}, bf16[384,768]{1,0:T(8,128)(2,1)}, u32[]{:S(2)}, u32[]{:S(2)}) collective-permute-start(bf16[384,768]{1,0:T(8,128)(2,1)S(1)} %slice.283), channel_id=1, source_target_pairs={{0,2},{1,3},{2,0},{3,1},{4,6},{5,7},{6,4},{7,5},{8,10},{9,11},{10,... | collective-permute-start | bytes 1769480 | tf_op jit(solution)/shard_map/ppermute | solution.py:49
  408.6 6.6 %collective-permute-start.51 = (bf16[2,768,768]{2,1,0:T(8,128)(2,1)}, bf16[2,768,768]{2,1,0:T(8,128)(2,1)S(1)}, u32[]{:S(2)}, u32[]{:S(2)}) collective-permute-start(bf16[2,768,768]{2,1,0:T(8,128)(2,1)} %get-tuple-element.246), channel_id=1, source_target_pairs={{0,1},{1,0},{2,3},{3,2},{4,5},{5,4},{6,7},{7,6},{8,9},{9,8},{10,11... | collective-permute-start | bytes 7077896 | tf_op jit(solution)/shard_map/ppermute | solution.py:49
  411.2 14.6 %collective-permute-start.49 = (bf16[384,768]{1,0:T(8,128)(2,1)S(1)}, bf16[384,768]{1,0:T(8,128)(2,1)S(1)}, u32[]{:S(2)}, u32[]{:S(2)}) collective-permute-start(bf16[384,768]{1,0:T(8,128)(2,1)S(1)} %slice.282), channel_id=1, source_target_pairs={{0,2},{1,3},{2,0},{3,1},{4,6},{5,7},{6,4},{7,5},{8,10},{9,11},{10,... | collective-permute-start | bytes 1769480 | tf_op jit(solution)/shard_map/ppermute | solution.py:49
  411.7 16.1 %collective-permute-start.53 = (bf16[768,768]{1,0:T(8,128)(2,1)}, bf16[768,768]{1,0:T(8,128)(2,1)}, u32[]{:S(2)}, u32[]{:S(2)}) collective-permute-start(bf16[768,768]{1,0:T(8,128)(2,1)} %get-tuple-element.250), channel_id=1, source_target_pairs={{0,1},{1,0},{2,3},{3,2},{4,5},{5,4},{6,7},{7,6},{8,9},{9,8},{10,11... | collective-permute-start | bytes 3538952 | tf_op jit(solution)/shard_map/ppermute | solution.py:49
  426.6 17.2 %collective-permute-start.52 = (bf16[480,768]{1,0:T(8,128)(2,1)}, bf16[480,768]{1,0:T(8,128)(2,1)S(1)}, u32[]{:S(2)}, u32[]{:S(2)}) collective-permute-start(bf16[480,768]{1,0:T(8,128)(2,1)} %pad_maximum_fusion.4), channel_id=1, source_target_pairs={{0,2},{1,3},{2,0},{3,1},{4,6},{5,7},{6,4},{7,5},{8,10},{9,11},{10,... | collective-permute-start | bytes 2211848 | tf_op jit(solution)/shard_map/ppermute | solution.py:49
  427.0 15.4 %collective-permute-start.48 = (bf16[384,768]{1,0:T(8,128)(2,1)}, bf16[384,768]{1,0:T(8,128)(2,1)}, u32[]{:S(2)}, u32[]{:S(2)}) collective-permute-start(bf16[384,768]{1,0:T(8,128)(2,1)} %fusion.4), channel_id=1, source_target_pairs={{0,12},{4,0},{8,4},{12,8},{1,13},{5,1},{9,5},{13,9},{2,14},{6,2},{... | collective-permute-start | bytes 1769480 | tf_op jit(solution)/shard_map/ppermute | solution.py:53
  445.7 16.7 %collective-permute-start.56 = (bf16[4,96,777]{2,1,0:T(8,128)(2,1)S(1)}, bf16[4,96,777]{2,1,0:T(8,128)(2,1)S(1)}, u32[]{:S(2)}, u32[]{:S(2)}) collective-permute-start(bf16[4,96,777]{2,1,0:T(8,128)(2,1)S(1)} %get-tuple-element.319), channel_id=1, source_target_pairs={{0,16},{16,0},{1,17},{17,1},{2,18},{18,2},{3,19},{19,3},{4,20},{20... | collective-permute-start | bytes 1790216 | tf_op jit(solution)/shard_map/ppermute | solution.py:49
  449.1 13.2 %collective-permute-start.55 = (bf16[384,768]{1,0:T(8,128)(2,1)}, bf16[384,768]{1,0:T(8,128)(2,1)}, u32[]{:S(2)}, u32[]{:S(2)}) collective-permute-start(bf16[384,768]{1,0:T(8,128)(2,1)} %slice.281), channel_id=1, source_target_pairs={{0,2},{1,3},{2,0},{3,1},{4,6},{5,7},{6,4},{7,5},{8,10},{9,11},{10,... | collective-permute-start | bytes 1769480 | tf_op jit(solution)/shard_map/ppermute | solution.py:49
  450.7 17.8 %collective-permute-start.54 = (bf16[384,768]{1,0:T(8,128)(2,1)}, bf16[384,768]{1,0:T(8,128)(2,1)}, u32[]{:S(2)}, u32[]{:S(2)}) collective-permute-start(bf16[384,768]{1,0:T(8,128)(2,1)} %add_convert_fusion.2), channel_id=1, source_target_pairs={{0,12},{4,0},{8,4},{12,8},{1,13},{5,1},{9,5},{13,9},{2,14},{6,2},{... | collective-permute-start | bytes 1769480 | tf_op jit(solution)/shard_map/ppermute | solution.py:53
  462.3 46.3 %collective-permute-start.63 = (bf16[480,768]{1,0:T(8,128)(2,1)}, bf16[480,768]{1,0:T(8,128)(2,1)}, u32[]{:S(2)}, u32[]{:S(2)}) collective-permute-start(bf16[480,768]{1,0:T(8,128)(2,1)} %slice_bitcast_fusion), channel_id=1, source_target_pairs={{0,2},{1,3},{2,0},{3,1},{4,6},{5,7},{6,4},{7,5},{8,10},{9,11},{10,... | collective-permute-start | bytes 2211848 | tf_op jit(solution)/shard_map/ppermute | solution.py:49
  471.5 7.0 %collective-permute-start.57 = (bf16[96,777]{0,1:T(8,128)(2,1)}, bf16[96,777]{0,1:T(8,128)(2,1)}, u32[]{:S(2)}, u32[]{:S(2)}) collective-permute-start(bf16[96,777]{0,1:T(8,128)(2,1)} %get-tuple-element.324), channel_id=1, source_target_pairs={{0,4},{4,0},{8,12},{12,8},{1,5},{5,1},{9,13},{13,9},{2,6},{6,2},{1... | collective-permute-start | bytes 447560 | tf_op jit(solution)/shard_map/ppermute | solution.py:49
  471.5 9.8 %collective-permute-start.59 = (bf16[96,777]{0,1:T(8,128)(2,1)S(1)}, bf16[96,777]{0,1:T(8,128)(2,1)}, u32[]{:S(2)}, u32[]{:S(2)}) collective-permute-start(bf16[96,777]{0,1:T(8,128)(2,1)S(1)} %get-tuple-element.325), channel_id=1, source_target_pairs={{0,12},{4,8},{8,4},{12,0},{1,13},{5,9},{9,5},{13,1},{2,14},{6,10},... | collective-permute-start | bytes 447560 | tf_op jit(solution)/shard_map/ppermute | solution.py:49
  471.5 31.3 %collective-permute-start.58 = (bf16[96,777]{0,1:T(8,128)(2,1)S(1)}, bf16[96,777]{0,1:T(8,128)(2,1)}, u32[]{:S(2)}, u32[]{:S(2)}) collective-permute-start(bf16[96,777]{0,1:T(8,128)(2,1)S(1)} %get-tuple-element.326), channel_id=1, source_target_pairs={{0,8},{4,12},{8,0},{12,4},{1,9},{5,13},{9,1},{13,5},{2,10},{6,14},... | collective-permute-start | bytes 447560 | tf_op jit(solution)/shard_map/ppermute | solution.py:49
  475.3 35.2 %collective-permute-start.65 = (bf16[384,768]{1,0:T(8,128)(2,1)S(1)}, bf16[384,768]{1,0:T(8,128)(2,1)}, u32[]{:S(2)}, u32[]{:S(2)}) collective-permute-start(bf16[384,768]{1,0:T(8,128)(2,1)S(1)} %copy-done.15), channel_id=1, source_target_pairs={{2,12},{3,13},{6,0},{7,1},{10,4},{11,5},{14,8},{15,9},{18,28},{19,... | collective-permute-start | bytes 1769480 | tf_op jit(solution)/shard_map/ppermute | solution.py:1116
  478.5 32.0 %collective-permute-start.64 = (bf16[384,768]{1,0:T(8,128)(2,1)S(1)}, bf16[384,768]{1,0:T(8,128)(2,1)S(1)}, u32[]{:S(2)}, u32[]{:S(2)}) collective-permute-start(bf16[384,768]{1,0:T(8,128)(2,1)S(1)} %copy-done.15), channel_id=1, source_target_pairs={{0,12},{1,13},{4,0},{5,1},{8,4},{9,5},{12,8},{13,9},{16,28},{17,29... | collective-permute-start | bytes 1769480 | tf_op jit(solution)/shard_map/ppermute | solution.py:1116
  504.3 13.3 %collective-permute-start.62 = (bf16[96,10]{0,1:T(8,128)(2,1)S(1)}, bf16[96,10]{0,1:T(8,128)(2,1)S(1)}, u32[]{:S(2)}, u32[]{:S(2)}) collective-permute-start(bf16[96,10]{0,1:T(8,128)(2,1)S(1)} %fusion.17), channel_id=1, source_target_pairs={{0,3},{1,2},{2,1},{3,0},{4,7},{5,6},{6,5},{7,4},{8,11},{9,10},{10,... | collective-permute-start | bytes 5768 | tf_op jit(solution)/shard_map/ppermute | solution.py:49
  508.5 9.2 %collective-permute-start.61 = (bf16[96,10]{0,1:T(8,128)(2,1)S(1)}, bf16[96,10]{0,1:T(8,128)(2,1)S(1)}, u32[]{:S(2)}, u32[]{:S(2)}) collective-permute-start(bf16[96,10]{0,1:T(8,128)(2,1)S(1)} %fusion.17), channel_id=1, source_target_pairs={{0,2},{1,3},{2,0},{3,1},{4,6},{5,7},{6,4},{7,5},{8,10},{9,11},{10,... | collective-permute-start | bytes 5768 | tf_op jit(solution)/shard_map/ppermute | solution.py:49
  508.7 9.0 %collective-permute-start.60 = (bf16[96,10]{0,1:T(8,128)(2,1)S(1)}, bf16[96,10]{0,1:T(8,128)(2,1)S(1)}, u32[]{:S(2)}, u32[]{:S(2)}) collective-permute-start(bf16[96,10]{0,1:T(8,128)(2,1)S(1)} %fusion.17), channel_id=1, source_target_pairs={{0,1},{1,0},{2,3},{3,2},{4,5},{5,4},{6,7},{7,6},{8,9},{9,8},{10,11... | collective-permute-start | bytes 5768 | tf_op jit(solution)/shard_map/ppermute | solution.py:49
  (51 other events, 313.0 us)
Sparse Core Ops, SparseCore 0:
  60.0 102.7 all-gather.2
  164.4 87.9 all-gather.4
  254.6 85.7 reduce-scatter.4
  342.6 85.7 reduce-scatter.2

commit v7 on v6

--- a/solution.py
+++ b/solution.py
@@ -285,11 +285,10 @@
 def attend_backward_kernel(sizes, info, query, lse_prompt, lse_cont, local, *rest):
     count_remote = sizes[2] - 1
     remote, rest = rest[:count_remote], rest[count_remote:]
-    query_weight, pair_weight, *rest = rest
+    pair_weight, *rest = rest
     grads, mixed, rest = rest[:4], rest[4:8], rest[8:]
     grad_query, grad_local, *rest, grad, centre, sum_local, sum_remote = rest
     grad_remote, rest = rest[:count_remote], rest[count_remote:]
-    *rest, keep_local, send_local = rest
     keep_remote, send_remote = rest[: len(rest) // 2], rest[len(rest) // 2 :]
     lse = (lse_prompt, lse_cont)
     width = query.shape[0]
@@ -353,13 +352,7 @@
             if outs:
                 flat = part.reshape(half * CHUNK, 2 * width)
                 outs[place][...] = low(dot_last(flat, pair_weight[...]))
-    for at, out in enumerate((keep_local.at[1], send_local.at[1], keep_local.at[0], send_local.at[0])):
-        chunks = slice(at * half, (at + 1) * half)
-        part = low(sum_local[chunks])
-        grad_local[chunks] = part
-        flat = part.reshape(half * CHUNK, 2 * width)
-        part = grad_query[:, at * each : (at + 1) * each].T
-        out[...] = low(dot_last(flat, pair_weight[...]) + dot_last(part, query_weight[...]))
+    grad_local[...] = low(sum_local[...])
 
 
 def attend_cost(factor, sizes, heads):
@@ -389,12 +382,11 @@
 
 
 def attend_backward(
-    sizes, info, query, lse_prompt, lse_cont, local, remote, query_weight, pair_weight, grads, mixed
+    sizes, info, query, lse_prompt, lse_cont, local, remote, pair_weight, grads, mixed
 ):
     pairs = [local] + list(remote)
     remote_rows = 2 * len(remote) if len(remote) <= 4 else 0
-    each = shape((grads[0].shape[1], query_weight.shape[0]))
-    both = shape((2,) + each.shape)
+    each = shape((grads[0].shape[1], pair_weight.shape[0]))
     count = len(remote)
     return pl.pallas_call(
         functools.partial(attend_backward_kernel, sizes),
@@ -402,11 +394,9 @@
             shape(query.shape),
             *(shape(one.shape) for one in pairs),
             *([each] * remote_rows),
-            both,
-            both,
-        ),
-        in_specs=[SM] + [VM] * (5 + len(pairs) + 2 * len(grads)),
-        out_specs=(VM,) * (3 + len(pairs) + remote_rows),
+        ),
+        in_specs=[SM] + [VM] * (4 + len(pairs) + 2 * len(grads)),
+        out_specs=(VM,) * (1 + len(pairs) + remote_rows),
         scratch_shapes=[
             pltpu.VMEM(query.shape, BF16),
             pltpu.VMEM((8, query.shape[1]), F32),
@@ -416,7 +406,7 @@
         compiler_params=ROOM,
         cost_estimate=attend_cost(40, sizes, query.shape[0] // HD),
         name="attend_backward",
-    )(info, query, lse_prompt, lse_cont, *pairs, query_weight, pair_weight, *grads, *mixed)
+    )(info, query, lse_prompt, lse_cont, *pairs, pair_weight, *grads, *mixed)
 
 
 def rows_remote_kernel(grad_pairs, pair_weight, keep, send):
@@ -439,6 +429,42 @@
         ),
         name="rows_remote",
     )(grad_pairs, pair_weight)
+
+
+def rows_local_kernel(grad_pairs, grad_query, query_weight, pair_weight, keep, send):
+    half = grad_pairs.shape[0] // 2
+    wide = grad_pairs.shape[2]
+    each = half * CHUNK
+    query_rows = grad_query[...].T
+    rows = dot_last(grad_pairs[...].reshape(2 * each, wide), pair_weight[...])
+    rows = rows + dot_last(query_rows, query_weight[...])
+    keep[0] = low(rows[:each])
+    send[0] = low(rows[each:])
+
+
+def rows_local(grad_pairs, grad_query, query_weight, pair_weight, each):
+    width = pair_weight.shape[0]
+    chunks = 2 * each // CHUNK
+    return pl.pallas_call(
+        rows_local_kernel,
+        grid=(2,),
+        in_specs=[
+            pl.BlockSpec((chunks,) + grad_pairs.shape[1:], lambda at: (1 - at, 0, 0)),
+            pl.BlockSpec((grad_query.shape[0], 2 * each), lambda at: (0, 1 - at)),
+            pl.BlockSpec(query_weight.shape, lambda at: (0, 0)),
+            pl.BlockSpec(pair_weight.shape, lambda at: (0, 0)),
+        ],
+        out_specs=(
+            pl.BlockSpec((1, each, width), lambda at: (at, 0, 0)),
+            pl.BlockSpec((1, each, width), lambda at: (at, 0, 0)),
+        ),
+        out_shape=(shape((2, each, width)), shape((2, each, width))),
+        compiler_params=ROOM,
+        cost_estimate=pl.CostEstimate(
+            flops=6 * 2 * each * pair_weight.size, bytes_accessed=2 * 10**7, transcendentals=0
+        ),
+        name="rows_local",
+    )(grad_pairs, grad_query, query_weight, pair_weight)
 
 
 def qkv_grad_kernel(places, grad_query, *rest):
@@ -1046,13 +1072,12 @@
         lse_cont,
         local,
         remote,
-        query_weight,
         pair_weight,
         grad_near,
         mixed,
     )
     count = ctx_count - 1
-    grad_remote, (*remote_rows, local_keep, local_send) = grads[:count], grads[count:]
+    grad_remote, remote_rows = grads[:count], grads[count:]
     if remote_rows:
         remote_rows = list(zip(remote_rows[:count], remote_rows[count:]))
     else:
@@ -1073,8 +1098,8 @@
     near = across(message)
     grad_pairs, message = lax.optimization_barrier(([grad_local, *grad_remote], message))
     qkv_part = qkv_grad(grad_query, grad_pairs, rows)
-    near, qkv_part, following, local_send, proj_send, remote_rows[2:] = lax.optimization_barrier(
-        (near, qkv_part, following, local_send, proj_send, remote_rows[2:])
+    near, qkv_part, following, grad_local, proj_send, remote_rows[2:] = lax.optimization_barrier(
+        (near, qkv_part, following, grad_local, proj_send, remote_rows[2:])
     )
     running = low(piece + near.astype(F32))
     for place in range(1, count):
@@ -1085,6 +1110,9 @@
         if place < count - 1:
             following = chip_rows(*remote_rows[place + 1])
         if place == 1:
+            local_keep, local_send = rows_local(
+                grad_local, grad_query, query_weight, pair_weight, tok_dev
+            )
             local_send = beside(local_send)
             far_message = low(local_keep[0].astype(F32) + local_send[0].astype(F32))
             first_rows = (tok_dev - local_width) // 2

time: 531 us -> 533 us (level)
    pallas_call x0 -> x1, Pallas kernels: none -> 7.29 us  [rows_local(): pl.pallas_call(rows_local_kernel, grid=(2,), in_specs=[pl.BlockSpec((chun...]
    unnamed x104 -> x106, local copies, waits for them, and re-layouts: 16.3 us -> 16.2 us
  transfers between devices with their start and end apart: 70 -> 70, of which waited for: 26 -> 27; matrix products, arithmetic and copies ran while one was open for 10% -> 10% of each run, Pallas kernels for 38% -> 38%
where the time goes in v7:
time: 533 us; the launch traced here: 528 us
  Pallas kernels  204 us (38%)
  waiting for transfers between devices  170 us (32%)
  starting transfers between devices  74.3 us (14%)
  local copies, waits for them, and re-layouts  37.6 us (7%)
  other arithmetic  25.8 us (5%)
  between operations  14.8 us (3%)
    ppermute x59, waiting for transfers between devices, xor_swap(): lax.ppermute(value, axis, [(place, place ^ mask) for place in range(size)])  123 us
    ppermute x59, starting transfers between devices, xor_swap(): lax.ppermute(value, axis, [(place, place ^ mask) for place in range(size)])  61.8 us
    ppermute x5, waiting for transfers between devices, ring_step(): lax.ppermute(value, axis, [(place, (place + shift) % size) for place in r...  46.3 us
    pallas_call x1, Pallas kernels, attend_backward(): pl.pallas_call(functools.partial(attend_backward_kernel, sizes), out_shap...  43.3 us
    pallas_call x1, Pallas kernels, attend_forward(): pl.pallas_call(functools.partial(attend_forward_kernel, sizes), out_shape...  23.1 us
    pallas_call x1, Pallas kernels, expert_back(): pl.pallas_call(expert_back_kernel, grid=(units // UNITS,), in_specs=[whol...  16.3 us
    unnamed x106, local copies, waits for them, and re-layouts  16.2 us
    pallas_call x1, Pallas kernels, qkv_grad(): pl.pallas_call(functools.partial(qkv_grad_kernel, len(pairs)), out_shape=...  14.6 us
  transfers between devices with their start and end apart: 70, of which 27 were waited for; matrix products, arithmetic and copies ran while one was open for 10% of the time, Pallas kernels for 38%

profile of v7, /device:TPU:25, one launch (start us, length us, event | category | flops | bytes accessed | tf_op | source)
XLA Modules:
  0.0 528.3 jit_solution(133683729368281844)
XLA Ops:
  7.2 3.0 normalize.1
  14.0 2.2 collective-permute-start
  16.2 8.6 %collective-permute-done.3.rest_3_.rest_7_ = bf16[384,768]{1,0:T(8,128)(2,1)} collective-permute-done((bf16[384,768]{1,0:T(8,128)(2,1)}, bf16[384,768]{1,0:T(8,128)(2,1)}, u32[]{:S(2)}, u32[]{:S(2)}) %collective-permute-start.3) | collective-permute-done | bytes 589856 | tf_op jit(solution)/shard_map/ppermute | solution.py:49
  24.7 2.0 fusion.34
  26.7 4.1 collective-permute-done.1
  32.7 1.5 collective-permute-start.4
  34.5 12.1 %collective-permute-done.6 = bf16[1,4,96,776]{3,2,1,0:T(8,128)(2,1)S(1)} collective-permute-done((bf16[1,4,96,776]{3,2,1,0:T(8,128)(2,1)S(1)}, bf16[1,4,96,776]{3,2,1,0:T(8,128)(2,1)S(1)}, u32[]{:S(2)}, u32[]{:S(2)}) %collective-permute-start.6) | collective-permute-done | bytes 596000 | tf_op jit(solution)/shard_map/ppermute | solution.py:49
  47.2 2.3 collective-permute-start.7
  49.5 10.3 %collective-permute-done.7.rest_0_.rest_14_ = bf16[384,768]{1,0:T(8,128)(2,1)} collective-permute-done((bf16[384,768]{1,0:T(8,128)(2,1)}, bf16[384,768]{1,0:T(8,128)(2,1)}, u32[]{:S(2)}, u32[]{:S(2)}) %collective-permute-start.7) | collective-permute-done | bytes 589856 | tf_op jit(solution)/shard_map/ppermute | solution.py:53
  59.9 3.6 collective-permute-start.10
  68.1 11.7 %collective-permute-done.8.rest_1_.rest_11_ = bf16[384,768]{1,0:T(8,128)(2,1)} collective-permute-done((bf16[384,768]{1,0:T(8,128)(2,1)}, bf16[384,768]{1,0:T(8,128)(2,1)}, u32[]{:S(2)}, u32[]{:S(2)}) %collective-permute-start.8) | collective-permute-done | bytes 589856 | tf_op jit(solution)/shard_map/ppermute | solution.py:49
  80.1 4.3 collective-permute-start.9
  86.4 1.8 collective-permute-start.13
  88.2 8.3 %project_local.1 = (bf16[192,3072]{1,0:T(8,128)(2,1)}, bf16[24,128,384]{2,1,0:T(8,128)(2,1)}) custom-call(bf16[768,192]{1,0:T(8,128)(2,1)} %get-tuple-element.321.query_weight, bf16[768,384]{1,0:T(8,128)(2,1)} %slice.224.pair_weight.rest_3_, bf16[768,768]{1,0:T(8,128)(2,1)} %get-tuple-element.143.rest_0_.rest_4_, ...), custom_call_target="tpu_custom_call" | custom-call | flops 2717908992 | bytes 10000000 | tf_op jit(solution)/shard_map/project_local/pallas_call | solution.py:219
  96.5 24.8 %collective-permute-done.9.rest_0_.rest_18_ = bf16[384,768]{1,0:T(8,128)(2,1)S(1)} collective-permute-done((bf16[384,768]{1,0:T(8,128)(2,1)}, bf16[384,768]{1,0:T(8,128)(2,1)S(1)}, u32[]{:S(2)}, u32[]{:S(2)}) %collective-permute-start.9) | collective-permute-done | bytes 589856 | tf_op jit(solution)/shard_map/ppermute | solution.py:53
  123.6 4.6 collective-permute-start.14
  128.9 3.4 collective-permute-done.18.rest_1_.rest_19_
  132.3 5.0 collective-permute-start.20
  139.6 4.2 project_remote.3.rest_0_
  143.8 4.2 project_remote.4.rest_1_
  150.7 4.2 project_remote.5.rest_2_
  155.0 23.1 %attend_forward.1 = (bf16[192,768]{1,0:T(8,128)(2,1)}, bf16[192,768]{1,0:T(8,128)(2,1)}, bf16[192,768]{1,0:T(8,128)(2,1)}, bf16[192,768]{1,0:T(8,128)(2,1)}, f32...) custom-call(s32[49]{0:T(128)} %pad_add_fusion.1.info, bf16[192,3072]{1,0:T(8,128)(2,1)} %get-tuple-element.158.query, ...), custom_call_target="tpu_custom_call" | custom-call | flops 9663676416 | bytes 10000000 | tf_op jit(solution)/shard_map/attend_forward/pallas_call | solution.py:368
  184.2 1.9 slice_bitcast_fusion.4
  186.6 7.2 %collective-permute-done.23.rest_3_ = bf16[192,768]{1,0:T(8,128)(2,1)S(1)} collective-permute-done((bf16[192,768]{1,0:T(8,128)(2,1)}, bf16[192,768]{1,0:T(8,128)(2,1)S(1)}, u32[]{:S(2)}, u32[]{:S(2)}) %collective-permute-start.23) | collective-permute-done | bytes 294944 | tf_op jit(solution)/shard_map/ppermute | solution.py:49
  194.5 8.6 %middle_rows.1 = (bf16[480,768]{1,0:T(8,128)(2,1)}, bf16[480,768]{1,0:T(8,128)(2,1)}, bf16[480,768]{1,0:T(8,128)(2,1)}, bf16[480,768]{1,0:T(8,128)(2,1)}, f32[76...) custom-call(bf16[768,768]{1,0:T(8,128)(2,1)} %tokens.5, bf16[768,768]{1,0:T(8,128)(2,1)} %cotangent.5, ...), custom_call_target="tpu_custom_call" | custom-call | tf_op jit(solution)/shard_map/middle_rows/pallas_call | solution.py:598
  208.6 7.3 %collective-permute-done.27.refs_2_ = bf16[240,768]{1,0:T(8,128)(2,1)S(1)} collective-permute-done((bf16[240,768]{1,0:T(8,128)(2,1)S(1)}, bf16[240,768]{1,0:T(8,128)(2,1)S(1)}, u32[]{:S(2)}, u32[]{:S(2)}) %collective-permute-start.27) | collective-permute-done | bytes 368672 | tf_op jit(solution)/shard_map/ppermute | solution.py:49
  217.0 7.3 %collective-permute-done.29.refs_4_ = bf16[240,768]{1,0:T(8,128)(2,1)S(1)} collective-permute-done((bf16[240,768]{1,0:T(8,128)(2,1)S(1)}, bf16[240,768]{1,0:T(8,128)(2,1)S(1)}, u32[]{:S(2)}, u32[]{:S(2)}) %collective-permute-start.29) | collective-permute-done | bytes 368672 | tf_op jit(solution)/shard_map/ppermute | solution.py:49
  228.2 14.0 %expert_hidden.1 = (bf16[960,3072]{1,0:T(8,128)(2,1)}, bf16[960,3072]{1,0:T(8,128)(2,1)}, bf16[768,960]{1,0:T(8,128)(2,1)}) custom-call(bf16[480,768]{1,0:T(8,128)(2,1)} %get-tuple-element.176.refs_0_, bf16[480,768]{1,0:T(8,128)(2,1)} %copy-done.21, bf16[240,768]{1,0:T(8,128)(2,1)} %copy-done.34, bf16[240,768]{1,0:T(8,128)(2,1)} %copy-done.35, ...), custom_call_target="tpu_custom_call" | custom-call | flops 4529848320 | bytes 16515072 | tf_op jit(solution)/shard_map/expert_hidden/pallas_call | solution.py:813
  243.2 9.8 %expert_down_grad.1 = (bf16[768,3072]{1,0:T(8,128)(2,1)}, bf16[960,768]{1,0:T(8,128)(2,1)}) custom-call(bf16[480,768]{1,0:T(8,128)(2,1)} %get-tuple-element.183.refs_0_, bf16[480,768]{1,0:T(8,128)(2,1)} %copy-done.20, bf16[240,768]{1,0:T(8,128)(2,1)} %copy-done.37, bf16[240,768]{1,0:T(8,128)(2,1)} %copy-done.38, bf16[240,768]{1,0:T(8,128)(2,1)} %copy-done.39, ...), custom_call_target="tpu_custom_call" | custom-call | flops 4529848320 | bytes 16515072 | tf_op jit(solution)/shard_map/expert_down_grad/pallas_call | solution.py:850
  253.1 9.5 %expert_out.1 = (bf16[480,768]{1,0:T(8,128)(2,1)}, bf16[480,768]{1,0:T(8,128)(2,1)}) custom-call(bf16[960,3072]{1,0:T(8,128)(2,1)} %get-tuple-element.187.refs_5_.hidden, bf16[3072,768]{1,0:T(8,128)(2,1)} %bitcast.109), custom_call_target="tpu_custom_call" | custom-call | flops 4529848320 | bytes 16515072 | tf_op jit(solution)/shard_map/expert_out/pallas_call | solution.py:829
  262.5 3.6 collective-permute-start.34
  266.1 2.1 collective-permute-done.34.rest_1_
  270.5 2.1 collective-permute-start.37
  272.6 16.3 %expert_back.1 = (bf16[480,768]{1,0:T(8,128)(2,1)}, bf16[480,768]{1,0:T(8,128)(2,1)}, bf16[960,3072]{1,0:T(8,128)(2,1)}) custom-call(bf16[960,768]{1,0:T(8,128)(2,1)} %get-tuple-element.186.grads, bf16[960,3072]{1,0:T(8,128)(2,1)} %get-tuple-element.192.slope, bf16[768,3072]{1,0:T(8,128)(2,1)} %bitcast.108, bf16[3072,768]{1,0:T(8,128)(2,1)} %bitcast.110), custom_call_target="tpu_custom_call" | custom-call | flops 9059696640 | bytes 21233664 | tf_op jit(solution)/shard_map/expert_back/pallas_call | solution.py:867
  293.2 2.1 collective-permute-start.41
  296.2 6.1 %made_rows.1 = (bf16[768,768]{1,0:T(8,128)(2,1)}, bf16[768,8]{1,0:T(8,128)(2,1)}, f32[8,768]{1,0:T(8,128)}) custom-call(bf16[768,768]{1,0:T(8,128)(2,1)} %cotangent.5, s32[768,1]{1,0:T(8,128)} %copy.103.ids, s32[768,1]{1,0:T(8,128)} %broadcast_in_dim.45.place_column, f32[768,768]{1,0:T(8,128)} %get-tuple-element.169.middle, ...), custom_call_target="tpu_custom_call" | custom-call | tf_op jit(solution)/shard_map/made_rows/pallas_call | solution.py:647
  302.3 7.8 %collective-permute-done.41.rest_8_ = bf16[240,768]{1,0:T(8,128)(2,1)S(1)} collective-permute-done((bf16[240,768]{1,0:T(8,128)(2,1)S(1)}, bf16[240,768]{1,0:T(8,128)(2,1)S(1)}, u32[]{:S(2)}, u32[]{:S(2)}) %collective-permute-start.41) | collective-permute-done | bytes 368672 | tf_op jit(solution)/shard_map/ppermute | solution.py:49
  310.9 8.7 %back_rows.1 = (f32[768,768]{1,0:T(8,128)}, bf16[768,768]{1,0:T(8,128)(2,1)}, f32[8,768]{1,0:T(8,128)}, bf16[192,768]{1,0:T(8,128)(2,1)}, bf16[192,768]{1,0:T(8,...) custom-call(bf16[768,768]{1,0:T(8,128)(2,1)} %cotangent.5, f32[2,768]{1,0:T(2,128)} %gains.7, ...), custom_call_target="tpu_custom_call" | custom-call | tf_op jit(solution)/shard_map/back_rows/pallas_call | solution.py:689
  319.5 1.5 collective-permute-start.42
  321.1 1.4 collective-permute-start.43
  322.8 9.2 %expert_up_grad.1 = bf16[768,3072]{1,0:T(8,128)(2,1)} custom-call(bf16[768,960]{1,0:T(8,128)(2,1)} %get-tuple-element.216.rows_flip, bf16[960,3072]{1,0:T(8,128)(2,1)} %get-tuple-element.217.grad_pre), custom_call_target="tpu_custom_call" | custom-call | flops 4529848320 | bytes 16515072 | tf_op jit(solution)/shard_map/expert_up_grad/pallas_call | solution.py:896
  332.0 3.7 proj_grad.1
  337.5 43.3 %attend_backward.1 = (bf16[192,3072]{1,0:T(8,128)(2,1)}, bf16[24,128,384]{2,1,0:T(8,128)(2,1)}, bf16[12,128,384]{2,1,0:T(8,128)(2,1)}, bf16[12,128,384]{2,1,0:T(...) custom-call(s32[49]{0:T(128)} %pad_add_fusion.1.info, ...), custom_call_target="tpu_custom_call" | custom-call | flops 24159191040 | bytes 10000000 | tf_op jit(solution)/shard_map/attend_backward/pallas_call | solution.py:391
  381.4 2.5 collective-permute-done.47
  383.9 1.6 convert_add_fusion.1
  388.0 1.5 collective-permute-start.46
  389.4 14.6 %qkv_grad.1 = bf16[768,576]{1,0:T(8,128)(2,1)} custom-call(bf16[192,3072]{1,0:T(8,128)(2,1)} %get-tuple-element.224.grad_query, bf16[24,128,384]{2,1,0:T(8,128)(2,1)} %get-tuple-element.244.rest_0_.grad_pairs, bf16[12,128,384]{2,1,0:T(8,128)(2,1)} %get-tuple-element.230.rest_1_, bf16[12,128,384]{2,1,0:T(8,128)(2,1)} %get-tuple-element.231.rest_2_, ...), custom_call_target="tpu_custom_call" | custom-call | flops 6794772480 | bytes 20000000 | tf_op jit(solution)/shard_map/qkv_grad/pallas_call | solution.py:493
  404.1 7.3 %rows_local.1 = (bf16[2,768,768]{2,1,0:T(8,128)(2,1)}, bf16[2,768,768]{2,1,0:T(8,128)(2,1)}) custom-call(bf16[24,128,384]{2,1,0:T(8,128)(2,1)} %get-tuple-element.244.rest_0_.grad_pairs, bf16[192,3072]{1,0:T(8,128)(2,1)} %get-tuple-element.224.grad_query, bf16[768,192]{1,0:T(8,128)(2,1)} %get-tuple-element.321.query_weight, ...), custom_call_target="tpu_custom_call" | custom-call | flops 2717908992 | bytes 20000000 | tf_op jit(solution)/shard_map/rows_local/pallas_call | solution.py:448
  412.0 2.1 fusion.4
  419.5 9.1 %collective-permute-done.49 = bf16[384,768]{1,0:T(8,128)(2,1)S(1)} collective-permute-done((bf16[384,768]{1,0:T(8,128)(2,1)S(1)}, bf16[384,768]{1,0:T(8,128)(2,1)S(1)}, u32[]{:S(2)}, u32[]{:S(2)}) %collective-permute-start.49) | collective-permute-done | bytes 589856 | tf_op jit(solution)/shard_map/ppermute | solution.py:49
  430.9 1.9 convert_add_fusion
  434.3 11.2 %collective-permute-done.48 = bf16[384,768]{1,0:T(8,128)(2,1)} collective-permute-done((bf16[384,768]{1,0:T(8,128)(2,1)}, bf16[384,768]{1,0:T(8,128)(2,1)}, u32[]{:S(2)}, u32[]{:S(2)}) %collective-permute-start.48) | collective-permute-done | bytes 589856 | tf_op jit(solution)/shard_map/ppermute | solution.py:53
  446.7 1.5 pad_maximum_fusion.1
  449.6 2.1 add_convert_fusion.2
  453.8 11.0 %collective-permute-done.55 = bf16[384,768]{1,0:T(8,128)(2,1)} collective-permute-done((bf16[384,768]{1,0:T(8,128)(2,1)}, bf16[384,768]{1,0:T(8,128)(2,1)}, u32[]{:S(2)}, u32[]{:S(2)}) %collective-permute-start.55) | collective-permute-done | bytes 589856 | tf_op jit(solution)/shard_map/ppermute | solution.py:49
  467.0 1.4 convert_bitcast_fusion
  468.5 2.9 bitcast_convert_fusion
  471.4 2.3 add_convert_fusion.1
  474.5 2.6 collective-permute-start.58
  479.5 2.0 copy.113
  481.4 2.8 collective-permute-start.64
  484.2 21.4 %collective-permute-done.58 = bf16[96,777]{0,1:T(8,128)(2,1)} collective-permute-done((bf16[96,777]{0,1:T(8,128)(2,1)S(1)}, bf16[96,777]{0,1:T(8,128)(2,1)}, u32[]{:S(2)}, u32[]{:S(2)}) %collective-permute-start.58) | collective-permute-done | bytes 149216 | tf_op jit(solution)/shard_map/ppermute | solution.py:49
  507.1 3.8 collective-permute-start.62
  513.9 6.4 %final_rows.1 = f32[768,768]{1,0:T(8,128)} custom-call(s32[1]{0:T(128)} %bitcast.46.first, bf16[768,768]{1,0:T(8,128)(2,1)} %tokens.5, f32[2,768]{1,0:T(2,128)} %gains.7, f32[768,768]{1,0:T(8,128)} %get-tuple-element.269.grad_middle, bf16[2,768,768]{2,1,0:T(8,128)(2,1)} %get-tuple-element.245.kept, bf16[2,768,768]{2,1,0:T(8,128)(2,1)} %copy-done.3, ...), custom_call_target="tpu_custom_call" | custom-call | tf_op jit(solution)/shard_map/final_rows/pallas_call | solution.py:522
  (301 shorter events, 78.8 us)
Async XLA Ops:
  7.2 221.0 %all-gather.3.cloned.1.call-start = ((), (), s32[]{:S(2)}) async-start(), calls=%async_computation.2 | async-start | bytes 5898240 | tf_op jit(solution)/shard_map/all_gather | solution.py:983
  10.2 14.5 %collective-permute-start.3 = (bf16[384,768]{1,0:T(8,128)(2,1)}, bf16[384,768]{1,0:T(8,128)(2,1)}, u32[]{:S(2)}, u32[]{:S(2)}) collective-permute-start(bf16[384,768]{1,0:T(8,128)(2,1)} %get-tuple-element.144), channel_id=1, source_target_pairs={{0,2},{1,3},{2,0},{3,1},{4,6},{5,7},{6,4},{7,5},{8,10},{9,11},{10,... | collective-permute-start | bytes 1769480 | tf_op jit(solution)/shard_map/ppermute | solution.py:49
  12.6 14.1 %collective-permute-start.2 = (bf16[96,776]{0,1:T(8,128)(2,1)S(1)}, bf16[96,776]{0,1:T(8,128)(2,1)S(1)}, u32[]{:S(2)}, u32[]{:S(2)}) collective-permute-start(bf16[96,776]{0,1:T(8,128)(2,1)S(1)} %pad_maximum_fusion.17), channel_id=1, source_target_pairs={{0,12},{4,8},{8,4},{12,0},{1,13},{5,9},{9,5},{13,1},{2,14},{6,10},... | collective-permute-start | bytes 446984 | tf_op jit(solution)/shard_map/ppermute | solution.py:49
  12.6 18.1 %collective-permute-start.1 = (bf16[96,776]{0,1:T(8,128)(2,1)S(1)}, bf16[96,776]{0,1:T(8,128)(2,1)S(1)}, u32[]{:S(2)}, u32[]{:S(2)}) collective-permute-start(bf16[96,776]{0,1:T(8,128)(2,1)S(1)} %pad_maximum_fusion.17), channel_id=1, source_target_pairs={{0,8},{4,12},{8,0},{12,4},{1,9},{5,13},{9,1},{13,5},{2,10},{6,14},... | collective-permute-start | bytes 446984 | tf_op jit(solution)/shard_map/ppermute | solution.py:49
  14.0 16.8 %collective-permute-start = (bf16[96,776]{0,1:T(8,128)(2,1)S(1)}, bf16[96,776]{0,1:T(8,128)(2,1)S(1)}, u32[]{:S(2)}, u32[]{:S(2)}) collective-permute-start(bf16[96,776]{0,1:T(8,128)(2,1)S(1)} %pad_maximum_fusion.17), channel_id=1, source_target_pairs={{0,4},{4,0},{8,12},{12,8},{1,5},{5,1},{9,13},{13,9},{2,6},{6,2},{1... | collective-permute-start | bytes 446984 | tf_op jit(solution)/shard_map/ppermute | solution.py:49
  31.4 15.2 %collective-permute-start.6 = (bf16[1,4,96,776]{3,2,1,0:T(8,128)(2,1)S(1)}, bf16[1,4,96,776]{3,2,1,0:T(8,128)(2,1)S(1)}, u32[]{:S(2)}, u32[]{:S(2)}) collective-permute-start(bf16[1,4,96,776]{3,2,1,0:T(8,128)(2,1)S(1)} %copy.89), channel_id=1, source_target_pairs={{0,16},{16,0},{1,17},{17,1},{2,18},{18,2},{3,19},{19,3},{4,20},{20... | collective-permute-start | bytes 1787912 | tf_op jit(solution)/shard_map/ppermute | solution.py:49
  32.7 14.3 %collective-permute-start.4 = (bf16[384,768]{1,0:T(8,128)(2,1)}, bf16[384,768]{1,0:T(8,128)(2,1)}, u32[]{:S(2)}, u32[]{:S(2)}) collective-permute-start(bf16[384,768]{1,0:T(8,128)(2,1)} %get-tuple-element.145), channel_id=1, source_target_pairs={{0,4},{4,8},{8,12},{12,0},{1,5},{5,9},{9,13},{13,1},{2,6},{6,10},{... | collective-permute-start | bytes 1769480 | tf_op jit(solution)/shard_map/ppermute | solution.py:53
  34.2 13.0 %collective-permute-start.5 = (bf16[384,768]{1,0:T(8,128)(2,1)S(1)}, bf16[384,768]{1,0:T(8,128)(2,1)}, u32[]{:S(2)}, u32[]{:S(2)}) collective-permute-start(bf16[384,768]{1,0:T(8,128)(2,1)S(1)} %get-tuple-element.322), channel_id=1, source_target_pairs={{0,2},{1,3},{2,0},{3,1},{4,6},{5,7},{6,4},{7,5},{8,10},{9,11},{10,... | collective-permute-start | bytes 1769480 | tf_op jit(solution)/shard_map/ppermute | solution.py:49
  47.2 12.6 %collective-permute-start.7 = (bf16[384,768]{1,0:T(8,128)(2,1)}, bf16[384,768]{1,0:T(8,128)(2,1)}, u32[]{:S(2)}, u32[]{:S(2)}) collective-permute-start(bf16[384,768]{1,0:T(8,128)(2,1)} %collective-permute-done.4.rest_0_.rest_10_), channel_id=1, source_target_pairs={{0,4},{4,8},{8,12},{12,0},{1,5},{5,9},{9,13},{13,1},{2,6},{6,10},{... | collective-permute-start | bytes 1769480 | tf_op jit(solution)/shard_map/ppermute | solution.py:53
  59.9 193.2 %all-gather.5.cloned.1.call-start = ((), (), s32[]{:S(2)}) async-start(), calls=%async_computation.3 | async-start | bytes 5898240 | tf_op jit(solution)/shard_map/all_gather | solution.py:984
  59.9 28.3 %collective-permute-start.10 = (bf16[768,768]{1,0:T(8,128)(2,1)}, bf16[768,768]{1,0:T(8,128)(2,1)}, u32[]{:S(2)}, u32[]{:S(2)}) collective-permute-start(bf16[768,768]{1,0:T(8,128)(2,1)} %get-tuple-element.143.rest_0_.rest_4_), channel_id=1, source_target_pairs={{0,1},{1,0},{2,3},{3,2},{4,5},{5,4},{6,7},{7,6},{8,9},{9,8},{10,11... | collective-permute-start | bytes 3538952 | tf_op jit(solution)/shard_map/ppermute | solution.py:49
  64.9 21.5 %collective-permute-start.12 = (bf16[384,768]{1,0:T(8,128)(2,1)}, bf16[384,768]{1,0:T(8,128)(2,1)}, u32[]{:S(2)}, u32[]{:S(2)}) collective-permute-start(bf16[384,768]{1,0:T(8,128)(2,1)} %collective-permute-done.3.rest_3_.rest_7_), channel_id=1, source_target_pairs={{0,1},{1,0},{2,3},{3,2},{4,5},{5,4},{6,7},{7,6},{8,9},{9,8},{10,11... | collective-permute-start | bytes 1769480 | tf_op jit(solution)/shard_map/ppermute | solution.py:49
  65.1 14.8 %collective-permute-start.8 = (bf16[384,768]{1,0:T(8,128)(2,1)}, bf16[384,768]{1,0:T(8,128)(2,1)}, u32[]{:S(2)}, u32[]{:S(2)}) collective-permute-start(bf16[384,768]{1,0:T(8,128)(2,1)} %collective-permute-done.4.rest_0_.rest_10_), channel_id=1, source_target_pairs={{0,2},{1,3},{2,0},{3,1},{4,6},{5,7},{6,4},{7,5},{8,10},{9,11},{10,... | collective-permute-start | bytes 1769480 | tf_op jit(solution)/shard_map/ppermute | solution.py:49
  66.9 21.3 %collective-permute-start.11 = (bf16[384,768]{1,0:T(8,128)(2,1)}, bf16[384,768]{1,0:T(8,128)(2,1)}, u32[]{:S(2)}, u32[]{:S(2)}) collective-permute-start(bf16[384,768]{1,0:T(8,128)(2,1)} %collective-permute-done.5.rest_2_.rest_6_), channel_id=1, source_target_pairs={{0,1},{1,0},{2,3},{3,2},{4,5},{5,4},{6,7},{7,6},{8,9},{9,8},{10,11... | collective-permute-start | bytes 1769480 | tf_op jit(solution)/shard_map/ppermute | solution.py:49
  67.9 399.1 %reduce-scatter.5.cloned.1.call-start = ((), (), s32[]{:S(2)}) async-start(), calls=%async_computation.5 | async-start | bytes 5898240 | tf_op jit(solution)/shard_map/reduce_scatter | solution.py:1051
  79.9 41.5 %collective-permute-start.15 = (bf16[384,768]{1,0:T(8,128)(2,1)}, bf16[384,768]{1,0:T(8,128)(2,1)S(1)}, u32[]{:S(2)}, u32[]{:S(2)}) collective-permute-start(bf16[384,768]{1,0:T(8,128)(2,1)} %collective-permute-done.7.rest_0_.rest_14_), channel_id=1, source_target_pairs={{0,2},{1,3},{2,0},{3,1},{4,6},{5,7},{6,4},{7,5},{8,10},{9,11},{10,... | collective-permute-start | bytes 1769480 | tf_op jit(solution)/shard_map/ppermute | solution.py:49
  80.1 41.2 %collective-permute-start.9 = (bf16[384,768]{1,0:T(8,128)(2,1)}, bf16[384,768]{1,0:T(8,128)(2,1)S(1)}, u32[]{:S(2)}, u32[]{:S(2)}) collective-permute-start(bf16[384,768]{1,0:T(8,128)(2,1)} %collective-permute-done.7.rest_0_.rest_14_), channel_id=1, source_target_pairs={{0,4},{4,8},{8,12},{12,0},{1,5},{5,9},{9,13},{13,1},{2,6},{6,10},{... | collective-permute-start | bytes 1769480 | tf_op jit(solution)/shard_map/ppermute | solution.py:53
  86.4 42.4 %collective-permute-start.13 = (bf16[384,768]{1,0:T(8,128)(2,1)}, bf16[384,768]{1,0:T(8,128)(2,1)}, u32[]{:S(2)}, u32[]{:S(2)}) collective-permute-start(bf16[384,768]{1,0:T(8,128)(2,1)} %collective-permute-done.4.rest_0_.rest_10_), channel_id=1, source_target_pairs={{0,1},{1,0},{2,3},{3,2},{4,5},{5,4},{6,7},{7,6},{8,9},{9,8},{10,11... | collective-permute-start | bytes 1769480 | tf_op jit(solution)/shard_map/ppermute | solution.py:49
  121.3 10.9 %collective-permute-start.18 = (bf16[384,768]{1,0:T(8,128)(2,1)S(1)}, bf16[384,768]{1,0:T(8,128)(2,1)}, u32[]{:S(2)}, u32[]{:S(2)}) collective-permute-start(bf16[384,768]{1,0:T(8,128)(2,1)S(1)} %collective-permute-done.9.rest_0_.rest_18_), channel_id=1, source_target_pairs={{0,2},{1,3},{2,0},{3,1},{4,6},{5,7},{6,4},{7,5},{8,10},{9,11},{10,... | collective-permute-start | bytes 1769480 | tf_op jit(solution)/shard_map/ppermute | solution.py:49
  123.6 14.4 %collective-permute-start.14 = (bf16[384,768]{1,0:T(8,128)(2,1)}, bf16[384,768]{1,0:T(8,128)(2,1)}, u32[]{:S(2)}, u32[]{:S(2)}) collective-permute-start(bf16[384,768]{1,0:T(8,128)(2,1)} %collective-permute-done.8.rest_1_.rest_11_), channel_id=1, source_target_pairs={{0,1},{1,0},{2,3},{3,2},{4,5},{5,4},{6,7},{7,6},{8,9},{9,8},{10,11... | collective-permute-start | bytes 1769480 | tf_op jit(solution)/shard_map/ppermute | solution.py:49
  128.2 15.6 %collective-permute-start.16 = (bf16[384,768]{1,0:T(8,128)(2,1)}, bf16[384,768]{1,0:T(8,128)(2,1)}, u32[]{:S(2)}, u32[]{:S(2)}) collective-permute-start(bf16[384,768]{1,0:T(8,128)(2,1)} %collective-permute-done.7.rest_0_.rest_14_), channel_id=1, source_target_pairs={{0,1},{1,0},{2,3},{3,2},{4,5},{5,4},{6,7},{7,6},{8,9},{9,8},{10,11... | collective-permute-start | bytes 1769480 | tf_op jit(solution)/shard_map/ppermute | solution.py:49
  128.3 15.6 %collective-permute-start.17 = (bf16[384,768]{1,0:T(8,128)(2,1)S(1)}, bf16[384,768]{1,0:T(8,128)(2,1)}, u32[]{:S(2)}, u32[]{:S(2)}) collective-permute-start(bf16[384,768]{1,0:T(8,128)(2,1)S(1)} %collective-permute-done.15.rest_1_.rest_15_), channel_id=1, source_target_pairs={{0,1},{1,0},{2,3},{3,2},{4,5},{5,4},{6,7},{7,6},{8,9},{9,8},{10,11... | collective-permute-start | bytes 1769480 | tf_op jit(solution)/shard_map/ppermute | solution.py:49
  128.8 21.9 %collective-permute-start.19 = (bf16[384,768]{1,0:T(8,128)(2,1)S(1)}, bf16[384,768]{1,0:T(8,128)(2,1)}, u32[]{:S(2)}, u32[]{:S(2)}) collective-permute-start(bf16[384,768]{1,0:T(8,128)(2,1)S(1)} %collective-permute-done.9.rest_0_.rest_18_), channel_id=1, source_target_pairs={{0,1},{1,0},{2,3},{3,2},{4,5},{5,4},{6,7},{7,6},{8,9},{9,8},{10,11... | collective-permute-start | bytes 1769480 | tf_op jit(solution)/shard_map/ppermute | solution.py:49
  132.3 18.5 %collective-permute-start.20 = (bf16[384,768]{1,0:T(8,128)(2,1)}, bf16[384,768]{1,0:T(8,128)(2,1)}, u32[]{:S(2)}, u32[]{:S(2)}) collective-permute-start(bf16[384,768]{1,0:T(8,128)(2,1)} %collective-permute-done.18.rest_1_.rest_19_), channel_id=1, source_target_pairs={{0,1},{1,0},{2,3},{3,2},{4,5},{5,4},{6,7},{7,6},{8,9},{9,8},{10,11... | collective-permute-start | bytes 1769480 | tf_op jit(solution)/shard_map/ppermute | solution.py:49
  138.0 10.9 %collective-permute-start.24 = (bf16[1,192,768]{1,2,0:T(8,128)(2,1)S(1)}, bf16[1,192,768]{1,2,0:T(8,128)(2,1)S(1)}, u32[]{:S(2)}, u32[]{:S(2)}) collective-permute-start(bf16[1,192,768]{1,2,0:T(8,128)(2,1)S(1)} %bitcast.92), channel_id=1, source_target_pairs={{0,2},{1,3},{2,0},{3,1},{4,6},{5,7},{6,4},{7,5},{8,10},{9,11},{10,... | collective-permute-start | bytes 884744 | tf_op jit(solution)/shard_map/ppermute | solution.py:49
  150.1 34.2 %collective-permute-start.25 = (bf16[2,192,768]{2,1,0:T(8,128)(2,1)}, bf16[2,192,768]{2,1,0:T(8,128)(2,1)}, u32[]{:S(2)}, u32[]{:S(2)}) collective-permute-start(bf16[2,192,768]{2,1,0:T(8,128)(2,1)} %copy.99), channel_id=1, source_target_pairs={{0,1},{1,0},{2,3},{3,2},{4,5},{5,4},{6,7},{7,6},{8,9},{9,8},{10,11... | collective-permute-start | bytes 1769480 | tf_op jit(solution)/shard_map/ppermute | solution.py:49
  178.1 8.1 %collective-permute-start.21 = (bf16[192,768]{1,0:T(8,128)(2,1)}, bf16[192,768]{1,0:T(8,128)(2,1)S(1)}, u32[]{:S(2)}, u32[]{:S(2)}) collective-permute-start(bf16[192,768]{1,0:T(8,128)(2,1)} %get-tuple-element.165.rest_9_), channel_id=1, source_target_pairs={{0,1},{1,0},{2,3},{3,2},{4,5},{5,4},{6,7},{7,6},{8,9},{9,8},{10,11... | collective-permute-start | bytes 884744 | tf_op jit(solution)/shard_map/ppermute | solution.py:49
  178.1 8.5 %collective-permute-start.22 = (bf16[192,768]{1,0:T(8,128)(2,1)}, bf16[192,768]{1,0:T(8,128)(2,1)S(1)}, u32[]{:S(2)}, u32[]{:S(2)}) collective-permute-start(bf16[192,768]{1,0:T(8,128)(2,1)} %get-tuple-element.166.rest_10_), channel_id=1, source_target_pairs={{0,2},{1,3},{2,0},{3,1},{4,6},{5,7},{6,4},{7,5},{8,10},{9,11},{10,... | collective-permute-start | bytes 884744 | tf_op jit(solution)/shard_map/ppermute | solution.py:49
  179.3 14.6 %collective-permute-start.23 = (bf16[192,768]{1,0:T(8,128)(2,1)}, bf16[192,768]{1,0:T(8,128)(2,1)S(1)}, u32[]{:S(2)}, u32[]{:S(2)}) collective-permute-start(bf16[192,768]{1,0:T(8,128)(2,1)} %get-tuple-element.167.rest_11_), channel_id=1, source_target_pairs={{0,3},{1,2},{2,1},{3,0},{4,7},{5,6},{6,5},{7,4},{8,11},{9,10},{10,... | collective-permute-start | bytes 884744 | tf_op jit(solution)/shard_map/ppermute | solution.py:49
  205.7 10.2 %collective-permute-start.27 = (bf16[240,768]{1,0:T(8,128)(2,1)S(1)}, bf16[240,768]{1,0:T(8,128)(2,1)S(1)}, u32[]{:S(2)}, u32[]{:S(2)}) collective-permute-start(bf16[240,768]{1,0:T(8,128)(2,1)S(1)} %pad_maximum_fusion.5), channel_id=1, source_target_pairs={{0,2},{1,3},{2,0},{3,1},{16,18},{17,19},{18,16},{19,17},{4,6},{5,7... | collective-permute-start | bytes 1105928 | tf_op jit(solution)/shard_map/ppermute | solution.py:49
  206.8 10.2 %collective-permute-start.28 = (bf16[240,768]{1,0:T(8,128)(2,1)S(1)}, bf16[240,768]{1,0:T(8,128)(2,1)S(1)}, u32[]{:S(2)}, u32[]{:S(2)}) collective-permute-start(bf16[240,768]{1,0:T(8,128)(2,1)S(1)} %pad_maximum_fusion.6), channel_id=1, source_target_pairs={{0,16},{1,17},{2,18},{3,19},{16,0},{17,1},{18,2},{19,3},{4,20},{5,... | collective-permute-start | bytes 1105928 | tf_op jit(solution)/shard_map/ppermute | solution.py:49
  207.9 16.5 %collective-permute-start.29 = (bf16[240,768]{1,0:T(8,128)(2,1)S(1)}, bf16[240,768]{1,0:T(8,128)(2,1)S(1)}, u32[]{:S(2)}, u32[]{:S(2)}) collective-permute-start(bf16[240,768]{1,0:T(8,128)(2,1)S(1)} %pad_maximum_fusion.7), channel_id=1, source_target_pairs={{0,18},{1,19},{2,16},{3,17},{16,2},{17,3},{18,0},{19,1},{4,22},{5,... | collective-permute-start | bytes 1105928 | tf_op jit(solution)/shard_map/ppermute | solution.py:49
  225.3 16.9 %collective-permute-start.31 = (bf16[240,768]{1,0:T(8,128)(2,1)S(1)}, bf16[240,768]{1,0:T(8,128)(2,1)S(1)}, u32[]{:S(2)}, u32[]{:S(2)}) collective-permute-start(bf16[240,768]{1,0:T(8,128)(2,1)S(1)} %pad_maximum_fusion.8), channel_id=1, source_target_pairs={{0,2},{1,3},{2,0},{3,1},{16,18},{17,19},{18,16},{19,17},{4,6},{5,7... | collective-permute-start | bytes 1105928 | tf_op jit(solution)/shard_map/ppermute | solution.py:49
  226.5 15.7 %collective-permute-start.32 = (bf16[240,768]{1,0:T(8,128)(2,1)S(1)}, bf16[240,768]{1,0:T(8,128)(2,1)S(1)}, u32[]{:S(2)}, u32[]{:S(2)}) collective-permute-start(bf16[240,768]{1,0:T(8,128)(2,1)S(1)} %pad_maximum_fusion.9), channel_id=1, source_target_pairs={{0,16},{1,17},{2,18},{3,19},{16,0},{17,1},{18,2},{19,3},{4,20},{5,... | collective-permute-start | bytes 1105928 | tf_op jit(solution)/shard_map/ppermute | solution.py:49
  227.2 15.0 %collective-permute-start.33 = (bf16[240,768]{1,0:T(8,128)(2,1)S(1)}, bf16[240,768]{1,0:T(8,128)(2,1)S(1)}, u32[]{:S(2)}, u32[]{:S(2)}) collective-permute-start(bf16[240,768]{1,0:T(8,128)(2,1)S(1)} %pad_maximum_fusion.10), channel_id=1, source_target_pairs={{0,18},{1,19},{2,16},{3,17},{16,2},{17,3},{18,0},{19,1},{4,22},{5,... | collective-permute-start | bytes 1105928 | tf_op jit(solution)/shard_map/ppermute | solution.py:49
  253.0 215.4 %reduce-scatter.3.cloned.1.call-start = ((), (), s32[]{:S(2)}) async-start(), calls=%async_computation.4 | async-start | bytes 5898240 | tf_op jit(solution)/shard_map/reduce_scatter | solution.py:1066
  269.7 19.2 %collective-permute-start.35 = (bf16[240,768]{1,0:T(8,128)(2,1)S(1)}, bf16[240,768]{1,0:T(8,128)(2,1)S(1)}, u32[]{:S(2)}, u32[]{:S(2)}) collective-permute-start(bf16[240,768]{1,0:T(8,128)(2,1)S(1)} %pad_maximum_fusion.11), channel_id=1, source_target_pairs={{0,2},{1,3},{2,0},{3,1},{16,18},{17,19},{18,16},{19,17},{4,6},{5,7... | collective-permute-start | bytes 1105928 | tf_op jit(solution)/shard_map/ppermute | solution.py:49
  269.8 19.1 %collective-permute-start.36 = (bf16[240,768]{1,0:T(8,128)(2,1)S(1)}, bf16[240,768]{1,0:T(8,128)(2,1)S(1)}, u32[]{:S(2)}, u32[]{:S(2)}) collective-permute-start(bf16[240,768]{1,0:T(8,128)(2,1)S(1)} %pad_maximum_fusion.12), channel_id=1, source_target_pairs={{0,16},{1,17},{2,18},{3,19},{16,0},{17,1},{18,2},{19,3},{4,20},{5,... | collective-permute-start | bytes 1105928 | tf_op jit(solution)/shard_map/ppermute | solution.py:49
  270.5 18.4 %collective-permute-start.37 = (bf16[240,768]{1,0:T(8,128)(2,1)S(1)}, bf16[240,768]{1,0:T(8,128)(2,1)S(1)}, u32[]{:S(2)}, u32[]{:S(2)}) collective-permute-start(bf16[240,768]{1,0:T(8,128)(2,1)S(1)} %pad_maximum_fusion.13), channel_id=1, source_target_pairs={{0,18},{1,19},{2,16},{3,17},{16,2},{17,3},{18,0},{19,1},{4,22},{5,... | collective-permute-start | bytes 1105928 | tf_op jit(solution)/shard_map/ppermute | solution.py:49
  292.4 10.0 %collective-permute-start.39 = (bf16[240,768]{1,0:T(8,128)(2,1)S(1)}, bf16[240,768]{1,0:T(8,128)(2,1)S(1)}, u32[]{:S(2)}, u32[]{:S(2)}) collective-permute-start(bf16[240,768]{1,0:T(8,128)(2,1)S(1)} %pad_maximum_fusion.14), channel_id=1, source_target_pairs={{0,2},{1,3},{2,0},{3,1},{16,18},{17,19},{18,16},{19,17},{4,6},{5,7... | collective-permute-start | bytes 1105928 | tf_op jit(solution)/shard_map/ppermute | solution.py:49
  292.5 9.8 %collective-permute-start.40 = (bf16[240,768]{1,0:T(8,128)(2,1)S(1)}, bf16[240,768]{1,0:T(8,128)(2,1)S(1)}, u32[]{:S(2)}, u32[]{:S(2)}) collective-permute-start(bf16[240,768]{1,0:T(8,128)(2,1)S(1)} %pad_maximum_fusion.15), channel_id=1, source_target_pairs={{0,16},{1,17},{2,18},{3,19},{16,0},{17,1},{18,2},{19,3},{4,20},{5,... | collective-permute-start | bytes 1105928 | tf_op jit(solution)/shard_map/ppermute | solution.py:49
  293.2 16.9 %collective-permute-start.41 = (bf16[240,768]{1,0:T(8,128)(2,1)S(1)}, bf16[240,768]{1,0:T(8,128)(2,1)S(1)}, u32[]{:S(2)}, u32[]{:S(2)}) collective-permute-start(bf16[240,768]{1,0:T(8,128)(2,1)S(1)} %pad_maximum_fusion.16), channel_id=1, source_target_pairs={{0,18},{1,19},{2,16},{3,17},{16,2},{17,3},{18,0},{19,1},{4,22},{5,... | collective-permute-start | bytes 1105928 | tf_op jit(solution)/shard_map/ppermute | solution.py:49
  319.5 16.2 %collective-permute-start.42 = (bf16[192,768]{1,0:T(8,128)(2,1)}, bf16[192,768]{1,0:T(8,128)(2,1)S(1)}, u32[]{:S(2)}, u32[]{:S(2)}) collective-permute-start(bf16[192,768]{1,0:T(8,128)(2,1)} %get-tuple-element.210), channel_id=1, source_target_pairs={{0,1},{1,0},{2,3},{3,2},{4,5},{5,4},{6,7},{7,6},{8,9},{9,8},{10,11... | collective-permute-start | bytes 884744 | tf_op jit(solution)/shard_map/ppermute | solution.py:49
  321.1 14.7 %collective-permute-start.43 = (bf16[192,768]{1,0:T(8,128)(2,1)}, bf16[192,768]{1,0:T(8,128)(2,1)S(1)}, u32[]{:S(2)}, u32[]{:S(2)}) collective-permute-start(bf16[192,768]{1,0:T(8,128)(2,1)} %get-tuple-element.211), channel_id=1, source_target_pairs={{0,2},{1,3},{2,0},{3,1},{4,6},{5,7},{6,4},{7,5},{8,10},{9,11},{10,... | collective-permute-start | bytes 884744 | tf_op jit(solution)/shard_map/ppermute | solution.py:49
  322.5 14.3 %collective-permute-start.44 = (bf16[192,768]{1,0:T(8,128)(2,1)}, bf16[192,768]{1,0:T(8,128)(2,1)S(1)}, u32[]{:S(2)}, u32[]{:S(2)}) collective-permute-start(bf16[192,768]{1,0:T(8,128)(2,1)} %get-tuple-element.212), channel_id=1, source_target_pairs={{0,3},{1,2},{2,1},{3,0},{4,7},{5,6},{6,5},{7,4},{8,11},{9,10},{10,... | collective-permute-start | bytes 884744 | tf_op jit(solution)/shard_map/ppermute | solution.py:49
  380.9 6.0 %collective-permute-start.45 = (bf16[768,768]{1,0:T(8,128)(2,1)}, bf16[768,768]{1,0:T(8,128)(2,1)S(1)}, u32[]{:S(2)}, u32[]{:S(2)}) collective-permute-start(bf16[768,768]{1,0:T(8,128)(2,1)} %get-tuple-element.223), channel_id=1, source_target_pairs={{0,1},{1,0},{2,3},{3,2},{4,5},{5,4},{6,7},{7,6},{8,9},{9,8},{10,11... | collective-permute-start | bytes 3538952 | tf_op jit(solution)/shard_map/ppermute | solution.py:49
  388.0 16.1 %collective-permute-start.46 = (bf16[384,768]{1,0:T(8,128)(2,1)S(1)}, bf16[384,768]{1,0:T(8,128)(2,1)}, u32[]{:S(2)}, u32[]{:S(2)}) collective-permute-start(bf16[384,768]{1,0:T(8,128)(2,1)S(1)} %slice.283), channel_id=1, source_target_pairs={{0,2},{1,3},{2,0},{3,1},{4,6},{5,7},{6,4},{7,5},{8,10},{9,11},{10,... | collective-permute-start | bytes 1769480 | tf_op jit(solution)/shard_map/ppermute | solution.py:49
  411.4 5.7 %collective-permute-start.51 = (bf16[2,768,768]{2,1,0:T(8,128)(2,1)}, bf16[2,768,768]{2,1,0:T(8,128)(2,1)S(1)}, u32[]{:S(2)}, u32[]{:S(2)}) collective-permute-start(bf16[2,768,768]{2,1,0:T(8,128)(2,1)} %get-tuple-element.246), channel_id=1, source_target_pairs={{0,1},{1,0},{2,3},{3,2},{4,5},{5,4},{6,7},{7,6},{8,9},{9,8},{10,11... | collective-permute-start | bytes 7077896 | tf_op jit(solution)/shard_map/ppermute | solution.py:49
  414.0 14.5 %collective-permute-start.49 = (bf16[384,768]{1,0:T(8,128)(2,1)S(1)}, bf16[384,768]{1,0:T(8,128)(2,1)S(1)}, u32[]{:S(2)}, u32[]{:S(2)}) collective-permute-start(bf16[384,768]{1,0:T(8,128)(2,1)S(1)} %slice.282), channel_id=1, source_target_pairs={{0,2},{1,3},{2,0},{3,1},{4,6},{5,7},{6,4},{7,5},{8,10},{9,11},{10,... | collective-permute-start | bytes 1769480 | tf_op jit(solution)/shard_map/ppermute | solution.py:49
  414.8 16.0 %collective-permute-start.53 = (bf16[768,768]{1,0:T(8,128)(2,1)}, bf16[768,768]{1,0:T(8,128)(2,1)}, u32[]{:S(2)}, u32[]{:S(2)}) collective-permute-start(bf16[768,768]{1,0:T(8,128)(2,1)} %get-tuple-element.250), channel_id=1, source_target_pairs={{0,1},{1,0},{2,3},{3,2},{4,5},{5,4},{6,7},{7,6},{8,9},{9,8},{10,11... | collective-permute-start | bytes 3538952 | tf_op jit(solution)/shard_map/ppermute | solution.py:49
  429.4 17.1 %collective-permute-start.52 = (bf16[480,768]{1,0:T(8,128)(2,1)}, bf16[480,768]{1,0:T(8,128)(2,1)S(1)}, u32[]{:S(2)}, u32[]{:S(2)}) collective-permute-start(bf16[480,768]{1,0:T(8,128)(2,1)} %pad_maximum_fusion.4), channel_id=1, source_target_pairs={{0,2},{1,3},{2,0},{3,1},{4,6},{5,7},{6,4},{7,5},{8,10},{9,11},{10,... | collective-permute-start | bytes 2211848 | tf_op jit(solution)/shard_map/ppermute | solution.py:49
  430.1 15.4 %collective-permute-start.48 = (bf16[384,768]{1,0:T(8,128)(2,1)}, bf16[384,768]{1,0:T(8,128)(2,1)}, u32[]{:S(2)}, u32[]{:S(2)}) collective-permute-start(bf16[384,768]{1,0:T(8,128)(2,1)} %fusion.4), channel_id=1, source_target_pairs={{0,12},{4,0},{8,4},{12,8},{1,13},{5,1},{9,5},{13,9},{2,14},{6,2},{... | collective-permute-start | bytes 1769480 | tf_op jit(solution)/shard_map/ppermute | solution.py:53
  448.3 17.1 %collective-permute-start.56 = (bf16[4,96,777]{2,1,0:T(8,128)(2,1)S(1)}, bf16[4,96,777]{2,1,0:T(8,128)(2,1)S(1)}, u32[]{:S(2)}, u32[]{:S(2)}) collective-permute-start(bf16[4,96,777]{2,1,0:T(8,128)(2,1)S(1)} %get-tuple-element.319), channel_id=1, source_target_pairs={{0,16},{16,0},{1,17},{17,1},{2,18},{18,2},{3,19},{19,3},{4,20},{20... | collective-permute-start | bytes 1790216 | tf_op jit(solution)/shard_map/ppermute | solution.py:49
  451.7 13.1 %collective-permute-start.55 = (bf16[384,768]{1,0:T(8,128)(2,1)}, bf16[384,768]{1,0:T(8,128)(2,1)}, u32[]{:S(2)}, u32[]{:S(2)}) collective-permute-start(bf16[384,768]{1,0:T(8,128)(2,1)} %slice.281), channel_id=1, source_target_pairs={{0,2},{1,3},{2,0},{3,1},{4,6},{5,7},{6,4},{7,5},{8,10},{9,11},{10,... | collective-permute-start | bytes 1769480 | tf_op jit(solution)/shard_map/ppermute | solution.py:49
  453.7 17.7 %collective-permute-start.54 = (bf16[384,768]{1,0:T(8,128)(2,1)}, bf16[384,768]{1,0:T(8,128)(2,1)}, u32[]{:S(2)}, u32[]{:S(2)}) collective-permute-start(bf16[384,768]{1,0:T(8,128)(2,1)} %add_convert_fusion.2), channel_id=1, source_target_pairs={{0,12},{4,0},{8,4},{12,8},{1,13},{5,1},{9,5},{13,9},{2,14},{6,2},{... | collective-permute-start | bytes 1769480 | tf_op jit(solution)/shard_map/ppermute | solution.py:53
  464.8 46.8 %collective-permute-start.63 = (bf16[480,768]{1,0:T(8,128)(2,1)}, bf16[480,768]{1,0:T(8,128)(2,1)}, u32[]{:S(2)}, u32[]{:S(2)}) collective-permute-start(bf16[480,768]{1,0:T(8,128)(2,1)} %slice_bitcast_fusion), channel_id=1, source_target_pairs={{0,2},{1,3},{2,0},{3,1},{4,6},{5,7},{6,4},{7,5},{8,10},{9,11},{10,... | collective-permute-start | bytes 2211848 | tf_op jit(solution)/shard_map/ppermute | solution.py:49
  474.4 7.0 %collective-permute-start.57 = (bf16[96,777]{0,1:T(8,128)(2,1)}, bf16[96,777]{0,1:T(8,128)(2,1)}, u32[]{:S(2)}, u32[]{:S(2)}) collective-permute-start(bf16[96,777]{0,1:T(8,128)(2,1)} %get-tuple-element.324), channel_id=1, source_target_pairs={{0,4},{4,0},{8,12},{12,8},{1,5},{5,1},{9,13},{13,9},{2,6},{6,2},{1... | collective-permute-start | bytes 447560 | tf_op jit(solution)/shard_map/ppermute | solution.py:49
  474.4 9.8 %collective-permute-start.59 = (bf16[96,777]{0,1:T(8,128)(2,1)S(1)}, bf16[96,777]{0,1:T(8,128)(2,1)}, u32[]{:S(2)}, u32[]{:S(2)}) collective-permute-start(bf16[96,777]{0,1:T(8,128)(2,1)S(1)} %get-tuple-element.325), channel_id=1, source_target_pairs={{0,12},{4,8},{8,4},{12,0},{1,13},{5,9},{9,5},{13,1},{2,14},{6,10},... | collective-permute-start | bytes 447560 | tf_op jit(solution)/shard_map/ppermute | solution.py:49
  474.5 31.2 %collective-permute-start.58 = (bf16[96,777]{0,1:T(8,128)(2,1)S(1)}, bf16[96,777]{0,1:T(8,128)(2,1)}, u32[]{:S(2)}, u32[]{:S(2)}) collective-permute-start(bf16[96,777]{0,1:T(8,128)(2,1)S(1)} %get-tuple-element.326), channel_id=1, source_target_pairs={{0,8},{4,12},{8,0},{12,4},{1,9},{5,13},{9,1},{13,5},{2,10},{6,14},... | collective-permute-start | bytes 447560 | tf_op jit(solution)/shard_map/ppermute | solution.py:49
  478.2 34.9 %collective-permute-start.65 = (bf16[384,768]{1,0:T(8,128)(2,1)S(1)}, bf16[384,768]{1,0:T(8,128)(2,1)}, u32[]{:S(2)}, u32[]{:S(2)}) collective-permute-start(bf16[384,768]{1,0:T(8,128)(2,1)S(1)} %copy-done.15), channel_id=1, source_target_pairs={{2,12},{3,13},{6,0},{7,1},{10,4},{11,5},{14,8},{15,9},{18,28},{19,... | collective-permute-start | bytes 1769480 | tf_op jit(solution)/shard_map/ppermute | solution.py:1144
  481.4 31.7 %collective-permute-start.64 = (bf16[384,768]{1,0:T(8,128)(2,1)S(1)}, bf16[384,768]{1,0:T(8,128)(2,1)S(1)}, u32[]{:S(2)}, u32[]{:S(2)}) collective-permute-start(bf16[384,768]{1,0:T(8,128)(2,1)S(1)} %copy-done.15), channel_id=1, source_target_pairs={{0,12},{1,13},{4,0},{5,1},{8,4},{9,5},{12,8},{13,9},{16,28},{17,29... | collective-permute-start | bytes 1769480 | tf_op jit(solution)/shard_map/ppermute | solution.py:1144
  507.1 13.1 %collective-permute-start.62 = (bf16[96,10]{0,1:T(8,128)(2,1)S(1)}, bf16[96,10]{0,1:T(8,128)(2,1)S(1)}, u32[]{:S(2)}, u32[]{:S(2)}) collective-permute-start(bf16[96,10]{0,1:T(8,128)(2,1)S(1)} %fusion.17), channel_id=1, source_target_pairs={{0,3},{1,2},{2,1},{3,0},{4,7},{5,6},{6,5},{7,4},{8,11},{9,10},{10,... | collective-permute-start | bytes 5768 | tf_op jit(solution)/shard_map/ppermute | solution.py:49
  510.9 9.4 %collective-permute-start.61 = (bf16[96,10]{0,1:T(8,128)(2,1)S(1)}, bf16[96,10]{0,1:T(8,128)(2,1)S(1)}, u32[]{:S(2)}, u32[]{:S(2)}) collective-permute-start(bf16[96,10]{0,1:T(8,128)(2,1)S(1)} %fusion.17), channel_id=1, source_target_pairs={{0,2},{1,3},{2,0},{3,1},{4,6},{5,7},{6,4},{7,5},{8,10},{9,11},{10,... | collective-permute-start | bytes 5768 | tf_op jit(solution)/shard_map/ppermute | solution.py:49
  511.6 8.7 %collective-permute-start.60 = (bf16[96,10]{0,1:T(8,128)(2,1)S(1)}, bf16[96,10]{0,1:T(8,128)(2,1)S(1)}, u32[]{:S(2)}, u32[]{:S(2)}) collective-permute-start(bf16[96,10]{0,1:T(8,128)(2,1)S(1)} %fusion.17), channel_id=1, source_target_pairs={{0,1},{1,0},{2,3},{3,2},{4,5},{5,4},{6,7},{7,6},{8,9},{9,8},{10,11... | collective-permute-start | bytes 5768 | tf_op jit(solution)/shard_map/ppermute | solution.py:49
  (52 other events, 319.1 us)
Sparse Core Ops, SparseCore 0:
  60.0 102.7 all-gather.2
  164.4 87.9 all-gather.4
  254.7 85.7 reduce-scatter.4
  342.6 85.7 reduce-scatter.2
